TPU v7x, 512 devices: a whole 4x8x8 slice. The times are simulated.
512 devices in a mesh: dp: 8 (over x, y_lo), seq: 64 (over y_hi, z, core).
Axes of the slice: x: 4, y: 8 (y_hi: 4, y_lo: 2; y = y_hi * 2 + y_lo), z: 8, core: 2. Of those that a mesh axis runs over, the one named last changes fastest.
Arguments:
- tokens: bfloat16 [8, 64, 128, 1152], P('dp', 'seq'), may hold values from -6 to 6
- spatial_qkv: bfloat16 [8, 64, 128, 1728], P('dp', 'seq'), may hold values from -160 to 160
- spatial_out_weight: bfloat16 [576, 1152], P('seq'), may hold values from -0.25 to 0.25
- temporal_qkv_weight: bfloat16 [1152, 1728], P(None, 'seq'), may hold values from -8 to 8
- temporal_out_weight: bfloat16 [576, 1152], P('seq'), may hold values from -0.25 to 0.25
- modulation: float32 [8, 4, 1152], P('dp'), may hold values from -3 to 3
- cotangent: bfloat16 [8, 64, 128, 1152], P('dp', 'seq'), may hold values from -30 to 30
Outputs:
- token_grad: bfloat16 [8, 64, 128, 1152], P('dp', 'seq')
- qkv_grad: bfloat16 [8, 64, 128, 1728], P('dp', 'seq')
- modulation_grad: float32 [8, 4, 1152], P('dp')
- out_weight_grad: float32 [576, 1152], P('seq')
All inputs are finite; a program needn't handle non-finite values.
Results may differ from a plain program's by a relative error of at most 0.025.
Values may be sent and summed in bfloat16 or wider, within the bound.
No kernel may reach another device: no remote copies, remote signals or barrier semaphores. Data moves between devices by JAX's collectives and lax.ppermute only.
A program may use at most 64 MiB of HBM per device.

v0:
```python
import math

import jax
import jax.numpy as jnp
from jax import lax
from jax.sharding import PartitionSpec as P

HEADS = 8
HS = 72
ATT = 576


def spatial_block(states, packed, gate_row, out_weight):
    groups, length, _ = packed.shape
    queries = packed[..., :ATT].reshape(groups, length, HEADS, HS)
    keys_part = packed[..., ATT : 2 * ATT].reshape(groups, length, HEADS, HS)
    values_part = packed[..., 2 * ATT :].reshape(groups, length, HEADS, HS)
    scores = jnp.einsum(
        "gqhe,gkhe->ghqk", queries, keys_part, preferred_element_type=jnp.float32
    ) * (1.0 / math.sqrt(HS))
    row_max = lax.stop_gradient(jnp.max(scores, -1, keepdims=True))
    weights = jnp.exp(scores - row_max)
    probabilities = (weights / jnp.sum(weights, -1, keepdims=True)).astype(jnp.bfloat16)
    mixture = jnp.einsum(
        "ghqk,gkhe->gqhe", probabilities, values_part, preferred_element_type=jnp.float32
    )
    mixture = mixture.astype(jnp.bfloat16).reshape(groups * length, ATT)
    project = jnp.dot(mixture, out_weight, preferred_element_type=jnp.float32).reshape(states.shape)
    return (states.astype(jnp.float32) + gate_row * project).astype(jnp.bfloat16)


def temporal_norm(states, shift_row, scale_row, weight):
    average = jnp.mean(states, -1, keepdims=True)
    centered = states - average
    variance = jnp.mean(centered * centered, -1, keepdims=True)
    normed = (centered * lax.rsqrt(variance + 1e-06) * (1.0 + scale_row) + shift_row).astype(
        jnp.bfloat16
    )
    flattened = normed.reshape(-1, states.shape[-1])
    packed = jnp.dot(flattened, weight, preferred_element_type=jnp.float32).astype(jnp.bfloat16)
    return packed.reshape(states.shape[:-1] + (3 * ATT,))


def temporal_attend(packed):
    frames, places, _ = packed.shape
    queries = packed[..., :ATT].reshape(frames, places, HEADS, HS)
    keys_part = packed[..., ATT : 2 * ATT].reshape(frames, places, HEADS, HS)
    values_part = packed[..., 2 * ATT :].reshape(frames, places, HEADS, HS)
    scores = jnp.einsum(
        "fphe,gphe->phfg", queries, keys_part, preferred_element_type=jnp.float32
    ) * (1.0 / math.sqrt(HS))
    row_max = lax.stop_gradient(jnp.max(scores, -1, keepdims=True))
    weights = jnp.exp(scores - row_max)
    probabilities = (weights / jnp.sum(weights, -1, keepdims=True)).astype(jnp.bfloat16)
    mixture = jnp.einsum(
        "phfg,gphe->fphe", probabilities, values_part, preferred_element_type=jnp.float32
    )
    return mixture.astype(jnp.bfloat16).reshape(frames, places, ATT)


def temporal_out(states, mixture, gate_row, weight):
    project = jnp.dot(mixture.reshape(-1, ATT), weight, preferred_element_type=jnp.float32)
    return states + gate_row * project.reshape(states.shape)


def temporal_full(states, shift_row, scale_row, gate_row, qkv_weight, out_weight):
    packed = temporal_norm(states, shift_row, scale_row, qkv_weight)
    mixture = temporal_attend(packed)
    return (temporal_out(states, mixture, gate_row, out_weight), mixture)


def body(
    tokens,
    spatial_qkv,
    spatial_out_weight,
    temporal_qkv_weight,
    temporal_out_weight,
    modulation,
    cotangent,
):
    out_spatial, qkv_weight, out_temporal = (
        lax.all_gather(spatial_out_weight, "seq", axis=0, tiled=True),
        lax.all_gather(temporal_qkv_weight, "seq", axis=1, tiled=True),
        lax.all_gather(temporal_out_weight, "seq", axis=0, tiled=True),
    )
    width = tokens.shape[3]
    factors = modulation[0]
    gate_spatial = factors[0]
    shift_row = factors[1]
    scale_row = factors[2]
    gate_temporal = factors[3]

    def spatial_part(states_in, packed_in, gate_in):
        return spatial_block(states_in, packed_in, gate_in, out_spatial)

    hidden, spatial_back = jax.vjp(spatial_part, tokens[0], spatial_qkv[0], gate_spatial)
    arrived = lax.all_to_all(hidden[None], "seq", split_axis=2, concat_axis=1, tiled=True)[0]

    def temporal_part(states_in, shift_in, scale_in, gate_in):
        return temporal_full(states_in, shift_in, scale_in, gate_in, qkv_weight, out_temporal)

    result, temporal_back, mixture = jax.vjp(
        temporal_part,
        arrived.astype(jnp.float32),
        shift_row,
        scale_row,
        gate_temporal,
        has_aux=True,
    )
    incoming = lax.all_to_all(cotangent, "seq", split_axis=2, concat_axis=1, tiled=True)[0].astype(
        jnp.float32
    )
    state_grad, shift_grad, scale_grad, gate_grad = temporal_back(incoming)
    hidden_grad = lax.all_to_all(
        state_grad.astype(jnp.bfloat16)[None], "seq", split_axis=1, concat_axis=2, tiled=True
    )[0]
    token_grad, packed_grad_spatial, gate_spatial_grad = spatial_back(hidden_grad)
    factor_grads = jnp.stack([gate_spatial_grad, shift_grad, scale_grad, gate_grad])[None]
    modulation_grad = lax.psum(factor_grads, "seq")
    scaled = (incoming * gate_temporal).astype(jnp.bfloat16).reshape(-1, width)
    mixed_flat = mixture.reshape(-1, mixture.shape[-1])
    row_count = temporal_out_weight.shape[0]
    contract = (((0,), (0,)), ((), ()))
    local_term = lax.dot_general(mixed_flat, scaled, contract, preferred_element_type=jnp.float32)
    total = lax.psum(local_term, ("dp", "seq"))
    weight_grad = lax.dynamic_slice_in_dim(total, lax.axis_index("seq") * row_count, row_count, 0)
    return (token_grad[None], packed_grad_spatial[None], modulation_grad, weight_grad)


def solution(mesh):
    return jax.shard_map(
        body,
        mesh=mesh,
        in_specs=(
            P("dp", "seq", None, None),
            P("dp", "seq", None, None),
            P("seq", None),
            P(None, "seq"),
            P("seq", None),
            P("dp", None, None),
            P("dp", "seq", None, None),
        ),
        out_specs=(
            P("dp", "seq", None, None),
            P("dp", "seq", None, None),
            P("dp", None, None),
            P("seq", None),
        ),
        check_vma=False,
    )
```

profile of v0, /device:TPU:1, one launch (start us, length us, event | category | flops | bytes accessed | tf_op | source)
XLA Modules:
  0.0 621.3 jit_solution(7220134669623110811)
XLA Ops:
  9.4 1.5 copy.281
  11.4 2.4 reduce.22
  14.6 17.6 %all-to-all-start = ((bf16[64,2,1152]{2,1,0:T(2,128)(2,1)}), bf16[64,2,1152]{2,1,0:T(2,128)(2,1)S(1)}, u32[]{:S(2)}, u32[]{:S(2)}) async-start(bf16[64,2,1152]{2,1,0:T(2,128)(2,1)} %reshape.432), calls=%async_computation | async-start | bytes 589824 | tf_op jit(solution)/shard_map/all_to_all | solution.py:110
  35.3 11.9 %all-to-all-done = bf16[64,2,1152]{2,1,0:T(2,128)(2,1)S(1)} async-done(((bf16[64,2,1152]{2,1,0:T(2,128)(2,1)}), bf16[64,2,1152]{2,1,0:T(2,128)(2,1)S(1)}, u32[]{:S(2)}, u32[]{:S(2)}) %all-to-all-start) | async-done | bytes 294944 | tf_op jit(solution)/shard_map/all_to_all | solution.py:110
  47.5 57.0 %all-gather.9.cloned.1.call-done = bf16[64,9,1152]{2,1,0:T(8,128)(2,1)} async-done(((bf16[1,9,1152]{2,1,0:T(8,128)(2,1)}), bf16[64,9,1152]{2,1,0:T(8,128)(2,1)}) %all-gather.9.cloned.1.call-update) | async-done | bytes 1327120 | tf_op jit(solution)/shard_map/all_gather | solution.py:82
  104.5 2.6 reshape.420
  109.0 2.4 reduce.23
  112.2 7.3 %all-to-all-start.1 = ((bf16[64,2,1152]{2,1,0:T(2,128)(2,1)}), bf16[64,2,1152]{2,1,0:T(2,128)(2,1)S(1)}, u32[]{:S(2)}, u32[]{:S(2)}) async-start(bf16[64,2,1152]{2,1,0:T(2,128)(2,1)} %reshape.434), calls=%async_computation.1 | async-start | bytes 589824 | tf_op jit(solution)/shard_map/all_to_all | solution.py:97
  119.6 1.4 reshape.409
  122.2 70.3 %all-gather.7.cloned.1.call-done = bf16[64,9,1152]{2,1,0:T(8,128)(2,1)} async-done(((bf16[1,9,1152]{2,1,0:T(8,128)(2,1)}), bf16[64,9,1152]{2,1,0:T(8,128)(2,1)}) %all-gather.7.cloned.1.call-update) | async-done | bytes 1327120 | tf_op jit(solution)/shard_map/all_gather | solution.py:84
  192.5 2.6 reshape.418
  195.1 1.9 convolution_convert_fusion.13
  199.1 3.7 reshape.423
  203.2 1.4 reshape.414
  206.3 74.4 %all-gather.11.cloned.1.call-done = bf16[64,27,1152]{2,1,0:T(8,128)(2,1)} async-done(((bf16[1,27,1152]{2,1,0:T(8,128)(2,1)}), bf16[64,27,1152]{2,1,0:T(8,128)(2,1)}) %all-gather.11.cloned.1.call-update) | async-done | bytes 3981328 | tf_op jit(solution)/shard_map/all_gather | solution.py:83
  280.7 7.2 %reshape.422 = bf16[1728,1152]{1,0:T(8,128)(2,1)} reshape(bf16[64,27,1152]{2,1,0:T(8,128)(2,1)} %all-gather.11.cloned.1.call-done) | data formatting | bytes 7962624
  288.0 3.4 convolution_convert_fusion.1
  293.8 1.4 fusion.93
  295.2 1.5 fusion.10
  297.8 2.5 fusion.11
  300.3 1.7 fusion.12
  305.1 3.6 fusion.19
  309.6 1.2 reshape.413
  310.7 1.5 fusion.88
  312.5 1.5 fusion.16
  315.1 7.8 %all-to-all-start.2 = ((bf16[1,64,2,1152]{3,2,0,1:T(2,128)(2,1)}), bf16[1,64,2,1152]{3,2,0,1:T(2,128)(2,1)S(1)}, u32[]{:S(2)}, u32[]{:S(2)}) async-start(bf16[1,64,2,1152]{3,2,0,1:T(2,128)(2,1)} %copy.173), calls=%async_computation.2 | async-start | bytes 589824 | tf_op jit(solution)/shard_map/all_to_all | solution.py:114
  323.2 1.5 fusion.13
  325.3 2.1 fusion.25
  328.8 1.6 fusion.9
  332.2 5.4 all-to-all-done.2
  340.1 270.5 %psum.14 = f32[1,4,1152]{2,1,0:T(4,128)} all-reduce(f32[1,4,1152]{2,1,0:T(4,128)S(1)} %maximum_bitcast_fusion), channel_id=1, replica_groups=mesh['dp'=8,'seq'=64] {'seq'}, use_global_device_ids=true, to_apply=%region_14.0 | all-reduce | flops 4608 | bytes 36864 | tf_op jit(solution)/shard_map/psum | solution.py:119
  613.2 1.5 constant_dynamic-slice_fusion
  (162 shorter events, 32.2 us)
Async XLA Ops:
  7.2 97.4 %all-gather.9.cloned.1.call-start = ((), (), s32[]{:S(2)}) async-start(), calls=%async_computation.5 | async-start | bytes 2396160 | tf_op jit(solution)/shard_map/all_gather | solution.py:82
  7.9 184.6 %all-gather.7.cloned.1.call-start = ((), (), s32[]{:S(2)}) async-start(), calls=%async_computation.4 | async-start | bytes 2396160 | tf_op jit(solution)/shard_map/all_gather | solution.py:84
  8.6 272.1 %all-gather.11.cloned.1.call-start = ((), (), s32[]{:S(2)}) async-start(), calls=%async_computation.6 | async-start | bytes 4792320 | tf_op jit(solution)/shard_map/all_gather | solution.py:83
  9.4 22.9 %copy-start.11 = (bf16[1,1,128,1728]{2,3,1,0:T(8,128)(2,1)S(1)}, bf16[1,1,128,1728]{2,3,1,0:T(8,128)(2,1)}, u32[]{:S(2)}) copy-start(bf16[1,1,128,1728]{2,3,1,0:T(8,128)(2,1)} %param.8) | copy-start | bytes 1327108
  13.8 19.7 %copy-start.27 = (f32[1,4,1152]{2,1,0:T(4,128)S(1)}, f32[1,4,1152]{2,1,0:T(4,128)}, u32[]{:S(2)}) copy-start(f32[1,4,1152]{2,1,0:T(4,128)} %param.12) | copy-start | bytes 55300
  14.6 32.6 %all-to-all-start = ((bf16[64,2,1152]{2,1,0:T(2,128)(2,1)}), bf16[64,2,1152]{2,1,0:T(2,128)(2,1)S(1)}, u32[]{:S(2)}, u32[]{:S(2)}) async-start(bf16[64,2,1152]{2,1,0:T(2,128)(2,1)} %reshape.432), calls=%async_computation | async-start | bytes 589824 | tf_op jit(solution)/shard_map/all_to_all | solution.py:110
  32.3 3.0 copy-start.7
  32.3 3.0 copy-start.15
  32.3 3.0 copy-start.17
  112.2 90.5 %all-to-all-start.1 = ((bf16[64,2,1152]{2,1,0:T(2,128)(2,1)}), bf16[64,2,1152]{2,1,0:T(2,128)(2,1)S(1)}, u32[]{:S(2)}, u32[]{:S(2)}) async-start(bf16[64,2,1152]{2,1,0:T(2,128)(2,1)} %reshape.434), calls=%async_computation.1 | async-start | bytes 589824 | tf_op jit(solution)/shard_map/all_to_all | solution.py:97
  204.5 83.4 %copy-start.29 = (f32[128]{0:T(128)}, f32[128]{0:T(128)S(1)}, u32[]{:S(2)}) copy-start(f32[128]{0:T(128)S(1)} %broadcast_multiply_fusion) | copy-start | bytes 1540
  204.9 83.0 %copy-start.39 = (f32[128]{0:T(128)}, f32[128]{0:T(128)S(1)}, u32[]{:S(2)}) copy-start(f32[128]{0:T(128)S(1)} %multiply_reduce_fusion.1) | copy-start | bytes 1540
  204.9 83.0 %copy-start.34 = (f32[128]{0:T(128)}, f32[128]{0:T(128)S(1)}, u32[]{:S(2)}) copy-start(f32[128]{0:T(128)S(1)} %get-tuple-element.23) | copy-start | bytes 1540
  206.3 81.6 %copy-start.21 = (f32[1152]{0:T(1024)S(1)}, f32[1152]{0:T(1024)}, u32[]{:S(2)}) copy-start(f32[1152]{0:T(1024)} %get-tuple-element.10) | copy-start | bytes 13828
  292.2 3.0 copy-start.6
  292.5 2.7 copy-start.13
  293.8 2.9 copy-start.4
  297.8 2.6 copy-start.32
  305.1 3.8 copy-start.40
  305.1 4.3 copy-start.19
  308.7 3.8 copy-start.3
  308.7 3.8 copy-start.36
  312.5 10.7 %copy-start.5 = (bf16[64,2,8,72]{3,2,1,0:T(8,128)(2,1)S(1)}, bf16[64,2,8,72]{3,2,1,0:T(8,128)(2,1)}, u32[]{:S(2)}) copy-start(bf16[64,2,8,72]{3,2,1,0:T(8,128)(2,1)} %copy-done.4) | copy-start | bytes 442372
  312.5 10.6 %copy-start.14 = (bf16[64,2,8,72]{3,2,1,0:T(8,128)(2,1)S(1)}, bf16[64,2,8,72]{3,2,1,0:T(8,128)(2,1)}, u32[]{:S(2)}) copy-start(bf16[64,2,8,72]{3,2,1,0:T(8,128)(2,1)} %copy-done.13) | copy-start | bytes 442372
  312.5 10.6 %copy-start.33 = (f32[2,8,64]{2,1,0:T(8,128)S(1)}, f32[2,8,64]{2,1,0:T(8,128)}, u32[]{:S(2)}) copy-start(f32[2,8,64]{2,1,0:T(8,128)} %copy-done.31) | copy-start | bytes 12292
  315.1 22.5 %all-to-all-start.2 = ((bf16[1,64,2,1152]{3,2,0,1:T(2,128)(2,1)}), bf16[1,64,2,1152]{3,2,0,1:T(2,128)(2,1)S(1)}, u32[]{:S(2)}, u32[]{:S(2)}) async-start(bf16[1,64,2,1152]{3,2,0,1:T(2,128)(2,1)} %copy.173), calls=%async_computation.2 | async-start | bytes 589824 | tf_op jit(solution)/shard_map/all_to_all | solution.py:114
  322.9 290.3 %all-reduce.8.cloned.1.call-start = ((), (), s32[]{:S(2)}) async-start(), calls=%async_computation.3 | async-start | bytes 5308416 | tf_op jit(solution)/shard_map/psum | solution.py:125
  327.4 4.2 copy-start.22
  328.8 8.9 %copy-start.2 = (f32[128,1152]{1,0:T(8,128)S(1)}, f32[128,1152]{1,0:T(8,128)}, u32[]{:S(2)}) copy-start(f32[128,1152]{1,0:T(8,128)} %copy-done.1) | copy-start | bytes 1769476
  338.4 272.2 %copy-start.16 = (bf16[1,128,576]{1,2,0:T(8,128)(2,1)S(1)}, bf16[1,128,576]{1,2,0:T(8,128)(2,1)}, u32[]{:S(2)}) copy-start(bf16[1,128,576]{1,2,0:T(8,128)(2,1)} %copy-done.15) | copy-start | bytes 442372
  338.4 272.2 %copy-start.18 = (bf16[1,128,576]{1,2,0:T(8,128)(2,1)S(1)}, bf16[1,128,576]{1,2,0:T(8,128)(2,1)}, u32[]{:S(2)}) copy-start(bf16[1,128,576]{1,2,0:T(8,128)(2,1)} %copy-done.17) | copy-start | bytes 442372
  338.4 272.2 %copy-start.38 = (f32[8,128]{1,0:T(8,128)S(1)}, f32[8,128]{1,0:T(8,128)}, u32[]{:S(2)}) copy-start(f32[8,128]{1,0:T(8,128)} %copy-done.37) | copy-start | bytes 12292
  (16 other events, 22.4 us)
Sparse Core Ops, SparseCore 0:
  11.3 93.2 all-gather.8
  107.8 84.6 all-gather.6
  195.8 84.8 all-gather.10
  328.4 281.1 all-reduce.7
where the time goes:
time: 628 us; the launch traced here: 621 us
  blocking collectives  271 us (43%)
  waiting for transfers between devices  221 us (35%)
  local copies, waits for them, and re-layouts  43.9 us (7%)
  starting transfers between devices  33.1 us (5%)
  matrix products  26.8 us (4%)
  between operations  14.5 us (2%)
  other arithmetic  11.2 us (2%)
    psum x1, blocking collectives, body(): modulation_grad = lax.psum(factor_grads, 'seq')  271 us
    all_gather x1, waiting for transfers between devices, body(): lax.all_gather(temporal_qkv_weight, 'seq', axis=1, tiled=True)  74.4 us
    all_gather x1, waiting for transfers between devices, body(): lax.all_gather(temporal_out_weight, 'seq', axis=0, tiled=True)  70.3 us
    all_gather x1, waiting for transfers between devices, body(): lax.all_gather(spatial_out_weight, 'seq', axis=0, tiled=True)  57 us
    unnamed x92, local copies, waits for them, and re-layouts  22.4 us
    all_to_all x1, starting transfers between devices, body(): lax.all_to_all(cotangent, 'seq', split_axis=2, concat_axis=1, tiled=True)[0]  17.6 us
  transfers between devices with their start and end apart: 7, of which 5 were waited for; matrix products, arithmetic and copies ran while one was open for 7% of the time, Pallas kernels for 0%

commit v1 on v0

v1 whole, which is shorter than its diff:
```python
import math

import jax
import jax.numpy as jnp
from jax import lax
from jax.experimental import pallas as pl
from jax.experimental.pallas import tpu as pltpu
from jax.sharding import Mesh
from jax.sharding import PartitionSpec as P

D = 1152
HEADS = 8
HS = 72
ATT = 576
ROWS = 128
SCALE = 1.0 / math.sqrt(HS)
SEQ = ("yhi", "z", "core")
CHIPS = ("yhi", "z")
DP = ("x", "ylo")
BF = jnp.bfloat16
F32 = jnp.float32


def nn(a, b):
    return lax.dot_general(a, b, (((1,), (0,)), ((), ())), preferred_element_type=F32)


def nt(a, b):
    return lax.dot_general(a, b, (((1,), (1,)), ((), ())), preferred_element_type=F32)


def tn(a, b):
    return lax.dot_general(a, b, (((0,), (0,)), ((), ())), preferred_element_type=F32)


def head_masks():
    head = lax.broadcasted_iota(jnp.int32, (ROWS, ATT), 1) // HS
    return [head == h for h in range(HEADS)]


def stack_heads(masks, a):
    zero = jnp.zeros_like(a)
    return jnp.concatenate([jnp.where(m, a, zero) for m in masks], 0)


def pick_heads(masks, a):
    out = a[:ROWS]
    for h in range(1, HEADS):
        out = jnp.where(masks[h], a[h * ROWS : (h + 1) * ROWS], out)
    return out


def softmax_rows(scores):
    top = jnp.max(scores, -1, keepdims=True)
    weights = jnp.exp(scores - top)
    return weights / jnp.sum(weights, -1, keepdims=True)


def attend(masks, q, k, v, same):
    q_stack = stack_heads(masks, q)
    scores = nt(q_stack, k) * SCALE
    if same is not None:
        scores = jnp.where(same, scores, -1e30)
    probs = softmax_rows(scores)
    probs_b = probs.astype(BF)
    mixed = pick_heads(masks, nn(probs_b, v)).astype(BF)
    return q_stack, probs, probs_b, mixed


def attend_back(masks, q_stack, k, v, probs, probs_b, d_mixed):
    d_stack = stack_heads(masks, d_mixed)
    d_probs = nt(d_stack, v).astype(BF).astype(F32)
    d_v = tn(probs_b, d_stack)
    d_scores = probs * (d_probs - jnp.sum(d_probs * probs, -1, keepdims=True)) * SCALE
    d_scores = d_scores.astype(BF)
    d_q = pick_heads(masks, nn(d_scores, k))
    d_k = tn(d_scores, q_stack)
    return d_q.astype(BF), d_k.astype(BF), d_v.astype(BF)


def spatial_forward_kernel(qkv, mixed):
    q, k, v = qkv[:, :ATT], qkv[:, ATT : 2 * ATT], qkv[:, 2 * ATT :]
    mixed[...] = attend(head_masks(), q, k, v, None)[3]


def spatial_backward_kernel(qkv, d_mixed, out):
    q, k, v = qkv[:, :ATT], qkv[:, ATT : 2 * ATT], qkv[:, 2 * ATT :]
    masks = head_masks()
    q_stack, probs, probs_b, _ = attend(masks, q, k, v, None)
    d_q, d_k, d_v = attend_back(masks, q_stack, k, v, probs, probs_b, d_mixed[...])
    out[:, :ATT] = d_q
    out[:, ATT : 2 * ATT] = d_k
    out[:, 2 * ATT :] = d_v


def temporal_kernel(
    core, tokens, cotangent, mixed_s, w_so, w_qkv, w_out, factors,
    hidden_grad, d_mixed_s, factor_grads, out_keep, out_send,
):
    gate_s, shift, scale, gate_t = (factors[i : i + 1, :] for i in range(4))
    project = nn(mixed_s[...], w_so[...])
    hidden = (tokens[...].astype(F32) + gate_s * project).astype(BF).astype(F32)
    centered = hidden - jnp.mean(hidden, -1, keepdims=True)
    inverse = lax.rsqrt(jnp.mean(centered * centered, -1, keepdims=True) + 1e-06)
    unit = centered * inverse
    normed = (unit * (1.0 + scale) + shift).astype(BF)
    wq, wk, wv = (w_qkv[i * ATT : (i + 1) * ATT, :] for i in range(3))
    q, k, v = (nt(normed, w).astype(BF) for w in (wq, wk, wv))

    masks = head_masks()
    row = lax.broadcasted_iota(jnp.int32, (HEADS * ROWS, ROWS), 0)
    col = lax.broadcasted_iota(jnp.int32, (HEADS * ROWS, ROWS), 1)
    same = ((row ^ col) & 1) == 0
    q_stack, probs, probs_b, mixed = attend(masks, q, k, v, same)

    cot = cotangent[...].astype(F32)
    scaled = (cot * gate_t).astype(BF)
    me = core[0]
    source = lax.broadcasted_iota(jnp.int32, (ATT, ATT), 0)
    target = lax.broadcasted_iota(jnp.int32, (ATT, ATT), 1)
    half = target // 288
    rest = target - half * 288
    chip = rest // 9
    wanted = chip * 18 + (half ^ me) * 9 + (rest - chip * 9)
    order = jnp.where(source == wanted, 1.0, 0.0).astype(BF)
    product = tn(nn(mixed, order).astype(BF), scaled)
    out_keep[...] = product[:288]
    out_send[...] = product[288:].astype(BF)

    d_mixed = nt(scaled, w_out[...]).astype(BF)
    d_q, d_k, d_v = attend_back(masks, q_stack, k, v, probs, probs_b, d_mixed)
    d_normed = (nn(d_q, wq) + nn(d_k, wk) + nn(d_v, wv)).astype(BF).astype(F32)
    d_unit = d_normed * (1.0 + scale)
    d_hidden = inverse * (
        d_unit
        - jnp.mean(d_unit, -1, keepdims=True)
        - unit * jnp.mean(d_unit * unit, -1, keepdims=True)
    )
    grad = (cot + d_hidden).astype(BF)
    hidden_grad[...] = grad
    grad = grad.astype(F32)
    d_mixed_s[...] = nt((grad * gate_s).astype(BF), w_so[...]).astype(BF)
    project_t = nn(mixed, w_out[...])
    factor_grads[0:1, :] = jnp.sum(grad * project, 0, keepdims=True)
    factor_grads[1:2, :] = jnp.sum(d_normed, 0, keepdims=True)
    factor_grads[2:3, :] = jnp.sum(d_normed * unit, 0, keepdims=True)
    factor_grads[3:4, :] = jnp.sum(cot * project_t, 0, keepdims=True)


def call(kernel, outs, *args, scalars=0, flops=10**9):
    specs = [pl.BlockSpec(memory_space=pltpu.SMEM)] * scalars
    specs += [pl.BlockSpec(memory_space=pltpu.VMEM)] * (len(args) - scalars)
    out_shape = [jax.ShapeDtypeStruct(s, d) for s, d in outs]
    return pl.pallas_call(
        kernel,
        out_shape=out_shape,
        in_specs=specs,
        out_specs=[pl.BlockSpec(memory_space=pltpu.VMEM)] * len(outs),
        compiler_params=pltpu.CompilerParams(vmem_limit_bytes=48 * 2**20),
        cost_estimate=pl.CostEstimate(flops=flops, bytes_accessed=10**7, transcendentals=10**5),
    )(*args)


def exchange(a):
    return lax.all_to_all(a, SEQ, 0, 0, tiled=True)


def body(tokens, qkv, w_so, w_qkv, w_out, factors, cotangent):
    tokens, qkv, cotangent, factors = tokens[0, 0], qkv[0, 0], cotangent[0, 0], factors[0]
    shard = jnp.concatenate([w_so, w_out, w_qkv.T], 0)
    gathered = lax.all_gather(shard, SEQ, axis=0)
    w_so = gathered[:, :9].reshape(ATT, D)
    w_out = gathered[:, 9:18].reshape(ATT, D)
    w_qkv = gathered[:, 18:].reshape(3 * ATT, D)

    tokens_p = exchange(tokens.reshape(64, 2, D)).reshape(ROWS, D)
    cot_p = exchange(cotangent.reshape(64, 2, D)).reshape(ROWS, D)
    (mixed_s,) = call(spatial_forward_kernel, [((ROWS, ATT), BF)], qkv)
    mixed_p = exchange(mixed_s.reshape(64, 2, ATT)).reshape(ROWS, ATT)

    core = lax.axis_index("core").astype(jnp.int32).reshape(1)
    hidden_grad, d_mixed, factor_part, out_keep, out_send = call(
        temporal_kernel,
        [((ROWS, D), BF), ((ROWS, ATT), BF), ((4, D), F32), ((288, D), F32), ((288, D), BF)],
        core, tokens_p, cot_p, mixed_p, w_so, w_qkv, w_out, factors,
        scalars=1, flops=4 * 10**9,
    )

    out_other = lax.ppermute(out_send, "core", [(0, 1), (1, 0)])
    packed = jnp.concatenate([hidden_grad, d_mixed], 1)
    back = exchange(packed.reshape(64, 2, D + ATT)).reshape(ROWS, D + ATT)
    token_grad = back[:, :D]
    (qkv_grad,) = call(spatial_backward_kernel, [((ROWS, 3 * ATT), BF)], qkv, back[:, D:])

    out_part = (out_keep + out_other.astype(F32)).astype(BF).reshape(32, 2, 9 * D // 2)
    out_part = lax.all_to_all(out_part, CHIPS, 0, 0, tiled=True)
    out_part = jnp.sum(out_part.astype(F32), 0)
    out_part = lax.all_to_all(jnp.broadcast_to(out_part[None], (8, 2, 9 * D // 2)), DP, 0, 0, tiled=True)
    out_grad = jnp.sum(out_part, 0).reshape(9, D)

    factor_part = jnp.sum(exchange(factor_part.reshape(64, 1, 72)), 0)
    factor_grad = exchange(jnp.broadcast_to(factor_part[None], (64, 1, 72)))
    factor_grad = factor_grad.reshape(4, D)
    return token_grad[None, None], qkv_grad[None, None], factor_grad[None], out_grad


def solution(mesh):
    fine = Mesh(mesh.devices.reshape(4, 2, 4, 8, 2), DP + SEQ)
    frames = P(DP, SEQ, None, None)
    return jax.shard_map(
        body,
        mesh=fine,
        in_specs=(
            frames,
            frames,
            P(SEQ, None),
            P(None, SEQ),
            P(SEQ, None),
            P(DP, None, None),
            frames,
        ),
        out_specs=(frames, frames, P(DP, None, None), P(SEQ, None)),
        check_vma=False,
    )
```

time: 628 us -> 271 us (0.43)
  blocking collectives: 271 us -> 18.9 us
  waiting for transfers between devices: 221 us -> 122 us
  matrix products: 26.8 us -> 0 us
  starting transfers between devices: 33.1 us -> 51.3 us
  Pallas kernels: 0 us -> 13.8 us
  other arithmetic: 11.2 us -> 4.6 us
    psum x1 -> x0, blocking collectives: 271 us -> none  [body(): modulation_grad = lax.psum(factor_grads, 'seq')]
    all_gather x3 -> x1, waiting for transfers between devices: 202 us -> 35 us  [body(): gathered = lax.all_gather(shard, SEQ, axis=0)]
    all_to_all x3 -> x7, waiting for transfers between devices: 17.4 us -> 87.4 us  [the longest x5 64.3 us: exchange(): return lax.all_to_all(a, SEQ, 0, 0, tiled=True)]
    dot_general x17 -> x0, matrix products: 24.3 us -> none  [the longest x2 7.02 us: temporal_norm(): jnp.dot(flattened, weight, preferred_element_type=jnp.float32)]
    all_to_all x0 -> x1, blocking collectives: none -> 18.9 us  [exchange(): return lax.all_to_all(a, SEQ, 0, 0, tiled=True)]
    all_to_all x3 -> x7, starting transfers between devices: 32.7 us -> 49.1 us  [the longest x5 40.6 us: exchange(): return lax.all_to_all(a, SEQ, 0, 0, tiled=True)]
    unnamed x92 -> x20, local copies, waits for them, and re-layouts: 22.4 us -> 6.81 us
    reshape x10 -> x12, local copies, waits for them, and re-layouts: 3.84 us -> 19.4 us  [the longest x1 7.18 us: body(): w_qkv = gathered[:, 18:].reshape(3 * ATT, D)]
  transfers between devices with their start and end apart: 7 -> 9, of which waited for: 5 -> 8; matrix products, arithmetic and copies ran while one was open for 7% -> 6% of each run, Pallas kernels for 0% -> 1%
where the time goes in v1:
time: 271 us; the launch traced here: 269 us
  waiting for transfers between devices  122 us (45%)
  starting transfers between devices  51.3 us (19%)
  local copies, waits for them, and re-layouts  44.1 us (16%)
  blocking collectives  18.9 us (7%)
  between operations  14.2 us (5%)
  Pallas kernels  13.8 us (5%)
  other arithmetic  4.6 us (2%)
    all_to_all x5, waiting for transfers between devices, exchange(): return lax.all_to_all(a, SEQ, 0, 0, tiled=True)  64.3 us
    all_to_all x5, starting transfers between devices, exchange(): return lax.all_to_all(a, SEQ, 0, 0, tiled=True)  40.6 us
    all_gather x1, waiting for transfers between devices, body(): gathered = lax.all_gather(shard, SEQ, axis=0)  35 us
    all_to_all x1, waiting for transfers between devices, body(): out_part = lax.all_to_all(out_part, CHIPS, 0, 0, tiled=True)  22.1 us
    all_to_all x1, blocking collectives, exchange(): return lax.all_to_all(a, SEQ, 0, 0, tiled=True)  18.9 us
    pallas_call x3, Pallas kernels, call(): pl.pallas_call(kernel, out_shape=out_shape, in_specs=specs, out_specs=[pl...  13.8 us
    reshape x1, local copies, waits for them, and re-layouts, body(): w_qkv = gathered[:, 18:].reshape(3 * ATT, D)  7.18 us
    slice x1, local copies, waits for them, and re-layouts, body(): w_qkv = gathered[:, 18:].reshape(3 * ATT, D)  7.01 us
  transfers between devices with their start and end apart: 9, of which 8 were waited for; matrix products, arithmetic and copies ran while one was open for 6% of the time, Pallas kernels for 1%

profile of v1, /device:TPU:1, one launch (start us, length us, event | category | flops | bytes accessed | tf_op | source)
XLA Modules:
  0.0 269.4 jit_solution(1273168968708360542)
XLA Ops:
  7.2 1.6 maximum_bitcast_fusion
  8.8 1.2 copy.21
  10.1 1.5 shard_map.102
  12.3 17.6 %all-to-all-start.2 = ((bf16[64,2,576]{2,1,0:T(2,128)(2,1)}), bf16[64,2,576]{2,1,0:T(2,128)(2,1)S(1)}, u32[]{:S(2)}, u32[]{:S(2)}) async-start(bf16[64,2,576]{2,1,0:T(2,128)(2,1)} %reshape.56), calls=%async_computation.2 | async-start | bytes 327680 | tf_op jit(solution)/shard_map/all_to_all | solution.py:165
  30.8 11.9 %all-to-all-done.2 = bf16[64,2,576]{2,1,0:T(2,128)(2,1)S(1)} async-done(((bf16[64,2,576]{2,1,0:T(2,128)(2,1)}), bf16[64,2,576]{2,1,0:T(2,128)(2,1)S(1)}, u32[]{:S(2)}, u32[]{:S(2)}) %all-to-all-start.2) | async-done | bytes 147488 | tf_op jit(solution)/shard_map/all_to_all | solution.py:165
  42.8 5.3 %all-to-all-start = ((bf16[64,2,1152]{2,1,0:T(2,128)(2,1)}), bf16[64,2,1152]{2,1,0:T(2,128)(2,1)S(1)}, u32[]{:S(2)}, u32[]{:S(2)}) async-start(bf16[64,2,1152]{2,1,0:T(2,128)(2,1)} %reshape_squeeze.6), calls=%async_computation | async-start | bytes 589824 | tf_op jit(solution)/shard_map/all_to_all | solution.py:165
  48.9 13.5 %all-to-all-done = bf16[64,2,1152]{2,1,0:T(2,128)(2,1)S(1)} async-done(((bf16[64,2,1152]{2,1,0:T(2,128)(2,1)}), bf16[64,2,1152]{2,1,0:T(2,128)(2,1)S(1)}, u32[]{:S(2)}, u32[]{:S(2)}) %all-to-all-start) | async-done | bytes 294944 | tf_op jit(solution)/shard_map/all_to_all | solution.py:165
  62.4 6.7 %all-to-all-start.1 = ((bf16[64,2,1152]{2,1,0:T(2,128)(2,1)}), bf16[64,2,1152]{2,1,0:T(2,128)(2,1)S(1)}, u32[]{:S(2)}, u32[]{:S(2)}) async-start(bf16[64,2,1152]{2,1,0:T(2,128)(2,1)} %reshape_squeeze.7), calls=%async_computation.1 | async-start | bytes 589824 | tf_op jit(solution)/shard_map/all_to_all | solution.py:165
  70.8 12.8 %all-to-all-done.1 = bf16[64,2,1152]{2,1,0:T(2,128)(2,1)S(1)} async-done(((bf16[64,2,1152]{2,1,0:T(2,128)(2,1)}), bf16[64,2,1152]{2,1,0:T(2,128)(2,1)S(1)}, u32[]{:S(2)}, u32[]{:S(2)}) %all-to-all-start.1) | async-done | bytes 294944 | tf_op jit(solution)/shard_map/all_to_all | solution.py:165
  84.4 35.0 %all-gather.4.cloned.1.call-done = bf16[64,45,1152]{2,1,0:T(8,128)(2,1)} async-done(((bf16[1,45,1152]{2,1,0:T(8,128)(2,1)}), bf16[64,45,1152]{2,1,0:T(8,128)(2,1)}) %all-gather.4.cloned.1.call-update) | async-done | bytes 6635536 | tf_op jit(solution)/shard_map/all_gather | solution.py:171
  119.4 5.8 %fusion = (bf16[64,9,1152]{2,1,0:T(8,128)(2,1)}, bf16[64,9,1152]{2,1,0:T(8,128)(2,1)}) fusion(bf16[64,45,1152]{2,1,0:T(8,128)(2,1)} %all-gather.4.cloned.1.call-done), kind=kLoop, calls=%fused_computation.5 | loop fusion | bytes 5308416 | tf_op jit(solution)/shard_map/slice | solution.py:173
  125.3 2.6 reshape.58.w_so
  127.9 2.6 reshape.60.w_out
  130.6 7.0 %slice.21 = bf16[64,27,1152]{2,1,0:T(8,128)(2,1)} slice(bf16[64,45,1152]{2,1,0:T(8,128)(2,1)} %all-gather.4.cloned.1.call-done), slice={[0:64], [18:45], [0:1152]} | slice | bytes 7962624 | tf_op jit(solution)/shard_map/slice | solution.py:174
  137.6 7.2 %reshape.59.w_qkv = bf16[1728,1152]{1,0:T(8,128)(2,1)} reshape(bf16[64,27,1152]{2,1,0:T(8,128)(2,1)} %slice.21) | data formatting | bytes 7962624 | tf_op jit(solution)/shard_map/reshape | solution.py:174
  144.7 1.0 copy-done.1
  147.6 10.2 %shard_map.103 = (bf16[128,1152]{1,0:T(8,128)(2,1)S(1)}, bf16[128,576]{1,0:T(8,128)(2,1)S(1)}, f32[4,1152]{1,0:T(4,128)S(1)}, f32[288,1152]{1,0:T(8,128)S(1)}, bf16[288,1152]{1,0:T(8,128)(2,1)}) custom-call(s32[1]{0:T(128)} %bitcast.core, bf16[128,1152]{1,0:T(8,128)(2,1)S(1)} %copy-done.1, bf16[128,1152]{1,0:T(8,128)(2,1)S(1)} %copy-done.2, ...), custom_call_target="tpu_custom_call" | custom-call | flops 4000000000 | bytes 10000000 | tf_op jit(solution)/shard_map/pallas_call | solution.py:154
  157.8 1.1 copy-done
  159.5 2.2 collective-permute-start
  161.8 18.9 %all_to_all.40 = f32[64,1,72]{2,1,0:T(1,128)S(1)} all-to-all(f32[64,1,72]{2,1,0:T(1,128)S(1)} %bitcast.18), channel_id=1, replica_groups=mesh['x'=4,'ylo'=2,'yhi'=4,'z'=8,'core'=2] {'yhi','z','core'}, dimensions={0} | all-to-all | bytes 36864 | tf_op jit(solution)/shard_map/all_to_all | solution.py:165
  181.5 4.9 %all-to-all-start.5 = ((f32[64,1,72]{2,1,0:T(1,128)}), f32[64,1,72]{2,1,0:T(1,128)S(1)}, u32[]{:S(2)}, u32[]{:S(2)}) async-start(f32[64,1,72]{2,1,0:T(1,128)} %broadcast_in_dim.20), calls=%async_computation.5 | async-start | bytes 65536 | tf_op jit(solution)/shard_map/all_to_all | solution.py:165
  186.4 1.5 add_convert_fusion
  187.9 1.6 reshape.64
  189.6 8.5 %all-to-all-done.5 = f32[64,1,72]{2,1,0:T(1,128)S(1)} async-done(((f32[64,1,72]{2,1,0:T(1,128)}), f32[64,1,72]{2,1,0:T(1,128)S(1)}, u32[]{:S(2)}, u32[]{:S(2)}) %all-to-all-start.5) | async-done | bytes 18464 | tf_op jit(solution)/shard_map/all_to_all | solution.py:165
  198.1 3.9 %all-to-all-start.6 = ((bf16[32,2,5184]{2,1,0:T(2,128)(2,1)}), bf16[32,2,5184]{2,1,0:T(2,128)(2,1)S(1)}, u32[]{:S(2)}, u32[]{:S(2)}) async-start(bf16[32,2,5184]{2,1,0:T(2,128)(2,1)} %reshape.64), calls=%async_computation.6 | async-start | bytes 1343488 | tf_op jit(solution)/shard_map/all_to_all | solution.py:196
  203.0 22.1 %all-to-all-done.6 = bf16[32,2,5184]{2,1,0:T(2,128)(2,1)S(1)} async-done(((bf16[32,2,5184]{2,1,0:T(2,128)(2,1)}), bf16[32,2,5184]{2,1,0:T(2,128)(2,1)S(1)}, u32[]{:S(2)}, u32[]{:S(2)}) %all-to-all-start.6) | async-done | bytes 663584 | tf_op jit(solution)/shard_map/all_to_all | solution.py:196
  225.1 6.0 %all-to-all-start.3 = ((bf16[64,2,1728]{2,1,0:T(2,128)(2,1)}), bf16[64,2,1728]{2,1,0:T(2,128)(2,1)S(1)}, u32[]{:S(2)}, u32[]{:S(2)}) async-start(bf16[64,2,1728]{2,1,0:T(2,128)(2,1)} %reshape.61), calls=%async_computation.3 | async-start | bytes 917504 | tf_op jit(solution)/shard_map/all_to_all | solution.py:165
  231.7 17.5 %all-to-all-done.3 = bf16[64,2,1728]{2,1,0:T(2,128)(2,1)S(1)} async-done(((bf16[64,2,1728]{2,1,0:T(2,128)(2,1)}), bf16[64,2,1728]{2,1,0:T(2,128)(2,1)S(1)}, u32[]{:S(2)}, u32[]{:S(2)}) %all-to-all-start.3) | async-done | bytes 442400 | tf_op jit(solution)/shard_map/all_to_all | solution.py:165
  250.0 4.6 %all-to-all-start.7 = ((f32[8,2,5184]{2,1,0:T(2,128)}), f32[8,2,5184]{2,1,0:T(2,128)S(1)}, u32[]{:S(2)}, u32[]{:S(2)}) async-start(f32[8,2,5184]{2,1,0:T(2,128)} %broadcast_in_dim.21), calls=%async_computation.7 | async-start | bytes 671744 | tf_op jit(solution)/shard_map/all_to_all | solution.py:198
  256.9 2.0 shard_map.104
  259.0 1.0 copy.24
  260.7 1.0 all-to-all-done.7
  (40 shorter events, 14.5 us)
Async XLA Ops:
  7.2 112.3 %all-gather.4.cloned.1.call-start = ((), (), s32[]{:S(2)}) async-start(), calls=%async_computation.8 | async-start | bytes 7188480 | tf_op jit(solution)/shard_map/all_gather | solution.py:171
  10.0 20.0 %copy-start.7 = (bf16[1,1,128,1152]{3,2,1,0:T(8,128)(2,1)S(1)}, bf16[1,1,128,1152]{3,2,1,0:T(8,128)(2,1)}, u32[]{:S(2)}) copy-start(bf16[1,1,128,1152]{3,2,1,0:T(8,128)(2,1)} %param.7) | copy-start | bytes 884740
  10.0 38.0 %copy-start.8 = (bf16[1,1,128,1152]{3,2,1,0:T(8,128)(2,1)S(1)}, bf16[1,1,128,1152]{3,2,1,0:T(8,128)(2,1)}, u32[]{:S(2)}) copy-start(bf16[1,1,128,1152]{3,2,1,0:T(8,128)(2,1)} %param.13) | copy-start | bytes 884740
  12.3 30.4 %all-to-all-start.2 = ((bf16[64,2,576]{2,1,0:T(2,128)(2,1)}), bf16[64,2,576]{2,1,0:T(2,128)(2,1)S(1)}, u32[]{:S(2)}, u32[]{:S(2)}) async-start(bf16[64,2,576]{2,1,0:T(2,128)(2,1)} %reshape.56), calls=%async_computation.2 | async-start | bytes 327680 | tf_op jit(solution)/shard_map/all_to_all | solution.py:165
  42.8 19.7 %all-to-all-start = ((bf16[64,2,1152]{2,1,0:T(2,128)(2,1)}), bf16[64,2,1152]{2,1,0:T(2,128)(2,1)S(1)}, u32[]{:S(2)}, u32[]{:S(2)}) async-start(bf16[64,2,1152]{2,1,0:T(2,128)(2,1)} %reshape_squeeze.6), calls=%async_computation | async-start | bytes 589824 | tf_op jit(solution)/shard_map/all_to_all | solution.py:165
  62.4 21.2 %all-to-all-start.1 = ((bf16[64,2,1152]{2,1,0:T(2,128)(2,1)}), bf16[64,2,1152]{2,1,0:T(2,128)(2,1)S(1)}, u32[]{:S(2)}, u32[]{:S(2)}) async-start(bf16[64,2,1152]{2,1,0:T(2,128)(2,1)} %reshape_squeeze.7), calls=%async_computation.1 | async-start | bytes 589824 | tf_op jit(solution)/shard_map/all_to_all | solution.py:165
  137.6 7.2 %copy-start.6 = (f32[1,4,1152]{2,1,0:T(4,128)S(1)}, f32[1,4,1152]{2,1,0:T(4,128)}, u32[]{:S(2)}) copy-start(f32[1,4,1152]{2,1,0:T(4,128)} %param.12) | copy-start | bytes 55300
  144.7 1.0 copy-start.1
  145.7 1.0 copy-start.2
  146.7 0.9 copy-start.5
  157.8 1.1 copy-start
  158.9 0.7 copy-start.3
  159.5 26.8 %collective-permute-start = (bf16[288,1152]{1,0:T(8,128)(2,1)}, bf16[288,1152]{1,0:T(8,128)(2,1)S(1)}, u32[]{:S(2)}, u32[]{:S(2)}) collective-permute-start(bf16[288,1152]{1,0:T(8,128)(2,1)} %get-tuple-element.13), channel_id=1, source_target_pairs={{0,1},{1,0},{2,3},{3,2},{4,5},{5,4},{6,7},{7,6},{8,9},{9,8},{10,11... | collective-permute-start | bytes 1990664 | tf_op jit(solution)/shard_map/ppermute | solution.py:189
  181.5 16.6 %all-to-all-start.5 = ((f32[64,1,72]{2,1,0:T(1,128)}), f32[64,1,72]{2,1,0:T(1,128)S(1)}, u32[]{:S(2)}, u32[]{:S(2)}) async-start(f32[64,1,72]{2,1,0:T(1,128)} %broadcast_in_dim.20), calls=%async_computation.5 | async-start | bytes 65536 | tf_op jit(solution)/shard_map/all_to_all | solution.py:165
  186.4 15.6 %copy-start.4 = (bf16[128,576]{1,0:T(8,128)(2,1)S(1)}, bf16[128,576]{1,0:T(8,128)(2,1)}, u32[]{:S(2)}) copy-start(bf16[128,576]{1,0:T(8,128)(2,1)} %copy-done.3) | copy-start | bytes 442372
  198.1 27.0 %all-to-all-start.6 = ((bf16[32,2,5184]{2,1,0:T(2,128)(2,1)}), bf16[32,2,5184]{2,1,0:T(2,128)(2,1)S(1)}, u32[]{:S(2)}, u32[]{:S(2)}) async-start(bf16[32,2,5184]{2,1,0:T(2,128)(2,1)} %reshape.64), calls=%async_computation.6 | async-start | bytes 1343488 | tf_op jit(solution)/shard_map/all_to_all | solution.py:196
  225.1 24.1 %all-to-all-start.3 = ((bf16[64,2,1728]{2,1,0:T(2,128)(2,1)}), bf16[64,2,1728]{2,1,0:T(2,128)(2,1)S(1)}, u32[]{:S(2)}, u32[]{:S(2)}) async-start(bf16[64,2,1728]{2,1,0:T(2,128)(2,1)} %reshape.61), calls=%async_computation.3 | async-start | bytes 917504 | tf_op jit(solution)/shard_map/all_to_all | solution.py:165
  250.0 11.6 %all-to-all-start.7 = ((f32[8,2,5184]{2,1,0:T(2,128)}), f32[8,2,5184]{2,1,0:T(2,128)S(1)}, u32[]{:S(2)}, u32[]{:S(2)}) async-start(f32[8,2,5184]{2,1,0:T(2,128)} %broadcast_in_dim.21), calls=%async_computation.7 | async-start | bytes 671744 | tf_op jit(solution)/shard_map/all_to_all | solution.py:198
Sparse Core Ops, SparseCore 0:
  11.3 108.1 all-gather.3

commit v2 on v1

--- a/solution.py
+++ b/solution.py
@@ -93,10 +93,85 @@
     out[:, 2 * ATT :] = d_v
 
 
+def compact_kernel(core, shards, own_so, own_out, own_qkv, h0, h1, c0, c1, c2, c3, so, out, qkv):
+    for i in range(16):
+        shard = shards[i].astype(F32)
+        so[9 * i : 9 * i + 9, :] = shard[:9]
+        out[9 * i : 9 * i + 9, :] = shard[9:18]
+        qkv[27 * i : 27 * i + 27, :] = shard[18:]
+    own_so[...] = so[...].astype(BF)
+    own_out[...] = out[...].astype(BF)
+    own_qkv[...] = qkv[...].astype(BF)
+    at_qkv = pl.multiple_of(core[0] * 208, 16)
+    at = pl.multiple_of(core[0] * 64, 16)
+    h0[...] = own_qkv[pl.ds(at_qkv, 192), :]
+    h1[0:32, :] = own_qkv[pl.ds(pl.multiple_of(at_qkv + 192, 16), 32), :]
+    h1[32:112, :] = own_so[pl.ds(at, 80), :]
+    h1[112:192, :] = own_out[pl.ds(at, 80), :]
+    c0[...] = h0[0:96, :]
+    c1[...] = h0[96:192, :]
+    c2[...] = h1[0:96, :]
+    c3[...] = h1[96:192, :]
+
+
+SECTIONS = ((0, 0, 224), (1, 224, 304), (2, 304, 384))
+BLOCK = (432, 144, 144)
+STEP = (208, 64, 64)
+
+
+def part_copies(ref, start, lo, hi, half, block, targets):
+    copies = []
+    for section, first, last in SECTIONS:
+        first = first + 16 * half
+        a, b = max(lo, first), min(hi, last)
+        if a < b:
+            row = a - SECTIONS[section][1] + STEP[section] * half
+            to = pl.multiple_of(block * BLOCK[section] + row, 16)
+            copies.append(
+                (ref.at[pl.ds(start + a - lo, b - a)], targets[section].at[pl.ds(to, b - a)])
+            )
+    return copies
+
+
+def assemble(place, own, near, swapped, targets, sems):
+    own_so, own_out, own_qkv = own
+    b0, b1, c0, c1, d0, d1, d2, d3 = near
+    o1, o2 = swapped
+    for me in range(2):
+
+        @pl.when(place[0] == me)
+        def _():
+            cls = place[1]
+            b, c, d = cls ^ 2, cls ^ 1, cls ^ 3
+            pairs = []
+            for ref, section in ((own_qkv, 0), (own_so, 1), (own_out, 2)):
+                to = pl.multiple_of(cls * BLOCK[section], 16)
+                pairs.append((ref, targets[section].at[pl.ds(to, BLOCK[section])]))
+            for ref0, ref1, block in ((b0, b1, b), (c0, c1, c)):
+                pairs += part_copies(ref0, 0, 0, 192, me, block, targets)
+                pairs += part_copies(ref1, 0, 192, 384, me, block, targets)
+            for i, ref in enumerate((d0, d1, d2, d3)):
+                pairs += part_copies(ref, 0, 96 * i, 96 * i + 96, me, d, targets)
+            pairs += part_copies(o1, 0, 0, 384, 1 - me, b, targets)
+            pairs += part_copies(o1, 384, 0, 384, 1 - me, c, targets)
+            pairs += part_copies(o2, 0, 0, 384, 1 - me, d, targets)
+            copies = [pltpu.make_async_copy(a, z, sems.at[i]) for i, (a, z) in enumerate(pairs)]
+            for copy in copies:
+                copy.start()
+            for copy in copies:
+                copy.wait()
+
+
 def temporal_kernel(
-    core, tokens, cotangent, mixed_s, w_so, w_qkv, w_out, factors,
+    place, tokens, cotangent, mixed_s, factors,
+    own_so, own_out, own_qkv, b0, b1, c0, c1, d0, d1, d2, d3, o1, o2,
     hidden_grad, d_mixed_s, factor_grads, out_keep, out_send,
+    w_qkv, w_so, w_out, sems,
 ):
+    assemble(
+        place, (own_so, own_out, own_qkv), (b0, b1, c0, c1, d0, d1, d2, d3), (o1, o2),
+        (w_qkv, w_so, w_out), sems,
+    )
     gate_s, shift, scale, gate_t = (factors[i : i + 1, :] for i in range(4))
     project = nn(mixed_s[...], w_so[...])
     hidden = (tokens[...].astype(F32) + gate_s * project).astype(BF).astype(F32)
@@ -115,17 +190,10 @@
 
     cot = cotangent[...].astype(F32)
     scaled = (cot * gate_t).astype(BF)
-    me = core[0]
-    source = lax.broadcasted_iota(jnp.int32, (ATT, ATT), 0)
-    target = lax.broadcasted_iota(jnp.int32, (ATT, ATT), 1)
-    half = target // 288
-    rest = target - half * 288
-    chip = rest // 9
-    wanted = chip * 18 + (half ^ me) * 9 + (rest - chip * 9)
-    order = jnp.where(source == wanted, 1.0, 0.0).astype(BF)
-    product = tn(nn(mixed, order).astype(BF), scaled)
-    out_keep[...] = product[:288]
-    out_send[...] = product[288:].astype(BF)
+    left, right = scaled[:, :ATT], scaled[:, ATT:]
+    first = place[0] == 0
+    out_keep[...] = tn(mixed, jnp.where(first, left, right))
+    out_send[...] = tn(mixed, jnp.where(first, right, left)).astype(BF)
 
     d_mixed = nt(scaled, w_out[...]).astype(BF)
     d_q, d_k, d_v = attend_back(masks, q_stack, k, v, probs, probs_b, d_mixed)
@@ -147,15 +215,17 @@
     factor_grads[3:4, :] = jnp.sum(cot * project_t, 0, keepdims=True)
 
 
-def call(kernel, outs, *args, scalars=0, flops=10**9):
+def call(kernel, outs, *args, scalars=0, remote=0, scratch=(), flops=10**9):
+    vmem = pl.BlockSpec(memory_space=pltpu.VMEM)
     specs = [pl.BlockSpec(memory_space=pltpu.SMEM)] * scalars
-    specs += [pl.BlockSpec(memory_space=pltpu.VMEM)] * (len(args) - scalars)
-    out_shape = [jax.ShapeDtypeStruct(s, d) for s, d in outs]
+    specs += [vmem] * (len(args) - scalars - remote)
+    specs += [pl.BlockSpec(memory_space=pl.ANY)] * remote
     return pl.pallas_call(
         kernel,
-        out_shape=out_shape,
+        out_shape=[jax.ShapeDtypeStruct(s, d) for s, d in outs],
         in_specs=specs,
-        out_specs=[pl.BlockSpec(memory_space=pltpu.VMEM)] * len(outs),
+        out_specs=[vmem] * len(outs),
+        scratch_shapes=list(scratch),
         compiler_params=pltpu.CompilerParams(vmem_limit_bytes=48 * 2**20),
         cost_estimate=pl.CostEstimate(flops=flops, bytes_accessed=10**7, transcendentals=10**5),
     )(*args)
@@ -165,43 +235,106 @@
     return lax.all_to_all(a, SEQ, 0, 0, tiled=True)
 
 
+PLANE = ("x", "ylo", "yhi")
+
+
+def plane_index(x, y):
+    return (x % 4) * 8 + (y % 2) * 4 + (y % 8) // 2
+
+
+def from_neighbour(a, dx, dy):
+    pairs = [(plane_index(x + dx, y + dy), plane_index(x, y)) for x in range(4) for y in range(8)]
+    return lax.ppermute(a, PLANE, pairs)
+
+
+def transpose_classes(a):
+    pairs = []
+    for x in range(4):
+        for ylo in range(2):
+            for yhi in range(4):
+                cls = (x % 2) * 2 + ylo
+                source = ((x // 2) * 2 + yhi // 2) * 8 + (yhi % 2) * 4 + cls
+                pairs.append((source, x * 8 + ylo * 4 + yhi))
+    return lax.ppermute(a, PLANE, pairs)
+
+
+def swap_cores(a):
+    return lax.ppermute(a, "core", [(0, 1), (1, 0)])
+
+
+def gather_weights(w_so, w_qkv, w_out, core):
+    shard = jnp.concatenate([w_so, w_out, w_qkv.T], 0)
+    shard = transpose_classes(shard)
+    shards = lax.all_gather(shard, "core", axis=0)
+    shards = lax.all_gather(shards, "z", axis=0).reshape(16, 45, D)
+    rows = lambda n: ((n, D), BF)
+    own_so, own_out, own_qkv, h0, h1, *corners = call(
+        compact_kernel,
+        [rows(144), rows(144), rows(432), rows(192), rows(192)] + [rows(96)] * 4,
+        core, shards, scalars=1,
+        scratch=[pltpu.VMEM((144, D), F32), pltpu.VMEM((144, D), F32), pltpu.VMEM((432, D), F32)],
+    )
+    near = [
+        from_neighbour(h0, 1, 0),
+        from_neighbour(h1, -1, 0),
+        from_neighbour(h0, 0, 1),
+        from_neighbour(h1, 0, -1),
+    ]
+    steps = ((1, 1), (1, -1), (-1, 1), (-1, -1))
+    diagonal = [from_neighbour(a, dx, dy) for a, (dx, dy) in zip(corners, steps)]
+    swapped = [swap_cores(jnp.concatenate(near, 0)), swap_cores(jnp.concatenate(diagonal, 0))]
+    return [own_so, own_out, own_qkv] + near + diagonal + swapped
+
+
 def body(tokens, qkv, w_so, w_qkv, w_out, factors, cotangent):
     tokens, qkv, cotangent, factors = tokens[0, 0], qkv[0, 0], cotangent[0, 0], factors[0]
-    shard = jnp.concatenate([w_so, w_out, w_qkv.T], 0)
-    gathered = lax.all_gather(shard, SEQ, axis=0)
-    w_so = gathered[:, :9].reshape(ATT, D)
-    w_out = gathered[:, 9:18].reshape(ATT, D)
-    w_qkv = gathered[:, 18:].reshape(3 * ATT, D)
-
-    tokens_p = exchange(tokens.reshape(64, 2, D)).reshape(ROWS, D)
-    cot_p = exchange(cotangent.reshape(64, 2, D)).reshape(ROWS, D)
+    core = lax.axis_index("core").astype(jnp.int32)
+    cls = (lax.axis_index("x") % 2) * 2 + lax.axis_index("ylo")
+    place = jnp.stack([core, cls.astype(jnp.int32)])
+    weights = gather_weights(w_so, w_qkv, w_out, core.reshape(1))
+
     (mixed_s,) = call(spatial_forward_kernel, [((ROWS, ATT), BF)], qkv)
-    mixed_p = exchange(mixed_s.reshape(64, 2, ATT)).reshape(ROWS, ATT)
-
-    core = lax.axis_index("core").astype(jnp.int32).reshape(1)
+    sent = jnp.concatenate([tokens, cotangent, mixed_s], 1).reshape(64, 2, 2 * D + ATT)
+    sent = exchange(sent).reshape(ROWS, 2 * D + ATT)
+
     hidden_grad, d_mixed, factor_part, out_keep, out_send = call(
         temporal_kernel,
-        [((ROWS, D), BF), ((ROWS, ATT), BF), ((4, D), F32), ((288, D), F32), ((288, D), BF)],
-        core, tokens_p, cot_p, mixed_p, w_so, w_qkv, w_out, factors,
-        scalars=1, flops=4 * 10**9,
-    )
-
-    out_other = lax.ppermute(out_send, "core", [(0, 1), (1, 0)])
-    packed = jnp.concatenate([hidden_grad, d_mixed], 1)
-    back = exchange(packed.reshape(64, 2, D + ATT)).reshape(ROWS, D + ATT)
-    token_grad = back[:, :D]
-    (qkv_grad,) = call(spatial_backward_kernel, [((ROWS, 3 * ATT), BF)], qkv, back[:, D:])
-
-    out_part = (out_keep + out_other.astype(F32)).astype(BF).reshape(32, 2, 9 * D // 2)
-    out_part = lax.all_to_all(out_part, CHIPS, 0, 0, tiled=True)
-    out_part = jnp.sum(out_part.astype(F32), 0)
-    out_part = lax.all_to_all(jnp.broadcast_to(out_part[None], (8, 2, 9 * D // 2)), DP, 0, 0, tiled=True)
-    out_grad = jnp.sum(out_part, 0).reshape(9, D)
-
-    factor_part = jnp.sum(exchange(factor_part.reshape(64, 1, 72)), 0)
-    factor_grad = exchange(jnp.broadcast_to(factor_part[None], (64, 1, 72)))
-    factor_grad = factor_grad.reshape(4, D)
-    return token_grad[None, None], qkv_grad[None, None], factor_grad[None], out_grad
+        [((ROWS, D), BF), ((ROWS, ATT), BF), ((4, D), F32), ((ATT, ATT), F32), ((ATT, ATT), BF)],
+        place, sent[:, :D], sent[:, D : 2 * D], sent[:, 2 * D :], factors, *weights,
+        scalars=1, remote=len(weights), flops=4 * 10**9,
+        scratch=[
+            pltpu.VMEM((3 * ATT, D), BF),
+            pltpu.VMEM((ATT, D), BF),
+            pltpu.VMEM((ATT, D), BF),
+            pltpu.SemaphoreType.DMA((48,)),
+        ],
+    )
+
+    out_part = (out_keep + swap_cores(out_send).astype(F32)).astype(BF)
+    packed = jnp.concatenate(
+        [
+            jnp.concatenate([hidden_grad, d_mixed], 1).reshape(64, 2, D + ATT),
+            out_part.reshape(64, 2, 9 * ATT // 2),
+            jnp.broadcast_to(factor_part.astype(BF).reshape(1, 2, 2, D), (32, 2, 2, D)).reshape(64, 2, D),
+            jnp.zeros((64, 2, 32), BF),
+        ],
+        2,
+    )
+    back = exchange(packed)
+    rows = back[:, :, : D + ATT].reshape(ROWS, D + ATT)
+    token_grad = rows[:, :D]
+    (qkv_grad,) = call(spatial_backward_kernel, [((ROWS, 3 * ATT), BF)], qkv, rows[:, D:])
+
+    out_part = back[:, :, D + ATT : D + ATT + 9 * ATT // 2].astype(F32)
+    out_part = jnp.sum(out_part.reshape(32, 2, 2, 9 * ATT // 2), 0)
+    out_part = jnp.broadcast_to(out_part.reshape(1, 2, 9 * ATT), (8, 2, 9 * ATT))
+    out_part = jnp.sum(lax.all_to_all(out_part, DP, 0, 0, tiled=True), 0)
+    out_grad = out_part.reshape(2, 9, ATT).transpose(1, 0, 2).reshape(9, D)
+
+    mine = jnp.sum(back[:, :, D + ATT + 9 * ATT // 2 :][:, :, :D].astype(F32), 0)
+    other = swap_cores(mine)
+    factor_grad = jnp.where(core == 0, jnp.stack([mine, other]), jnp.stack([other, mine]))
+    return token_grad[None, None], qkv_grad[None, None], factor_grad.reshape(1, 4, D), out_grad
 
 
 def solution(mesh):

time: 271 us -> 269 us (level)
  starting transfers between devices: 51.3 us -> 69.8 us
  local copies, waits for them, and re-layouts: 44.1 us -> 32.7 us
  blocking collectives: 18.9 us -> 8.62 us
  waiting for transfers between devices: 122 us -> 112 us
  other arithmetic: 4.6 us -> 8.88 us
  Pallas kernels: 13.8 us -> 17.8 us
    ppermute x1 -> x13, starting transfers between devices: 2.16 us -> 39.8 us  [the longest x8 29.2 us: from_neighbour(): return lax.ppermute(a, PLANE, pairs)]
    all_to_all x5 -> x2, waiting for transfers between devices: 64.3 us -> 44.1 us  [exchange(): return lax.all_to_all(a, SEQ, 0, 0, tiled=True)]
    all_to_all x2 -> x1, waiting for transfers between devices: 23.1 us -> 3.25 us  [body(): out_part = jnp.sum(lax.all_to_all(out_part, DP, 0, 0, tiled=True), 0)]
    all_to_all x1 -> x0, blocking collectives: 18.9 us -> none  [exchange(): return lax.all_to_all(a, SEQ, 0, 0, tiled=True)]
    ppermute x1 -> x13, waiting for transfers between devices: 0.01 us -> 15.6 us  [the longest x8 13.8 us: from_neighbour(): return lax.ppermute(a, PLANE, pairs)]
    all_gather x1, waiting for transfers between devices: 35 us -> 49.4 us  [gather_weights(): shards = lax.all_gather(shards, 'z', axis=0).reshape(16, 45, D)]
    all_to_all x5 -> x2, starting transfers between devices: 40.6 us -> 26.6 us  [exchange(): return lax.all_to_all(a, SEQ, 0, 0, tiled=True)]
    reshape x12 -> x6, local copies, waits for them, and re-layouts: 19.4 us -> 5.51 us  [the longest x1 2.9 us: body(): sent = exchange(sent).reshape(ROWS, 2 * D + ATT)]
  transfers between devices with their start and end apart: 9 -> 17, of which waited for: 8 -> 8; matrix products, arithmetic and copies ran while one was open for 6% -> 8% of each run, Pallas kernels for 1% -> 1%
where the time goes in v2:
time: 269 us; the launch traced here: 265 us
  waiting for transfers between devices  112 us (42%)
  starting transfers between devices  69.8 us (26%)
  local copies, waits for them, and re-layouts  32.7 us (12%)
  Pallas kernels  17.8 us (7%)
  between operations  14.5 us (5%)
  other arithmetic  8.88 us (3%)
  blocking collectives  8.62 us (3%)
    all_gather x1, waiting for transfers between devices, gather_weights(): shards = lax.all_gather(shards, 'z', axis=0).reshape(16, 45, D)  49.4 us
    all_to_all x2, waiting for transfers between devices, exchange(): return lax.all_to_all(a, SEQ, 0, 0, tiled=True)  44.1 us
    ppermute x8, starting transfers between devices, from_neighbour(): return lax.ppermute(a, PLANE, pairs)  29.2 us
    all_to_all x2, starting transfers between devices, exchange(): return lax.all_to_all(a, SEQ, 0, 0, tiled=True)  26.6 us
    pallas_call x4, Pallas kernels, call(): pl.pallas_call(kernel, out_shape=[jax.ShapeDtypeStruct(s, d) for s, d in...  17.8 us
    ppermute x8, waiting for transfers between devices, from_neighbour(): return lax.ppermute(a, PLANE, pairs)  13.8 us
    ppermute x4, starting transfers between devices, swap_cores(): return lax.ppermute(a, 'core', [(0, 1), (1, 0)])  9.95 us
    unnamed x28, local copies, waits for them, and re-layouts  9.18 us
  transfers between devices with their start and end apart: 17, of which 8 were waited for; matrix products, arithmetic and copies ran while one was open for 8% of the time, Pallas kernels for 1%

profile of v2, /device:TPU:1, one launch (start us, length us, event | category | flops | bytes accessed | tf_op | source)
XLA Modules:
  0.0 264.7 jit_solution(5855694237584640071)
XLA Ops:
  8.8 8.6 %all-gather.2 = bf16[2,45,1152]{2,1,0:T(8,128)(2,1)} all-gather(bf16[1,45,1152]{2,1,0:T(8,128)(2,1)S(1)} %bitcast.26), channel_id=2, replica_groups=mesh['x'=4,'ylo'=2,'yhi'=4,'z'=8,'core'=2] {'core'}, dimensions={0}, use_global_device_ids=true | all-gather | bytes 311040 | tf_op jit(solution)/shard_map/all_gather | solution.py:268
  18.7 49.4 %all-gather.5.cloned.1.call-done.shards = bf16[16,45,1152]{2,1,0:T(8,128)(2,1)} async-done(((bf16[2,45,1152]{2,1,0:T(8,128)(2,1)}), bf16[16,45,1152]{2,1,0:T(8,128)(2,1)}) %all-gather.5.cloned.1.call-update) | async-done | bytes 1658896 | tf_op jit(solution)/shard_map/all_gather | solution.py:269
  74.8 4.3 %collective-permute-start.1 = (bf16[192,1152]{1,0:T(8,128)(2,1)S(1)}, bf16[192,1152]{1,0:T(8,128)(2,1)S(1)}, u32[]{:S(2)}, u32[]{:S(2)}) collective-permute-start(bf16[192,1152]{1,0:T(8,128)(2,1)S(1)} %get-tuple-element.21), channel_id=1, source_target_pairs={{128,0},{192,64},{144,16},{208,80},{160,32},{224,96},{176,48},{240... | collective-permute-start | bytes 1327112 | tf_op jit(solution)/shard_map/ppermute | solution.py:247
  79.1 4.5 %collective-permute-start.3 = (bf16[192,1152]{1,0:T(8,128)(2,1)S(1)}, bf16[192,1152]{1,0:T(8,128)(2,1)S(1)}, u32[]{:S(2)}, u32[]{:S(2)}) collective-permute-start(bf16[192,1152]{1,0:T(8,128)(2,1)S(1)} %get-tuple-element.21), channel_id=1, source_target_pairs={{64,0},{16,64},{80,16},{32,80},{96,32},{48,96},{112,48},{0,112},{1... | collective-permute-start | bytes 1327112 | tf_op jit(solution)/shard_map/ppermute | solution.py:247
  83.6 1.9 collective-permute-start.2
  85.5 1.9 collective-permute-start.4
  87.4 1.5 shard_map.102
  89.7 1.8 concatenate.25
  91.5 1.8 concatenate.26
  93.3 2.7 %pad_maximum_fusion.2 = bf16[64,2,2880]{2,1,0:T(2,128)(2,1)} fusion(bf16[64,2,576]{2,1,0:T(2,128)(2,1)} %concatenate.27, bf16[64,2,1152]{2,1,0:T(2,128)(2,1)} %concatenate.26, bf16[64,2,1152]{2,1,0:T(2,128)(2,1)} %concatenate.25), kind=kLoop, calls=%fused_computation.4 | loop fusion | flops 2211840 | bytes 1474560 | tf_op jit(solution)/shard_map/concatenate | solution.py:297
  96.0 14.0 %all-to-all-start = ((bf16[64,2,2880]{2,1,0:T(2,128)(2,1)}), bf16[64,2,2880]{2,1,0:T(2,128)(2,1)}, u32[]{:S(2)}, u32[]{:S(2)}) async-start(bf16[64,2,2880]{2,1,0:T(2,128)(2,1)} %pad_maximum_fusion.2), calls=%async_computation | async-start | bytes 1507328 | tf_op jit(solution)/shard_map/all_to_all | solution.py:235
  111.4 2.4 collective-permute-start.9
  113.9 7.2 %collective-permute-start.5 = (bf16[96,1152]{1,0:T(8,128)(2,1)S(1)}, bf16[96,1152]{1,0:T(8,128)(2,1)S(1)}, u32[]{:S(2)}, u32[]{:S(2)}) collective-permute-start(bf16[96,1152]{1,0:T(8,128)(2,1)S(1)} %copy-done.6), channel_id=1, source_target_pairs={{192,0},{144,64},{208,16},{160,80},{224,32},{176,96},{240,48},{128... | collective-permute-start | bytes 663560 | tf_op jit(solution)/shard_map/ppermute | solution.py:247
  121.1 1.9 collective-permute-start.6
  123.1 5.5 %collective-permute-start.7 = (bf16[96,1152]{1,0:T(8,128)(2,1)S(1)}, bf16[96,1152]{1,0:T(8,128)(2,1)S(1)}, u32[]{:S(2)}, u32[]{:S(2)}) collective-permute-start(bf16[96,1152]{1,0:T(8,128)(2,1)S(1)} %copy-done.2), channel_id=1, source_target_pairs={{448,0},{400,64},{464,16},{416,80},{480,32},{432,96},{496,48},{384... | collective-permute-start | bytes 663560 | tf_op jit(solution)/shard_map/ppermute | solution.py:247
  128.6 1.9 collective-permute-start.8
  130.5 2.7 %collective-permute-done.5.d0 = bf16[96,1152]{1,0:T(8,128)(2,1)S(1)} collective-permute-done((bf16[96,1152]{1,0:T(8,128)(2,1)S(1)}, bf16[96,1152]{1,0:T(8,128)(2,1)S(1)}, u32[]{:S(2)}, u32[]{:S(2)}) %collective-permute-start.5) | collective-permute-done | bytes 221216 | tf_op jit(solution)/shard_map/ppermute | solution.py:247
  133.2 3.9 %collective-permute-done.6.d1 = bf16[96,1152]{1,0:T(8,128)(2,1)S(1)} collective-permute-done((bf16[96,1152]{1,0:T(8,128)(2,1)S(1)}, bf16[96,1152]{1,0:T(8,128)(2,1)S(1)}, u32[]{:S(2)}, u32[]{:S(2)}) %collective-permute-start.6) | collective-permute-done | bytes 221216 | tf_op jit(solution)/shard_map/ppermute | solution.py:247
  137.1 4.2 %collective-permute-done.7.d2 = bf16[96,1152]{1,0:T(8,128)(2,1)S(1)} collective-permute-done((bf16[96,1152]{1,0:T(8,128)(2,1)S(1)}, bf16[96,1152]{1,0:T(8,128)(2,1)S(1)}, u32[]{:S(2)}, u32[]{:S(2)}) %collective-permute-start.7) | collective-permute-done | bytes 221216 | tf_op jit(solution)/shard_map/ppermute | solution.py:247
  141.3 2.9 %collective-permute-done.8.d3 = bf16[96,1152]{1,0:T(8,128)(2,1)S(1)} collective-permute-done((bf16[96,1152]{1,0:T(8,128)(2,1)S(1)}, bf16[96,1152]{1,0:T(8,128)(2,1)S(1)}, u32[]{:S(2)}, u32[]{:S(2)}) %collective-permute-start.8) | collective-permute-done | bytes 221216 | tf_op jit(solution)/shard_map/ppermute | solution.py:247
  145.2 3.2 %collective-permute-start.10 = (bf16[384,1152]{1,0:T(8,128)(2,1)}, bf16[384,1152]{1,0:T(8,128)(2,1)}, u32[]{:S(2)}, u32[]{:S(2)}) collective-permute-start(bf16[384,1152]{1,0:T(8,128)(2,1)} %pad_maximum_fusion.1), channel_id=1, source_target_pairs={{0,1},{1,0},{2,3},{3,2},{4,5},{5,4},{6,7},{7,6},{8,9},{9,8},{10,11... | collective-permute-start | bytes 2654216 | tf_op jit(solution)/shard_map/ppermute | solution.py:262
  148.5 2.9 %reshape.69 = bf16[128,2880]{1,0:T(8,128)(2,1)} reshape(bf16[64,2,2880]{2,1,0:T(2,128)(2,1)} %all-to-all-done) | data formatting | bytes 1474560 | tf_op jit(solution)/shard_map/reshape | solution.py:298
  154.5 13.6 %shard_map.104 = (bf16[128,1152]{1,0:T(8,128)(2,1)S(1)}, bf16[128,576]{1,0:T(8,128)(2,1)S(1)}, f32[4,1152]{1,0:T(4,128)S(1)}, f32[576,576]{1,0:T(8,128)}, bf16[576,576]{1,0:T(8,128)(2,1)}) custom-call(s32[2]{0:T(128)S(1)} %pad_add_fusion.place, bf16[128,1152]{1,0:T(8,128)(2,1)S(1)} %get-tuple-element.57.tokens, ...), custom_call_target="tpu_custom_call" | custom-call | flops 4000000000 | bytes 10000000 | tf_op jit(solution)/shard_map/pallas_call | solution.py:223
  168.1 2.2 collective-permute-start.11
  170.5 1.9 collective-permute-done.11
  175.4 7.6 %concatenate.33 = bf16[64,2,5504]{2,1,0:T(2,128)(2,1)} concatenate(bf16[64,2,1728]{2,1,0:T(2,128)(2,1)S(1)} %reshape.71, bf16[64,2,2592]{2,1,0:T(2,128)(2,1)S(1)} %reshape.72, bf16[64,2,1152]{2,1,0:T(2,128)(2,1)S(1)} %bitcast.24, bf16[64,2,32]{2,1,0:T(2,128)(2,1)S(1)} %broadcast_in_dim.25), dimensions={2} | concatenate | bytes 2818048 | tf_op jit(solution)/shard_map/concatenate | solution.py:314
  182.9 12.5 %all-to-all-start.1 = ((bf16[64,2,5504]{2,1,0:T(2,128)(2,1)}), bf16[64,2,5504]{2,1,0:T(2,128)(2,1)S(1)}, u32[]{:S(2)}, u32[]{:S(2)}) async-start(bf16[64,2,5504]{2,1,0:T(2,128)(2,1)} %concatenate.33), calls=%async_computation.1 | async-start | bytes 2818048 | tf_op jit(solution)/shard_map/all_to_all | solution.py:235
  195.5 44.1 %all-to-all-done.1 = bf16[64,2,5504]{2,1,0:T(2,128)(2,1)S(1)} async-done(((bf16[64,2,5504]{2,1,0:T(2,128)(2,1)}), bf16[64,2,5504]{2,1,0:T(2,128)(2,1)S(1)}, u32[]{:S(2)}, u32[]{:S(2)}) %all-to-all-start.1) | async-done | bytes 1409056 | tf_op jit(solution)/shard_map/all_to_all | solution.py:235
  240.2 2.1 collective-permute-start.12
  245.8 3.4 %all-to-all-start.2 = ((f32[8,2,5184]{2,1,0:T(2,128)}), f32[8,2,5184]{2,1,0:T(2,128)S(1)}, u32[]{:S(2)}, u32[]{:S(2)}) async-start(f32[8,2,5184]{2,1,0:T(2,128)} %broadcast_in_dim.29), calls=%async_computation.2 | async-start | bytes 671744 | tf_op jit(solution)/shard_map/all_to_all | solution.py:331
  250.0 2.0 shard_map.105
  253.7 3.3 %all-to-all-done.2 = f32[8,2,5184]{2,1,0:T(2,128)S(1)} async-done(((f32[8,2,5184]{2,1,0:T(2,128)}), f32[8,2,5184]{2,1,0:T(2,128)S(1)}, u32[]{:S(2)}, u32[]{:S(2)}) %all-to-all-start.2) | async-done | bytes 331808 | tf_op jit(solution)/shard_map/all_to_all | solution.py:331
  (71 shorter events, 26.2 us)
Async XLA Ops:
  7.2 61.0 %all-gather.5.cloned.1.call-start = ((), (), s32[]{:S(2)}) async-start(), calls=%async_computation.3 | async-start | bytes 1990656 | tf_op jit(solution)/shard_map/all_gather | solution.py:269
  8.1 0.7 collective-permute-start
  68.1 1.5 copy-start
  70.3 0.7 copy-start.1
  70.9 0.7 copy-start.3
  71.7 0.7 copy-start.5
  72.4 1.0 copy-start.8
  73.3 0.7 copy-start.9
  74.0 0.7 copy-start.11
  74.8 35.3 %collective-permute-start.1 = (bf16[192,1152]{1,0:T(8,128)(2,1)S(1)}, bf16[192,1152]{1,0:T(8,128)(2,1)S(1)}, u32[]{:S(2)}, u32[]{:S(2)}) collective-permute-start(bf16[192,1152]{1,0:T(8,128)(2,1)S(1)} %get-tuple-element.21), channel_id=1, source_target_pairs={{128,0},{192,64},{144,16},{208,80},{160,32},{224,96},{176,48},{240... | collective-permute-start | bytes 1327112 | tf_op jit(solution)/shard_map/ppermute | solution.py:247
  79.1 31.0 %collective-permute-start.3 = (bf16[192,1152]{1,0:T(8,128)(2,1)S(1)}, bf16[192,1152]{1,0:T(8,128)(2,1)S(1)}, u32[]{:S(2)}, u32[]{:S(2)}) collective-permute-start(bf16[192,1152]{1,0:T(8,128)(2,1)S(1)} %get-tuple-element.21), channel_id=1, source_target_pairs={{64,0},{16,64},{80,16},{32,80},{96,32},{48,96},{112,48},{0,112},{1... | collective-permute-start | bytes 1327112 | tf_op jit(solution)/shard_map/ppermute | solution.py:247
  83.6 26.5 %collective-permute-start.2 = (bf16[192,1152]{1,0:T(8,128)(2,1)S(1)}, bf16[192,1152]{1,0:T(8,128)(2,1)S(1)}, u32[]{:S(2)}, u32[]{:S(2)}) collective-permute-start(bf16[192,1152]{1,0:T(8,128)(2,1)S(1)} %get-tuple-element.22), channel_id=1, source_target_pairs={{384,0},{448,64},{400,16},{464,80},{416,32},{480,96},{432,48},{496... | collective-permute-start | bytes 1327112 | tf_op jit(solution)/shard_map/ppermute | solution.py:247
  85.5 24.6 %collective-permute-start.4 = (bf16[192,1152]{1,0:T(8,128)(2,1)S(1)}, bf16[192,1152]{1,0:T(8,128)(2,1)S(1)}, u32[]{:S(2)}, u32[]{:S(2)}) collective-permute-start(bf16[192,1152]{1,0:T(8,128)(2,1)S(1)} %get-tuple-element.22), channel_id=1, source_target_pairs={{112,0},{0,64},{64,16},{16,80},{80,32},{32,96},{96,48},{48,112},{2... | collective-permute-start | bytes 1327112 | tf_op jit(solution)/shard_map/ppermute | solution.py:247
  96.0 52.5 %all-to-all-start = ((bf16[64,2,2880]{2,1,0:T(2,128)(2,1)}), bf16[64,2,2880]{2,1,0:T(2,128)(2,1)}, u32[]{:S(2)}, u32[]{:S(2)}) async-start(bf16[64,2,2880]{2,1,0:T(2,128)(2,1)} %pad_maximum_fusion.2), calls=%async_computation | async-start | bytes 1507328 | tf_op jit(solution)/shard_map/all_to_all | solution.py:235
  110.0 3.8 %copy-start.6 = (bf16[96,1152]{1,0:T(8,128)(2,1)S(1)}, bf16[96,1152]{1,0:T(8,128)(2,1)}, u32[]{:S(2)}) copy-start(bf16[96,1152]{1,0:T(8,128)(2,1)} %copy-done.5) | copy-start | bytes 663556
  110.1 11.1 %copy-start.4 = (bf16[96,1152]{1,0:T(8,128)(2,1)S(1)}, bf16[96,1152]{1,0:T(8,128)(2,1)}, u32[]{:S(2)}) copy-start(bf16[96,1152]{1,0:T(8,128)(2,1)} %copy-done.3) | copy-start | bytes 663556
  110.1 13.0 %copy-start.2 = (bf16[96,1152]{1,0:T(8,128)(2,1)S(1)}, bf16[96,1152]{1,0:T(8,128)(2,1)}, u32[]{:S(2)}) copy-start(bf16[96,1152]{1,0:T(8,128)(2,1)} %copy-done.1) | copy-start | bytes 663556
  111.4 42.0 %collective-permute-start.9 = (bf16[768,1152]{1,0:T(8,128)(2,1)}, bf16[768,1152]{1,0:T(8,128)(2,1)}, u32[]{:S(2)}, u32[]{:S(2)}) collective-permute-start(bf16[768,1152]{1,0:T(8,128)(2,1)} %pad_maximum_fusion), channel_id=1, source_target_pairs={{0,1},{1,0},{2,3},{3,2},{4,5},{5,4},{6,7},{7,6},{8,9},{9,8},{10,11... | collective-permute-start | bytes 5308424 | tf_op jit(solution)/shard_map/ppermute | solution.py:262
  113.9 19.3 %collective-permute-start.5 = (bf16[96,1152]{1,0:T(8,128)(2,1)S(1)}, bf16[96,1152]{1,0:T(8,128)(2,1)S(1)}, u32[]{:S(2)}, u32[]{:S(2)}) collective-permute-start(bf16[96,1152]{1,0:T(8,128)(2,1)S(1)} %copy-done.6), channel_id=1, source_target_pairs={{192,0},{144,64},{208,16},{160,80},{224,32},{176,96},{240,48},{128... | collective-permute-start | bytes 663560 | tf_op jit(solution)/shard_map/ppermute | solution.py:247
  121.1 16.0 %collective-permute-start.6 = (bf16[96,1152]{1,0:T(8,128)(2,1)S(1)}, bf16[96,1152]{1,0:T(8,128)(2,1)S(1)}, u32[]{:S(2)}, u32[]{:S(2)}) collective-permute-start(bf16[96,1152]{1,0:T(8,128)(2,1)S(1)} %copy-done.4), channel_id=1, source_target_pairs={{240,0},{128,64},{192,16},{144,80},{208,32},{160,96},{224,48},{176... | collective-permute-start | bytes 663560 | tf_op jit(solution)/shard_map/ppermute | solution.py:247
  123.1 18.2 %collective-permute-start.7 = (bf16[96,1152]{1,0:T(8,128)(2,1)S(1)}, bf16[96,1152]{1,0:T(8,128)(2,1)S(1)}, u32[]{:S(2)}, u32[]{:S(2)}) collective-permute-start(bf16[96,1152]{1,0:T(8,128)(2,1)S(1)} %copy-done.2), channel_id=1, source_target_pairs={{448,0},{400,64},{464,16},{416,80},{480,32},{432,96},{496,48},{384... | collective-permute-start | bytes 663560 | tf_op jit(solution)/shard_map/ppermute | solution.py:247
  128.6 15.7 %collective-permute-start.8 = (bf16[96,1152]{1,0:T(8,128)(2,1)S(1)}, bf16[96,1152]{1,0:T(8,128)(2,1)S(1)}, u32[]{:S(2)}, u32[]{:S(2)}) collective-permute-start(bf16[96,1152]{1,0:T(8,128)(2,1)S(1)} %get-tuple-element.26), channel_id=1, source_target_pairs={{496,0},{384,64},{448,16},{400,80},{464,32},{416,96},{480,48},{432... | collective-permute-start | bytes 663560 | tf_op jit(solution)/shard_map/ppermute | solution.py:247
  145.2 8.3 %copy-start.7 = (f32[1,4,1152]{2,1,0:T(4,128)S(1)}, f32[1,4,1152]{2,1,0:T(4,128)}, u32[]{:S(2)}) copy-start(f32[1,4,1152]{2,1,0:T(4,128)} %param.12) | copy-start | bytes 55300
  145.2 8.3 %copy-start.10 = (bf16[144,1152]{1,0:T(8,128)(2,1)S(1)}, bf16[144,1152]{1,0:T(8,128)(2,1)}, u32[]{:S(2)}) copy-start(bf16[144,1152]{1,0:T(8,128)(2,1)} %copy-done.9) | copy-start | bytes 995332
  145.2 8.2 %collective-permute-start.10 = (bf16[384,1152]{1,0:T(8,128)(2,1)}, bf16[384,1152]{1,0:T(8,128)(2,1)}, u32[]{:S(2)}, u32[]{:S(2)}) collective-permute-start(bf16[384,1152]{1,0:T(8,128)(2,1)} %pad_maximum_fusion.1), channel_id=1, source_target_pairs={{0,1},{1,0},{2,3},{3,2},{4,5},{5,4},{6,7},{7,6},{8,9},{9,8},{10,11... | collective-permute-start | bytes 2654216 | tf_op jit(solution)/shard_map/ppermute | solution.py:262
  153.5 1.0 copy-start.12
  168.1 4.3 %collective-permute-start.11 = (bf16[576,576]{1,0:T(8,128)(2,1)}, bf16[576,576]{1,0:T(8,128)(2,1)S(1)}, u32[]{:S(2)}, u32[]{:S(2)}) collective-permute-start(bf16[576,576]{1,0:T(8,128)(2,1)} %get-tuple-element.30), channel_id=1, source_target_pairs={{0,1},{1,0},{2,3},{3,2},{4,5},{5,4},{6,7},{7,6},{8,9},{9,8},{10,11... | collective-permute-start | bytes 1990664 | tf_op jit(solution)/shard_map/ppermute | solution.py:262
  182.9 56.7 %all-to-all-start.1 = ((bf16[64,2,5504]{2,1,0:T(2,128)(2,1)}), bf16[64,2,5504]{2,1,0:T(2,128)(2,1)S(1)}, u32[]{:S(2)}, u32[]{:S(2)}) async-start(bf16[64,2,5504]{2,1,0:T(2,128)(2,1)} %concatenate.33), calls=%async_computation.1 | async-start | bytes 2818048 | tf_op jit(solution)/shard_map/all_to_all | solution.py:235
  240.2 12.8 %collective-permute-start.12 = (f32[2,1152]{1,0:T(2,128)S(1)}, f32[2,1152]{1,0:T(2,128)S(1)}, u32[]{:S(2)}, u32[]{:S(2)}) collective-permute-start(f32[2,1152]{1,0:T(2,128)S(1)} %convert_reduce_fusion.1), channel_id=1, source_target_pairs={{0,1},{1,0},{2,3},{3,2},{4,5},{5,4},{6,7},{7,6},{8,9},{9,8},{10,11... | collective-permute-start | bytes 27656 | tf_op jit(solution)/shard_map/ppermute | solution.py:262
  245.8 11.1 %all-to-all-start.2 = ((f32[8,2,5184]{2,1,0:T(2,128)}), f32[8,2,5184]{2,1,0:T(2,128)S(1)}, u32[]{:S(2)}, u32[]{:S(2)}) async-start(f32[8,2,5184]{2,1,0:T(2,128)} %broadcast_in_dim.29), calls=%async_computation.2 | async-start | bytes 671744 | tf_op jit(solution)/shard_map/all_to_all | solution.py:331
Sparse Core Ops, SparseCore 0:
  17.6 50.4 all-gather.4

commit v3 on v2

v3 whole, which is shorter than its diff:
```python
import math

import jax
import jax.numpy as jnp
from jax import lax
from jax.experimental import pallas as pl
from jax.experimental.pallas import tpu as pltpu
from jax.sharding import Mesh
from jax.sharding import PartitionSpec as P

D = 1152
HEADS = 8
HS = 72
ATT = 576
ROWS = 128
SCALE = 1.0 / math.sqrt(HS)
SEQ = ("yhi", "z", "core")
CHIPS = ("yhi", "z")
DP = ("x", "ylo")
BF = jnp.bfloat16
F32 = jnp.float32


def nn(a, b):
    return lax.dot_general(a, b, (((1,), (0,)), ((), ())), preferred_element_type=F32)


def nt(a, b):
    return lax.dot_general(a, b, (((1,), (1,)), ((), ())), preferred_element_type=F32)


def tn(a, b):
    return lax.dot_general(a, b, (((0,), (0,)), ((), ())), preferred_element_type=F32)


def head_masks():
    head = lax.broadcasted_iota(jnp.int32, (ROWS, ATT), 1) // HS
    return [head == h for h in range(HEADS)]


def stack_heads(masks, a):
    zero = jnp.zeros_like(a)
    return jnp.concatenate([jnp.where(m, a, zero) for m in masks], 0)


def pick_heads(masks, a):
    out = a[:ROWS]
    for h in range(1, HEADS):
        out = jnp.where(masks[h], a[h * ROWS : (h + 1) * ROWS], out)
    return out


def softmax_rows(scores):
    top = jnp.max(scores, -1, keepdims=True)
    weights = jnp.exp(scores - top)
    return weights / jnp.sum(weights, -1, keepdims=True)


def attend(masks, q, k, v, same):
    q_stack = stack_heads(masks, q)
    scores = nt(q_stack, k) * SCALE
    if same is not None:
        scores = jnp.where(same, scores, -1e30)
    probs = softmax_rows(scores)
    probs_b = probs.astype(BF)
    mixed = pick_heads(masks, nn(probs_b, v)).astype(BF)
    return q_stack, probs, probs_b, mixed


def attend_back(masks, q_stack, k, v, probs, probs_b, d_mixed):
    d_stack = stack_heads(masks, d_mixed)
    d_probs = nt(d_stack, v).astype(BF).astype(F32)
    d_v = tn(probs_b, d_stack)
    d_scores = probs * (d_probs - jnp.sum(d_probs * probs, -1, keepdims=True)) * SCALE
    d_scores = d_scores.astype(BF)
    d_q = pick_heads(masks, nn(d_scores, k))
    d_k = tn(d_scores, q_stack)
    return d_q.astype(BF), d_k.astype(BF), d_v.astype(BF)


def spatial_forward_kernel(qkv, mixed):
    q, k, v = qkv[:, :ATT], qkv[:, ATT : 2 * ATT], qkv[:, 2 * ATT :]
    mixed[...] = attend(head_masks(), q, k, v, None)[3]


def spatial_backward_kernel(qkv, d_mixed, out):
    q, k, v = qkv[:, :ATT], qkv[:, ATT : 2 * ATT], qkv[:, 2 * ATT :]
    masks = head_masks()
    q_stack, probs, probs_b, _ = attend(masks, q, k, v, None)
    d_q, d_k, d_v = attend_back(masks, q_stack, k, v, probs, probs_b, d_mixed[...])
    out[:, :ATT] = d_q
    out[:, ATT : 2 * ATT] = d_k
    out[:, 2 * ATT :] = d_v


def compact_kernel(place, mine, other, own_so, own_out, own_qkv, part, slots, so, out, qkv):
    core, z = place[0], place[2]
    for i in range(4):
        slots[core * 4 + i] = mine[i]
        slots[(1 - core) * 4 + i] = other[i]
    for target in range(8):
        delta = (target - z) & 7
        slot = jnp.where(delta <= 4, delta, 12 - delta)
        for c in range(2):
            i = target * 2 + c
            shard = slots[slot, c].astype(F32)
            so[9 * i : 9 * i + 9, :] = shard[:9]
            out[9 * i : 9 * i + 9, :] = shard[9:18]
            qkv[27 * i : 27 * i + 27, :] = shard[18:]
    own_so[...] = so[...].astype(BF)
    own_out[...] = out[...].astype(BF)
    own_qkv[...] = qkv[...].astype(BF)
    at_qkv = pl.multiple_of(core * 208, 16)
    at = pl.multiple_of(core * 64, 16)
    part[0:224, :] = own_qkv[pl.ds(at_qkv, 224), :]
    part[224:304, :] = own_so[pl.ds(at, 80), :]
    part[304:384, :] = own_out[pl.ds(at, 80), :]


SECTIONS = ((0, 0, 224), (1, 224, 304), (2, 304, 384))
BLOCK = (432, 144, 144)
STEP = (208, 64, 64)


def part_copies(ref, half, block, targets):
    copies = []
    for section, first, last in SECTIONS:
        first = first + 16 * half
        row = first - SECTIONS[section][1] + STEP[section] * half
        to = pl.multiple_of(block * BLOCK[section] + row, 16)
        rows = last - first
        copies.append((ref.at[pl.ds(first, rows)], targets[section].at[pl.ds(to, rows)]))
    return copies


def assemble(place, own, near, swapped, targets, sems):
    for me in range(2):

        @pl.when(place[0] == me)
        def _():
            cls = place[1]
            pairs = []
            for section, ref in enumerate(own):
                to = pl.multiple_of(cls * BLOCK[section], 16)
                pairs.append((ref, targets[section].at[pl.ds(to, BLOCK[section])]))
            for flip, ref, other in zip((2, 1, 3), near, swapped):
                pairs += part_copies(ref, me, cls ^ flip, targets)
                pairs += part_copies(other, 1 - me, cls ^ flip, targets)
            copies = [pltpu.make_async_copy(a, z, sems.at[i]) for i, (a, z) in enumerate(pairs)]
            for copy in copies:
                copy.start()
            for copy in copies:
                copy.wait()


def temporal_kernel(
    place, sent, factors, own_qkv, own_so, own_out, b, c, d, other_b, other_c, other_d,
    packed, out_keep, out_send, w_qkv, w_so, w_out, sems,
):
    assemble(
        place, (own_qkv, own_so, own_out), (b, c, d), (other_b, other_c, other_d),
        (w_qkv, w_so, w_out), sems,
    )
    tokens, cotangent, mixed_s = sent[:, :D], sent[:, D : 2 * D], sent[:, 2 * D :]
    gate_s, shift, scale, gate_t = (factors[i : i + 1, :] for i in range(4))
    project = nn(mixed_s, w_so[...])
    hidden = (tokens.astype(F32) + gate_s * project).astype(BF).astype(F32)
    centered = hidden - jnp.mean(hidden, -1, keepdims=True)
    inverse = lax.rsqrt(jnp.mean(centered * centered, -1, keepdims=True) + 1e-06)
    unit = centered * inverse
    normed = (unit * (1.0 + scale) + shift).astype(BF)
    wq, wk, wv = (w_qkv[i * ATT : (i + 1) * ATT, :] for i in range(3))
    q, k, v = (nt(normed, w).astype(BF) for w in (wq, wk, wv))

    masks = head_masks()
    row = lax.broadcasted_iota(jnp.int32, (HEADS * ROWS, ROWS), 0)
    col = lax.broadcasted_iota(jnp.int32, (HEADS * ROWS, ROWS), 1)
    same = ((row ^ col) & 1) == 0
    q_stack, probs, probs_b, mixed = attend(masks, q, k, v, same)

    cot = cotangent.astype(F32)
    scaled = (cot * gate_t).astype(BF)
    left, right = scaled[:, :ATT], scaled[:, ATT:]
    first = place[0] == 0
    out_keep[...] = tn(mixed, jnp.where(first, left, right))
    out_send[...] = tn(mixed, jnp.where(first, right, left)).astype(BF)

    d_mixed = nt(scaled, w_out[...]).astype(BF)
    d_q, d_k, d_v = attend_back(masks, q_stack, k, v, probs, probs_b, d_mixed)
    d_normed = (nn(d_q, wq) + nn(d_k, wk) + nn(d_v, wv)).astype(BF).astype(F32)
    d_unit = d_normed * (1.0 + scale)
    d_hidden = inverse * (
        d_unit
        - jnp.mean(d_unit, -1, keepdims=True)
        - unit * jnp.mean(d_unit * unit, -1, keepdims=True)
    )
    grad = (cot + d_hidden).astype(BF)
    packed[:, :D] = grad
    grad = grad.astype(F32)
    d_mixed_s = nt((grad * gate_s).astype(BF), w_so[...]).astype(BF)
    packed[:, D : D + 640] = jnp.concatenate([d_mixed_s, jnp.zeros((ROWS, 64), BF)], 1)
    project_t = nn(mixed, w_out[...])
    factor_grads = [
        jnp.sum(grad * project, 0, keepdims=True),
        jnp.sum(d_normed, 0, keepdims=True),
        jnp.sum(d_normed * unit, 0, keepdims=True),
        jnp.sum(cot * project_t, 0, keepdims=True),
    ]
    tile = jnp.concatenate(factor_grads * 4, 0).astype(BF)
    for i in range(8):
        packed[16 * i : 16 * i + 16, D + 640 :] = tile


def call(kernel, outs, *args, scalars=0, remote=0, scratch=(), flops=10**9):
    vmem = pl.BlockSpec(memory_space=pltpu.VMEM)
    specs = [pl.BlockSpec(memory_space=pltpu.SMEM)] * scalars
    specs += [vmem] * (len(args) - scalars - remote)
    specs += [pl.BlockSpec(memory_space=pl.ANY)] * remote
    return pl.pallas_call(
        kernel,
        out_shape=[jax.ShapeDtypeStruct(s, d) for s, d in outs],
        in_specs=specs,
        out_specs=[vmem] * len(outs),
        scratch_shapes=list(scratch),
        compiler_params=pltpu.CompilerParams(vmem_limit_bytes=48 * 2**20),
        cost_estimate=pl.CostEstimate(flops=flops, bytes_accessed=10**7, transcendentals=10**5),
    )(*args)


def exchange(a):
    return lax.all_to_all(a, SEQ, 0, 0, tiled=True)


AXES = DP + SEQ


def device(x, y, z, core):
    ylo, yhi = y % 2, (y % 8) // 2
    return ((((x % 4) * 2 + ylo) * 4 + yhi) * 8 + z % 8) * 2 + core


def receive(a, source):
    pairs = []
    for x in range(4):
        for y in range(8):
            for z in range(8):
                for core in range(2):
                    pairs.append((device(*source(x, y, z, core), core), device(x, y, z, core)))
    return lax.ppermute(a, AXES, pairs)


def swap_cores(a):
    return lax.ppermute(a, "core", [(0, 1), (1, 0)])


OFFSETS = ((0, 1, 2, 3), (4, -1, -2, -3))


def shard_source(step):
    def source(x, y, z, core):
        ylo, yhi = y % 2, y // 2
        cls = (x % 2) * 2 + ylo
        return (x // 2) * 2 + yhi // 2, cls * 2 + yhi % 2, z + OFFSETS[core][step]

    return source


def near_source(dx, dy):
    def source(x, y, z, core):
        sign = 1 - 2 * core
        return x + sign * dx, y + sign * dy, z

    return source


def gather_weights(w_so, w_qkv, w_out, place, packed):
    shard = jnp.concatenate([w_so, w_out, w_qkv.T], 0)
    shards = lax.all_gather(shard, "core", axis=0)
    mine = [receive(shards, shard_source(i)) for i in range(4)]
    mine, packed = lax.optimization_barrier((jnp.stack(mine), packed))
    other = swap_cores(mine)
    rows = lambda n: ((n, D), BF)
    own_so, own_out, own_qkv, part = call(
        compact_kernel, [rows(144), rows(144), rows(432), rows(384)], place, mine, other, scalars=1,
        scratch=[
            pltpu.VMEM((8, 2, 45, D), BF),
            pltpu.VMEM((144, D), F32),
            pltpu.VMEM((144, D), F32),
            pltpu.VMEM((432, D), F32),
        ],
    )
    part, packed = lax.optimization_barrier((part, packed))
    near = [receive(part, near_source(dx, dy)) for dx, dy in ((1, 0), (0, 1), (1, 1))]
    return [own_qkv, own_so, own_out] + near + [swap_cores(a) for a in near], packed


def body(tokens, qkv, w_so, w_qkv, w_out, factors, cotangent):
    tokens, qkv, cotangent, factors = tokens[0, 0], qkv[0, 0], cotangent[0, 0], factors[0]
    core = lax.axis_index("core")
    cls = (lax.axis_index("x") % 2) * 2 + lax.axis_index("ylo")
    place = jnp.stack([core, cls, lax.axis_index("z")]).astype(jnp.int32)

    (mixed_s,) = call(spatial_forward_kernel, [((ROWS, ATT), BF)], qkv)
    sent = jnp.concatenate([tokens, cotangent, mixed_s], 1).reshape(64, 2, 2 * D + ATT)
    weights, sent = gather_weights(w_so, w_qkv, w_out, place, sent)
    sent = exchange(sent).reshape(ROWS, 2 * D + ATT)

    packed, out_keep, out_send = call(
        temporal_kernel,
        [((ROWS, 2 * D + 640), BF), ((ATT, ATT), F32), ((ATT, ATT), BF)],
        place, sent, factors, *weights,
        scalars=1, remote=len(weights), flops=4 * 10**9,
        scratch=[
            pltpu.VMEM((3 * ATT, D), BF),
            pltpu.VMEM((ATT, D), BF),
            pltpu.VMEM((ATT, D), BF),
            pltpu.SemaphoreType.DMA((24,)),
        ],
    )

    out_part = (out_keep + swap_cores(out_send).astype(F32)).astype(BF)
    out_part = out_part.reshape(64, 2, 9 * ATT // 2)
    width = 2 * D + 640
    back = exchange(jnp.concatenate([packed.reshape(64, 2, width), out_part], 2))

    out_part = back[:, :, width:].astype(F32).reshape(32, 2, 2, 9 * ATT // 2)
    out_part = jnp.sum(out_part, 0).reshape(1, 2, 9 * ATT)
    out_part = jnp.broadcast_to(out_part, (8, 2, 9 * ATT))
    out_part = jnp.sum(lax.all_to_all(out_part, DP, 0, 0, tiled=True), 0)
    out_grad = out_part.reshape(2, 9, ATT).transpose(1, 0, 2).reshape(9, D)

    rows = back[:, :, : D + ATT].reshape(ROWS, D + ATT)
    token_grad = rows[:, :D]
    (qkv_grad,) = call(spatial_backward_kernel, [((ROWS, 3 * ATT), BF)], qkv, rows[:, D:])

    mine = jnp.sum(back[:, :, D + 640 : width].astype(F32), 0)
    other = swap_cores(mine)
    factor_grad = jnp.where(core == 0, jnp.stack([mine, other]), jnp.stack([other, mine]))
    return token_grad[None, None], qkv_grad[None, None], factor_grad.reshape(1, 4, D), out_grad


def solution(mesh):
    fine = Mesh(mesh.devices.reshape(4, 2, 4, 8, 2), DP + SEQ)
    frames = P(DP, SEQ, None, None)
    return jax.shard_map(
        body,
        mesh=fine,
        in_specs=(
            frames,
            frames,
            P(SEQ, None),
            P(None, SEQ),
            P(SEQ, None),
            P(DP, None, None),
            frames,
        ),
        out_specs=(frames, frames, P(DP, None, None), P(SEQ, None)),
        check_vma=False,
    )
```

time: 269 us -> 224 us (0.83)
  local copies, waits for them, and re-layouts: 32.7 us -> 11.3 us
  waiting for transfers between devices: 112 us -> 97.6 us
  between operations: 14.5 us -> 0.98 us
  starting transfers between devices: 69.8 us -> 77.5 us
    all_gather x1 -> x0, waiting for transfers between devices: 49.4 us -> none  [gather_weights(): shards = lax.all_gather(shards, 'z', axis=0).reshape(16, 45, D)]
    all_to_all x2, waiting for transfers between devices: 44.1 us -> 62.7 us  [exchange(): return lax.all_to_all(a, SEQ, 0, 0, tiled=True)]
    ppermute x9 -> x7, waiting for transfers between devices: 13.8 us -> 27.7 us  [receive(): return lax.ppermute(a, AXES, pairs)]
    concatenate x1 -> x0, local copies, waits for them, and re-layouts: 7.58 us -> none  [body(): jnp.concatenate([jnp.concatenate([hidden_grad, d_mixed], 1).reshape(64, 2...]
    unnamed x28 -> x8, local copies, waits for them, and re-layouts: 9.18 us -> 2.15 us
    ppermute x4 -> x6, starting transfers between devices: 9.95 us -> 16.7 us  [swap_cores(): return lax.ppermute(a, 'core', [(0, 1), (1, 0)])]
    slice x3 -> x1, local copies, waits for them, and re-layouts: 3.3 us -> 0.47 us  [body(): out_part = back[:, :, width:].astype(F32).reshape(32, 2, 2, 9 * ATT // 2)]
    ppermute x9 -> x7, starting transfers between devices: 29.8 us -> 28.5 us  [receive(): return lax.ppermute(a, AXES, pairs)]
  transfers between devices with their start and end apart: 17 -> 16, of which waited for: 8 -> 8; matrix products, arithmetic and copies ran while one was open for 8% -> 5% of each run, Pallas kernels for 1% -> 2%
where the time goes in v3:
time: 224 us; the launch traced here: 220 us
  waiting for transfers between devices  97.6 us (44%)
  starting transfers between devices  77.5 us (35%)
  Pallas kernels  16.5 us (7%)
  local copies, waits for them, and re-layouts  11.3 us (5%)
  blocking collectives  8.48 us (4%)
  other arithmetic  7.65 us (3%)
    all_to_all x2, waiting for transfers between devices, exchange(): return lax.all_to_all(a, SEQ, 0, 0, tiled=True)  62.7 us
    all_to_all x2, starting transfers between devices, exchange(): return lax.all_to_all(a, SEQ, 0, 0, tiled=True)  28.8 us
    ppermute x7, starting transfers between devices, receive(): return lax.ppermute(a, AXES, pairs)  28.5 us
    ppermute x7, waiting for transfers between devices, receive(): return lax.ppermute(a, AXES, pairs)  27.7 us
    ppermute x6, starting transfers between devices, swap_cores(): return lax.ppermute(a, 'core', [(0, 1), (1, 0)])  16.7 us
    pallas_call x4, Pallas kernels, call(): pl.pallas_call(kernel, out_shape=[jax.ShapeDtypeStruct(s, d) for s, d in...  16.5 us
    all_gather x1, blocking collectives, gather_weights(): shards = lax.all_gather(shard, 'core', axis=0)  8.48 us
  transfers between devices with their start and end apart: 16, of which 8 were waited for; matrix products, arithmetic and copies ran while one was open for 5% of the time, Pallas kernels for 2%

profile of v3, /device:TPU:1, one launch (start us, length us, event | category | flops | bytes accessed | tf_op | source)
XLA Modules:
  0.0 220.1 jit_solution(9500236853591847653)
XLA Ops:
  1.6 8.5 %all-gather.1 = bf16[2,45,1152]{2,1,0:T(8,128)(2,1)S(1)} all-gather(bf16[1,45,1152]{2,1,0:T(8,128)(2,1)S(1)} %maximum_bitcast_fusion), channel_id=2, replica_groups=mesh['x'=4,'ylo'=2,'yhi'=4,'z'=8,'core'=2] {'core'}, dimensions={0}, use_global_device_ids=true | all-gather | bytes 311040 | tf_op jit(solution)/shard_map/all_gather | solution.py:278
  10.1 1.9 collective-permute-start.2
  12.0 2.5 %collective-permute-start.1 = (bf16[2,45,1152]{2,1,0:T(8,128)(2,1)S(1)}, bf16[2,45,1152]{2,1,0:T(8,128)(2,1)S(1)}, u32[]{:S(2)}, u32[]{:S(2)}) collective-permute-start(bf16[2,45,1152]{2,1,0:T(8,128)(2,1)S(1)} %all-gather.1), channel_id=1, source_target_pairs={{2,0},{15,1},{4,2},{1,3},{6,4},{3,5},{8,6},{5,7},{10,8},{7,9},{12,... | collective-permute-start | bytes 622088 | tf_op jit(solution)/shard_map/ppermute | solution.py:249
  14.5 7.9 %collective-permute-start = (bf16[2,45,1152]{2,1,0:T(8,128)(2,1)S(1)}, bf16[2,45,1152]{2,1,0:T(8,128)(2,1)S(1)}, u32[]{:S(2)}, u32[]{:S(2)}) collective-permute-start(bf16[2,45,1152]{2,1,0:T(8,128)(2,1)S(1)} %all-gather.1), channel_id=1, source_target_pairs={{0,0},{9,1},{2,2},{11,3},{4,4},{13,5},{6,6},{15,7},{8,8},{1,9},{10... | collective-permute-start | bytes 622088 | tf_op jit(solution)/shard_map/ppermute | solution.py:249
  22.5 1.9 collective-permute-start.3
  26.8 1.5 shard_map.102
  28.4 1.6 pad_maximum_fusion.2
  30.8 3.4 %collective-permute-done = bf16[2,45,1152]{2,1,0:T(8,128)(2,1)S(1)} collective-permute-done((bf16[2,45,1152]{2,1,0:T(8,128)(2,1)S(1)}, bf16[2,45,1152]{2,1,0:T(8,128)(2,1)S(1)}, u32[]{:S(2)}, u32[]{:S(2)}) %collective-permute-start) | collective-permute-done | bytes 207392 | tf_op jit(solution)/shard_map/ppermute | solution.py:249
  34.1 23.5 %collective-permute-done.3 = bf16[2,45,1152]{2,1,0:T(8,128)(2,1)S(1)} collective-permute-done((bf16[2,45,1152]{2,1,0:T(8,128)(2,1)S(1)}, bf16[2,45,1152]{2,1,0:T(8,128)(2,1)S(1)}, u32[]{:S(2)}, u32[]{:S(2)}) %collective-permute-start.3) | collective-permute-done | bytes 207392 | tf_op jit(solution)/shard_map/ppermute | solution.py:249
  58.3 5.6 %collective-permute-start.4 = (bf16[4,2,45,1152]{3,0,2,1:T(4,128)(2,1)S(1)}, bf16[4,2,45,1152]{3,0,2,1:T(4,128)(2,1)S(1)}, u32[]{:S(2)}, u32[]{:S(2)}) collective-permute-start(bf16[4,2,45,1152]{3,0,2,1:T(4,128)(2,1)S(1)} %copy.29), channel_id=1, source_target_pairs={{0,1},{1,0},{2,3},{3,2},{4,5},{5,4},{6,7},{7,6},{8,9},{9,8},{10,11... | collective-permute-start | bytes 2488328 | tf_op jit(solution)/shard_map/ppermute | solution.py:253
  63.9 1.9 collective-permute-done.4
  65.9 2.2 %shard_map.103 = (bf16[144,1152]{1,0:T(8,128)(2,1)S(1)}, bf16[144,1152]{1,0:T(8,128)(2,1)S(1)}, bf16[432,1152]{1,0:T(8,128)(2,1)S(1)}, bf16[384,1152]{1,0:T(8,128)(2,1)}) custom-call(s32[3]{0:T(128)S(1)} %pad_add_fusion.place, bf16[4,2,45,1152]{3,2,1,0:T(8,128)(2,1)S(1)} %pad_maximum_fusion.1.mine, bf16[4,2,45,1152]{3,2,1,0:T(8,128)(2,1)S(1)} %copy.30.other), custom_call_target="tpu_custom_call" | custom-call | flops 1000000000 | bytes 10000000 | tf_op jit(solution)/shard_map/pallas_call | solution.py:219
  69.1 9.4 %collective-permute-start.7 = (bf16[384,1152]{1,0:T(8,128)(2,1)}, bf16[384,1152]{1,0:T(8,128)(2,1)S(1)}, u32[]{:S(2)}, u32[]{:S(2)}) collective-permute-start(bf16[384,1152]{1,0:T(8,128)(2,1)} %get-tuple-element.22), channel_id=1, source_target_pairs={{192,0},{497,1},{194,2},{499,3},{196,4},{501,5},{198,6},{503,7},{2... | collective-permute-start | bytes 2654216 | tf_op jit(solution)/shard_map/ppermute | solution.py:249
  78.5 2.9 %collective-permute-start.6 = (bf16[384,1152]{1,0:T(8,128)(2,1)}, bf16[384,1152]{1,0:T(8,128)(2,1)}, u32[]{:S(2)}, u32[]{:S(2)}) collective-permute-start(bf16[384,1152]{1,0:T(8,128)(2,1)} %get-tuple-element.22), channel_id=1, source_target_pairs={{64,0},{113,1},{66,2},{115,3},{68,4},{117,5},{70,6},{119,7},{72,8}... | collective-permute-start | bytes 2654216 | tf_op jit(solution)/shard_map/ppermute | solution.py:249
  81.4 1.9 collective-permute-start.5
  83.4 16.3 %all-to-all-start = ((bf16[64,2,2880]{2,1,0:T(2,128)(2,1)}), bf16[64,2,2880]{2,1,0:T(2,128)(2,1)S(1)}, u32[]{:S(2)}, u32[]{:S(2)}) async-start(bf16[64,2,2880]{2,1,0:T(2,128)(2,1)} %pad_maximum_fusion.2), calls=%async_computation | async-start | bytes 1507328 | tf_op jit(solution)/shard_map/all_to_all | solution.py:231
  99.7 2.4 %collective-permute-start.10 = (bf16[384,1152]{1,0:T(8,128)(2,1)S(1)}, bf16[384,1152]{1,0:T(8,128)(2,1)}, u32[]{:S(2)}, u32[]{:S(2)}) collective-permute-start(bf16[384,1152]{1,0:T(8,128)(2,1)S(1)} %collective-permute-done.7.d), channel_id=1, source_target_pairs={{0,1},{1,0},{2,3},{3,2},{4,5},{5,4},{6,7},{7,6},{8,9},{9,8},{10,11... | collective-permute-start | bytes 2654216 | tf_op jit(solution)/shard_map/ppermute | solution.py:253
  102.1 2.0 collective-permute-start.9
  104.0 2.4 %collective-permute-start.8 = (bf16[384,1152]{1,0:T(8,128)(2,1)}, bf16[384,1152]{1,0:T(8,128)(2,1)}, u32[]{:S(2)}, u32[]{:S(2)}) collective-permute-start(bf16[384,1152]{1,0:T(8,128)(2,1)} %collective-permute-done.5.b), channel_id=1, source_target_pairs={{0,1},{1,0},{2,3},{3,2},{4,5},{5,4},{6,7},{7,6},{8,9},{9,8},{10,11... | collective-permute-start | bytes 2654216 | tf_op jit(solution)/shard_map/ppermute | solution.py:253
  106.4 16.9 %all-to-all-done = bf16[64,2,2880]{2,1,0:T(2,128)(2,1)S(1)} async-done(((bf16[64,2,2880]{2,1,0:T(2,128)(2,1)}), bf16[64,2,2880]{2,1,0:T(2,128)(2,1)S(1)}, u32[]{:S(2)}, u32[]{:S(2)}) %all-to-all-start) | async-done | bytes 737312 | tf_op jit(solution)/shard_map/all_to_all | solution.py:231
  124.0 10.7 %shard_map.104 = (bf16[128,2944]{1,0:T(8,128)(2,1)S(1)}, f32[576,576]{1,0:T(8,128)}, bf16[576,576]{1,0:T(8,128)(2,1)}) custom-call(s32[3]{0:T(128)S(1)} %pad_add_fusion.place, bf16[128,2880]{1,0:T(8,128)(2,1)S(1)} %reshape.60.sent, f32[4,1152]{1,0:T(4,128)S(1)} %bitcast.27, bf16[432,1152]{1,0:T(8,128)(2,1)} %copy-done.1, ...), custom_call_target="tpu_custom_call" | custom-call | flops 4000000000 | bytes 10000000 | tf_op jit(solution)/shard_map/pallas_call | solution.py:219
  134.7 1.9 collective-permute-start.11
  136.9 2.1 collective-permute-done.11
  139.0 1.5 add_convert_fusion
  140.5 1.3 reshape.62
  141.8 2.4 %pad_maximum_fusion = bf16[64,2,5536]{2,1,0:T(2,128)(2,1)} fusion(bf16[64,2,2592]{2,1,0:T(2,128)(2,1)S(1)} %reshape.62, bf16[64,2,2944]{2,1,0:T(2,128)(2,1)S(1)} %reshape.61), kind=kLoop, calls=%fused_computation.1 | loop fusion | flops 2834432 | bytes 2834432 | tf_op jit(solution)/shard_map/concatenate | solution.py:324
  144.2 12.5 %all-to-all-start.1 = ((bf16[64,2,5536]{2,1,0:T(2,128)(2,1)}), bf16[64,2,5536]{2,1,0:T(2,128)(2,1)S(1)}, u32[]{:S(2)}, u32[]{:S(2)}) async-start(bf16[64,2,5536]{2,1,0:T(2,128)(2,1)} %pad_maximum_fusion), calls=%async_computation.1 | async-start | bytes 2883584 | tf_op jit(solution)/shard_map/all_to_all | solution.py:231
  156.8 45.7 %all-to-all-done.1 = bf16[64,2,5536]{2,1,0:T(2,128)(2,1)S(1)} async-done(((bf16[64,2,5536]{2,1,0:T(2,128)(2,1)}), bf16[64,2,5536]{2,1,0:T(2,128)(2,1)S(1)}, u32[]{:S(2)}, u32[]{:S(2)}) %all-to-all-start.1) | async-done | bytes 1417248 | tf_op jit(solution)/shard_map/all_to_all | solution.py:231
  202.8 2.5 %collective-permute-start.12 = (f32[2,1152]{1,0:T(2,128)S(1)}, f32[2,1152]{1,0:T(2,128)S(1)}, u32[]{:S(2)}, u32[]{:S(2)}) collective-permute-start(f32[2,1152]{1,0:T(2,128)S(1)} %convert_reduce_fusion.1), channel_id=1, source_target_pairs={{0,1},{1,0},{2,3},{3,2},{4,5},{5,4},{6,7},{7,6},{8,9},{9,8},{10,11... | collective-permute-start | bytes 27656 | tf_op jit(solution)/shard_map/ppermute | solution.py:253
  207.9 3.4 %all-to-all-start.2 = ((f32[8,2,5184]{2,1,0:T(2,128)}), f32[8,2,5184]{2,1,0:T(2,128)S(1)}, u32[]{:S(2)}, u32[]{:S(2)}) async-start(f32[8,2,5184]{2,1,0:T(2,128)} %broadcast_in_dim.16), calls=%async_computation.2 | async-start | bytes 671744 | tf_op jit(solution)/shard_map/all_to_all | solution.py:329
  212.1 2.0 shard_map.105
  215.8 3.3 %all-to-all-done.2 = f32[8,2,5184]{2,1,0:T(2,128)S(1)} async-done(((f32[8,2,5184]{2,1,0:T(2,128)}), f32[8,2,5184]{2,1,0:T(2,128)S(1)}, u32[]{:S(2)}, u32[]{:S(2)}) %all-to-all-start.2) | async-done | bytes 331808 | tf_op jit(solution)/shard_map/all_to_all | solution.py:329
  (42 shorter events, 13.0 us)
Async XLA Ops:
  0.6 26.0 %copy-start.2 = (bf16[1,1,128,1728]{2,3,1,0:T(8,128)(2,1)S(1)}, bf16[1,1,128,1728]{2,3,1,0:T(8,128)(2,1)}, u32[]{:S(2)}) copy-start(bf16[1,1,128,1728]{2,3,1,0:T(8,128)(2,1)} %param.8) | copy-start | bytes 1327108
  10.1 19.9 %collective-permute-start.2 = (bf16[2,45,1152]{2,1,0:T(8,128)(2,1)S(1)}, bf16[2,45,1152]{2,1,0:T(8,128)(2,1)S(1)}, u32[]{:S(2)}, u32[]{:S(2)}) collective-permute-start(bf16[2,45,1152]{2,1,0:T(8,128)(2,1)S(1)} %all-gather.1), channel_id=1, source_target_pairs={{4,0},{13,1},{6,2},{15,3},{8,4},{1,5},{10,6},{3,7},{12,8},{5,9},{1... | collective-permute-start | bytes 622088 | tf_op jit(solution)/shard_map/ppermute | solution.py:249
  12.0 18.7 %collective-permute-start.1 = (bf16[2,45,1152]{2,1,0:T(8,128)(2,1)S(1)}, bf16[2,45,1152]{2,1,0:T(8,128)(2,1)S(1)}, u32[]{:S(2)}, u32[]{:S(2)}) collective-permute-start(bf16[2,45,1152]{2,1,0:T(8,128)(2,1)S(1)} %all-gather.1), channel_id=1, source_target_pairs={{2,0},{15,1},{4,2},{1,3},{6,4},{3,5},{8,6},{5,7},{10,8},{7,9},{12,... | collective-permute-start | bytes 622088 | tf_op jit(solution)/shard_map/ppermute | solution.py:249
  14.5 19.6 %collective-permute-start = (bf16[2,45,1152]{2,1,0:T(8,128)(2,1)S(1)}, bf16[2,45,1152]{2,1,0:T(8,128)(2,1)S(1)}, u32[]{:S(2)}, u32[]{:S(2)}) collective-permute-start(bf16[2,45,1152]{2,1,0:T(8,128)(2,1)S(1)} %all-gather.1), channel_id=1, source_target_pairs={{0,0},{9,1},{2,2},{11,3},{4,4},{13,5},{6,6},{15,7},{8,8},{1,9},{10... | collective-permute-start | bytes 622088 | tf_op jit(solution)/shard_map/ppermute | solution.py:249
  22.5 35.2 %collective-permute-start.3 = (bf16[2,45,1152]{2,1,0:T(8,128)(2,1)S(1)}, bf16[2,45,1152]{2,1,0:T(8,128)(2,1)S(1)}, u32[]{:S(2)}, u32[]{:S(2)}) collective-permute-start(bf16[2,45,1152]{2,1,0:T(8,128)(2,1)S(1)} %all-gather.1), channel_id=1, source_target_pairs={{6,0},{11,1},{8,2},{13,3},{10,4},{15,5},{12,6},{1,7},{14,8},{3,9},... | collective-permute-start | bytes 622088 | tf_op jit(solution)/shard_map/ppermute | solution.py:249
  58.3 7.5 %collective-permute-start.4 = (bf16[4,2,45,1152]{3,0,2,1:T(4,128)(2,1)S(1)}, bf16[4,2,45,1152]{3,0,2,1:T(4,128)(2,1)S(1)}, u32[]{:S(2)}, u32[]{:S(2)}) collective-permute-start(bf16[4,2,45,1152]{3,0,2,1:T(4,128)(2,1)S(1)} %copy.29), channel_id=1, source_target_pairs={{0,1},{1,0},{2,3},{3,2},{4,5},{5,4},{6,7},{7,6},{8,9},{9,8},{10,11... | collective-permute-start | bytes 2488328 | tf_op jit(solution)/shard_map/ppermute | solution.py:253
  68.1 1.0 copy-start.1
  69.1 54.9 %copy-start = (f32[1,4,1152]{2,1,0:T(4,128)S(1)}, f32[1,4,1152]{2,1,0:T(4,128)}, u32[]{:S(2)}) copy-start(f32[1,4,1152]{2,1,0:T(4,128)} %param.12) | copy-start | bytes 55300
  69.1 30.6 %collective-permute-start.7 = (bf16[384,1152]{1,0:T(8,128)(2,1)}, bf16[384,1152]{1,0:T(8,128)(2,1)S(1)}, u32[]{:S(2)}, u32[]{:S(2)}) collective-permute-start(bf16[384,1152]{1,0:T(8,128)(2,1)} %get-tuple-element.22), channel_id=1, source_target_pairs={{192,0},{497,1},{194,2},{499,3},{196,4},{501,5},{198,6},{503,7},{2... | collective-permute-start | bytes 2654216 | tf_op jit(solution)/shard_map/ppermute | solution.py:249
  78.5 23.5 %collective-permute-start.6 = (bf16[384,1152]{1,0:T(8,128)(2,1)}, bf16[384,1152]{1,0:T(8,128)(2,1)}, u32[]{:S(2)}, u32[]{:S(2)}) collective-permute-start(bf16[384,1152]{1,0:T(8,128)(2,1)} %get-tuple-element.22), channel_id=1, source_target_pairs={{64,0},{113,1},{66,2},{115,3},{68,4},{117,5},{70,6},{119,7},{72,8}... | collective-permute-start | bytes 2654216 | tf_op jit(solution)/shard_map/ppermute | solution.py:249
  81.4 22.6 %collective-permute-start.5 = (bf16[384,1152]{1,0:T(8,128)(2,1)}, bf16[384,1152]{1,0:T(8,128)(2,1)}, u32[]{:S(2)}, u32[]{:S(2)}) collective-permute-start(bf16[384,1152]{1,0:T(8,128)(2,1)} %get-tuple-element.22), channel_id=1, source_target_pairs={{128,0},{385,1},{130,2},{387,3},{132,4},{389,5},{134,6},{391,7},{1... | collective-permute-start | bytes 2654216 | tf_op jit(solution)/shard_map/ppermute | solution.py:249
  83.4 40.0 %all-to-all-start = ((bf16[64,2,2880]{2,1,0:T(2,128)(2,1)}), bf16[64,2,2880]{2,1,0:T(2,128)(2,1)S(1)}, u32[]{:S(2)}, u32[]{:S(2)}) async-start(bf16[64,2,2880]{2,1,0:T(2,128)(2,1)} %pad_maximum_fusion.2), calls=%async_computation | async-start | bytes 1507328 | tf_op jit(solution)/shard_map/all_to_all | solution.py:231
  99.7 24.3 %collective-permute-start.10 = (bf16[384,1152]{1,0:T(8,128)(2,1)S(1)}, bf16[384,1152]{1,0:T(8,128)(2,1)}, u32[]{:S(2)}, u32[]{:S(2)}) collective-permute-start(bf16[384,1152]{1,0:T(8,128)(2,1)S(1)} %collective-permute-done.7.d), channel_id=1, source_target_pairs={{0,1},{1,0},{2,3},{3,2},{4,5},{5,4},{6,7},{7,6},{8,9},{9,8},{10,11... | collective-permute-start | bytes 2654216 | tf_op jit(solution)/shard_map/ppermute | solution.py:253
  102.1 21.9 %collective-permute-start.9 = (bf16[384,1152]{1,0:T(8,128)(2,1)}, bf16[384,1152]{1,0:T(8,128)(2,1)}, u32[]{:S(2)}, u32[]{:S(2)}) collective-permute-start(bf16[384,1152]{1,0:T(8,128)(2,1)} %collective-permute-done.6.c), channel_id=1, source_target_pairs={{0,1},{1,0},{2,3},{3,2},{4,5},{5,4},{6,7},{7,6},{8,9},{9,8},{10,11... | collective-permute-start | bytes 2654216 | tf_op jit(solution)/shard_map/ppermute | solution.py:253
  104.0 19.9 %collective-permute-start.8 = (bf16[384,1152]{1,0:T(8,128)(2,1)}, bf16[384,1152]{1,0:T(8,128)(2,1)}, u32[]{:S(2)}, u32[]{:S(2)}) collective-permute-start(bf16[384,1152]{1,0:T(8,128)(2,1)} %collective-permute-done.5.b), channel_id=1, source_target_pairs={{0,1},{1,0},{2,3},{3,2},{4,5},{5,4},{6,7},{7,6},{8,9},{9,8},{10,11... | collective-permute-start | bytes 2654216 | tf_op jit(solution)/shard_map/ppermute | solution.py:253
  134.7 4.3 %collective-permute-start.11 = (bf16[576,576]{1,0:T(8,128)(2,1)}, bf16[576,576]{1,0:T(8,128)(2,1)S(1)}, u32[]{:S(2)}, u32[]{:S(2)}) collective-permute-start(bf16[576,576]{1,0:T(8,128)(2,1)} %get-tuple-element.25), channel_id=1, source_target_pairs={{0,1},{1,0},{2,3},{3,2},{4,5},{5,4},{6,7},{7,6},{8,9},{9,8},{10,11... | collective-permute-start | bytes 1990664 | tf_op jit(solution)/shard_map/ppermute | solution.py:253
  144.2 58.3 %all-to-all-start.1 = ((bf16[64,2,5536]{2,1,0:T(2,128)(2,1)}), bf16[64,2,5536]{2,1,0:T(2,128)(2,1)S(1)}, u32[]{:S(2)}, u32[]{:S(2)}) async-start(bf16[64,2,5536]{2,1,0:T(2,128)(2,1)} %pad_maximum_fusion), calls=%async_computation.1 | async-start | bytes 2883584 | tf_op jit(solution)/shard_map/all_to_all | solution.py:231
  202.8 12.4 %collective-permute-start.12 = (f32[2,1152]{1,0:T(2,128)S(1)}, f32[2,1152]{1,0:T(2,128)S(1)}, u32[]{:S(2)}, u32[]{:S(2)}) collective-permute-start(f32[2,1152]{1,0:T(2,128)S(1)} %convert_reduce_fusion.1), channel_id=1, source_target_pairs={{0,1},{1,0},{2,3},{3,2},{4,5},{5,4},{6,7},{7,6},{8,9},{9,8},{10,11... | collective-permute-start | bytes 27656 | tf_op jit(solution)/shard_map/ppermute | solution.py:253
  207.9 11.2 %all-to-all-start.2 = ((f32[8,2,5184]{2,1,0:T(2,128)}), f32[8,2,5184]{2,1,0:T(2,128)S(1)}, u32[]{:S(2)}, u32[]{:S(2)}) async-start(f32[8,2,5184]{2,1,0:T(2,128)} %broadcast_in_dim.16), calls=%async_computation.2 | async-start | bytes 671744 | tf_op jit(solution)/shard_map/all_to_all | solution.py:329

commit v4 on v3

--- a/solution.py
+++ b/solution.py
@@ -83,11 +83,13 @@
     mixed[...] = attend(head_masks(), q, k, v, None)[3]
 
 
-def spatial_backward_kernel(qkv, d_mixed, out):
+def spatial_backward_kernel(qkv, hidden_grad, factors, w_so, out):
     q, k, v = qkv[:, :ATT], qkv[:, ATT : 2 * ATT], qkv[:, 2 * ATT :]
     masks = head_masks()
+    gated = (hidden_grad[...].astype(F32) * factors[0:1, :]).astype(BF)
+    d_mixed = nt(gated, w_so[...]).astype(BF)
     q_stack, probs, probs_b, _ = attend(masks, q, k, v, None)
-    d_q, d_k, d_v = attend_back(masks, q_stack, k, v, probs, probs_b, d_mixed[...])
+    d_q, d_k, d_v = attend_back(masks, q_stack, k, v, probs, probs_b, d_mixed)
     out[:, :ATT] = d_q
     out[:, ATT : 2 * ATT] = d_k
     out[:, 2 * ATT :] = d_v
@@ -155,7 +157,7 @@
 
 def temporal_kernel(
     place, sent, factors, own_qkv, own_so, own_out, b, c, d, other_b, other_c, other_d,
-    packed, out_keep, out_send, w_qkv, w_so, w_out, sems,
+    hidden_grad, factor_grads, out_keep, out_send, w_so, w_qkv, w_out, sems,
 ):
     assemble(
         place, (own_qkv, own_so, own_out), (b, c, d), (other_b, other_c, other_d),
@@ -195,20 +197,13 @@
         - unit * jnp.mean(d_unit * unit, -1, keepdims=True)
     )
     grad = (cot + d_hidden).astype(BF)
-    packed[:, :D] = grad
+    hidden_grad[...] = grad
     grad = grad.astype(F32)
-    d_mixed_s = nt((grad * gate_s).astype(BF), w_so[...]).astype(BF)
-    packed[:, D : D + 640] = jnp.concatenate([d_mixed_s, jnp.zeros((ROWS, 64), BF)], 1)
     project_t = nn(mixed, w_out[...])
-    factor_grads = [
-        jnp.sum(grad * project, 0, keepdims=True),
-        jnp.sum(d_normed, 0, keepdims=True),
-        jnp.sum(d_normed * unit, 0, keepdims=True),
-        jnp.sum(cot * project_t, 0, keepdims=True),
-    ]
-    tile = jnp.concatenate(factor_grads * 4, 0).astype(BF)
-    for i in range(8):
-        packed[16 * i : 16 * i + 16, D + 640 :] = tile
+    factor_grads[0:1, :] = jnp.sum(grad * project, 0, keepdims=True)
+    factor_grads[1:2, :] = jnp.sum(d_normed, 0, keepdims=True)
+    factor_grads[2:3, :] = jnp.sum(d_normed * unit, 0, keepdims=True)
+    factor_grads[3:4, :] = jnp.sum(cot * project_t, 0, keepdims=True)
 
 
 def call(kernel, outs, *args, scalars=0, remote=0, scratch=(), flops=10**9):
@@ -256,13 +251,14 @@
 OFFSETS = ((0, 1, 2, 3), (4, -1, -2, -3))
 
 
-def shard_source(step):
-    def source(x, y, z, core):
-        ylo, yhi = y % 2, y // 2
-        cls = (x % 2) * 2 + ylo
-        return (x // 2) * 2 + yhi // 2, cls * 2 + yhi % 2, z + OFFSETS[core][step]
-
-    return source
+def class_source(x, y, z, core):
+    ylo, yhi = y % 2, y // 2
+    cls = (x % 2) * 2 + ylo
+    return (x // 2) * 2 + yhi // 2, cls * 2 + yhi % 2, z
+
+
+def line_source(step):
+    return lambda x, y, z, core: (x, y, z + OFFSETS[core][step])
 
 
 def near_source(dx, dy):
@@ -273,11 +269,11 @@
     return source
 
 
-def gather_weights(w_so, w_qkv, w_out, place, packed):
-    shard = jnp.concatenate([w_so, w_out, w_qkv.T], 0)
+def gather_weights(w_so, w_qkv, w_out, place, sent):
+    shard = receive(jnp.concatenate([w_so, w_out, w_qkv.T], 0), class_source)
     shards = lax.all_gather(shard, "core", axis=0)
-    mine = [receive(shards, shard_source(i)) for i in range(4)]
-    mine, packed = lax.optimization_barrier((jnp.stack(mine), packed))
+    mine = [receive(shards, line_source(i)) for i in range(4)]
+    mine, sent = lax.optimization_barrier((jnp.stack(mine), exchange(sent)))
     other = swap_cores(mine)
     rows = lambda n: ((n, D), BF)
     own_so, own_out, own_qkv, part = call(
@@ -289,54 +285,58 @@
             pltpu.VMEM((432, D), F32),
         ],
     )
-    part, packed = lax.optimization_barrier((part, packed))
     near = [receive(part, near_source(dx, dy)) for dx, dy in ((1, 0), (0, 1), (1, 1))]
-    return [own_qkv, own_so, own_out] + near + [swap_cores(a) for a in near], packed
+    return [own_qkv, own_so, own_out] + near + [swap_cores(a) for a in near], sent
 
 
 def body(tokens, qkv, w_so, w_qkv, w_out, factors, cotangent):
     tokens, qkv, cotangent, factors = tokens[0, 0], qkv[0, 0], cotangent[0, 0], factors[0]
-    core = lax.axis_index("core")
+    core, yhi = lax.axis_index("core"), lax.axis_index("yhi")
     cls = (lax.axis_index("x") % 2) * 2 + lax.axis_index("ylo")
     place = jnp.stack([core, cls, lax.axis_index("z")]).astype(jnp.int32)
 
     (mixed_s,) = call(spatial_forward_kernel, [((ROWS, ATT), BF)], qkv)
     sent = jnp.concatenate([tokens, cotangent, mixed_s], 1).reshape(64, 2, 2 * D + ATT)
     weights, sent = gather_weights(w_so, w_qkv, w_out, place, sent)
-    sent = exchange(sent).reshape(ROWS, 2 * D + ATT)
-
-    packed, out_keep, out_send = call(
+    sent = sent.reshape(ROWS, 2 * D + ATT)
+
+    hidden_grad, factor_part, out_keep, out_send, w_so = call(
         temporal_kernel,
-        [((ROWS, 2 * D + 640), BF), ((ATT, ATT), F32), ((ATT, ATT), BF)],
+        [((ROWS, D), BF), ((4, D), F32), ((ATT, ATT), F32), ((ATT, ATT), BF), ((ATT, D), BF)],
         place, sent, factors, *weights,
         scalars=1, remote=len(weights), flops=4 * 10**9,
         scratch=[
             pltpu.VMEM((3 * ATT, D), BF),
             pltpu.VMEM((ATT, D), BF),
-            pltpu.VMEM((ATT, D), BF),
             pltpu.SemaphoreType.DMA((24,)),
         ],
     )
 
     out_part = (out_keep + swap_cores(out_send).astype(F32)).astype(BF)
-    out_part = out_part.reshape(64, 2, 9 * ATT // 2)
-    width = 2 * D + 640
-    back = exchange(jnp.concatenate([packed.reshape(64, 2, width), out_part], 2))
-
-    out_part = back[:, :, width:].astype(F32).reshape(32, 2, 2, 9 * ATT // 2)
+    half = 9 * ATT // 2
+    factor_part = factor_part.astype(BF).reshape(1, 2, 1, 2, 2, D // 2)
+    factor_part = jnp.broadcast_to(factor_part, (2, 2, 8, 2, 2, D // 2)).reshape(64, 2, D // 2)
+    packed = [hidden_grad.reshape(64, 2, D), out_part.reshape(64, 2, half), factor_part]
+    back = exchange(jnp.concatenate(packed, 2))
+
+    out_part = back[:, :, D : D + half].astype(F32).reshape(32, 2, 2, half)
     out_part = jnp.sum(out_part, 0).reshape(1, 2, 9 * ATT)
     out_part = jnp.broadcast_to(out_part, (8, 2, 9 * ATT))
     out_part = jnp.sum(lax.all_to_all(out_part, DP, 0, 0, tiled=True), 0)
     out_grad = out_part.reshape(2, 9, ATT).transpose(1, 0, 2).reshape(9, D)
 
-    rows = back[:, :, : D + ATT].reshape(ROWS, D + ATT)
-    token_grad = rows[:, :D]
-    (qkv_grad,) = call(spatial_backward_kernel, [((ROWS, 3 * ATT), BF)], qkv, rows[:, D:])
-
-    mine = jnp.sum(back[:, :, D + 640 : width].astype(F32), 0)
+    token_grad = back[:, :, :D].reshape(ROWS, D)
+    (qkv_grad,) = call(
+        spatial_backward_kernel, [((ROWS, 3 * ATT), BF)], qkv, token_grad, factors, w_so
+    )
+
+    mine = jnp.sum(back[:, :, D + half :].astype(F32), 0).reshape(1, D)
     other = swap_cores(mine)
-    factor_grad = jnp.where(core == 0, jnp.stack([mine, other]), jnp.stack([other, mine]))
-    return token_grad[None, None], qkv_grad[None, None], factor_grad.reshape(1, 4, D), out_grad
+    rows = jnp.where(core == 0, jnp.concatenate([mine, other]), jnp.concatenate([other, mine]))
+    other = lax.ppermute(rows, "yhi", [(0, 1), (1, 0), (2, 3), (3, 2)])
+    low = yhi % 2 == 0
+    factor_grad = jnp.where(low, jnp.concatenate([rows, other]), jnp.concatenate([other, rows]))
+    return token_grad[None, None], qkv_grad[None, None], factor_grad[None], out_grad
 
 
 def solution(mesh):

time: 224 us -> 212 us (0.946)
  waiting for transfers between devices: 97.6 us -> 75.1 us
  starting transfers between devices: 77.5 us -> 88.3 us
  local copies, waits for them, and re-layouts: 11.3 us -> 21.9 us
  blocking collectives: 8.48 us -> 2.06 us
  other arithmetic: 7.65 us -> 5.05 us
    all_to_all x2, waiting for transfers between devices: 62.7 us -> 33.1 us  [exchange(): return lax.all_to_all(a, SEQ, 0, 0, tiled=True)]
    ppermute x7 -> x8, starting transfers between devices: 28.5 us -> 39.2 us  [receive(): return lax.ppermute(a, AXES, pairs)]
    ppermute x7 -> x8, waiting for transfers between devices: 27.7 us -> 34.1 us  [receive(): return lax.ppermute(a, AXES, pairs)]
    all_gather x1, blocking collectives: 8.48 us -> 2.06 us  [gather_weights(): shards = lax.all_gather(shard, 'core', axis=0)]
    concatenate x0 -> x2, local copies, waits for them, and re-layouts: none -> 5.44 us  [the longest x1 5.35 us: body(): back = exchange(jnp.concatenate(packed, 2))]
    unnamed x8 -> x26, local copies, waits for them, and re-layouts: 2.15 us -> 5.57 us
    all_to_all x1, waiting for transfers between devices: 3.35 us -> 0.01 us  [body(): out_part = jnp.sum(lax.all_to_all(out_part, DP, 0, 0, tiled=True), 0)]
    ppermute x0 -> x1, waiting for transfers between devices: none -> 3.1 us  [body(): other = lax.ppermute(rows, 'yhi', [(0, 1), (1, 0), (2, 3), (3, 2)])]
  transfers between devices with their start and end apart: 16 -> 18, of which waited for: 8 -> 11; matrix products, arithmetic and copies ran while one was open for 5% -> 3% of each run, Pallas kernels for 2% -> 1%
where the time goes in v4:
time: 212 us; the launch traced here: 209 us
  starting transfers between devices  88.3 us (42%)
  waiting for transfers between devices  75.1 us (35%)
  local copies, waits for them, and re-layouts  21.9 us (10%)
  Pallas kernels  15.5 us (7%)
  other arithmetic  5.05 us (2%)
    ppermute x8, starting transfers between devices, receive(): return lax.ppermute(a, AXES, pairs)  39.2 us
    ppermute x8, waiting for transfers between devices, receive(): return lax.ppermute(a, AXES, pairs)  34.1 us
    all_to_all x2, waiting for transfers between devices, exchange(): return lax.all_to_all(a, SEQ, 0, 0, tiled=True)  33.1 us
    all_to_all x2, starting transfers between devices, exchange(): return lax.all_to_all(a, SEQ, 0, 0, tiled=True)  27.1 us
    ppermute x6, starting transfers between devices, swap_cores(): return lax.ppermute(a, 'core', [(0, 1), (1, 0)])  16.1 us
    pallas_call x4, Pallas kernels, call(): pl.pallas_call(kernel, out_shape=[jax.ShapeDtypeStruct(s, d) for s, d in...  15.5 us
    unnamed x26, local copies, waits for them, and re-layouts  5.57 us
    concatenate x1, local copies, waits for them, and re-layouts, body(): back = exchange(jnp.concatenate(packed, 2))  5.35 us
  transfers between devices with their start and end apart: 18, of which 11 were waited for; matrix products, arithmetic and copies ran while one was open for 3% of the time, Pallas kernels for 1%

profile of v4, /device:TPU:1, one launch (start us, length us, event | category | flops | bytes accessed | tf_op | source)
XLA Modules:
  0.0 209.0 jit_solution(18227090165380341130)
XLA Ops:
  6.3 17.6 %all-to-all-start = ((bf16[64,2,2880]{2,1,0:T(2,128)(2,1)}), bf16[64,2,2880]{2,1,0:T(2,128)(2,1)S(1)}, u32[]{:S(2)}, u32[]{:S(2)}) async-start(bf16[64,2,2880]{2,1,0:T(2,128)(2,1)} %pad_maximum_fusion.1), calls=%async_computation | async-start | bytes 1507328 | tf_op jit(solution)/shard_map/all_to_all | solution.py:226
  24.7 2.1 all-gather.1
  26.8 4.1 %collective-permute-start.3 = (bf16[2,45,1152]{2,1,0:T(8,128)(2,1)S(1)}, bf16[2,45,1152]{2,1,0:T(8,128)(2,1)S(1)}, u32[]{:S(2)}, u32[]{:S(2)}) collective-permute-start(bf16[2,45,1152]{2,1,0:T(8,128)(2,1)S(1)} %all-gather.1), channel_id=1, source_target_pairs={{4,0},{13,1},{6,2},{15,3},{8,4},{1,5},{10,6},{3,7},{12,8},{5,9},{1... | collective-permute-start | bytes 622088 | tf_op jit(solution)/shard_map/ppermute | solution.py:244
  30.9 3.1 %collective-permute-start.2 = (bf16[2,45,1152]{2,1,0:T(8,128)(2,1)S(1)}, bf16[2,45,1152]{2,1,0:T(8,128)(2,1)S(1)}, u32[]{:S(2)}, u32[]{:S(2)}) collective-permute-start(bf16[2,45,1152]{2,1,0:T(8,128)(2,1)S(1)} %all-gather.1), channel_id=1, source_target_pairs={{2,0},{15,1},{4,2},{1,3},{6,4},{3,5},{8,6},{5,7},{10,8},{7,9},{12,... | collective-permute-start | bytes 622088 | tf_op jit(solution)/shard_map/ppermute | solution.py:244
  34.0 4.3 %collective-permute-start.1 = (bf16[2,45,1152]{2,1,0:T(8,128)(2,1)S(1)}, bf16[2,45,1152]{2,1,0:T(8,128)(2,1)S(1)}, u32[]{:S(2)}, u32[]{:S(2)}) collective-permute-start(bf16[2,45,1152]{2,1,0:T(8,128)(2,1)S(1)} %all-gather.1), channel_id=1, source_target_pairs={{0,0},{9,1},{2,2},{11,3},{4,4},{13,5},{6,6},{15,7},{8,8},{1,9},{10... | collective-permute-start | bytes 622088 | tf_op jit(solution)/shard_map/ppermute | solution.py:244
  38.3 4.0 %collective-permute-start.4 = (bf16[2,45,1152]{2,1,0:T(8,128)(2,1)S(1)}, bf16[2,45,1152]{2,1,0:T(8,128)(2,1)S(1)}, u32[]{:S(2)}, u32[]{:S(2)}) collective-permute-start(bf16[2,45,1152]{2,1,0:T(8,128)(2,1)S(1)} %all-gather.1), channel_id=1, source_target_pairs={{6,0},{11,1},{8,2},{13,3},{10,4},{15,5},{12,6},{1,7},{14,8},{3,9},... | collective-permute-start | bytes 622088 | tf_op jit(solution)/shard_map/ppermute | solution.py:244
  42.3 7.0 %collective-permute-done.3 = bf16[2,45,1152]{2,1,0:T(8,128)(2,1)S(1)} collective-permute-done((bf16[2,45,1152]{2,1,0:T(8,128)(2,1)S(1)}, bf16[2,45,1152]{2,1,0:T(8,128)(2,1)S(1)}, u32[]{:S(2)}, u32[]{:S(2)}) %collective-permute-start.3) | collective-permute-done | bytes 207392 | tf_op jit(solution)/shard_map/ppermute | solution.py:244
  49.2 2.6 %collective-permute-done.2 = bf16[2,45,1152]{2,1,0:T(8,128)(2,1)S(1)} collective-permute-done((bf16[2,45,1152]{2,1,0:T(8,128)(2,1)S(1)}, bf16[2,45,1152]{2,1,0:T(8,128)(2,1)S(1)}, u32[]{:S(2)}, u32[]{:S(2)}) %collective-permute-start.2) | collective-permute-done | bytes 207392 | tf_op jit(solution)/shard_map/ppermute | solution.py:244
  51.8 4.9 %collective-permute-done.1 = bf16[2,45,1152]{2,1,0:T(8,128)(2,1)S(1)} collective-permute-done((bf16[2,45,1152]{2,1,0:T(8,128)(2,1)S(1)}, bf16[2,45,1152]{2,1,0:T(8,128)(2,1)S(1)}, u32[]{:S(2)}, u32[]{:S(2)}) %collective-permute-start.1) | collective-permute-done | bytes 207392 | tf_op jit(solution)/shard_map/ppermute | solution.py:244
  56.7 8.2 %collective-permute-done.4 = bf16[2,45,1152]{2,1,0:T(8,128)(2,1)S(1)} collective-permute-done((bf16[2,45,1152]{2,1,0:T(8,128)(2,1)S(1)}, bf16[2,45,1152]{2,1,0:T(8,128)(2,1)S(1)}, u32[]{:S(2)}, u32[]{:S(2)}) %collective-permute-start.4) | collective-permute-done | bytes 207392 | tf_op jit(solution)/shard_map/ppermute | solution.py:244
  66.4 1.9 collective-permute-start.5
  68.4 2.4 %collective-permute-done.5 = bf16[4,2,45,1152]{3,0,2,1:T(4,128)(2,1)S(1)} collective-permute-done((bf16[4,2,45,1152]{3,0,2,1:T(4,128)(2,1)}, bf16[4,2,45,1152]{3,0,2,1:T(4,128)(2,1)S(1)}, u32[]{:S(2)}, u32[]{:S(2)}) %collective-permute-start.5) | collective-permute-done | bytes 829472 | tf_op jit(solution)/shard_map/ppermute | solution.py:248
  74.7 18.0 %collective-permute-start.8 = (bf16[384,1152]{1,0:T(8,128)(2,1)S(1)}, bf16[384,1152]{1,0:T(8,128)(2,1)S(1)}, u32[]{:S(2)}, u32[]{:S(2)}) collective-permute-start(bf16[384,1152]{1,0:T(8,128)(2,1)S(1)} %get-tuple-element.20), channel_id=1, source_target_pairs={{192,0},{497,1},{194,2},{499,3},{196,4},{501,5},{198,6},{503,7},{2... | collective-permute-start | bytes 2654216 | tf_op jit(solution)/shard_map/ppermute | solution.py:244
  92.7 3.1 %collective-permute-start.7 = (bf16[384,1152]{1,0:T(8,128)(2,1)S(1)}, bf16[384,1152]{1,0:T(8,128)(2,1)S(1)}, u32[]{:S(2)}, u32[]{:S(2)}) collective-permute-start(bf16[384,1152]{1,0:T(8,128)(2,1)S(1)} %get-tuple-element.20), channel_id=1, source_target_pairs={{64,0},{113,1},{66,2},{115,3},{68,4},{117,5},{70,6},{119,7},{72,8}... | collective-permute-start | bytes 2654216 | tf_op jit(solution)/shard_map/ppermute | solution.py:244
  95.8 1.9 collective-permute-start.6
  97.7 5.0 %collective-permute-done.8.d = bf16[384,1152]{1,0:T(8,128)(2,1)S(1)} collective-permute-done((bf16[384,1152]{1,0:T(8,128)(2,1)S(1)}, bf16[384,1152]{1,0:T(8,128)(2,1)S(1)}, u32[]{:S(2)}, u32[]{:S(2)}) %collective-permute-start.8) | collective-permute-done | bytes 884768 | tf_op jit(solution)/shard_map/ppermute | solution.py:244
  102.7 3.4 %collective-permute-start.11 = (bf16[384,1152]{1,0:T(8,128)(2,1)S(1)}, bf16[384,1152]{1,0:T(8,128)(2,1)}, u32[]{:S(2)}, u32[]{:S(2)}) collective-permute-start(bf16[384,1152]{1,0:T(8,128)(2,1)S(1)} %collective-permute-done.8.d), channel_id=1, source_target_pairs={{0,1},{1,0},{2,3},{3,2},{4,5},{5,4},{6,7},{7,6},{8,9},{9,8},{10,11... | collective-permute-start | bytes 2654216 | tf_op jit(solution)/shard_map/ppermute | solution.py:248
  106.1 6.5 %collective-permute-done.7.c = bf16[384,1152]{1,0:T(8,128)(2,1)S(1)} collective-permute-done((bf16[384,1152]{1,0:T(8,128)(2,1)S(1)}, bf16[384,1152]{1,0:T(8,128)(2,1)S(1)}, u32[]{:S(2)}, u32[]{:S(2)}) %collective-permute-start.7) | collective-permute-done | bytes 884768 | tf_op jit(solution)/shard_map/ppermute | solution.py:244
  112.7 3.5 %collective-permute-start.10 = (bf16[384,1152]{1,0:T(8,128)(2,1)S(1)}, bf16[384,1152]{1,0:T(8,128)(2,1)}, u32[]{:S(2)}, u32[]{:S(2)}) collective-permute-start(bf16[384,1152]{1,0:T(8,128)(2,1)S(1)} %collective-permute-done.7.c), channel_id=1, source_target_pairs={{0,1},{1,0},{2,3},{3,2},{4,5},{5,4},{6,7},{7,6},{8,9},{9,8},{10,11... | collective-permute-start | bytes 2654216 | tf_op jit(solution)/shard_map/ppermute | solution.py:248
  116.2 1.9 collective-permute-start.9
  118.2 2.2 %reshape.155.sent = bf16[128,2880]{1,0:T(8,128)(2,1)S(1)} reshape(bf16[64,2,2880]{2,1,0:T(2,128)(2,1)} %copy-done.7) | data formatting | bytes 1474560 | tf_op jit(solution)/shard_map/reshape | solution.py:301
  122.9 10.4 %shard_map.104 = (bf16[128,1152]{1,0:T(8,128)(2,1)S(1)}, f32[4,1152]{1,0:T(4,128)S(1)}, f32[576,576]{1,0:T(8,128)}, bf16[576,576]{1,0:T(8,128)(2,1)}, bf16[576,1152]{1,0:T(8,128)(2,1)}) custom-call(s32[3]{0:T(128)S(1)} %pad_add_fusion.place, bf16[128,2880]{1,0:T(8,128)(2,1)S(1)} %reshape.155.sent, f32[4,1152]{1,0:T(4,128)S(1)} %bitcast.26, ...), custom_call_target="tpu_custom_call" | custom-call | flops 4000000000 | bytes 10000000 | tf_op jit(solution)/shard_map/pallas_call | solution.py:214
  133.2 2.2 %collective-permute-start.12 = (bf16[576,576]{1,0:T(8,128)(2,1)}, bf16[576,576]{1,0:T(8,128)(2,1)S(1)}, u32[]{:S(2)}, u32[]{:S(2)}) collective-permute-start(bf16[576,576]{1,0:T(8,128)(2,1)} %get-tuple-element.23), channel_id=1, source_target_pairs={{0,1},{1,0},{2,3},{3,2},{4,5},{5,4},{6,7},{7,6},{8,9},{9,8},{10,11... | collective-permute-start | bytes 1990664 | tf_op jit(solution)/shard_map/ppermute | solution.py:248
  135.7 1.9 collective-permute-done.12
  140.5 5.3 %concatenate.71 = bf16[64,2,4320]{2,1,0:T(2,128)(2,1)} concatenate(bf16[64,2,1152]{2,1,0:T(2,128)(2,1)S(1)} %reshape.156, bf16[64,2,2592]{2,1,0:T(2,128)(2,1)S(1)} %reshape.157, bf16[64,2,576]{2,1,0:T(2,128)(2,1)S(1)} %bitcast.29), dimensions={2} | concatenate | bytes 2211840 | tf_op jit(solution)/shard_map/concatenate | solution.py:320
  145.8 9.5 %all-to-all-start.1 = ((bf16[64,2,4320]{2,1,0:T(2,128)(2,1)}), bf16[64,2,4320]{2,1,0:T(2,128)(2,1)S(1)}, u32[]{:S(2)}, u32[]{:S(2)}) async-start(bf16[64,2,4320]{2,1,0:T(2,128)(2,1)} %concatenate.71), calls=%async_computation.1 | async-start | bytes 2228224 | tf_op jit(solution)/shard_map/all_to_all | solution.py:226
  155.3 33.1 %all-to-all-done.1 = bf16[64,2,4320]{2,1,0:T(2,128)(2,1)S(1)} async-done(((bf16[64,2,4320]{2,1,0:T(2,128)(2,1)}), bf16[64,2,4320]{2,1,0:T(2,128)(2,1)S(1)}, u32[]{:S(2)}, u32[]{:S(2)}) %all-to-all-start.1) | async-done | bytes 1105952 | tf_op jit(solution)/shard_map/all_to_all | solution.py:226
  189.9 3.1 %collective-permute-start.13 = (f32[1,1152]{1,0:T(1,128)S(1)}, f32[1,1152]{1,0:T(1,128)S(1)}, u32[]{:S(2)}, u32[]{:S(2)}) collective-permute-start(f32[1,1152]{1,0:T(1,128)S(1)} %concatenate.72), channel_id=1, source_target_pairs={{0,1},{1,0},{2,3},{3,2},{4,5},{5,4},{6,7},{7,6},{8,9},{9,8},{10,11... | collective-permute-start | bytes 13832 | tf_op jit(solution)/shard_map/ppermute | solution.py:248
  195.1 3.7 %all-to-all-start.2 = ((f32[8,2,5184]{2,1,0:T(2,128)}), f32[8,2,5184]{2,1,0:T(2,128)S(1)}, u32[]{:S(2)}, u32[]{:S(2)}) async-start(f32[8,2,5184]{2,1,0:T(2,128)} %broadcast_in_dim.22), calls=%async_computation.2 | async-start | bytes 671744 | tf_op jit(solution)/shard_map/all_to_all | solution.py:325
  198.7 2.4 %shard_map.105 = bf16[128,1728]{1,0:T(8,128)(2,1)S(1)} custom-call(bf16[128,1728]{1,0:T(8,128)(2,1)S(1)} %bitcast.24, bf16[128,1152]{1,0:T(8,128)(2,1)S(1)} %reshape.159.hidden_grad, f32[4,1152]{1,0:T(4,128)S(1)} %bitcast.27, bf16[576,1152]{1,0:T(8,128)(2,1)S(1)} %copy-done.1), custom_call_target="tpu_custom_call" | custom-call | flops 1000000000 | bytes 10000000 | tf_op jit(solution)/shard_map/pallas_call | solution.py:214
  202.1 2.2 %collective-permute-start.14 = (f32[2,1152]{1,0:T(2,128)S(1)}, f32[2,1152]{1,0:T(2,128)S(1)}, u32[]{:S(2)}, u32[]{:S(2)}) collective-permute-start(f32[2,1152]{1,0:T(2,128)S(1)} %maximum_select_fusion.1), channel_id=1, source_target_pairs={{0,16},{16,0},{32,48},{48,32},{1,17},{17,1},{33,49},{49,33},{2,18}... | collective-permute-start | bytes 27656 | tf_op jit(solution)/shard_map/ppermute | solution.py:336
  204.3 3.1 %collective-permute-done.14 = f32[2,1152]{1,0:T(2,128)S(1)} collective-permute-done((f32[2,1152]{1,0:T(2,128)S(1)}, f32[2,1152]{1,0:T(2,128)S(1)}, u32[]{:S(2)}, u32[]{:S(2)}) %collective-permute-start.14) | collective-permute-done | bytes 9248 | tf_op jit(solution)/shard_map/ppermute | solution.py:336
  (68 shorter events, 23.4 us)
Async XLA Ops:
  0.6 2.2 %copy-start.8 = (bf16[1,1,128,1728]{2,3,1,0:T(8,128)(2,1)S(1)}, bf16[1,1,128,1728]{2,3,1,0:T(8,128)(2,1)}, u32[]{:S(2)}) copy-start(bf16[1,1,128,1728]{2,3,1,0:T(8,128)(2,1)} %param.8) | copy-start | bytes 1327108
  4.7 19.2 %copy-start.9 = (bf16[1152,27]{0,1:T(8,128)(2,1)S(1)}, bf16[1152,27]{0,1:T(8,128)(2,1)}, u32[]{:S(2)}) copy-start(bf16[1152,27]{0,1:T(8,128)(2,1)} %param.10) | copy-start | bytes 186628
  4.7 19.2 %copy-start.10 = (bf16[9,1152]{1,0:T(8,128)(2,1)S(1)}, bf16[9,1152]{1,0:T(8,128)(2,1)}, u32[]{:S(2)}) copy-start(bf16[9,1152]{1,0:T(8,128)(2,1)} %param.11) | copy-start | bytes 62212
  4.7 19.2 %copy-start.11 = (bf16[9,1152]{1,0:T(8,128)(2,1)S(1)}, bf16[9,1152]{1,0:T(8,128)(2,1)}, u32[]{:S(2)}) copy-start(bf16[9,1152]{1,0:T(8,128)(2,1)} %param.9) | copy-start | bytes 62212
  6.3 58.7 %all-to-all-start = ((bf16[64,2,2880]{2,1,0:T(2,128)(2,1)}), bf16[64,2,2880]{2,1,0:T(2,128)(2,1)S(1)}, u32[]{:S(2)}, u32[]{:S(2)}) async-start(bf16[64,2,2880]{2,1,0:T(2,128)(2,1)} %pad_maximum_fusion.1), calls=%async_computation | async-start | bytes 1507328 | tf_op jit(solution)/shard_map/all_to_all | solution.py:226
  24.0 0.7 collective-permute-start
  26.8 22.5 %collective-permute-start.3 = (bf16[2,45,1152]{2,1,0:T(8,128)(2,1)S(1)}, bf16[2,45,1152]{2,1,0:T(8,128)(2,1)S(1)}, u32[]{:S(2)}, u32[]{:S(2)}) collective-permute-start(bf16[2,45,1152]{2,1,0:T(8,128)(2,1)S(1)} %all-gather.1), channel_id=1, source_target_pairs={{4,0},{13,1},{6,2},{15,3},{8,4},{1,5},{10,6},{3,7},{12,8},{5,9},{1... | collective-permute-start | bytes 622088 | tf_op jit(solution)/shard_map/ppermute | solution.py:244
  30.9 21.0 %collective-permute-start.2 = (bf16[2,45,1152]{2,1,0:T(8,128)(2,1)S(1)}, bf16[2,45,1152]{2,1,0:T(8,128)(2,1)S(1)}, u32[]{:S(2)}, u32[]{:S(2)}) collective-permute-start(bf16[2,45,1152]{2,1,0:T(8,128)(2,1)S(1)} %all-gather.1), channel_id=1, source_target_pairs={{2,0},{15,1},{4,2},{1,3},{6,4},{3,5},{8,6},{5,7},{10,8},{7,9},{12,... | collective-permute-start | bytes 622088 | tf_op jit(solution)/shard_map/ppermute | solution.py:244
  34.0 22.8 %collective-permute-start.1 = (bf16[2,45,1152]{2,1,0:T(8,128)(2,1)S(1)}, bf16[2,45,1152]{2,1,0:T(8,128)(2,1)S(1)}, u32[]{:S(2)}, u32[]{:S(2)}) collective-permute-start(bf16[2,45,1152]{2,1,0:T(8,128)(2,1)S(1)} %all-gather.1), channel_id=1, source_target_pairs={{0,0},{9,1},{2,2},{11,3},{4,4},{13,5},{6,6},{15,7},{8,8},{1,9},{10... | collective-permute-start | bytes 622088 | tf_op jit(solution)/shard_map/ppermute | solution.py:244
  38.3 26.6 %collective-permute-start.4 = (bf16[2,45,1152]{2,1,0:T(8,128)(2,1)S(1)}, bf16[2,45,1152]{2,1,0:T(8,128)(2,1)S(1)}, u32[]{:S(2)}, u32[]{:S(2)}) collective-permute-start(bf16[2,45,1152]{2,1,0:T(8,128)(2,1)S(1)} %all-gather.1), channel_id=1, source_target_pairs={{6,0},{11,1},{8,2},{13,3},{10,4},{15,5},{12,6},{1,7},{14,8},{3,9},... | collective-permute-start | bytes 622088 | tf_op jit(solution)/shard_map/ppermute | solution.py:244
  65.1 3.3 %copy-start.7 = (bf16[64,2,2880]{2,1,0:T(2,128)(2,1)}, bf16[64,2,2880]{2,1,0:T(2,128)(2,1)S(1)}, u32[]{:S(2)}) copy-start(bf16[64,2,2880]{2,1,0:T(2,128)(2,1)S(1)} %all-to-all-done) | copy-start | bytes 2211844
  66.4 4.4 %collective-permute-start.5 = (bf16[4,2,45,1152]{3,0,2,1:T(4,128)(2,1)}, bf16[4,2,45,1152]{3,0,2,1:T(4,128)(2,1)S(1)}, u32[]{:S(2)}, u32[]{:S(2)}) collective-permute-start(bf16[4,2,45,1152]{3,0,2,1:T(4,128)(2,1)} %copy.29), channel_id=1, source_target_pairs={{0,1},{1,0},{2,3},{3,2},{4,5},{5,4},{6,7},{7,6},{8,9},{9,8},{10,11... | collective-permute-start | bytes 2488328 | tf_op jit(solution)/shard_map/ppermute | solution.py:248
  72.2 1.0 copy-start.2
  73.2 0.7 copy-start.3
  73.9 0.7 copy-start.5
  74.7 46.3 %copy-start = (f32[1,4,1152]{2,1,0:T(4,128)S(1)}, f32[1,4,1152]{2,1,0:T(4,128)}, u32[]{:S(2)}) copy-start(f32[1,4,1152]{2,1,0:T(4,128)} %param.12) | copy-start | bytes 55300
  74.7 28.1 %collective-permute-start.8 = (bf16[384,1152]{1,0:T(8,128)(2,1)S(1)}, bf16[384,1152]{1,0:T(8,128)(2,1)S(1)}, u32[]{:S(2)}, u32[]{:S(2)}) collective-permute-start(bf16[384,1152]{1,0:T(8,128)(2,1)S(1)} %get-tuple-element.20), channel_id=1, source_target_pairs={{192,0},{497,1},{194,2},{499,3},{196,4},{501,5},{198,6},{503,7},{2... | collective-permute-start | bytes 2654216 | tf_op jit(solution)/shard_map/ppermute | solution.py:244
  92.7 20.0 %collective-permute-start.7 = (bf16[384,1152]{1,0:T(8,128)(2,1)S(1)}, bf16[384,1152]{1,0:T(8,128)(2,1)S(1)}, u32[]{:S(2)}, u32[]{:S(2)}) collective-permute-start(bf16[384,1152]{1,0:T(8,128)(2,1)S(1)} %get-tuple-element.20), channel_id=1, source_target_pairs={{64,0},{113,1},{66,2},{115,3},{68,4},{117,5},{70,6},{119,7},{72,8}... | collective-permute-start | bytes 2654216 | tf_op jit(solution)/shard_map/ppermute | solution.py:244
  95.8 20.4 %collective-permute-start.6 = (bf16[384,1152]{1,0:T(8,128)(2,1)S(1)}, bf16[384,1152]{1,0:T(8,128)(2,1)}, u32[]{:S(2)}, u32[]{:S(2)}) collective-permute-start(bf16[384,1152]{1,0:T(8,128)(2,1)S(1)} %get-tuple-element.20), channel_id=1, source_target_pairs={{128,0},{385,1},{130,2},{387,3},{132,4},{389,5},{134,6},{391,7},{1... | collective-permute-start | bytes 2654216 | tf_op jit(solution)/shard_map/ppermute | solution.py:244
  102.7 17.7 %collective-permute-start.11 = (bf16[384,1152]{1,0:T(8,128)(2,1)S(1)}, bf16[384,1152]{1,0:T(8,128)(2,1)}, u32[]{:S(2)}, u32[]{:S(2)}) collective-permute-start(bf16[384,1152]{1,0:T(8,128)(2,1)S(1)} %collective-permute-done.8.d), channel_id=1, source_target_pairs={{0,1},{1,0},{2,3},{3,2},{4,5},{5,4},{6,7},{7,6},{8,9},{9,8},{10,11... | collective-permute-start | bytes 2654216 | tf_op jit(solution)/shard_map/ppermute | solution.py:248
  112.7 7.7 %collective-permute-start.10 = (bf16[384,1152]{1,0:T(8,128)(2,1)S(1)}, bf16[384,1152]{1,0:T(8,128)(2,1)}, u32[]{:S(2)}, u32[]{:S(2)}) collective-permute-start(bf16[384,1152]{1,0:T(8,128)(2,1)S(1)} %collective-permute-done.7.c), channel_id=1, source_target_pairs={{0,1},{1,0},{2,3},{3,2},{4,5},{5,4},{6,7},{7,6},{8,9},{9,8},{10,11... | collective-permute-start | bytes 2654216 | tf_op jit(solution)/shard_map/ppermute | solution.py:248
  116.2 4.7 %collective-permute-start.9 = (bf16[384,1152]{1,0:T(8,128)(2,1)}, bf16[384,1152]{1,0:T(8,128)(2,1)}, u32[]{:S(2)}, u32[]{:S(2)}) collective-permute-start(bf16[384,1152]{1,0:T(8,128)(2,1)} %collective-permute-done.6.b), channel_id=1, source_target_pairs={{0,1},{1,0},{2,3},{3,2},{4,5},{5,4},{6,7},{7,6},{8,9},{9,8},{10,11... | collective-permute-start | bytes 2654216 | tf_op jit(solution)/shard_map/ppermute | solution.py:248
  120.9 1.0 copy-start.4
  121.9 1.0 copy-start.6
  133.2 4.3 %collective-permute-start.12 = (bf16[576,576]{1,0:T(8,128)(2,1)}, bf16[576,576]{1,0:T(8,128)(2,1)S(1)}, u32[]{:S(2)}, u32[]{:S(2)}) collective-permute-start(bf16[576,576]{1,0:T(8,128)(2,1)} %get-tuple-element.23), channel_id=1, source_target_pairs={{0,1},{1,0},{2,3},{3,2},{4,5},{5,4},{6,7},{7,6},{8,9},{9,8},{10,11... | collective-permute-start | bytes 1990664 | tf_op jit(solution)/shard_map/ppermute | solution.py:248
  145.8 42.5 %all-to-all-start.1 = ((bf16[64,2,4320]{2,1,0:T(2,128)(2,1)}), bf16[64,2,4320]{2,1,0:T(2,128)(2,1)S(1)}, u32[]{:S(2)}, u32[]{:S(2)}) async-start(bf16[64,2,4320]{2,1,0:T(2,128)(2,1)} %concatenate.71), calls=%async_computation.1 | async-start | bytes 2228224 | tf_op jit(solution)/shard_map/all_to_all | solution.py:226
  189.9 8.8 %copy-start.1 = (bf16[576,1152]{1,0:T(8,128)(2,1)S(1)}, bf16[576,1152]{1,0:T(8,128)(2,1)}, u32[]{:S(2)}) copy-start(bf16[576,1152]{1,0:T(8,128)(2,1)} %get-tuple-element.25.w_so) | copy-start | bytes 3981316
  189.9 12.2 %collective-permute-start.13 = (f32[1,1152]{1,0:T(1,128)S(1)}, f32[1,1152]{1,0:T(1,128)S(1)}, u32[]{:S(2)}, u32[]{:S(2)}) collective-permute-start(f32[1,1152]{1,0:T(1,128)S(1)} %concatenate.72), channel_id=1, source_target_pairs={{0,1},{1,0},{2,3},{3,2},{4,5},{5,4},{6,7},{7,6},{8,9},{9,8},{10,11... | collective-permute-start | bytes 13832 | tf_op jit(solution)/shard_map/ppermute | solution.py:248
  195.1 13.0 %all-to-all-start.2 = ((f32[8,2,5184]{2,1,0:T(2,128)}), f32[8,2,5184]{2,1,0:T(2,128)S(1)}, u32[]{:S(2)}, u32[]{:S(2)}) async-start(f32[8,2,5184]{2,1,0:T(2,128)} %broadcast_in_dim.22), calls=%async_computation.2 | async-start | bytes 671744 | tf_op jit(solution)/shard_map/all_to_all | solution.py:325
  202.1 5.3 %collective-permute-start.14 = (f32[2,1152]{1,0:T(2,128)S(1)}, f32[2,1152]{1,0:T(2,128)S(1)}, u32[]{:S(2)}, u32[]{:S(2)}) collective-permute-start(f32[2,1152]{1,0:T(2,128)S(1)} %maximum_select_fusion.1), channel_id=1, source_target_pairs={{0,16},{16,0},{32,48},{48,32},{1,17},{17,1},{33,49},{49,33},{2,18}... | collective-permute-start | bytes 27656 | tf_op jit(solution)/shard_map/ppermute | solution.py:336

commit v5 on v4

--- a/solution.py
+++ b/solution.py
@@ -102,7 +102,9 @@
         slots[(1 - core) * 4 + i] = other[i]
     for target in range(8):
         delta = (target - z) & 7
-        slot = jnp.where(delta <= 4, delta, 12 - delta)
+        slot = jnp.where(delta < 2, 1 - delta, delta)
+        slot = jnp.where(delta == 4, 5, jnp.where(delta == 7, 4, slot))
+        slot = jnp.where(delta == 5, 7, slot)
         for c in range(2):
             i = target * 2 + c
             shard = slots[slot, c].astype(F32)
@@ -155,9 +157,10 @@
                 copy.wait()
 
 
-def temporal_kernel(
+def temporal_forward_kernel(
     place, sent, factors, own_qkv, own_so, own_out, b, c, d, other_b, other_c, other_d,
-    hidden_grad, factor_grads, out_keep, out_send, w_so, w_qkv, w_out, sems,
+    out_keep, out_send, w_so, w_out, w_qkv, q_out, k_out, v_out, probs_out, mixed_out,
+    unit_out, inverse_out, project_out, sems,
 ):
     assemble(
         place, (own_qkv, own_so, own_out), (b, c, d), (other_b, other_c, other_d),
@@ -166,44 +169,71 @@
     tokens, cotangent, mixed_s = sent[:, :D], sent[:, D : 2 * D], sent[:, 2 * D :]
     gate_s, shift, scale, gate_t = (factors[i : i + 1, :] for i in range(4))
     project = nn(mixed_s, w_so[...])
+    project_out[...] = project
     hidden = (tokens.astype(F32) + gate_s * project).astype(BF).astype(F32)
     centered = hidden - jnp.mean(hidden, -1, keepdims=True)
     inverse = lax.rsqrt(jnp.mean(centered * centered, -1, keepdims=True) + 1e-06)
+    inverse_out[...] = jnp.broadcast_to(inverse, (ROWS, 128))
     unit = centered * inverse
+    unit_out[...] = unit
     normed = (unit * (1.0 + scale) + shift).astype(BF)
-    wq, wk, wv = (w_qkv[i * ATT : (i + 1) * ATT, :] for i in range(3))
-    q, k, v = (nt(normed, w).astype(BF) for w in (wq, wk, wv))
-
-    masks = head_masks()
+    q, k, v = (nt(normed, w_qkv[i * ATT : (i + 1) * ATT, :]).astype(BF) for i in range(3))
+    q_out[...], k_out[...], v_out[...] = q, k, v
+
     row = lax.broadcasted_iota(jnp.int32, (HEADS * ROWS, ROWS), 0)
     col = lax.broadcasted_iota(jnp.int32, (HEADS * ROWS, ROWS), 1)
     same = ((row ^ col) & 1) == 0
-    q_stack, probs, probs_b, mixed = attend(masks, q, k, v, same)
-
-    cot = cotangent.astype(F32)
-    scaled = (cot * gate_t).astype(BF)
+    _, probs, _, mixed = attend(head_masks(), q, k, v, same)
+    probs_out[...] = probs
+    mixed_out[...] = mixed
+
+    scaled = (cotangent.astype(F32) * gate_t).astype(BF)
     left, right = scaled[:, :ATT], scaled[:, ATT:]
     first = place[0] == 0
     out_keep[...] = tn(mixed, jnp.where(first, left, right))
     out_send[...] = tn(mixed, jnp.where(first, right, left)).astype(BF)
 
+
+def temporal_backward_kernel(
+    sent, factors, w_so, w_out, w_qkv, q, k, v, probs, mixed, unit, inverse, project, packed
+):
+    scale, gate_t = factors[2:3, :], factors[3:4, :]
+    cot = sent[:, D : 2 * D].astype(F32)
+    scaled = (cot * gate_t).astype(BF)
+    masks = head_masks()
+    q, k, v, probs = q[...], k[...], v[...], probs[...]
     d_mixed = nt(scaled, w_out[...]).astype(BF)
-    d_q, d_k, d_v = attend_back(masks, q_stack, k, v, probs, probs_b, d_mixed)
+    q_stack = stack_heads(masks, q)
+    d_q, d_k, d_v = attend_back(masks, q_stack, k, v, probs, probs.astype(BF), d_mixed)
+    wq, wk, wv = (w_qkv[i * ATT : (i + 1) * ATT, :] for i in range(3))
     d_normed = (nn(d_q, wq) + nn(d_k, wk) + nn(d_v, wv)).astype(BF).astype(F32)
+    unit = unit[...]
     d_unit = d_normed * (1.0 + scale)
-    d_hidden = inverse * (
+    d_hidden = inverse[:, 0:1] * (
         d_unit
         - jnp.mean(d_unit, -1, keepdims=True)
         - unit * jnp.mean(d_unit * unit, -1, keepdims=True)
     )
     grad = (cot + d_hidden).astype(BF)
-    hidden_grad[...] = grad
-    grad = grad.astype(F32)
-    project_t = nn(mixed, w_out[...])
-    factor_grads[0:1, :] = jnp.sum(grad * project, 0, keepdims=True)
-    factor_grads[1:2, :] = jnp.sum(d_normed, 0, keepdims=True)
-    factor_grads[2:3, :] = jnp.sum(d_normed * unit, 0, keepdims=True)
-    factor_grads[3:4, :] = jnp.sum(cot * project_t, 0, keepdims=True)
+    packed[:, :D] = grad
+    project_t = nn(mixed[...], w_out[...])
+    factor_grads = (
+        jnp.sum(grad.astype(F32) * project[...], 0, keepdims=True),
+        jnp.sum(d_normed, 0, keepdims=True),
+        jnp.sum(d_normed * unit, 0, keepdims=True),
+        jnp.sum(cot * project_t, 0, keepdims=True),
+    )
+    zeros = jnp.zeros((16, 64), BF)
+    for parity in range(2):
+        rows = [
+            factor_grads[2 * parity + core][:, part * ATT : part * ATT + ATT]
+            for core in range(2)
+            for part in range(2)
+        ]
+        tile = jnp.concatenate([jnp.concatenate(rows * 4, 0).astype(BF), zeros], 1)
+        for yhi in (parity, parity + 2):
+            packed[32 * yhi : 32 * yhi + 16, D:] = tile
+            packed[32 * yhi + 16 : 32 * yhi + 32, D:] = tile
 
 
 def call(kernel, outs, *args, scalars=0, remote=0, scratch=(), flops=10**9):
@@ -217,7 +247,7 @@
         in_specs=specs,
         out_specs=[vmem] * len(outs),
         scratch_shapes=list(scratch),
-        compiler_params=pltpu.CompilerParams(vmem_limit_bytes=48 * 2**20),
+        compiler_params=pltpu.CompilerParams(vmem_limit_bytes=32 * 2**20),
         cost_estimate=pl.CostEstimate(flops=flops, bytes_accessed=10**7, transcendentals=10**5),
     )(*args)
 
@@ -248,7 +278,7 @@
     return lax.ppermute(a, "core", [(0, 1), (1, 0)])
 
 
-OFFSETS = ((0, 1, 2, 3), (4, -1, -2, -3))
+OFFSETS = ((1, 0, 2, 3), (-1, 4, -2, -3))
 
 
 def class_source(x, y, z, core):
@@ -273,6 +303,7 @@
     shard = receive(jnp.concatenate([w_so, w_out, w_qkv.T], 0), class_source)
     shards = lax.all_gather(shard, "core", axis=0)
     mine = [receive(shards, line_source(i)) for i in range(4)]
+    mine[0], sent = lax.optimization_barrier((mine[0], sent))
     mine, sent = lax.optimization_barrier((jnp.stack(mine), exchange(sent)))
     other = swap_cores(mine)
     rows = lambda n: ((n, D), BF)
@@ -300,26 +331,27 @@
     weights, sent = gather_weights(w_so, w_qkv, w_out, place, sent)
     sent = sent.reshape(ROWS, 2 * D + ATT)
 
-    hidden_grad, factor_part, out_keep, out_send, w_so = call(
-        temporal_kernel,
-        [((ROWS, D), BF), ((4, D), F32), ((ATT, ATT), F32), ((ATT, ATT), BF), ((ATT, D), BF)],
+    rows = lambda n, kind=BF: ((ROWS, n), kind)
+    out_keep, out_send, *saved = call(
+        temporal_forward_kernel,
+        [
+            ((ATT, ATT), F32), ((ATT, ATT), BF), ((ATT, D), BF), ((ATT, D), BF), ((3 * ATT, D), BF),
+            rows(ATT), rows(ATT), rows(ATT), ((HEADS * ROWS, ROWS), F32), rows(ATT),
+            rows(D, F32), rows(128, F32), rows(D, F32),
+        ],
         place, sent, factors, *weights,
         scalars=1, remote=len(weights), flops=4 * 10**9,
-        scratch=[
-            pltpu.VMEM((3 * ATT, D), BF),
-            pltpu.VMEM((ATT, D), BF),
-            pltpu.SemaphoreType.DMA((24,)),
-        ],
-    )
-
-    out_part = (out_keep + swap_cores(out_send).astype(F32)).astype(BF)
+        scratch=[pltpu.SemaphoreType.DMA((24,))],
+    )
+    w_so = saved[0]
+    out_other = swap_cores(out_send)
+    (packed,) = call(temporal_backward_kernel, [rows(D + 640)], sent, factors, *saved, flops=4 * 10**9)
+
     half = 9 * ATT // 2
-    factor_part = factor_part.astype(BF).reshape(1, 2, 1, 2, 2, D // 2)
-    factor_part = jnp.broadcast_to(factor_part, (2, 2, 8, 2, 2, D // 2)).reshape(64, 2, D // 2)
-    packed = [hidden_grad.reshape(64, 2, D), out_part.reshape(64, 2, half), factor_part]
-    back = exchange(jnp.concatenate(packed, 2))
-
-    out_part = back[:, :, D : D + half].astype(F32).reshape(32, 2, 2, half)
+    out_part = (out_keep + out_other.astype(F32)).astype(BF).reshape(64, 2, half)
+    back = exchange(jnp.concatenate([packed.reshape(64, 2, D + 640), out_part], 2))
+
+    out_part = back[:, :, D + 640 :].astype(F32).reshape(32, 2, 2, half)
     out_part = jnp.sum(out_part, 0).reshape(1, 2, 9 * ATT)
     out_part = jnp.broadcast_to(out_part, (8, 2, 9 * ATT))
     out_part = jnp.sum(lax.all_to_all(out_part, DP, 0, 0, tiled=True), 0)
@@ -330,7 +362,7 @@
         spatial_backward_kernel, [((ROWS, 3 * ATT), BF)], qkv, token_grad, factors, w_so
     )
 
-    mine = jnp.sum(back[:, :, D + half :].astype(F32), 0).reshape(1, D)
+    mine = jnp.sum(back[:, :, D : D + ATT].astype(F32), 0).reshape(1, D)
     other = swap_cores(mine)
     rows = jnp.where(core == 0, jnp.concatenate([mine, other]), jnp.concatenate([other, mine]))
     other = lax.ppermute(rows, "yhi", [(0, 1), (1, 0), (2, 3), (3, 2)])

time: 212 us -> 214 us (level)
  starting transfers between devices: 88.3 us -> 77.6 us
  waiting for transfers between devices: 75.1 us -> 83.5 us
  blocking collectives: 2.06 us -> 8.49 us
  local copies, waits for them, and re-layouts: 21.9 us -> 17.2 us
  other arithmetic: 5.05 us -> 7.65 us
    ppermute x8, waiting for transfers between devices: 34.1 us -> 44.2 us  [receive(): return lax.ppermute(a, AXES, pairs)]
    ppermute x8, starting transfers between devices: 39.2 us -> 30 us  [receive(): return lax.ppermute(a, AXES, pairs)]
    all_gather x1, blocking collectives: 2.06 us -> 8.49 us  [gather_weights(): shards = lax.all_gather(shard, 'core', axis=0)]
    concatenate x1 -> x0, local copies, waits for them, and re-layouts: 5.35 us -> none  [body(): back = exchange(jnp.concatenate(packed, 2))]
    pallas_call x4 -> x5, Pallas kernels: 15.5 us -> 16.9 us  [call(): pl.pallas_call(kernel, out_shape=[jax.ShapeDtypeStruct(s, d) for s, d in...]
    unnamed x26 -> x22, local copies, waits for them, and re-layouts: 5.57 us -> 5.61 us
  transfers between devices with their start and end apart: 18 -> 18, of which waited for: 11 -> 10; matrix products, arithmetic and copies ran while one was open for 3% -> 5% of each run, Pallas kernels for 1% -> 3%
where the time goes in v5:
time: 214 us; the launch traced here: 212 us
  waiting for transfers between devices  83.5 us (39%)
  starting transfers between devices  77.6 us (36%)
  local copies, waits for them, and re-layouts  17.2 us (8%)
  Pallas kernels  16.9 us (8%)
  blocking collectives  8.49 us (4%)
  other arithmetic  7.65 us (4%)
    ppermute x8, waiting for transfers between devices, receive(): return lax.ppermute(a, AXES, pairs)  44.2 us
    all_to_all x2, waiting for transfers between devices, exchange(): return lax.all_to_all(a, SEQ, 0, 0, tiled=True)  33 us
    ppermute x8, starting transfers between devices, receive(): return lax.ppermute(a, AXES, pairs)  30 us
    all_to_all x2, starting transfers between devices, exchange(): return lax.all_to_all(a, SEQ, 0, 0, tiled=True)  25.8 us
    pallas_call x5, Pallas kernels, call(): pl.pallas_call(kernel, out_shape=[jax.ShapeDtypeStruct(s, d) for s, d in...  16.9 us
    ppermute x6, starting transfers between devices, swap_cores(): return lax.ppermute(a, 'core', [(0, 1), (1, 0)])  14.1 us
    all_gather x1, blocking collectives, gather_weights(): shards = lax.all_gather(shard, 'core', axis=0)  8.49 us
    all_to_all x1, starting transfers between devices, body(): out_part = jnp.sum(lax.all_to_all(out_part, DP, 0, 0, tiled=True), 0)  5.77 us
  transfers between devices with their start and end apart: 18, of which 10 were waited for; matrix products, arithmetic and copies ran while one was open for 5% of the time, Pallas kernels for 3%

profile of v5, /device:TPU:1, one launch (start us, length us, event | category | flops | bytes accessed | tf_op | source)
XLA Modules:
  0.0 212.3 jit_solution(4091041089169358989)
XLA Ops:
  6.3 8.5 %all-gather.1 = bf16[2,45,1152]{2,1,0:T(8,128)(2,1)S(1)} all-gather(bf16[1,45,1152]{2,1,0:T(8,128)(2,1)S(1)} %bitcast.34), channel_id=2, replica_groups=mesh['x'=4,'ylo'=2,'yhi'=4,'z'=8,'core'=2] {'core'}, dimensions={0}, use_global_device_ids=true | all-gather | bytes 311040 | tf_op jit(solution)/shard_map/all_gather | solution.py:304
  14.8 1.9 collective-permute-start.1
  18.3 5.1 %collective-permute-done.1 = bf16[2,45,1152]{2,1,0:T(8,128)(2,1)S(1)} collective-permute-done((bf16[2,45,1152]{2,1,0:T(8,128)(2,1)S(1)}, bf16[2,45,1152]{2,1,0:T(8,128)(2,1)S(1)}, u32[]{:S(2)}, u32[]{:S(2)}) %collective-permute-start.1) | collective-permute-done | bytes 207392 | tf_op jit(solution)/shard_map/ppermute | solution.py:274
  23.4 18.4 %all-to-all-start = ((bf16[64,2,2880]{2,1,0:T(2,128)(2,1)}), bf16[64,2,2880]{2,1,0:T(2,128)(2,1)S(1)}, u32[]{:S(2)}, u32[]{:S(2)}) async-start(bf16[64,2,2880]{2,1,0:T(2,128)(2,1)} %pad_maximum_fusion.2), calls=%async_computation | async-start | bytes 1507328 | tf_op jit(solution)/shard_map/all_to_all | solution.py:256
  41.8 4.2 %collective-permute-start.3 = (bf16[2,45,1152]{2,1,0:T(8,128)(2,1)S(1)}, bf16[2,45,1152]{2,1,0:T(8,128)(2,1)S(1)}, u32[]{:S(2)}, u32[]{:S(2)}) collective-permute-start(bf16[2,45,1152]{2,1,0:T(8,128)(2,1)S(1)} %all-gather.1), channel_id=1, source_target_pairs={{4,0},{13,1},{6,2},{15,3},{8,4},{1,5},{10,6},{3,7},{12,8},{5,9},{1... | collective-permute-start | bytes 622088 | tf_op jit(solution)/shard_map/ppermute | solution.py:274
  46.0 5.2 %collective-permute-start.2 = (bf16[2,45,1152]{2,1,0:T(8,128)(2,1)S(1)}, bf16[2,45,1152]{2,1,0:T(8,128)(2,1)S(1)}, u32[]{:S(2)}, u32[]{:S(2)}) collective-permute-start(bf16[2,45,1152]{2,1,0:T(8,128)(2,1)S(1)} %all-gather.1), channel_id=1, source_target_pairs={{0,0},{9,1},{2,2},{11,3},{4,4},{13,5},{6,6},{15,7},{8,8},{1,9},{10... | collective-permute-start | bytes 622088 | tf_op jit(solution)/shard_map/ppermute | solution.py:274
  51.3 3.1 %collective-permute-start.4 = (bf16[2,45,1152]{2,1,0:T(8,128)(2,1)S(1)}, bf16[2,45,1152]{2,1,0:T(8,128)(2,1)S(1)}, u32[]{:S(2)}, u32[]{:S(2)}) collective-permute-start(bf16[2,45,1152]{2,1,0:T(8,128)(2,1)S(1)} %all-gather.1), channel_id=1, source_target_pairs={{6,0},{11,1},{8,2},{13,3},{10,4},{15,5},{12,6},{1,7},{14,8},{3,9},... | collective-permute-start | bytes 622088 | tf_op jit(solution)/shard_map/ppermute | solution.py:274
  54.4 14.8 %collective-permute-done.3 = bf16[2,45,1152]{2,1,0:T(8,128)(2,1)S(1)} collective-permute-done((bf16[2,45,1152]{2,1,0:T(8,128)(2,1)S(1)}, bf16[2,45,1152]{2,1,0:T(8,128)(2,1)S(1)}, u32[]{:S(2)}, u32[]{:S(2)}) %collective-permute-start.3) | collective-permute-done | bytes 207392 | tf_op jit(solution)/shard_map/ppermute | solution.py:274
  69.1 4.5 %collective-permute-done.2 = bf16[2,45,1152]{2,1,0:T(8,128)(2,1)S(1)} collective-permute-done((bf16[2,45,1152]{2,1,0:T(8,128)(2,1)S(1)}, bf16[2,45,1152]{2,1,0:T(8,128)(2,1)S(1)}, u32[]{:S(2)}, u32[]{:S(2)}) %collective-permute-start.2) | collective-permute-done | bytes 207392 | tf_op jit(solution)/shard_map/ppermute | solution.py:274
  73.7 7.8 %collective-permute-done.4 = bf16[2,45,1152]{2,1,0:T(8,128)(2,1)S(1)} collective-permute-done((bf16[2,45,1152]{2,1,0:T(8,128)(2,1)S(1)}, bf16[2,45,1152]{2,1,0:T(8,128)(2,1)S(1)}, u32[]{:S(2)}, u32[]{:S(2)}) %collective-permute-start.4) | collective-permute-done | bytes 207392 | tf_op jit(solution)/shard_map/ppermute | solution.py:274
  83.0 1.9 collective-permute-start.5
  85.0 2.4 %collective-permute-done.5 = bf16[4,2,45,1152]{3,0,2,1:T(4,128)(2,1)S(1)} collective-permute-done((bf16[4,2,45,1152]{3,0,2,1:T(4,128)(2,1)}, bf16[4,2,45,1152]{3,0,2,1:T(4,128)(2,1)S(1)}, u32[]{:S(2)}, u32[]{:S(2)}) %collective-permute-start.5) | collective-permute-done | bytes 829472 | tf_op jit(solution)/shard_map/ppermute | solution.py:278
  89.8 2.0 collective-permute-start.8
  91.8 8.9 %collective-permute-start.7 = (bf16[384,1152]{1,0:T(8,128)(2,1)S(1)}, bf16[384,1152]{1,0:T(8,128)(2,1)}, u32[]{:S(2)}, u32[]{:S(2)}) collective-permute-start(bf16[384,1152]{1,0:T(8,128)(2,1)S(1)} %get-tuple-element.32), channel_id=1, source_target_pairs={{64,0},{113,1},{66,2},{115,3},{68,4},{117,5},{70,6},{119,7},{72,8}... | collective-permute-start | bytes 2654216 | tf_op jit(solution)/shard_map/ppermute | solution.py:274
  100.7 4.0 %collective-permute-start.6 = (bf16[384,1152]{1,0:T(8,128)(2,1)S(1)}, bf16[384,1152]{1,0:T(8,128)(2,1)}, u32[]{:S(2)}, u32[]{:S(2)}) collective-permute-start(bf16[384,1152]{1,0:T(8,128)(2,1)S(1)} %get-tuple-element.32), channel_id=1, source_target_pairs={{128,0},{385,1},{130,2},{387,3},{132,4},{389,5},{134,6},{391,7},{1... | collective-permute-start | bytes 2654216 | tf_op jit(solution)/shard_map/ppermute | solution.py:274
  104.8 2.3 %collective-permute-done.8.d = bf16[384,1152]{1,0:T(8,128)(2,1)S(1)} collective-permute-done((bf16[384,1152]{1,0:T(8,128)(2,1)S(1)}, bf16[384,1152]{1,0:T(8,128)(2,1)S(1)}, u32[]{:S(2)}, u32[]{:S(2)}) %collective-permute-start.8) | collective-permute-done | bytes 884768 | tf_op jit(solution)/shard_map/ppermute | solution.py:274
  107.1 1.9 collective-permute-start.11
  109.0 9.7 %collective-permute-done.7.c = bf16[384,1152]{1,0:T(8,128)(2,1)} collective-permute-done((bf16[384,1152]{1,0:T(8,128)(2,1)S(1)}, bf16[384,1152]{1,0:T(8,128)(2,1)}, u32[]{:S(2)}, u32[]{:S(2)}) %collective-permute-start.7) | collective-permute-done | bytes 884768 | tf_op jit(solution)/shard_map/ppermute | solution.py:274
  118.7 3.3 %collective-permute-start.10 = (bf16[384,1152]{1,0:T(8,128)(2,1)}, bf16[384,1152]{1,0:T(8,128)(2,1)}, u32[]{:S(2)}, u32[]{:S(2)}) collective-permute-start(bf16[384,1152]{1,0:T(8,128)(2,1)} %collective-permute-done.7.c), channel_id=1, source_target_pairs={{0,1},{1,0},{2,3},{3,2},{4,5},{5,4},{6,7},{7,6},{8,9},{9,8},{10,11... | collective-permute-start | bytes 2654216 | tf_op jit(solution)/shard_map/ppermute | solution.py:278
  122.0 1.9 collective-permute-start.9
  124.0 2.2 %reshape.150.sent = bf16[128,2880]{1,0:T(8,128)(2,1)S(1)} reshape(bf16[64,2,2880]{2,1,0:T(2,128)(2,1)} %copy-done.7) | data formatting | bytes 1474560 | tf_op jit(solution)/shard_map/reshape | solution.py:332
  129.1 8.5 %shard_map.104 = (f32[576,576]{1,0:T(8,128)S(1)}, bf16[576,576]{1,0:T(8,128)(2,1)}, bf16[576,1152]{1,0:T(8,128)(2,1)S(1)}, bf16[576,1152]{1,0:T(8,128)(2,1)S(1)}...) custom-call(s32[3]{0:T(128)S(1)} %pad_add_fusion.place, ...), custom_call_target="tpu_custom_call" | custom-call | flops 4000000000 | bytes 10000000 | tf_op jit(solution)/shard_map/pallas_call | solution.py:244
  137.6 2.2 %collective-permute-start.12 = (bf16[576,576]{1,0:T(8,128)(2,1)}, bf16[576,576]{1,0:T(8,128)(2,1)}, u32[]{:S(2)}, u32[]{:S(2)}) collective-permute-start(bf16[576,576]{1,0:T(8,128)(2,1)} %get-tuple-element.45), channel_id=1, source_target_pairs={{0,1},{1,0},{2,3},{3,2},{4,5},{5,4},{6,7},{7,6},{8,9},{9,8},{10,11... | collective-permute-start | bytes 1990664 | tf_op jit(solution)/shard_map/ppermute | solution.py:278
  139.8 3.1 %shard_map.105 = bf16[128,1792]{1,0:T(8,128)(2,1)S(1)} custom-call(bf16[128,2880]{1,0:T(8,128)(2,1)S(1)} %reshape.150.sent, f32[4,1152]{1,0:T(4,128)S(1)} %bitcast.26, bf16[576,1152]{1,0:T(8,128)(2,1)S(1)} %get-tuple-element.33.w_so, bf16[576,1152]{1,0:T(8,128)(2,1)S(1)} %get-tuple-element.34.w_out, bf16[1728,1152]{1,0:T(8,128)(2,1)S(1)} %get-tuple-element.35.w_qkv, ...), custom_call_target="tpu_custom_call" | custom-call | flops 4000000000 | bytes 10000000 | tf_op jit(solution)/shard_map/pallas_call | solution.py:244
  147.6 2.1 pad_maximum_fusion
  149.7 7.4 %all-to-all-start.1 = ((bf16[64,2,4384]{2,1,0:T(2,128)(2,1)}), bf16[64,2,4384]{2,1,0:T(2,128)(2,1)S(1)}, u32[]{:S(2)}, u32[]{:S(2)}) async-start(bf16[64,2,4384]{2,1,0:T(2,128)(2,1)} %pad_maximum_fusion), calls=%async_computation.1 | async-start | bytes 2293760 | tf_op jit(solution)/shard_map/all_to_all | solution.py:256
  157.1 33.0 %all-to-all-done.1 = bf16[64,2,4384]{2,1,0:T(2,128)(2,1)S(1)} async-done(((bf16[64,2,4384]{2,1,0:T(2,128)(2,1)}), bf16[64,2,4384]{2,1,0:T(2,128)(2,1)S(1)}, u32[]{:S(2)}, u32[]{:S(2)}) %all-to-all-start.1) | async-done | bytes 1122336 | tf_op jit(solution)/shard_map/all_to_all | solution.py:256
  191.5 2.8 %collective-permute-start.13 = (f32[1,1152]{1,0:T(1,128)S(1)}, f32[1,1152]{1,0:T(1,128)S(1)}, u32[]{:S(2)}, u32[]{:S(2)}) collective-permute-start(f32[1,1152]{1,0:T(1,128)S(1)} %concatenate.72), channel_id=1, source_target_pairs={{0,1},{1,0},{2,3},{3,2},{4,5},{5,4},{6,7},{7,6},{8,9},{9,8},{10,11... | collective-permute-start | bytes 13832 | tf_op jit(solution)/shard_map/ppermute | solution.py:278
  196.3 5.8 %all-to-all-start.2 = ((f32[8,2,5184]{2,1,0:T(2,128)}), f32[8,2,5184]{2,1,0:T(2,128)S(1)}, u32[]{:S(2)}, u32[]{:S(2)}) async-start(f32[8,2,5184]{2,1,0:T(2,128)} %broadcast_in_dim.13), calls=%async_computation.2 | async-start | bytes 671744 | tf_op jit(solution)/shard_map/all_to_all | solution.py:357
  202.1 2.4 %shard_map.106 = bf16[128,1728]{1,0:T(8,128)(2,1)S(1)} custom-call(bf16[128,1728]{1,0:T(8,128)(2,1)S(1)} %bitcast.23, bf16[128,1152]{1,0:T(8,128)(2,1)S(1)} %reshape.153.hidden_grad, f32[4,1152]{1,0:T(4,128)S(1)} %bitcast.27, bf16[576,1152]{1,0:T(8,128)(2,1)S(1)} %copy-done.4), custom_call_target="tpu_custom_call" | custom-call | flops 1000000000 | bytes 10000000 | tf_op jit(solution)/shard_map/pallas_call | solution.py:244
  205.4 1.9 collective-permute-start.14
  207.4 3.3 %collective-permute-done.14 = f32[2,1152]{1,0:T(2,128)S(1)} collective-permute-done((f32[2,1152]{1,0:T(2,128)S(1)}, f32[2,1152]{1,0:T(2,128)S(1)}, u32[]{:S(2)}, u32[]{:S(2)}) %collective-permute-start.14) | collective-permute-done | bytes 9248 | tf_op jit(solution)/shard_map/ppermute | solution.py:368
  (62 shorter events, 24.6 us)
Async XLA Ops:
  0.6 3.8 %copy-start.9 = (bf16[1,1,128,1728]{2,3,1,0:T(8,128)(2,1)S(1)}, bf16[1,1,128,1728]{2,3,1,0:T(8,128)(2,1)}, u32[]{:S(2)}) copy-start(bf16[1,1,128,1728]{2,3,1,0:T(8,128)(2,1)} %param.8) | copy-start | bytes 1327108
  1.6 4.7 %collective-permute-start = (bf16[45,1152]{1,0:T(8,128)(2,1)S(1)}, bf16[45,1152]{1,0:T(8,128)(2,1)S(1)}, u32[]{:S(2)}, u32[]{:S(2)}) collective-permute-start(bf16[45,1152]{1,0:T(8,128)(2,1)S(1)} %pad_maximum_fusion.3), channel_id=1, source_target_pairs={{0,0},{1,1},{2,2},{3,3},{4,4},{5,5},{6,6},{7,7},{8,8},{9,9},{10,10... | collective-permute-start | bytes 311048 | tf_op jit(solution)/shard_map/ppermute | solution.py:274
  14.8 8.6 %collective-permute-start.1 = (bf16[2,45,1152]{2,1,0:T(8,128)(2,1)S(1)}, bf16[2,45,1152]{2,1,0:T(8,128)(2,1)S(1)}, u32[]{:S(2)}, u32[]{:S(2)}) collective-permute-start(bf16[2,45,1152]{2,1,0:T(8,128)(2,1)S(1)} %all-gather.1), channel_id=1, source_target_pairs={{2,0},{15,1},{4,2},{1,3},{6,4},{3,5},{8,6},{5,7},{10,8},{7,9},{12,... | collective-permute-start | bytes 622088 | tf_op jit(solution)/shard_map/ppermute | solution.py:274
  23.4 58.2 %all-to-all-start = ((bf16[64,2,2880]{2,1,0:T(2,128)(2,1)}), bf16[64,2,2880]{2,1,0:T(2,128)(2,1)S(1)}, u32[]{:S(2)}, u32[]{:S(2)}) async-start(bf16[64,2,2880]{2,1,0:T(2,128)(2,1)} %pad_maximum_fusion.2), calls=%async_computation | async-start | bytes 1507328 | tf_op jit(solution)/shard_map/all_to_all | solution.py:256
  41.8 27.3 %collective-permute-start.3 = (bf16[2,45,1152]{2,1,0:T(8,128)(2,1)S(1)}, bf16[2,45,1152]{2,1,0:T(8,128)(2,1)S(1)}, u32[]{:S(2)}, u32[]{:S(2)}) collective-permute-start(bf16[2,45,1152]{2,1,0:T(8,128)(2,1)S(1)} %all-gather.1), channel_id=1, source_target_pairs={{4,0},{13,1},{6,2},{15,3},{8,4},{1,5},{10,6},{3,7},{12,8},{5,9},{1... | collective-permute-start | bytes 622088 | tf_op jit(solution)/shard_map/ppermute | solution.py:274
  46.0 27.6 %collective-permute-start.2 = (bf16[2,45,1152]{2,1,0:T(8,128)(2,1)S(1)}, bf16[2,45,1152]{2,1,0:T(8,128)(2,1)S(1)}, u32[]{:S(2)}, u32[]{:S(2)}) collective-permute-start(bf16[2,45,1152]{2,1,0:T(8,128)(2,1)S(1)} %all-gather.1), channel_id=1, source_target_pairs={{0,0},{9,1},{2,2},{11,3},{4,4},{13,5},{6,6},{15,7},{8,8},{1,9},{10... | collective-permute-start | bytes 622088 | tf_op jit(solution)/shard_map/ppermute | solution.py:274
  51.3 30.2 %collective-permute-start.4 = (bf16[2,45,1152]{2,1,0:T(8,128)(2,1)S(1)}, bf16[2,45,1152]{2,1,0:T(8,128)(2,1)S(1)}, u32[]{:S(2)}, u32[]{:S(2)}) collective-permute-start(bf16[2,45,1152]{2,1,0:T(8,128)(2,1)S(1)} %all-gather.1), channel_id=1, source_target_pairs={{6,0},{11,1},{8,2},{13,3},{10,4},{15,5},{12,6},{1,7},{14,8},{3,9},... | collective-permute-start | bytes 622088 | tf_op jit(solution)/shard_map/ppermute | solution.py:274
  81.7 3.3 %copy-start.7 = (bf16[64,2,2880]{2,1,0:T(2,128)(2,1)}, bf16[64,2,2880]{2,1,0:T(2,128)(2,1)S(1)}, u32[]{:S(2)}) copy-start(bf16[64,2,2880]{2,1,0:T(2,128)(2,1)S(1)} %all-to-all-done) | copy-start | bytes 2211844
  83.0 4.4 %collective-permute-start.5 = (bf16[4,2,45,1152]{3,0,2,1:T(4,128)(2,1)}, bf16[4,2,45,1152]{3,0,2,1:T(4,128)(2,1)S(1)}, u32[]{:S(2)}, u32[]{:S(2)}) collective-permute-start(bf16[4,2,45,1152]{3,0,2,1:T(4,128)(2,1)} %copy.29), channel_id=1, source_target_pairs={{0,1},{1,0},{2,3},{3,2},{4,5},{5,4},{6,7},{7,6},{8,9},{9,8},{10,11... | collective-permute-start | bytes 2488328 | tf_op jit(solution)/shard_map/ppermute | solution.py:278
  88.8 1.0 copy-start.5
  89.8 36.9 %copy-start.2 = (f32[1,4,1152]{2,1,0:T(4,128)S(1)}, f32[1,4,1152]{2,1,0:T(4,128)}, u32[]{:S(2)}) copy-start(f32[1,4,1152]{2,1,0:T(4,128)} %param.12) | copy-start | bytes 55300
  89.8 17.3 %collective-permute-start.8 = (bf16[384,1152]{1,0:T(8,128)(2,1)S(1)}, bf16[384,1152]{1,0:T(8,128)(2,1)S(1)}, u32[]{:S(2)}, u32[]{:S(2)}) collective-permute-start(bf16[384,1152]{1,0:T(8,128)(2,1)S(1)} %get-tuple-element.32), channel_id=1, source_target_pairs={{192,0},{497,1},{194,2},{499,3},{196,4},{501,5},{198,6},{503,7},{2... | collective-permute-start | bytes 2654216 | tf_op jit(solution)/shard_map/ppermute | solution.py:274
  91.8 26.9 %collective-permute-start.7 = (bf16[384,1152]{1,0:T(8,128)(2,1)S(1)}, bf16[384,1152]{1,0:T(8,128)(2,1)}, u32[]{:S(2)}, u32[]{:S(2)}) collective-permute-start(bf16[384,1152]{1,0:T(8,128)(2,1)S(1)} %get-tuple-element.32), channel_id=1, source_target_pairs={{64,0},{113,1},{66,2},{115,3},{68,4},{117,5},{70,6},{119,7},{72,8}... | collective-permute-start | bytes 2654216 | tf_op jit(solution)/shard_map/ppermute | solution.py:274
  100.7 21.3 %collective-permute-start.6 = (bf16[384,1152]{1,0:T(8,128)(2,1)S(1)}, bf16[384,1152]{1,0:T(8,128)(2,1)}, u32[]{:S(2)}, u32[]{:S(2)}) collective-permute-start(bf16[384,1152]{1,0:T(8,128)(2,1)S(1)} %get-tuple-element.32), channel_id=1, source_target_pairs={{128,0},{385,1},{130,2},{387,3},{132,4},{389,5},{134,6},{391,7},{1... | collective-permute-start | bytes 2654216 | tf_op jit(solution)/shard_map/ppermute | solution.py:274
  107.1 19.6 %copy-start = (bf16[384,1152]{1,0:T(8,128)(2,1)}, bf16[384,1152]{1,0:T(8,128)(2,1)S(1)}, u32[]{:S(2)}) copy-start(bf16[384,1152]{1,0:T(8,128)(2,1)S(1)} %collective-permute-done.8.d) | copy-start | bytes 2654212
  107.1 19.1 %collective-permute-start.11 = (bf16[384,1152]{1,0:T(8,128)(2,1)S(1)}, bf16[384,1152]{1,0:T(8,128)(2,1)}, u32[]{:S(2)}, u32[]{:S(2)}) collective-permute-start(bf16[384,1152]{1,0:T(8,128)(2,1)S(1)} %collective-permute-done.8.d), channel_id=1, source_target_pairs={{0,1},{1,0},{2,3},{3,2},{4,5},{5,4},{6,7},{7,6},{8,9},{9,8},{10,11... | collective-permute-start | bytes 2654216 | tf_op jit(solution)/shard_map/ppermute | solution.py:278
  118.7 7.5 %collective-permute-start.10 = (bf16[384,1152]{1,0:T(8,128)(2,1)}, bf16[384,1152]{1,0:T(8,128)(2,1)}, u32[]{:S(2)}, u32[]{:S(2)}) collective-permute-start(bf16[384,1152]{1,0:T(8,128)(2,1)} %collective-permute-done.7.c), channel_id=1, source_target_pairs={{0,1},{1,0},{2,3},{3,2},{4,5},{5,4},{6,7},{7,6},{8,9},{9,8},{10,11... | collective-permute-start | bytes 2654216 | tf_op jit(solution)/shard_map/ppermute | solution.py:278
  122.0 4.7 %collective-permute-start.9 = (bf16[384,1152]{1,0:T(8,128)(2,1)}, bf16[384,1152]{1,0:T(8,128)(2,1)}, u32[]{:S(2)}, u32[]{:S(2)}) collective-permute-start(bf16[384,1152]{1,0:T(8,128)(2,1)} %collective-permute-done.6.b), channel_id=1, source_target_pairs={{0,1},{1,0},{2,3},{3,2},{4,5},{5,4},{6,7},{7,6},{8,9},{9,8},{10,11... | collective-permute-start | bytes 2654216 | tf_op jit(solution)/shard_map/ppermute | solution.py:278
  126.7 1.2 copy-start.1
  127.9 1.2 copy-start.6
  137.6 7.4 %collective-permute-start.12 = (bf16[576,576]{1,0:T(8,128)(2,1)}, bf16[576,576]{1,0:T(8,128)(2,1)}, u32[]{:S(2)}, u32[]{:S(2)}) collective-permute-start(bf16[576,576]{1,0:T(8,128)(2,1)} %get-tuple-element.45), channel_id=1, source_target_pairs={{0,1},{1,0},{2,3},{3,2},{4,5},{5,4},{6,7},{7,6},{8,9},{9,8},{10,11... | collective-permute-start | bytes 1990664 | tf_op jit(solution)/shard_map/ppermute | solution.py:278
  143.0 1.1 copy-start.3
  146.3 1.3 copy-start.8
  149.7 40.4 %all-to-all-start.1 = ((bf16[64,2,4384]{2,1,0:T(2,128)(2,1)}), bf16[64,2,4384]{2,1,0:T(2,128)(2,1)S(1)}, u32[]{:S(2)}, u32[]{:S(2)}) async-start(bf16[64,2,4384]{2,1,0:T(2,128)(2,1)} %pad_maximum_fusion), calls=%async_computation.1 | async-start | bytes 2293760 | tf_op jit(solution)/shard_map/all_to_all | solution.py:256
  191.5 10.6 %copy-start.4 = (bf16[576,1152]{1,0:T(8,128)(2,1)S(1)}, bf16[576,1152]{1,0:T(8,128)(2,1)}, u32[]{:S(2)}) copy-start(bf16[576,1152]{1,0:T(8,128)(2,1)} %copy-done.3) | copy-start | bytes 3981316
  191.5 13.9 %collective-permute-start.13 = (f32[1,1152]{1,0:T(1,128)S(1)}, f32[1,1152]{1,0:T(1,128)S(1)}, u32[]{:S(2)}, u32[]{:S(2)}) collective-permute-start(f32[1,1152]{1,0:T(1,128)S(1)} %concatenate.72), channel_id=1, source_target_pairs={{0,1},{1,0},{2,3},{3,2},{4,5},{5,4},{6,7},{7,6},{8,9},{9,8},{10,11... | collective-permute-start | bytes 13832 | tf_op jit(solution)/shard_map/ppermute | solution.py:278
  196.3 15.1 %all-to-all-start.2 = ((f32[8,2,5184]{2,1,0:T(2,128)}), f32[8,2,5184]{2,1,0:T(2,128)S(1)}, u32[]{:S(2)}, u32[]{:S(2)}) async-start(f32[8,2,5184]{2,1,0:T(2,128)} %broadcast_in_dim.13), calls=%async_computation.2 | async-start | bytes 671744 | tf_op jit(solution)/shard_map/all_to_all | solution.py:357
  205.4 5.3 %collective-permute-start.14 = (f32[2,1152]{1,0:T(2,128)S(1)}, f32[2,1152]{1,0:T(2,128)S(1)}, u32[]{:S(2)}, u32[]{:S(2)}) collective-permute-start(f32[2,1152]{1,0:T(2,128)S(1)} %maximum_select_fusion.1), channel_id=1, source_target_pairs={{0,16},{16,0},{32,48},{48,32},{1,17},{17,1},{33,49},{49,33},{2,18}... | collective-permute-start | bytes 27656 | tf_op jit(solution)/shard_map/ppermute | solution.py:368

commit v6 on v5

--- a/solution.py
+++ b/solution.py
@@ -223,17 +223,9 @@
         jnp.sum(d_normed * unit, 0, keepdims=True),
         jnp.sum(cot * project_t, 0, keepdims=True),
     )
-    zeros = jnp.zeros((16, 64), BF)
-    for parity in range(2):
-        rows = [
-            factor_grads[2 * parity + core][:, part * ATT : part * ATT + ATT]
-            for core in range(2)
-            for part in range(2)
-        ]
-        tile = jnp.concatenate([jnp.concatenate(rows * 4, 0).astype(BF), zeros], 1)
-        for yhi in (parity, parity + 2):
-            packed[32 * yhi : 32 * yhi + 16, D:] = tile
-            packed[32 * yhi + 16 : 32 * yhi + 32, D:] = tile
+    tile = jnp.concatenate(factor_grads * 4, 0).astype(BF)
+    for i in range(8):
+        packed[16 * i : 16 * i + 16, D:] = tile
 
 
 def call(kernel, outs, *args, scalars=0, remote=0, scratch=(), flops=10**9):
@@ -302,9 +294,9 @@
 def gather_weights(w_so, w_qkv, w_out, place, sent):
     shard = receive(jnp.concatenate([w_so, w_out, w_qkv.T], 0), class_source)
     shards = lax.all_gather(shard, "core", axis=0)
-    mine = [receive(shards, line_source(i)) for i in range(4)]
-    mine[0], sent = lax.optimization_barrier((mine[0], sent))
-    mine, sent = lax.optimization_barrier((jnp.stack(mine), exchange(sent)))
+    shards, sent = lax.optimization_barrier((shards, sent))
+    mine = jnp.stack([receive(shards, line_source(i)) for i in range(4)])
+    sent = exchange(sent).reshape(ROWS, 2 * D + ATT)
     other = swap_cores(mine)
     rows = lambda n: ((n, D), BF)
     own_so, own_out, own_qkv, part = call(
@@ -316,20 +308,20 @@
             pltpu.VMEM((432, D), F32),
         ],
     )
+    part, sent = lax.optimization_barrier((part, sent))
     near = [receive(part, near_source(dx, dy)) for dx, dy in ((1, 0), (0, 1), (1, 1))]
     return [own_qkv, own_so, own_out] + near + [swap_cores(a) for a in near], sent
 
 
 def body(tokens, qkv, w_so, w_qkv, w_out, factors, cotangent):
     tokens, qkv, cotangent, factors = tokens[0, 0], qkv[0, 0], cotangent[0, 0], factors[0]
-    core, yhi = lax.axis_index("core"), lax.axis_index("yhi")
+    core = lax.axis_index("core")
     cls = (lax.axis_index("x") % 2) * 2 + lax.axis_index("ylo")
     place = jnp.stack([core, cls, lax.axis_index("z")]).astype(jnp.int32)
 
     (mixed_s,) = call(spatial_forward_kernel, [((ROWS, ATT), BF)], qkv)
     sent = jnp.concatenate([tokens, cotangent, mixed_s], 1).reshape(64, 2, 2 * D + ATT)
     weights, sent = gather_weights(w_so, w_qkv, w_out, place, sent)
-    sent = sent.reshape(ROWS, 2 * D + ATT)
 
     rows = lambda n, kind=BF: ((ROWS, n), kind)
     out_keep, out_send, *saved = call(
@@ -345,13 +337,13 @@
     )
     w_so = saved[0]
     out_other = swap_cores(out_send)
-    (packed,) = call(temporal_backward_kernel, [rows(D + 640)], sent, factors, *saved, flops=4 * 10**9)
+    (packed,) = call(temporal_backward_kernel, [rows(2 * D)], sent, factors, *saved, flops=4 * 10**9)
 
     half = 9 * ATT // 2
     out_part = (out_keep + out_other.astype(F32)).astype(BF).reshape(64, 2, half)
-    back = exchange(jnp.concatenate([packed.reshape(64, 2, D + 640), out_part], 2))
-
-    out_part = back[:, :, D + 640 :].astype(F32).reshape(32, 2, 2, half)
+    back = exchange(jnp.concatenate([packed.reshape(64, 2, 2 * D), out_part], 2))
+
+    out_part = back[:, :, 2 * D :].astype(F32).reshape(32, 2, 2, half)
     out_part = jnp.sum(out_part, 0).reshape(1, 2, 9 * ATT)
     out_part = jnp.broadcast_to(out_part, (8, 2, 9 * ATT))
     out_part = jnp.sum(lax.all_to_all(out_part, DP, 0, 0, tiled=True), 0)
@@ -362,12 +354,9 @@
         spatial_backward_kernel, [((ROWS, 3 * ATT), BF)], qkv, token_grad, factors, w_so
     )
 
-    mine = jnp.sum(back[:, :, D : D + ATT].astype(F32), 0).reshape(1, D)
+    mine = jnp.sum(back[:, :, D : 2 * D].astype(F32), 0)
     other = swap_cores(mine)
-    rows = jnp.where(core == 0, jnp.concatenate([mine, other]), jnp.concatenate([other, mine]))
-    other = lax.ppermute(rows, "yhi", [(0, 1), (1, 0), (2, 3), (3, 2)])
-    low = yhi % 2 == 0
-    factor_grad = jnp.where(low, jnp.concatenate([rows, other]), jnp.concatenate([other, rows]))
+    factor_grad = jnp.where(core == 0, jnp.concatenate([mine, other]), jnp.concatenate([other, mine]))
     return token_grad[None, None], qkv_grad[None, None], factor_grad[None], out_grad
 
 

time: 214 us -> 211 us (0.986)
  blocking collectives: 8.49 us -> 53.5 us
  waiting for transfers between devices: 83.5 us -> 45.6 us
  starting transfers between devices: 77.6 us -> 62.3 us
  local copies, waits for them, and re-layouts: 17.2 us -> 20.3 us
  Pallas kernels: 16.9 us -> 19.5 us
    all_to_all x0 -> x1, blocking collectives: none -> 45.1 us  [exchange(): return lax.all_to_all(a, SEQ, 0, 0, tiled=True)]
    all_to_all x2 -> x1, waiting for transfers between devices: 33 us -> 0.01 us  [exchange(): return lax.all_to_all(a, SEQ, 0, 0, tiled=True)]
    all_to_all x2 -> x1, starting transfers between devices: 25.8 us -> 16.6 us  [exchange(): return lax.all_to_all(a, SEQ, 0, 0, tiled=True)]
    ppermute x8, starting transfers between devices: 30 us -> 26.5 us  [receive(): return lax.ppermute(a, AXES, pairs)]
    ppermute x1 -> x0, waiting for transfers between devices: 3.35 us -> none  [body(): other = lax.ppermute(rows, 'yhi', [(0, 1), (1, 0), (2, 3), (3, 2)])]
    ppermute x8, waiting for transfers between devices: 44.2 us -> 41.1 us  [receive(): return lax.ppermute(a, AXES, pairs)]
    pallas_call x5, Pallas kernels: 16.9 us -> 19.5 us  [call(): pl.pallas_call(kernel, out_shape=[jax.ShapeDtypeStruct(s, d) for s, d in...]
    unnamed x22 -> x26, local copies, waits for them, and re-layouts: 5.61 us -> 7.63 us
  transfers between devices with their start and end apart: 18 -> 16, of which waited for: 10 -> 8; matrix products, arithmetic and copies ran while one was open for 5% -> 6% of each run, Pallas kernels for 3% -> 4%
where the time goes in v6:
time: 211 us; the launch traced here: 210 us
  starting transfers between devices  62.3 us (30%)
  blocking collectives  53.5 us (25%)
  waiting for transfers between devices  45.6 us (22%)
  local copies, waits for them, and re-layouts  20.3 us (10%)
  Pallas kernels  19.5 us (9%)
  other arithmetic  7.73 us (4%)
    all_to_all x1, blocking collectives, exchange(): return lax.all_to_all(a, SEQ, 0, 0, tiled=True)  45.1 us
    ppermute x8, waiting for transfers between devices, receive(): return lax.ppermute(a, AXES, pairs)  41.1 us
    ppermute x8, starting transfers between devices, receive(): return lax.ppermute(a, AXES, pairs)  26.5 us
    pallas_call x5, Pallas kernels, call(): pl.pallas_call(kernel, out_shape=[jax.ShapeDtypeStruct(s, d) for s, d in...  19.5 us
    all_to_all x1, starting transfers between devices, exchange(): return lax.all_to_all(a, SEQ, 0, 0, tiled=True)  16.6 us
    ppermute x6, starting transfers between devices, swap_cores(): return lax.ppermute(a, 'core', [(0, 1), (1, 0)])  14.1 us
    all_gather x1, blocking collectives, gather_weights(): shards = lax.all_gather(shard, 'core', axis=0)  8.47 us
    unnamed x26, local copies, waits for them, and re-layouts  7.63 us
  transfers between devices with their start and end apart: 16, of which 8 were waited for; matrix products, arithmetic and copies ran while one was open for 6% of the time, Pallas kernels for 4%

profile of v6, /device:TPU:1, one launch (start us, length us, event | category | flops | bytes accessed | tf_op | source)
XLA Modules:
  0.0 209.8 jit_solution(9525563476936885072)
XLA Ops:
  4.7 1.5 shard_map.102
  6.3 1.6 pad_maximum_fusion.2
  7.9 8.5 %all-gather.1 = bf16[2,45,1152]{2,1,0:T(8,128)(2,1)S(1)} all-gather(bf16[1,45,1152]{2,1,0:T(8,128)(2,1)S(1)} %bitcast.33), channel_id=2, replica_groups=mesh['x'=4,'ylo'=2,'yhi'=4,'z'=8,'core'=2] {'core'}, dimensions={0}, use_global_device_ids=true | all-gather | bytes 311040 | tf_op jit(solution)/shard_map/all_gather | solution.py:296
  16.4 16.6 %all-to-all-start = ((bf16[64,2,2880]{2,1,0:T(2,128)(2,1)}), bf16[64,2,2880]{2,1,0:T(2,128)(2,1)}, u32[]{:S(2)}, u32[]{:S(2)}) async-start(bf16[64,2,2880]{2,1,0:T(2,128)(2,1)} %pad_maximum_fusion.2), calls=%async_computation | async-start | bytes 1507328 | tf_op jit(solution)/shard_map/all_to_all | solution.py:248
  33.0 5.1 %collective-permute-start.4 = (bf16[2,45,1152]{2,1,0:T(8,128)(2,1)S(1)}, bf16[2,45,1152]{2,1,0:T(8,128)(2,1)S(1)}, u32[]{:S(2)}, u32[]{:S(2)}) collective-permute-start(bf16[2,45,1152]{2,1,0:T(8,128)(2,1)S(1)} %all-gather.1), channel_id=1, source_target_pairs={{6,0},{11,1},{8,2},{13,3},{10,4},{15,5},{12,6},{1,7},{14,8},{3,9},... | collective-permute-start | bytes 622088 | tf_op jit(solution)/shard_map/ppermute | solution.py:266
  38.1 4.3 %collective-permute-start.3 = (bf16[2,45,1152]{2,1,0:T(8,128)(2,1)S(1)}, bf16[2,45,1152]{2,1,0:T(8,128)(2,1)S(1)}, u32[]{:S(2)}, u32[]{:S(2)}) collective-permute-start(bf16[2,45,1152]{2,1,0:T(8,128)(2,1)S(1)} %all-gather.1), channel_id=1, source_target_pairs={{4,0},{13,1},{6,2},{15,3},{8,4},{1,5},{10,6},{3,7},{12,8},{5,9},{1... | collective-permute-start | bytes 622088 | tf_op jit(solution)/shard_map/ppermute | solution.py:266
  42.4 3.1 %collective-permute-start.2 = (bf16[2,45,1152]{2,1,0:T(8,128)(2,1)S(1)}, bf16[2,45,1152]{2,1,0:T(8,128)(2,1)S(1)}, u32[]{:S(2)}, u32[]{:S(2)}) collective-permute-start(bf16[2,45,1152]{2,1,0:T(8,128)(2,1)S(1)} %all-gather.1), channel_id=1, source_target_pairs={{0,0},{9,1},{2,2},{11,3},{4,4},{13,5},{6,6},{15,7},{8,8},{1,9},{10... | collective-permute-start | bytes 622088 | tf_op jit(solution)/shard_map/ppermute | solution.py:266
  45.5 3.1 %collective-permute-start.1 = (bf16[2,45,1152]{2,1,0:T(8,128)(2,1)S(1)}, bf16[2,45,1152]{2,1,0:T(8,128)(2,1)S(1)}, u32[]{:S(2)}, u32[]{:S(2)}) collective-permute-start(bf16[2,45,1152]{2,1,0:T(8,128)(2,1)S(1)} %all-gather.1), channel_id=1, source_target_pairs={{2,0},{15,1},{4,2},{1,3},{6,4},{3,5},{8,6},{5,7},{10,8},{7,9},{12,... | collective-permute-start | bytes 622088 | tf_op jit(solution)/shard_map/ppermute | solution.py:266
  48.6 14.8 %collective-permute-done.4 = bf16[2,45,1152]{2,1,0:T(8,128)(2,1)S(1)} collective-permute-done((bf16[2,45,1152]{2,1,0:T(8,128)(2,1)S(1)}, bf16[2,45,1152]{2,1,0:T(8,128)(2,1)S(1)}, u32[]{:S(2)}, u32[]{:S(2)}) %collective-permute-start.4) | collective-permute-done | bytes 207392 | tf_op jit(solution)/shard_map/ppermute | solution.py:266
  63.4 3.9 %collective-permute-done.3 = bf16[2,45,1152]{2,1,0:T(8,128)(2,1)S(1)} collective-permute-done((bf16[2,45,1152]{2,1,0:T(8,128)(2,1)S(1)}, bf16[2,45,1152]{2,1,0:T(8,128)(2,1)S(1)}, u32[]{:S(2)}, u32[]{:S(2)}) %collective-permute-start.3) | collective-permute-done | bytes 207392 | tf_op jit(solution)/shard_map/ppermute | solution.py:266
  67.3 5.2 %collective-permute-done.2 = bf16[2,45,1152]{2,1,0:T(8,128)(2,1)S(1)} collective-permute-done((bf16[2,45,1152]{2,1,0:T(8,128)(2,1)S(1)}, bf16[2,45,1152]{2,1,0:T(8,128)(2,1)S(1)}, u32[]{:S(2)}, u32[]{:S(2)}) %collective-permute-start.2) | collective-permute-done | bytes 207392 | tf_op jit(solution)/shard_map/ppermute | solution.py:266
  72.5 1.6 collective-permute-done.1
  74.3 1.3 copy.29
  75.6 1.9 collective-permute-start.5
  77.6 2.4 %collective-permute-done.5 = bf16[4,2,45,1152]{3,0,2,1:T(4,128)(2,1)S(1)} collective-permute-done((bf16[4,2,45,1152]{3,0,2,1:T(4,128)(2,1)}, bf16[4,2,45,1152]{3,0,2,1:T(4,128)(2,1)S(1)}, u32[]{:S(2)}, u32[]{:S(2)}) %collective-permute-start.5) | collective-permute-done | bytes 829472 | tf_op jit(solution)/shard_map/ppermute | solution.py:270
  84.1 2.3 %reshape.95.sent = bf16[128,2880]{1,0:T(8,128)(2,1)S(1)} reshape(bf16[64,2,2880]{2,1,0:T(2,128)(2,1)} %all-to-all-done) | data formatting | bytes 1474560 | tf_op jit(solution)/shard_map/reshape | solution.py:299
  86.4 1.9 collective-permute-start.8
  88.3 4.3 %collective-permute-start.7 = (bf16[384,1152]{1,0:T(8,128)(2,1)S(1)}, bf16[384,1152]{1,0:T(8,128)(2,1)S(1)}, u32[]{:S(2)}, u32[]{:S(2)}) collective-permute-start(bf16[384,1152]{1,0:T(8,128)(2,1)S(1)} %copy-done.1), channel_id=1, source_target_pairs={{64,0},{113,1},{66,2},{115,3},{68,4},{117,5},{70,6},{119,7},{72,8}... | collective-permute-start | bytes 2654216 | tf_op jit(solution)/shard_map/ppermute | solution.py:266
  92.6 4.0 %collective-permute-start.6 = (bf16[384,1152]{1,0:T(8,128)(2,1)S(1)}, bf16[384,1152]{1,0:T(8,128)(2,1)S(1)}, u32[]{:S(2)}, u32[]{:S(2)}) collective-permute-start(bf16[384,1152]{1,0:T(8,128)(2,1)S(1)} %copy-done.1), channel_id=1, source_target_pairs={{128,0},{385,1},{130,2},{387,3},{132,4},{389,5},{134,6},{391,7},{1... | collective-permute-start | bytes 2654216 | tf_op jit(solution)/shard_map/ppermute | solution.py:266
  96.7 6.9 %collective-permute-done.8.d = bf16[384,1152]{1,0:T(8,128)(2,1)S(1)} collective-permute-done((bf16[384,1152]{1,0:T(8,128)(2,1)S(1)}, bf16[384,1152]{1,0:T(8,128)(2,1)S(1)}, u32[]{:S(2)}, u32[]{:S(2)}) %collective-permute-start.8) | collective-permute-done | bytes 884768 | tf_op jit(solution)/shard_map/ppermute | solution.py:266
  103.6 1.9 collective-permute-start.11
  105.5 8.7 %collective-permute-done.7.c = bf16[384,1152]{1,0:T(8,128)(2,1)S(1)} collective-permute-done((bf16[384,1152]{1,0:T(8,128)(2,1)S(1)}, bf16[384,1152]{1,0:T(8,128)(2,1)S(1)}, u32[]{:S(2)}, u32[]{:S(2)}) %collective-permute-start.7) | collective-permute-done | bytes 884768 | tf_op jit(solution)/shard_map/ppermute | solution.py:266
  114.2 1.9 collective-permute-start.10
  116.1 2.4 %collective-permute-start.9 = (bf16[384,1152]{1,0:T(8,128)(2,1)S(1)}, bf16[384,1152]{1,0:T(8,128)(2,1)S(1)}, u32[]{:S(2)}, u32[]{:S(2)}) collective-permute-start(bf16[384,1152]{1,0:T(8,128)(2,1)S(1)} %collective-permute-done.6.b), channel_id=1, source_target_pairs={{0,1},{1,0},{2,3},{3,2},{4,5},{5,4},{6,7},{7,6},{8,9},{9,8},{10,11... | collective-permute-start | bytes 2654216 | tf_op jit(solution)/shard_map/ppermute | solution.py:270
  118.5 2.0 collective-permute-done.9.other_b
  122.7 11.1 %shard_map.104 = (f32[576,576]{1,0:T(8,128)S(1)}, bf16[576,576]{1,0:T(8,128)(2,1)}, bf16[576,1152]{1,0:T(8,128)(2,1)S(1)}, bf16[576,1152]{1,0:T(8,128)(2,1)S(1)}...) custom-call(s32[3]{0:T(128)S(1)} %pad_add_fusion.place, ...), custom_call_target="tpu_custom_call" | custom-call | flops 4000000000 | bytes 10000000 | tf_op jit(solution)/shard_map/pallas_call | solution.py:236
  133.9 2.5 %collective-permute-start.12 = (bf16[576,576]{1,0:T(8,128)(2,1)}, bf16[576,576]{1,0:T(8,128)(2,1)}, u32[]{:S(2)}, u32[]{:S(2)}) collective-permute-start(bf16[576,576]{1,0:T(8,128)(2,1)} %get-tuple-element.45), channel_id=1, source_target_pairs={{0,1},{1,0},{2,3},{3,2},{4,5},{5,4},{6,7},{7,6},{8,9},{9,8},{10,11... | collective-permute-start | bytes 1990664 | tf_op jit(solution)/shard_map/ppermute | solution.py:270
  136.4 3.2 %shard_map.105 = bf16[128,2304]{1,0:T(8,128)(2,1)S(1)} custom-call(bf16[128,2880]{1,0:T(8,128)(2,1)S(1)} %reshape.95.sent, f32[4,1152]{1,0:T(4,128)S(1)} %bitcast.25, bf16[576,1152]{1,0:T(8,128)(2,1)S(1)} %get-tuple-element.33.w_so, bf16[576,1152]{1,0:T(8,128)(2,1)S(1)} %get-tuple-element.34.w_out, bf16[1728,1152]{1,0:T(8,128)(2,1)S(1)} %get-tuple-element.35.w_qkv, ...), custom_call_target="tpu_custom_call" | custom-call | flops 4000000000 | bytes 10000000 | tf_op jit(solution)/shard_map/pallas_call | solution.py:236
  145.4 45.1 %all_to_all.15 = bf16[64,2,4896]{2,1,0:T(2,128)(2,1)S(1)} all-to-all(bf16[64,2,4896]{2,1,0:T(2,128)(2,1)S(1)} %pad_maximum_fusion), channel_id=1, replica_groups=mesh['x'=4,'ylo'=2,'yhi'=4,'z'=8,'core'=2] {'yhi','z','core'}, dimensions={0} | all-to-all | bytes 2506752 | tf_op jit(solution)/shard_map/all_to_all | solution.py:248
  193.1 5.0 %all-to-all-start.2 = ((f32[8,2,5184]{2,1,0:T(2,128)}), f32[8,2,5184]{2,1,0:T(2,128)S(1)}, u32[]{:S(2)}, u32[]{:S(2)}) async-start(f32[8,2,5184]{2,1,0:T(2,128)} %broadcast_in_dim.13), calls=%async_computation.2 | async-start | bytes 671744 | tf_op jit(solution)/shard_map/all_to_all | solution.py:349
  199.3 3.5 %collective-permute-start.13 = (f32[2,1152]{1,0:T(2,128)S(1)}, f32[2,1152]{1,0:T(2,128)S(1)}, u32[]{:S(2)}, u32[]{:S(2)}) collective-permute-start(f32[2,1152]{1,0:T(2,128)S(1)} %convert_reduce_fusion.1), channel_id=1, source_target_pairs={{0,1},{1,0},{2,3},{3,2},{4,5},{5,4},{6,7},{7,6},{8,9},{9,8},{10,11... | collective-permute-start | bytes 27656 | tf_op jit(solution)/shard_map/ppermute | solution.py:270
  204.1 2.4 %shard_map.106 = bf16[128,1728]{1,0:T(8,128)(2,1)S(1)} custom-call(bf16[128,1728]{1,0:T(8,128)(2,1)S(1)} %bitcast.22, bf16[128,1152]{1,0:T(8,128)(2,1)S(1)} %reshape.98.hidden_grad, f32[4,1152]{1,0:T(4,128)S(1)} %bitcast.26, bf16[576,1152]{1,0:T(8,128)(2,1)S(1)} %copy-done.4), custom_call_target="tpu_custom_call" | custom-call | flops 1000000000 | bytes 10000000 | tf_op jit(solution)/shard_map/pallas_call | solution.py:236
  (60 shorter events, 24.8 us)
Async XLA Ops:
  0.6 3.8 %copy-start.11 = (bf16[1,1,128,1728]{2,3,1,0:T(8,128)(2,1)S(1)}, bf16[1,1,128,1728]{2,3,1,0:T(8,128)(2,1)}, u32[]{:S(2)}) copy-start(bf16[1,1,128,1728]{2,3,1,0:T(8,128)(2,1)} %param.8) | copy-start | bytes 1327108
  1.6 6.3 %collective-permute-start = (bf16[45,1152]{1,0:T(8,128)(2,1)S(1)}, bf16[45,1152]{1,0:T(8,128)(2,1)S(1)}, u32[]{:S(2)}, u32[]{:S(2)}) collective-permute-start(bf16[45,1152]{1,0:T(8,128)(2,1)S(1)} %pad_maximum_fusion.3), channel_id=1, source_target_pairs={{0,0},{1,1},{2,2},{3,3},{4,4},{5,5},{6,6},{7,7},{8,8},{9,9},{10,10... | collective-permute-start | bytes 311048 | tf_op jit(solution)/shard_map/ppermute | solution.py:266
  16.4 67.7 %all-to-all-start = ((bf16[64,2,2880]{2,1,0:T(2,128)(2,1)}), bf16[64,2,2880]{2,1,0:T(2,128)(2,1)}, u32[]{:S(2)}, u32[]{:S(2)}) async-start(bf16[64,2,2880]{2,1,0:T(2,128)(2,1)} %pad_maximum_fusion.2), calls=%async_computation | async-start | bytes 1507328 | tf_op jit(solution)/shard_map/all_to_all | solution.py:248
  33.0 30.4 %collective-permute-start.4 = (bf16[2,45,1152]{2,1,0:T(8,128)(2,1)S(1)}, bf16[2,45,1152]{2,1,0:T(8,128)(2,1)S(1)}, u32[]{:S(2)}, u32[]{:S(2)}) collective-permute-start(bf16[2,45,1152]{2,1,0:T(8,128)(2,1)S(1)} %all-gather.1), channel_id=1, source_target_pairs={{6,0},{11,1},{8,2},{13,3},{10,4},{15,5},{12,6},{1,7},{14,8},{3,9},... | collective-permute-start | bytes 622088 | tf_op jit(solution)/shard_map/ppermute | solution.py:266
  38.1 29.2 %collective-permute-start.3 = (bf16[2,45,1152]{2,1,0:T(8,128)(2,1)S(1)}, bf16[2,45,1152]{2,1,0:T(8,128)(2,1)S(1)}, u32[]{:S(2)}, u32[]{:S(2)}) collective-permute-start(bf16[2,45,1152]{2,1,0:T(8,128)(2,1)S(1)} %all-gather.1), channel_id=1, source_target_pairs={{4,0},{13,1},{6,2},{15,3},{8,4},{1,5},{10,6},{3,7},{12,8},{5,9},{1... | collective-permute-start | bytes 622088 | tf_op jit(solution)/shard_map/ppermute | solution.py:266
  42.4 30.1 %collective-permute-start.2 = (bf16[2,45,1152]{2,1,0:T(8,128)(2,1)S(1)}, bf16[2,45,1152]{2,1,0:T(8,128)(2,1)S(1)}, u32[]{:S(2)}, u32[]{:S(2)}) collective-permute-start(bf16[2,45,1152]{2,1,0:T(8,128)(2,1)S(1)} %all-gather.1), channel_id=1, source_target_pairs={{0,0},{9,1},{2,2},{11,3},{4,4},{13,5},{6,6},{15,7},{8,8},{1,9},{10... | collective-permute-start | bytes 622088 | tf_op jit(solution)/shard_map/ppermute | solution.py:266
  45.5 28.6 %collective-permute-start.1 = (bf16[2,45,1152]{2,1,0:T(8,128)(2,1)S(1)}, bf16[2,45,1152]{2,1,0:T(8,128)(2,1)S(1)}, u32[]{:S(2)}, u32[]{:S(2)}) collective-permute-start(bf16[2,45,1152]{2,1,0:T(8,128)(2,1)S(1)} %all-gather.1), channel_id=1, source_target_pairs={{2,0},{15,1},{4,2},{1,3},{6,4},{3,5},{8,6},{5,7},{10,8},{7,9},{12,... | collective-permute-start | bytes 622088 | tf_op jit(solution)/shard_map/ppermute | solution.py:266
  75.6 4.4 %collective-permute-start.5 = (bf16[4,2,45,1152]{3,0,2,1:T(4,128)(2,1)}, bf16[4,2,45,1152]{3,0,2,1:T(4,128)(2,1)S(1)}, u32[]{:S(2)}, u32[]{:S(2)}) collective-permute-start(bf16[4,2,45,1152]{3,0,2,1:T(4,128)(2,1)} %copy.29), channel_id=1, source_target_pairs={{0,1},{1,0},{2,3},{3,2},{4,5},{5,4},{6,7},{7,6},{8,9},{9,8},{10,11... | collective-permute-start | bytes 2488328 | tf_op jit(solution)/shard_map/ppermute | solution.py:270
  81.4 0.9 copy-start
  82.4 1.0 copy-start.5
  83.3 0.7 copy-start.7
  84.1 36.5 %copy-start.2 = (f32[1,4,1152]{2,1,0:T(4,128)S(1)}, f32[1,4,1152]{2,1,0:T(4,128)}, u32[]{:S(2)}) copy-start(f32[1,4,1152]{2,1,0:T(4,128)} %param.12) | copy-start | bytes 55300
  84.1 2.3 %copy-start.1 = (bf16[384,1152]{1,0:T(8,128)(2,1)S(1)}, bf16[384,1152]{1,0:T(8,128)(2,1)}, u32[]{:S(2)}) copy-start(bf16[384,1152]{1,0:T(8,128)(2,1)} %copy-done) | copy-start | bytes 2654212
  86.4 17.2 %collective-permute-start.8 = (bf16[384,1152]{1,0:T(8,128)(2,1)S(1)}, bf16[384,1152]{1,0:T(8,128)(2,1)S(1)}, u32[]{:S(2)}, u32[]{:S(2)}) collective-permute-start(bf16[384,1152]{1,0:T(8,128)(2,1)S(1)} %copy-done.1), channel_id=1, source_target_pairs={{192,0},{497,1},{194,2},{499,3},{196,4},{501,5},{198,6},{503,7},{2... | collective-permute-start | bytes 2654216 | tf_op jit(solution)/shard_map/ppermute | solution.py:266
  88.3 25.9 %collective-permute-start.7 = (bf16[384,1152]{1,0:T(8,128)(2,1)S(1)}, bf16[384,1152]{1,0:T(8,128)(2,1)S(1)}, u32[]{:S(2)}, u32[]{:S(2)}) collective-permute-start(bf16[384,1152]{1,0:T(8,128)(2,1)S(1)} %copy-done.1), channel_id=1, source_target_pairs={{64,0},{113,1},{66,2},{115,3},{68,4},{117,5},{70,6},{119,7},{72,8}... | collective-permute-start | bytes 2654216 | tf_op jit(solution)/shard_map/ppermute | solution.py:266
  92.6 23.5 %collective-permute-start.6 = (bf16[384,1152]{1,0:T(8,128)(2,1)S(1)}, bf16[384,1152]{1,0:T(8,128)(2,1)S(1)}, u32[]{:S(2)}, u32[]{:S(2)}) collective-permute-start(bf16[384,1152]{1,0:T(8,128)(2,1)S(1)} %copy-done.1), channel_id=1, source_target_pairs={{128,0},{385,1},{130,2},{387,3},{132,4},{389,5},{134,6},{391,7},{1... | collective-permute-start | bytes 2654216 | tf_op jit(solution)/shard_map/ppermute | solution.py:266
  103.6 14.9 %collective-permute-start.11 = (bf16[384,1152]{1,0:T(8,128)(2,1)S(1)}, bf16[384,1152]{1,0:T(8,128)(2,1)S(1)}, u32[]{:S(2)}, u32[]{:S(2)}) collective-permute-start(bf16[384,1152]{1,0:T(8,128)(2,1)S(1)} %collective-permute-done.8.d), channel_id=1, source_target_pairs={{0,1},{1,0},{2,3},{3,2},{4,5},{5,4},{6,7},{7,6},{8,9},{9,8},{10,11... | collective-permute-start | bytes 2654216 | tf_op jit(solution)/shard_map/ppermute | solution.py:270
  114.2 4.4 %collective-permute-start.10 = (bf16[384,1152]{1,0:T(8,128)(2,1)S(1)}, bf16[384,1152]{1,0:T(8,128)(2,1)S(1)}, u32[]{:S(2)}, u32[]{:S(2)}) collective-permute-start(bf16[384,1152]{1,0:T(8,128)(2,1)S(1)} %collective-permute-done.7.c), channel_id=1, source_target_pairs={{0,1},{1,0},{2,3},{3,2},{4,5},{5,4},{6,7},{7,6},{8,9},{9,8},{10,11... | collective-permute-start | bytes 2654216 | tf_op jit(solution)/shard_map/ppermute | solution.py:270
  116.1 4.4 %collective-permute-start.9 = (bf16[384,1152]{1,0:T(8,128)(2,1)S(1)}, bf16[384,1152]{1,0:T(8,128)(2,1)S(1)}, u32[]{:S(2)}, u32[]{:S(2)}) collective-permute-start(bf16[384,1152]{1,0:T(8,128)(2,1)S(1)} %collective-permute-done.6.b), channel_id=1, source_target_pairs={{0,1},{1,0},{2,3},{3,2},{4,5},{5,4},{6,7},{7,6},{8,9},{9,8},{10,11... | collective-permute-start | bytes 2654216 | tf_op jit(solution)/shard_map/ppermute | solution.py:270
  120.6 1.2 copy-start.6
  121.8 1.0 copy-start.8
  133.9 7.8 %collective-permute-start.12 = (bf16[576,576]{1,0:T(8,128)(2,1)}, bf16[576,576]{1,0:T(8,128)(2,1)}, u32[]{:S(2)}, u32[]{:S(2)}) collective-permute-start(bf16[576,576]{1,0:T(8,128)(2,1)} %get-tuple-element.45), channel_id=1, source_target_pairs={{0,1},{1,0},{2,3},{3,2},{4,5},{5,4},{6,7},{7,6},{8,9},{9,8},{10,11... | collective-permute-start | bytes 1990664 | tf_op jit(solution)/shard_map/ppermute | solution.py:270
  139.6 1.1 copy-start.3
  141.7 2.6 %copy-start.10 = (bf16[64,2,2304]{2,1,0:T(2,128)(2,1)S(1)}, bf16[64,2,2304]{2,1,0:T(2,128)(2,1)}, u32[]{:S(2)}) copy-start(bf16[64,2,2304]{2,1,0:T(2,128)(2,1)} %reshape.96) | copy-start | bytes 1769476
  190.5 1.0 copy-start.9
  192.1 12.0 %copy-start.4 = (bf16[576,1152]{1,0:T(8,128)(2,1)S(1)}, bf16[576,1152]{1,0:T(8,128)(2,1)}, u32[]{:S(2)}) copy-start(bf16[576,1152]{1,0:T(8,128)(2,1)} %copy-done.3) | copy-start | bytes 3981316
  193.1 15.8 %all-to-all-start.2 = ((f32[8,2,5184]{2,1,0:T(2,128)}), f32[8,2,5184]{2,1,0:T(2,128)S(1)}, u32[]{:S(2)}, u32[]{:S(2)}) async-start(f32[8,2,5184]{2,1,0:T(2,128)} %broadcast_in_dim.13), calls=%async_computation.2 | async-start | bytes 671744 | tf_op jit(solution)/shard_map/all_to_all | solution.py:349
  199.3 8.9 %collective-permute-start.13 = (f32[2,1152]{1,0:T(2,128)S(1)}, f32[2,1152]{1,0:T(2,128)S(1)}, u32[]{:S(2)}, u32[]{:S(2)}) collective-permute-start(f32[2,1152]{1,0:T(2,128)S(1)} %convert_reduce_fusion.1), channel_id=1, source_target_pairs={{0,1},{1,0},{2,3},{3,2},{4,5},{5,4},{6,7},{7,6},{8,9},{9,8},{10,11... | collective-permute-start | bytes 27656 | tf_op jit(solution)/shard_map/ppermute | solution.py:270

commit v7 on v6

--- a/solution.py
+++ b/solution.py
@@ -95,22 +95,13 @@
     out[:, 2 * ATT :] = d_v
 
 
-def compact_kernel(place, mine, other, own_so, own_out, own_qkv, part, slots, so, out, qkv):
-    core, z = place[0], place[2]
-    for i in range(4):
-        slots[core * 4 + i] = mine[i]
-        slots[(1 - core) * 4 + i] = other[i]
-    for target in range(8):
-        delta = (target - z) & 7
-        slot = jnp.where(delta < 2, 1 - delta, delta)
-        slot = jnp.where(delta == 4, 5, jnp.where(delta == 7, 4, slot))
-        slot = jnp.where(delta == 5, 7, slot)
-        for c in range(2):
-            i = target * 2 + c
-            shard = slots[slot, c].astype(F32)
-            so[9 * i : 9 * i + 9, :] = shard[:9]
-            out[9 * i : 9 * i + 9, :] = shard[9:18]
-            qkv[27 * i : 27 * i + 27, :] = shard[18:]
+def compact_kernel(place, shards, own_so, own_out, own_qkv, part, so, out, qkv):
+    core = place[0]
+    for i in range(16):
+        shard = shards[i].astype(F32)
+        so[9 * i : 9 * i + 9, :] = shard[:9]
+        out[9 * i : 9 * i + 9, :] = shard[9:18]
+        qkv[27 * i : 27 * i + 27, :] = shard[18:45]
     own_so[...] = so[...].astype(BF)
     own_out[...] = out[...].astype(BF)
     own_qkv[...] = qkv[...].astype(BF)
@@ -270,19 +261,12 @@
     return lax.ppermute(a, "core", [(0, 1), (1, 0)])
 
 
-OFFSETS = ((1, 0, 2, 3), (-1, 4, -2, -3))
-
-
 def class_source(x, y, z, core):
     ylo, yhi = y % 2, y // 2
     cls = (x % 2) * 2 + ylo
     return (x // 2) * 2 + yhi // 2, cls * 2 + yhi % 2, z
 
 
-def line_source(step):
-    return lambda x, y, z, core: (x, y, z + OFFSETS[core][step])
-
-
 def near_source(dx, dy):
     def source(x, y, z, core):
         sign = 1 - 2 * core
@@ -292,23 +276,18 @@
 
 
 def gather_weights(w_so, w_qkv, w_out, place, sent):
-    shard = receive(jnp.concatenate([w_so, w_out, w_qkv.T], 0), class_source)
-    shards = lax.all_gather(shard, "core", axis=0)
+    shard = jnp.concatenate([w_so, w_out, w_qkv.T, jnp.zeros((3, D), BF)], 0)
+    shard = receive(shard, class_source)
+    shards = lax.all_gather(shard, "core", axis=0, tiled=True)
     shards, sent = lax.optimization_barrier((shards, sent))
-    mine = jnp.stack([receive(shards, line_source(i)) for i in range(4)])
+    shards = lax.all_gather(shards, "z", axis=0, tiled=True).reshape(16, 48, D)
     sent = exchange(sent).reshape(ROWS, 2 * D + ATT)
-    other = swap_cores(mine)
+    shards, sent = lax.optimization_barrier((shards, sent))
     rows = lambda n: ((n, D), BF)
     own_so, own_out, own_qkv, part = call(
-        compact_kernel, [rows(144), rows(144), rows(432), rows(384)], place, mine, other, scalars=1,
-        scratch=[
-            pltpu.VMEM((8, 2, 45, D), BF),
-            pltpu.VMEM((144, D), F32),
-            pltpu.VMEM((144, D), F32),
-            pltpu.VMEM((432, D), F32),
-        ],
-    )
-    part, sent = lax.optimization_barrier((part, sent))
+        compact_kernel, [rows(144), rows(144), rows(432), rows(384)], place, shards, scalars=1,
+        scratch=[pltpu.VMEM((144, D), F32), pltpu.VMEM((144, D), F32), pltpu.VMEM((432, D), F32)],
+    )
     near = [receive(part, near_source(dx, dy)) for dx, dy in ((1, 0), (0, 1), (1, 1))]
     return [own_qkv, own_so, own_out] + near + [swap_cores(a) for a in near], sent
 
@@ -317,7 +296,7 @@
     tokens, qkv, cotangent, factors = tokens[0, 0], qkv[0, 0], cotangent[0, 0], factors[0]
     core = lax.axis_index("core")
     cls = (lax.axis_index("x") % 2) * 2 + lax.axis_index("ylo")
-    place = jnp.stack([core, cls, lax.axis_index("z")]).astype(jnp.int32)
+    place = jnp.stack([core, cls]).astype(jnp.int32)
 
     (mixed_s,) = call(spatial_forward_kernel, [((ROWS, ATT), BF)], qkv)
     sent = jnp.concatenate([tokens, cotangent, mixed_s], 1).reshape(64, 2, 2 * D + ATT)

time: 211 us -> 218 us (1.033)
  between operations: 0.98 us -> 14.3 us
  starting transfers between devices: 62.3 us -> 49.4 us
  waiting for transfers between devices: 45.6 us -> 56.2 us
  local copies, waits for them, and re-layouts: 20.3 us -> 12.3 us
  blocking collectives: 53.5 us -> 57.6 us
    ppermute x8 -> x4, waiting for transfers between devices: 41.1 us -> 10.4 us  [receive(): return lax.ppermute(a, AXES, pairs)]
    all_to_all x1, waiting for transfers between devices: 0.01 us -> 23.1 us  [exchange(): return lax.all_to_all(a, SEQ, 0, 0, tiled=True)]
    all_gather x0 -> x1, waiting for transfers between devices: none -> 20.3 us  [gather_weights(): shards = lax.all_gather(shards, 'z', axis=0, tiled=True).reshape(16, 48, D)]
    ppermute x8 -> x4, starting transfers between devices: 26.5 us -> 10.8 us  [receive(): return lax.ppermute(a, AXES, pairs)]
    all_to_all x1, blocking collectives: 45.1 us -> 49 us  [exchange(): return lax.all_to_all(a, SEQ, 0, 0, tiled=True)]
    unnamed x26 -> x14, local copies, waits for them, and re-layouts: 7.63 us -> 3.74 us
    ppermute x6 -> x5, starting transfers between devices: 14.1 us -> 17.5 us  [swap_cores(): return lax.ppermute(a, 'core', [(0, 1), (1, 0)])]
    ppermute x6 -> x5, waiting for transfers between devices: 4.45 us -> 2.39 us  [swap_cores(): return lax.ppermute(a, 'core', [(0, 1), (1, 0)])]
  transfers between devices with their start and end apart: 16 -> 12, of which waited for: 8 -> 6; matrix products, arithmetic and copies ran while one was open for 6% -> 4% of each run, Pallas kernels for 4% -> 3%
where the time goes in v7:
time: 218 us; the launch traced here: 217 us
  blocking collectives  57.6 us (26%)
  waiting for transfers between devices  56.2 us (26%)
  starting transfers between devices  49.4 us (23%)
  Pallas kernels  19.3 us (9%)
  between operations  14.3 us (7%)
  local copies, waits for them, and re-layouts  12.3 us (6%)
  other arithmetic  7.61 us (3%)
    all_to_all x1, blocking collectives, exchange(): return lax.all_to_all(a, SEQ, 0, 0, tiled=True)  49 us
    all_to_all x1, waiting for transfers between devices, exchange(): return lax.all_to_all(a, SEQ, 0, 0, tiled=True)  23.1 us
    all_gather x1, waiting for transfers between devices, gather_weights(): shards = lax.all_gather(shards, 'z', axis=0, tiled=True).reshape(16, 48, D)  20.3 us
    pallas_call x5, Pallas kernels, call(): pl.pallas_call(kernel, out_shape=[jax.ShapeDtypeStruct(s, d) for s, d in...  19.3 us
    ppermute x5, starting transfers between devices, swap_cores(): return lax.ppermute(a, 'core', [(0, 1), (1, 0)])  17.5 us
    all_to_all x1, starting transfers between devices, exchange(): return lax.all_to_all(a, SEQ, 0, 0, tiled=True)  16.5 us
    ppermute x4, starting transfers between devices, receive(): return lax.ppermute(a, AXES, pairs)  10.8 us
    ppermute x4, waiting for transfers between devices, receive(): return lax.ppermute(a, AXES, pairs)  10.4 us
  transfers between devices with their start and end apart: 12, of which 6 were waited for; matrix products, arithmetic and copies ran while one was open for 4% of the time, Pallas kernels for 3%

profile of v7, /device:TPU:1, one launch (start us, length us, event | category | flops | bytes accessed | tf_op | source)
XLA Modules:
  0.0 216.6 jit_solution(14989637852125921635)
XLA Ops:
  9.0 1.1 concatenate.41
  10.0 1.1 concatenate.42
  11.3 1.5 shard_map.102
  13.0 1.6 pad_maximum_fusion.1
  14.5 8.6 %all_gather.6 = bf16[96,1152]{1,0:T(8,128)(2,1)} all-gather(bf16[48,1152]{1,0:T(8,128)(2,1)S(1)} %collective-permute-done), channel_id=1, replica_groups=mesh['x'=4,'ylo'=2,'yhi'=4,'z'=8,'core'=2] {'core'}, dimensions={0}, use_global_device_ids=true | all-gather | bytes 331776 | tf_op jit(solution)/shard_map/all_gather | solution.py:281
  23.2 16.5 %all-to-all-start = ((bf16[64,2,2880]{2,1,0:T(2,128)(2,1)}), bf16[64,2,2880]{2,1,0:T(2,128)(2,1)S(1)}, u32[]{:S(2)}, u32[]{:S(2)}) async-start(bf16[64,2,2880]{2,1,0:T(2,128)(2,1)} %pad_maximum_fusion.1), calls=%async_computation | async-start | bytes 1507328 | tf_op jit(solution)/shard_map/all_to_all | solution.py:239
  39.7 23.1 %all-to-all-done = bf16[64,2,2880]{2,1,0:T(2,128)(2,1)S(1)} async-done(((bf16[64,2,2880]{2,1,0:T(2,128)(2,1)}), bf16[64,2,2880]{2,1,0:T(2,128)(2,1)S(1)}, u32[]{:S(2)}, u32[]{:S(2)}) %all-to-all-start) | async-done | bytes 737312 | tf_op jit(solution)/shard_map/all_to_all | solution.py:239
  63.4 20.3 %all-gather.2.cloned.1.call-done = bf16[768,1152]{1,0:T(8,128)(2,1)} async-done(((bf16[96,1152]{1,0:T(8,128)(2,1)}), bf16[768,1152]{1,0:T(8,128)(2,1)}) %all-gather.2.cloned.1.call-update) | async-done | bytes 1769488 | tf_op jit(solution)/shard_map/all_gather | solution.py:283
  83.7 1.5 copy-done
  85.2 1.1 shard_map.103
  86.3 1.9 collective-permute-start.3
  88.2 4.1 %collective-permute-start.2 = (bf16[384,1152]{1,0:T(8,128)(2,1)S(1)}, bf16[384,1152]{1,0:T(8,128)(2,1)S(1)}, u32[]{:S(2)}, u32[]{:S(2)}) collective-permute-start(bf16[384,1152]{1,0:T(8,128)(2,1)S(1)} %get-tuple-element.32), channel_id=1, source_target_pairs={{64,0},{113,1},{66,2},{115,3},{68,4},{117,5},{70,6},{119,7},{72,8}... | collective-permute-start | bytes 2654216 | tf_op jit(solution)/shard_map/ppermute | solution.py:257
  92.4 4.0 %collective-permute-start.1 = (bf16[384,1152]{1,0:T(8,128)(2,1)S(1)}, bf16[384,1152]{1,0:T(8,128)(2,1)S(1)}, u32[]{:S(2)}, u32[]{:S(2)}) collective-permute-start(bf16[384,1152]{1,0:T(8,128)(2,1)S(1)} %get-tuple-element.32), channel_id=1, source_target_pairs={{128,0},{385,1},{130,2},{387,3},{132,4},{389,5},{134,6},{391,7},{1... | collective-permute-start | bytes 2654216 | tf_op jit(solution)/shard_map/ppermute | solution.py:257
  96.4 7.1 %collective-permute-done.3.d = bf16[384,1152]{1,0:T(8,128)(2,1)S(1)} collective-permute-done((bf16[384,1152]{1,0:T(8,128)(2,1)S(1)}, bf16[384,1152]{1,0:T(8,128)(2,1)S(1)}, u32[]{:S(2)}, u32[]{:S(2)}) %collective-permute-start.3) | collective-permute-done | bytes 884768 | tf_op jit(solution)/shard_map/ppermute | solution.py:257
  103.5 4.1 %collective-permute-start.6 = (bf16[384,1152]{1,0:T(8,128)(2,1)S(1)}, bf16[384,1152]{1,0:T(8,128)(2,1)S(1)}, u32[]{:S(2)}, u32[]{:S(2)}) collective-permute-start(bf16[384,1152]{1,0:T(8,128)(2,1)S(1)} %collective-permute-done.3.d), channel_id=1, source_target_pairs={{0,1},{1,0},{2,3},{3,2},{4,5},{5,4},{6,7},{7,6},{8,9},{9,8},{10,11... | collective-permute-start | bytes 2654216 | tf_op jit(solution)/shard_map/ppermute | solution.py:261
  107.6 3.3 %collective-permute-done.2.c = bf16[384,1152]{1,0:T(8,128)(2,1)S(1)} collective-permute-done((bf16[384,1152]{1,0:T(8,128)(2,1)S(1)}, bf16[384,1152]{1,0:T(8,128)(2,1)S(1)}, u32[]{:S(2)}, u32[]{:S(2)}) %collective-permute-start.2) | collective-permute-done | bytes 884768 | tf_op jit(solution)/shard_map/ppermute | solution.py:257
  110.9 5.8 %collective-permute-start.5 = (bf16[384,1152]{1,0:T(8,128)(2,1)S(1)}, bf16[384,1152]{1,0:T(8,128)(2,1)S(1)}, u32[]{:S(2)}, u32[]{:S(2)}) collective-permute-start(bf16[384,1152]{1,0:T(8,128)(2,1)S(1)} %collective-permute-done.2.c), channel_id=1, source_target_pairs={{0,1},{1,0},{2,3},{3,2},{4,5},{5,4},{6,7},{7,6},{8,9},{9,8},{10,11... | collective-permute-start | bytes 2654216 | tf_op jit(solution)/shard_map/ppermute | solution.py:261
  116.7 1.9 collective-permute-start.4
  118.7 2.3 %collective-permute-done.4.other_b = bf16[384,1152]{1,0:T(8,128)(2,1)S(1)} collective-permute-done((bf16[384,1152]{1,0:T(8,128)(2,1)S(1)}, bf16[384,1152]{1,0:T(8,128)(2,1)S(1)}, u32[]{:S(2)}, u32[]{:S(2)}) %collective-permute-start.4) | collective-permute-done | bytes 884768 | tf_op jit(solution)/shard_map/ppermute | solution.py:261
  121.0 11.1 %shard_map.104 = (f32[576,576]{1,0:T(8,128)S(1)}, bf16[576,576]{1,0:T(8,128)(2,1)}, bf16[576,1152]{1,0:T(8,128)(2,1)S(1)}, bf16[576,1152]{1,0:T(8,128)(2,1)S(1)}...) custom-call(s32[2]{0:T(128)S(1)} %pad_add_fusion.place, ...), custom_call_target="tpu_custom_call" | custom-call | flops 4000000000 | bytes 10000000 | tf_op jit(solution)/shard_map/pallas_call | solution.py:227
  132.1 2.3 %collective-permute-start.7 = (bf16[576,576]{1,0:T(8,128)(2,1)}, bf16[576,576]{1,0:T(8,128)(2,1)}, u32[]{:S(2)}, u32[]{:S(2)}) collective-permute-start(bf16[576,576]{1,0:T(8,128)(2,1)} %get-tuple-element.45), channel_id=1, source_target_pairs={{0,1},{1,0},{2,3},{3,2},{4,5},{5,4},{6,7},{7,6},{8,9},{9,8},{10,11... | collective-permute-start | bytes 1990664 | tf_op jit(solution)/shard_map/ppermute | solution.py:261
  134.5 3.2 %shard_map.105 = bf16[128,2304]{1,0:T(8,128)(2,1)S(1)} custom-call(bf16[128,2880]{1,0:T(8,128)(2,1)S(1)} %reshape.99.sent, f32[4,1152]{1,0:T(4,128)S(1)} %bitcast.21, bf16[576,1152]{1,0:T(8,128)(2,1)S(1)} %get-tuple-element.33.w_so, bf16[576,1152]{1,0:T(8,128)(2,1)S(1)} %get-tuple-element.34.w_out, bf16[1728,1152]{1,0:T(8,128)(2,1)S(1)} %get-tuple-element.35.w_qkv, ...), custom_call_target="tpu_custom_call" | custom-call | flops 4000000000 | bytes 10000000 | tf_op jit(solution)/shard_map/pallas_call | solution.py:227
  137.6 1.1 copy-done.2
  138.7 1.0 reshape.100
  139.8 1.3 add_convert_fusion
  141.1 1.3 reshape.101
  142.4 1.1 pad_maximum_fusion
  143.5 49.0 %all_to_all.15 = bf16[64,2,4896]{2,1,0:T(2,128)(2,1)S(1)} all-to-all(bf16[64,2,4896]{2,1,0:T(2,128)(2,1)S(1)} %pad_maximum_fusion), channel_id=1, replica_groups=mesh['x'=4,'ylo'=2,'yhi'=4,'z'=8,'core'=2] {'yhi','z','core'}, dimensions={0} | all-to-all | bytes 2506752 | tf_op jit(solution)/shard_map/all_to_all | solution.py:239
  194.5 4.6 %all-to-all-start.2 = ((f32[8,2,5184]{2,1,0:T(2,128)}), f32[8,2,5184]{2,1,0:T(2,128)}, u32[]{:S(2)}, u32[]{:S(2)}) async-start(f32[8,2,5184]{2,1,0:T(2,128)} %broadcast_in_dim.17), calls=%async_computation.2 | async-start | bytes 671744 | tf_op jit(solution)/shard_map/all_to_all | solution.py:328
  199.4 3.3 %collective-permute-start.8 = (f32[2,1152]{1,0:T(2,128)S(1)}, f32[2,1152]{1,0:T(2,128)S(1)}, u32[]{:S(2)}, u32[]{:S(2)}) collective-permute-start(f32[2,1152]{1,0:T(2,128)S(1)} %convert_reduce_fusion.1), channel_id=1, source_target_pairs={{0,1},{1,0},{2,3},{3,2},{4,5},{5,4},{6,7},{7,6},{8,9},{9,8},{10,11... | collective-permute-start | bytes 27656 | tf_op jit(solution)/shard_map/ppermute | solution.py:261
  203.1 2.4 %shard_map.106 = bf16[128,1728]{1,0:T(8,128)(2,1)S(1)} custom-call(bf16[128,1728]{1,0:T(8,128)(2,1)S(1)} %bitcast.17, bf16[128,1152]{1,0:T(8,128)(2,1)S(1)} %reshape.102.hidden_grad, f32[4,1152]{1,0:T(4,128)S(1)} %bitcast.22, bf16[576,1152]{1,0:T(8,128)(2,1)S(1)} %copy-done.3), custom_call_target="tpu_custom_call" | custom-call | flops 1000000000 | bytes 10000000 | tf_op jit(solution)/shard_map/pallas_call | solution.py:227
  207.8 1.1 reduce_sum.29
  (40 shorter events, 8.7 us)
Async XLA Ops:
  7.2 4.0 %copy-start.5 = (bf16[1,1,128,1728]{2,3,1,0:T(8,128)(2,1)S(1)}, bf16[1,1,128,1728]{2,3,1,0:T(8,128)(2,1)}, u32[]{:S(2)}) copy-start(bf16[1,1,128,1728]{2,3,1,0:T(8,128)(2,1)} %param.8) | copy-start | bytes 1327108
  7.2 76.5 %all-gather.2.cloned.1.call-start = ((), (), s32[]{:S(2)}) async-start(), calls=%async_computation.3 | async-start | bytes 1990656 | tf_op jit(solution)/shard_map/all_gather | solution.py:283
  8.3 6.3 %collective-permute-start = (bf16[48,1152]{1,0:T(8,128)(2,1)S(1)}, bf16[48,1152]{1,0:T(8,128)(2,1)S(1)}, u32[]{:S(2)}, u32[]{:S(2)}) collective-permute-start(bf16[48,1152]{1,0:T(8,128)(2,1)S(1)} %maximum_maximum_fusion), channel_id=1, source_target_pairs={{0,0},{1,1},{2,2},{3,3},{4,4},{5,5},{6,6},{7,7},{8,8},{9,9},{10,10... | collective-permute-start | bytes 331784 | tf_op jit(solution)/shard_map/ppermute | solution.py:257
  23.2 39.7 %all-to-all-start = ((bf16[64,2,2880]{2,1,0:T(2,128)(2,1)}), bf16[64,2,2880]{2,1,0:T(2,128)(2,1)S(1)}, u32[]{:S(2)}, u32[]{:S(2)}) async-start(bf16[64,2,2880]{2,1,0:T(2,128)(2,1)} %pad_maximum_fusion.1), calls=%async_computation | async-start | bytes 1507328 | tf_op jit(solution)/shard_map/all_to_all | solution.py:239
  83.7 1.5 copy-start
  85.2 35.9 %copy-start.1 = (f32[1,4,1152]{2,1,0:T(4,128)S(1)}, f32[1,4,1152]{2,1,0:T(4,128)}, u32[]{:S(2)}) copy-start(f32[1,4,1152]{2,1,0:T(4,128)} %param.12) | copy-start | bytes 55300
  86.3 17.2 %collective-permute-start.3 = (bf16[384,1152]{1,0:T(8,128)(2,1)S(1)}, bf16[384,1152]{1,0:T(8,128)(2,1)S(1)}, u32[]{:S(2)}, u32[]{:S(2)}) collective-permute-start(bf16[384,1152]{1,0:T(8,128)(2,1)S(1)} %get-tuple-element.32), channel_id=1, source_target_pairs={{192,0},{497,1},{194,2},{499,3},{196,4},{501,5},{198,6},{503,7},{2... | collective-permute-start | bytes 2654216 | tf_op jit(solution)/shard_map/ppermute | solution.py:257
  88.2 22.6 %collective-permute-start.2 = (bf16[384,1152]{1,0:T(8,128)(2,1)S(1)}, bf16[384,1152]{1,0:T(8,128)(2,1)S(1)}, u32[]{:S(2)}, u32[]{:S(2)}) collective-permute-start(bf16[384,1152]{1,0:T(8,128)(2,1)S(1)} %get-tuple-element.32), channel_id=1, source_target_pairs={{64,0},{113,1},{66,2},{115,3},{68,4},{117,5},{70,6},{119,7},{72,8}... | collective-permute-start | bytes 2654216 | tf_op jit(solution)/shard_map/ppermute | solution.py:257
  92.4 24.3 %collective-permute-start.1 = (bf16[384,1152]{1,0:T(8,128)(2,1)S(1)}, bf16[384,1152]{1,0:T(8,128)(2,1)S(1)}, u32[]{:S(2)}, u32[]{:S(2)}) collective-permute-start(bf16[384,1152]{1,0:T(8,128)(2,1)S(1)} %get-tuple-element.32), channel_id=1, source_target_pairs={{128,0},{385,1},{130,2},{387,3},{132,4},{389,5},{134,6},{391,7},{1... | collective-permute-start | bytes 2654216 | tf_op jit(solution)/shard_map/ppermute | solution.py:257
  103.5 15.1 %collective-permute-start.6 = (bf16[384,1152]{1,0:T(8,128)(2,1)S(1)}, bf16[384,1152]{1,0:T(8,128)(2,1)S(1)}, u32[]{:S(2)}, u32[]{:S(2)}) collective-permute-start(bf16[384,1152]{1,0:T(8,128)(2,1)S(1)} %collective-permute-done.3.d), channel_id=1, source_target_pairs={{0,1},{1,0},{2,3},{3,2},{4,5},{5,4},{6,7},{7,6},{8,9},{9,8},{10,11... | collective-permute-start | bytes 2654216 | tf_op jit(solution)/shard_map/ppermute | solution.py:261
  110.9 7.9 %collective-permute-start.5 = (bf16[384,1152]{1,0:T(8,128)(2,1)S(1)}, bf16[384,1152]{1,0:T(8,128)(2,1)S(1)}, u32[]{:S(2)}, u32[]{:S(2)}) collective-permute-start(bf16[384,1152]{1,0:T(8,128)(2,1)S(1)} %collective-permute-done.2.c), channel_id=1, source_target_pairs={{0,1},{1,0},{2,3},{3,2},{4,5},{5,4},{6,7},{7,6},{8,9},{9,8},{10,11... | collective-permute-start | bytes 2654216 | tf_op jit(solution)/shard_map/ppermute | solution.py:261
  116.7 4.3 %collective-permute-start.4 = (bf16[384,1152]{1,0:T(8,128)(2,1)S(1)}, bf16[384,1152]{1,0:T(8,128)(2,1)S(1)}, u32[]{:S(2)}, u32[]{:S(2)}) collective-permute-start(bf16[384,1152]{1,0:T(8,128)(2,1)S(1)} %collective-permute-done.1.b), channel_id=1, source_target_pairs={{0,1},{1,0},{2,3},{3,2},{4,5},{5,4},{6,7},{7,6},{8,9},{9,8},{10,11... | collective-permute-start | bytes 2654216 | tf_op jit(solution)/shard_map/ppermute | solution.py:261
  132.1 7.6 %collective-permute-start.7 = (bf16[576,576]{1,0:T(8,128)(2,1)}, bf16[576,576]{1,0:T(8,128)(2,1)}, u32[]{:S(2)}, u32[]{:S(2)}) collective-permute-start(bf16[576,576]{1,0:T(8,128)(2,1)} %get-tuple-element.45), channel_id=1, source_target_pairs={{0,1},{1,0},{2,3},{3,2},{4,5},{5,4},{6,7},{7,6},{8,9},{9,8},{10,11... | collective-permute-start | bytes 1990664 | tf_op jit(solution)/shard_map/ppermute | solution.py:261
  137.6 1.1 copy-start.2
  139.8 2.6 %copy-start.4 = (bf16[64,2,2304]{2,1,0:T(2,128)(2,1)S(1)}, bf16[64,2,2304]{2,1,0:T(2,128)(2,1)}, u32[]{:S(2)}) copy-start(bf16[64,2,2304]{2,1,0:T(2,128)(2,1)} %reshape.100) | copy-start | bytes 1769476
  193.5 9.5 %copy-start.3 = (bf16[576,1152]{1,0:T(8,128)(2,1)S(1)}, bf16[576,1152]{1,0:T(8,128)(2,1)}, u32[]{:S(2)}) copy-start(bf16[576,1152]{1,0:T(8,128)(2,1)} %copy-done.2) | copy-start | bytes 3981316
  194.5 13.4 %all-to-all-start.2 = ((f32[8,2,5184]{2,1,0:T(2,128)}), f32[8,2,5184]{2,1,0:T(2,128)}, u32[]{:S(2)}, u32[]{:S(2)}) async-start(f32[8,2,5184]{2,1,0:T(2,128)} %broadcast_in_dim.17), calls=%async_computation.2 | async-start | bytes 671744 | tf_op jit(solution)/shard_map/all_to_all | solution.py:328
  199.4 7.8 %collective-permute-start.8 = (f32[2,1152]{1,0:T(2,128)S(1)}, f32[2,1152]{1,0:T(2,128)S(1)}, u32[]{:S(2)}, u32[]{:S(2)}) collective-permute-start(f32[2,1152]{1,0:T(2,128)S(1)} %convert_reduce_fusion.1), channel_id=1, source_target_pairs={{0,1},{1,0},{2,3},{3,2},{4,5},{5,4},{6,7},{7,6},{8,9},{9,8},{10,11... | collective-permute-start | bytes 27656 | tf_op jit(solution)/shard_map/ppermute | solution.py:261
Sparse Core Ops, SparseCore 0:
  23.3 60.3 all-gather.1

commit v8 on v7

--- a/solution.py
+++ b/solution.py
@@ -95,10 +95,12 @@
     out[:, 2 * ATT :] = d_v
 
 
-def compact_kernel(place, shards, own_so, own_out, own_qkv, part, so, out, qkv):
+def compact_kernel(place, mine, other, own_so, own_out, own_qkv, part, both, so, out, qkv):
     core = place[0]
+    both[core] = mine[...]
+    both[1 - core] = other[...]
     for i in range(16):
-        shard = shards[i].astype(F32)
+        shard = both[i % 2, 48 * (i // 2) : 48 * (i // 2) + 48, :].astype(F32)
         so[9 * i : 9 * i + 9, :] = shard[:9]
         out[9 * i : 9 * i + 9, :] = shard[9:18]
         qkv[27 * i : 27 * i + 27, :] = shard[18:45]
@@ -128,24 +130,35 @@
     return copies
 
 
-def assemble(place, own, near, swapped, targets, sems):
+COPIES = 7
+
+
+def start_copies(place, own, near, swapped, targets, sems):
     for me in range(2):
 
         @pl.when(place[0] == me)
         def _():
             cls = place[1]
-            pairs = []
+            pairs = [[] for _ in SECTIONS]
             for section, ref in enumerate(own):
                 to = pl.multiple_of(cls * BLOCK[section], 16)
-                pairs.append((ref, targets[section].at[pl.ds(to, BLOCK[section])]))
+                pairs[section].append((ref, targets[section].at[pl.ds(to, BLOCK[section])]))
             for flip, ref, other in zip((2, 1, 3), near, swapped):
-                pairs += part_copies(ref, me, cls ^ flip, targets)
-                pairs += part_copies(other, 1 - me, cls ^ flip, targets)
-            copies = [pltpu.make_async_copy(a, z, sems.at[i]) for i, (a, z) in enumerate(pairs)]
-            for copy in copies:
-                copy.start()
-            for copy in copies:
-                copy.wait()
+                for half in range(2):
+                    source = ref if half == me else other
+                    for section, pair in enumerate(part_copies(source, half, cls ^ flip, targets)):
+                        pairs[section].append(pair)
+            for section in (1, 0, 2):
+                for i, (a, z) in enumerate(pairs[section]):
+                    pltpu.make_async_copy(a, z, sems.at[section * COPIES + i]).start()
+
+
+def wait_copies(section, own, targets, sems):
+    first, last = SECTIONS[section][1:]
+    sizes = [BLOCK[section]] + [last - first, last - first - 16] * 3
+    for i, n in enumerate(sizes):
+        a, z = own[section].at[pl.ds(0, n)], targets[section].at[pl.ds(0, n)]
+        pltpu.make_async_copy(a, z, sems.at[section * COPIES + i]).wait()
 
 
 def temporal_forward_kernel(
@@ -153,12 +166,11 @@
     out_keep, out_send, w_so, w_out, w_qkv, q_out, k_out, v_out, probs_out, mixed_out,
     unit_out, inverse_out, project_out, sems,
 ):
-    assemble(
-        place, (own_qkv, own_so, own_out), (b, c, d), (other_b, other_c, other_d),
-        (w_qkv, w_so, w_out), sems,
-    )
+    own, targets = (own_qkv, own_so, own_out), (w_qkv, w_so, w_out)
+    start_copies(place, own, (b, c, d), (other_b, other_c, other_d), targets, sems)
     tokens, cotangent, mixed_s = sent[:, :D], sent[:, D : 2 * D], sent[:, 2 * D :]
     gate_s, shift, scale, gate_t = (factors[i : i + 1, :] for i in range(4))
+    wait_copies(1, own, targets, sems)
     project = nn(mixed_s, w_so[...])
     project_out[...] = project
     hidden = (tokens.astype(F32) + gate_s * project).astype(BF).astype(F32)
@@ -168,6 +180,7 @@
     unit = centered * inverse
     unit_out[...] = unit
     normed = (unit * (1.0 + scale) + shift).astype(BF)
+    wait_copies(0, own, targets, sems)
     q, k, v = (nt(normed, w_qkv[i * ATT : (i + 1) * ATT, :]).astype(BF) for i in range(3))
     q_out[...], k_out[...], v_out[...] = q, k, v
 
@@ -183,6 +196,7 @@
     first = place[0] == 0
     out_keep[...] = tn(mixed, jnp.where(first, left, right))
     out_send[...] = tn(mixed, jnp.where(first, right, left)).astype(BF)
+    wait_copies(2, own, targets, sems)
 
 
 def temporal_backward_kernel(
@@ -214,9 +228,17 @@
         jnp.sum(d_normed * unit, 0, keepdims=True),
         jnp.sum(cot * project_t, 0, keepdims=True),
     )
-    tile = jnp.concatenate(factor_grads * 4, 0).astype(BF)
-    for i in range(8):
-        packed[16 * i : 16 * i + 16, D:] = tile
+    zeros = jnp.zeros((16, 64), BF)
+    for parity in range(2):
+        rows = [
+            factor_grads[2 * parity + core][:, part * ATT : part * ATT + ATT]
+            for core in range(2)
+            for part in range(2)
+        ]
+        tile = jnp.concatenate([jnp.concatenate(rows * 4, 0).astype(BF), zeros], 1)
+        for yhi in (parity, parity + 2):
+            packed[32 * yhi : 32 * yhi + 16, D:] = tile
+            packed[32 * yhi + 16 : 32 * yhi + 32, D:] = tile
 
 
 def call(kernel, outs, *args, scalars=0, remote=0, scratch=(), flops=10**9):
@@ -277,17 +299,21 @@
 
 def gather_weights(w_so, w_qkv, w_out, place, sent):
     shard = jnp.concatenate([w_so, w_out, w_qkv.T, jnp.zeros((3, D), BF)], 0)
-    shard = receive(shard, class_source)
-    shards = lax.all_gather(shard, "core", axis=0, tiled=True)
-    shards, sent = lax.optimization_barrier((shards, sent))
-    shards = lax.all_gather(shards, "z", axis=0, tiled=True).reshape(16, 48, D)
+    shard, sent = lax.optimization_barrier((receive(shard, class_source), sent))
     sent = exchange(sent).reshape(ROWS, 2 * D + ATT)
-    shards, sent = lax.optimization_barrier((shards, sent))
+    mine = lax.all_gather(shard, "z", axis=0, tiled=True)
+    other = swap_cores(mine)
     rows = lambda n: ((n, D), BF)
     own_so, own_out, own_qkv, part = call(
-        compact_kernel, [rows(144), rows(144), rows(432), rows(384)], place, shards, scalars=1,
-        scratch=[pltpu.VMEM((144, D), F32), pltpu.VMEM((144, D), F32), pltpu.VMEM((432, D), F32)],
-    )
+        compact_kernel, [rows(144), rows(144), rows(432), rows(384)], place, mine, other, scalars=1,
+        scratch=[
+            pltpu.VMEM((2, 384, D), BF),
+            pltpu.VMEM((144, D), F32),
+            pltpu.VMEM((144, D), F32),
+            pltpu.VMEM((432, D), F32),
+        ],
+    )
+    part, sent = lax.optimization_barrier((part, sent))
     near = [receive(part, near_source(dx, dy)) for dx, dy in ((1, 0), (0, 1), (1, 1))]
     return [own_qkv, own_so, own_out] + near + [swap_cores(a) for a in near], sent
 
@@ -316,26 +342,29 @@
     )
     w_so = saved[0]
     out_other = swap_cores(out_send)
-    (packed,) = call(temporal_backward_kernel, [rows(2 * D)], sent, factors, *saved, flops=4 * 10**9)
+    (packed,) = call(temporal_backward_kernel, [rows(D + 640)], sent, factors, *saved, flops=4 * 10**9)
 
     half = 9 * ATT // 2
     out_part = (out_keep + out_other.astype(F32)).astype(BF).reshape(64, 2, half)
-    back = exchange(jnp.concatenate([packed.reshape(64, 2, 2 * D), out_part], 2))
-
-    out_part = back[:, :, 2 * D :].astype(F32).reshape(32, 2, 2, half)
-    out_part = jnp.sum(out_part, 0).reshape(1, 2, 9 * ATT)
+    back = exchange(jnp.concatenate([packed.reshape(64, 2, D + 640), out_part], 2))
+
+    out_part = back[:, :, D + 640 :].astype(F32).reshape(32, 2, 2, half)
+    out_part = jnp.sum(out_part, 0).astype(BF).reshape(1, 2, 9 * ATT)
     out_part = jnp.broadcast_to(out_part, (8, 2, 9 * ATT))
-    out_part = jnp.sum(lax.all_to_all(out_part, DP, 0, 0, tiled=True), 0)
+    out_part = jnp.sum(lax.all_to_all(out_part, DP, 0, 0, tiled=True).astype(F32), 0)
     out_grad = out_part.reshape(2, 9, ATT).transpose(1, 0, 2).reshape(9, D)
 
     token_grad = back[:, :, :D].reshape(ROWS, D)
+    mine = jnp.sum(back[:, :, D : D + ATT].astype(F32), 0).reshape(1, D)
+    other = swap_cores(mine)
+    rows = jnp.where(core == 0, jnp.concatenate([mine, other]), jnp.concatenate([other, mine]))
+    rows, token_grad = lax.optimization_barrier((rows, token_grad))
+    other = lax.ppermute(rows, "yhi", [(0, 1), (1, 0), (2, 3), (3, 2)])
     (qkv_grad,) = call(
         spatial_backward_kernel, [((ROWS, 3 * ATT), BF)], qkv, token_grad, factors, w_so
     )
-
-    mine = jnp.sum(back[:, :, D : 2 * D].astype(F32), 0)
-    other = swap_cores(mine)
-    factor_grad = jnp.where(core == 0, jnp.concatenate([mine, other]), jnp.concatenate([other, mine]))
+    low = lax.axis_index("yhi") % 2 == 0
+    factor_grad = jnp.where(low, jnp.concatenate([rows, other]), jnp.concatenate([other, rows]))
     return token_grad[None, None], qkv_grad[None, None], factor_grad[None], out_grad
 
 

time: 218 us -> 209 us (0.959)
  waiting for transfers between devices: 56.2 us -> 16.3 us
  blocking collectives: 57.6 us -> 86.9 us
  between operations: 14.3 us -> 0.99 us
  starting transfers between devices: 49.4 us -> 60.3 us
  local copies, waits for them, and re-layouts: 12.3 us -> 17 us
    all_gather x1, blocking collectives: 8.61 us -> 39.3 us  [gather_weights(): mine = lax.all_gather(shard, 'z', axis=0, tiled=True)]
    all_to_all x1, waiting for transfers between devices: 23.1 us -> 0.01 us  [exchange(): return lax.all_to_all(a, SEQ, 0, 0, tiled=True)]
    all_gather x1 -> x0, waiting for transfers between devices: 20.3 us -> none  [gather_weights(): shards = lax.all_gather(shards, 'z', axis=0, tiled=True).reshape(16, 48, D)]
    all_to_all x1, starting transfers between devices: 16.5 us -> 23.1 us  [exchange(): return lax.all_to_all(a, SEQ, 0, 0, tiled=True)]
    ppermute x0 -> x1, starting transfers between devices: none -> 3.71 us  [body(): other = lax.ppermute(rows, 'yhi', [(0, 1), (1, 0), (2, 3), (3, 2)])]
    ppermute x5 -> x6, starting transfers between devices: 17.5 us -> 19.5 us  [swap_cores(): return lax.ppermute(a, 'core', [(0, 1), (1, 0)])]
    unnamed x14 -> x22, local copies, waits for them, and re-layouts: 3.74 us -> 5.41 us
  transfers between devices with their start and end apart: 12 -> 13, of which waited for: 6 -> 5; matrix products, arithmetic and copies ran while one was open for 4% -> 5% of each run, Pallas kernels for 3% -> 4%
where the time goes in v8:
time: 209 us
  blocking collectives  86.9 us (42%)
  starting transfers between devices  60.3 us (29%)
  Pallas kernels  19.7 us (9%)
  local copies, waits for them, and re-layouts  17 us (8%)
  waiting for transfers between devices  16.3 us (8%)
  other arithmetic  7.39 us (4%)
    all_to_all x1, blocking collectives, exchange(): return lax.all_to_all(a, SEQ, 0, 0, tiled=True)  47.6 us
    all_gather x1, blocking collectives, gather_weights(): mine = lax.all_gather(shard, 'z', axis=0, tiled=True)  39.3 us
    all_to_all x1, starting transfers between devices, exchange(): return lax.all_to_all(a, SEQ, 0, 0, tiled=True)  23.1 us
    pallas_call x5, Pallas kernels, call(): pl.pallas_call(kernel, out_shape=[jax.ShapeDtypeStruct(s, d) for s, d in...  19.7 us
    ppermute x6, starting transfers between devices, swap_cores(): return lax.ppermute(a, 'core', [(0, 1), (1, 0)])  19.5 us
    ppermute x4, waiting for transfers between devices, receive(): return lax.ppermute(a, AXES, pairs)  11.9 us
    ppermute x4, starting transfers between devices, receive(): return lax.ppermute(a, AXES, pairs)  9.27 us
    unnamed x22, local copies, waits for them, and re-layouts  5.41 us
  transfers between devices with their start and end apart: 13, of which 5 were waited for; matrix products, arithmetic and copies ran while one was open for 5% of the time, Pallas kernels for 4%

profile of v8, /device:TPU:1, one launch (start us, length us, event | category | flops | bytes accessed | tf_op | source)
XLA Modules:
  0.0 208.5 jit_solution(17490651926995192854)
XLA Ops:
  4.8 1.5 shard_map.102
  6.4 1.6 pad_maximum_fusion.1
  8.0 23.1 %all-to-all-start = ((bf16[64,2,2880]{2,1,0:T(2,128)(2,1)}), bf16[64,2,2880]{2,1,0:T(2,128)(2,1)}, u32[]{:S(2)}, u32[]{:S(2)}) async-start(bf16[64,2,2880]{2,1,0:T(2,128)(2,1)} %pad_maximum_fusion.1), calls=%async_computation | async-start | bytes 1507328 | tf_op jit(solution)/shard_map/all_to_all | solution.py:261
  31.1 39.3 %all_gather.3.mine = bf16[384,1152]{1,0:T(8,128)(2,1)S(1)} all-gather(bf16[48,1152]{1,0:T(8,128)(2,1)S(1)} %collective-permute-done), channel_id=1, replica_groups=mesh['x'=4,'ylo'=2,'yhi'=4,'z'=8,'core'=2] {'z'}, dimensions={0}, use_global_device_ids=true | all-gather | bytes 995328 | tf_op jit(solution)/shard_map/all_gather | solution.py:304
  70.4 6.5 %collective-permute-start.1 = (bf16[384,1152]{1,0:T(8,128)(2,1)S(1)}, bf16[384,1152]{1,0:T(8,128)(2,1)S(1)}, u32[]{:S(2)}, u32[]{:S(2)}) collective-permute-start(bf16[384,1152]{1,0:T(8,128)(2,1)S(1)} %all_gather.3.mine), channel_id=1, source_target_pairs={{0,1},{1,0},{2,3},{3,2},{4,5},{5,4},{6,7},{7,6},{8,9},{9,8},{10,11... | collective-permute-start | bytes 2654216 | tf_op jit(solution)/shard_map/ppermute | solution.py:283
  77.0 1.9 collective-permute-done.1.other
  79.0 1.3 shard_map.103
  82.2 2.3 %reshape.103.sent = bf16[128,2880]{1,0:T(8,128)(2,1)S(1)} reshape(bf16[64,2,2880]{2,1,0:T(2,128)(2,1)} %all-to-all-done) | data formatting | bytes 1474560 | tf_op jit(solution)/shard_map/reshape | solution.py:303
  84.5 1.9 collective-permute-start.4
  86.4 2.4 %collective-permute-start.3 = (bf16[384,1152]{1,0:T(8,128)(2,1)S(1)}, bf16[384,1152]{1,0:T(8,128)(2,1)S(1)}, u32[]{:S(2)}, u32[]{:S(2)}) collective-permute-start(bf16[384,1152]{1,0:T(8,128)(2,1)S(1)} %copy-done.2), channel_id=1, source_target_pairs={{64,0},{113,1},{66,2},{115,3},{68,4},{117,5},{70,6},{119,7},{72,8}... | collective-permute-start | bytes 2654216 | tf_op jit(solution)/shard_map/ppermute | solution.py:279
  88.8 4.3 %collective-permute-start.2 = (bf16[384,1152]{1,0:T(8,128)(2,1)S(1)}, bf16[384,1152]{1,0:T(8,128)(2,1)S(1)}, u32[]{:S(2)}, u32[]{:S(2)}) collective-permute-start(bf16[384,1152]{1,0:T(8,128)(2,1)S(1)} %copy-done.2), channel_id=1, source_target_pairs={{128,0},{385,1},{130,2},{387,3},{132,4},{389,5},{134,6},{391,7},{1... | collective-permute-start | bytes 2654216 | tf_op jit(solution)/shard_map/ppermute | solution.py:279
  93.1 8.6 %collective-permute-done.4.d = bf16[384,1152]{1,0:T(8,128)(2,1)S(1)} collective-permute-done((bf16[384,1152]{1,0:T(8,128)(2,1)S(1)}, bf16[384,1152]{1,0:T(8,128)(2,1)S(1)}, u32[]{:S(2)}, u32[]{:S(2)}) %collective-permute-start.4) | collective-permute-done | bytes 884768 | tf_op jit(solution)/shard_map/ppermute | solution.py:279
  101.7 1.9 collective-permute-start.7
  103.6 3.1 %collective-permute-done.3.c = bf16[384,1152]{1,0:T(8,128)(2,1)S(1)} collective-permute-done((bf16[384,1152]{1,0:T(8,128)(2,1)S(1)}, bf16[384,1152]{1,0:T(8,128)(2,1)S(1)}, u32[]{:S(2)}, u32[]{:S(2)}) %collective-permute-start.3) | collective-permute-done | bytes 884768 | tf_op jit(solution)/shard_map/ppermute | solution.py:279
  106.7 4.1 %collective-permute-start.6 = (bf16[384,1152]{1,0:T(8,128)(2,1)S(1)}, bf16[384,1152]{1,0:T(8,128)(2,1)S(1)}, u32[]{:S(2)}, u32[]{:S(2)}) collective-permute-start(bf16[384,1152]{1,0:T(8,128)(2,1)S(1)} %collective-permute-done.3.c), channel_id=1, source_target_pairs={{0,1},{1,0},{2,3},{3,2},{4,5},{5,4},{6,7},{7,6},{8,9},{9,8},{10,11... | collective-permute-start | bytes 2654216 | tf_op jit(solution)/shard_map/ppermute | solution.py:283
  111.1 1.9 collective-permute-start.5
  113.0 2.4 %collective-permute-done.5.other_b = bf16[384,1152]{1,0:T(8,128)(2,1)S(1)} collective-permute-done((bf16[384,1152]{1,0:T(8,128)(2,1)S(1)}, bf16[384,1152]{1,0:T(8,128)(2,1)S(1)}, u32[]{:S(2)}, u32[]{:S(2)}) %collective-permute-start.5) | collective-permute-done | bytes 884768 | tf_op jit(solution)/shard_map/ppermute | solution.py:283
  115.4 1.2 copy-done.7
  116.6 11.3 %shard_map.104 = (f32[576,576]{1,0:T(8,128)S(1)}, bf16[576,576]{1,0:T(8,128)(2,1)}, bf16[576,1152]{1,0:T(8,128)(2,1)S(1)}, bf16[576,1152]{1,0:T(8,128)(2,1)S(1)}...) custom-call(s32[2]{0:T(128)S(1)} %pad_add_fusion.place, ...), custom_call_target="tpu_custom_call" | custom-call | flops 4000000000 | bytes 10000000 | tf_op jit(solution)/shard_map/pallas_call | solution.py:249
  127.9 2.3 %collective-permute-start.8 = (bf16[576,576]{1,0:T(8,128)(2,1)}, bf16[576,576]{1,0:T(8,128)(2,1)}, u32[]{:S(2)}, u32[]{:S(2)}) collective-permute-start(bf16[576,576]{1,0:T(8,128)(2,1)} %get-tuple-element.47), channel_id=1, source_target_pairs={{0,1},{1,0},{2,3},{3,2},{4,5},{5,4},{6,7},{7,6},{8,9},{9,8},{10,11... | collective-permute-start | bytes 1990664 | tf_op jit(solution)/shard_map/ppermute | solution.py:283
  130.2 3.3 %shard_map.105 = bf16[128,1792]{1,0:T(8,128)(2,1)S(1)} custom-call(bf16[128,2880]{1,0:T(8,128)(2,1)S(1)} %reshape.103.sent, f32[4,1152]{1,0:T(4,128)S(1)} %bitcast.20, bf16[576,1152]{1,0:T(8,128)(2,1)S(1)} %get-tuple-element.35.w_so, bf16[576,1152]{1,0:T(8,128)(2,1)S(1)} %get-tuple-element.36.w_out, bf16[1728,1152]{1,0:T(8,128)(2,1)S(1)} %get-tuple-element.37.w_qkv, ...), custom_call_target="tpu_custom_call" | custom-call | flops 4000000000 | bytes 10000000 | tf_op jit(solution)/shard_map/pallas_call | solution.py:249
  133.5 1.1 copy-done.4
  135.5 1.3 add_convert_fusion
  136.8 1.3 reshape.105
  139.1 47.6 %all_to_all.15 = bf16[64,2,4384]{2,1,0:T(2,128)(2,1)} all-to-all(bf16[64,2,4384]{2,1,0:T(2,128)(2,1)S(1)} %pad_maximum_fusion), channel_id=1, replica_groups=mesh['x'=4,'ylo'=2,'yhi'=4,'z'=8,'core'=2] {'yhi','z','core'}, dimensions={0} | all-to-all | bytes 2244608 | tf_op jit(solution)/shard_map/all_to_all | solution.py:261
  186.7 1.1 convert_reduce_fusion.1
  187.9 2.7 %collective-permute-start.9 = (f32[1,1152]{1,0:T(1,128)S(1)}, f32[1,1152]{1,0:T(1,128)S(1)}, u32[]{:S(2)}, u32[]{:S(2)}) collective-permute-start(f32[1,1152]{1,0:T(1,128)S(1)} %reshape.106), channel_id=1, source_target_pairs={{0,1},{1,0},{2,3},{3,2},{4,5},{5,4},{6,7},{7,6},{8,9},{9,8},{10,11... | collective-permute-start | bytes 13832 | tf_op jit(solution)/shard_map/ppermute | solution.py:283
  190.6 1.6 slice.14
  192.9 1.2 slice.13
  195.1 4.7 %all-to-all-start.2 = ((bf16[8,2,5184]{2,1,0:T(2,128)(2,1)}), bf16[8,2,5184]{2,1,0:T(2,128)(2,1)S(1)}, u32[]{:S(2)}, u32[]{:S(2)}) async-start(bf16[8,2,5184]{2,1,0:T(2,128)(2,1)} %broadcast_in_dim.18), calls=%async_computation.2 | async-start | bytes 335872 | tf_op jit(solution)/shard_map/all_to_all | solution.py:354
  199.8 3.7 %collective-permute-start.10 = (f32[2,1152]{1,0:T(2,128)S(1)}, f32[2,1152]{1,0:T(2,128)S(1)}, u32[]{:S(2)}, u32[]{:S(2)}) collective-permute-start(f32[2,1152]{1,0:T(2,128)S(1)} %maximum_select_fusion.1), channel_id=1, source_target_pairs={{0,16},{16,0},{32,48},{48,32},{1,17},{17,1},{33,49},{49,33},{2,18}... | collective-permute-start | bytes 27656 | tf_op jit(solution)/shard_map/ppermute | solution.py:362
  203.5 2.4 %shard_map.106 = bf16[128,1728]{1,0:T(8,128)(2,1)S(1)} custom-call(bf16[128,1728]{1,0:T(8,128)(2,1)S(1)} %bitcast.16, bf16[128,1152]{1,0:T(8,128)(2,1)S(1)} %reshape.107.hidden_grad, f32[4,1152]{1,0:T(4,128)S(1)} %bitcast.21, bf16[576,1152]{1,0:T(8,128)(2,1)S(1)} %copy-done.5), custom_call_target="tpu_custom_call" | custom-call | flops 1000000000 | bytes 10000000 | tf_op jit(solution)/shard_map/pallas_call | solution.py:249
  (50 shorter events, 12.7 us)
Async XLA Ops:
  0.6 3.9 %copy-start.9 = (bf16[1,1,128,1728]{2,3,1,0:T(8,128)(2,1)S(1)}, bf16[1,1,128,1728]{2,3,1,0:T(8,128)(2,1)}, u32[]{:S(2)}) copy-start(bf16[1,1,128,1728]{2,3,1,0:T(8,128)(2,1)} %param.8) | copy-start | bytes 1327108
  1.7 6.3 %collective-permute-start = (bf16[48,1152]{1,0:T(8,128)(2,1)S(1)}, bf16[48,1152]{1,0:T(8,128)(2,1)S(1)}, u32[]{:S(2)}, u32[]{:S(2)}) collective-permute-start(bf16[48,1152]{1,0:T(8,128)(2,1)S(1)} %maximum_maximum_fusion), channel_id=1, source_target_pairs={{0,0},{1,1},{2,2},{3,3},{4,4},{5,5},{6,6},{7,7},{8,8},{9,9},{10,10... | collective-permute-start | bytes 331784 | tf_op jit(solution)/shard_map/ppermute | solution.py:279
  8.0 74.2 %all-to-all-start = ((bf16[64,2,2880]{2,1,0:T(2,128)(2,1)}), bf16[64,2,2880]{2,1,0:T(2,128)(2,1)}, u32[]{:S(2)}, u32[]{:S(2)}) async-start(bf16[64,2,2880]{2,1,0:T(2,128)(2,1)} %pad_maximum_fusion.1), calls=%async_computation | async-start | bytes 1507328 | tf_op jit(solution)/shard_map/all_to_all | solution.py:261
  70.4 8.6 %collective-permute-start.1 = (bf16[384,1152]{1,0:T(8,128)(2,1)S(1)}, bf16[384,1152]{1,0:T(8,128)(2,1)S(1)}, u32[]{:S(2)}, u32[]{:S(2)}) collective-permute-start(bf16[384,1152]{1,0:T(8,128)(2,1)S(1)} %all_gather.3.mine), channel_id=1, source_target_pairs={{0,1},{1,0},{2,3},{3,2},{4,5},{5,4},{6,7},{7,6},{8,9},{9,8},{10,11... | collective-permute-start | bytes 2654216 | tf_op jit(solution)/shard_map/ppermute | solution.py:283
  80.2 1.0 copy-start.1
  81.2 1.0 copy-start.6
  82.1 33.2 %copy-start.3 = (f32[1,4,1152]{2,1,0:T(4,128)S(1)}, f32[1,4,1152]{2,1,0:T(4,128)}, u32[]{:S(2)}) copy-start(f32[1,4,1152]{2,1,0:T(4,128)} %param.12) | copy-start | bytes 55300
  82.2 2.3 %copy-start.2 = (bf16[384,1152]{1,0:T(8,128)(2,1)S(1)}, bf16[384,1152]{1,0:T(8,128)(2,1)}, u32[]{:S(2)}) copy-start(bf16[384,1152]{1,0:T(8,128)(2,1)} %copy-done.1) | copy-start | bytes 2654212
  84.5 17.2 %collective-permute-start.4 = (bf16[384,1152]{1,0:T(8,128)(2,1)S(1)}, bf16[384,1152]{1,0:T(8,128)(2,1)S(1)}, u32[]{:S(2)}, u32[]{:S(2)}) collective-permute-start(bf16[384,1152]{1,0:T(8,128)(2,1)S(1)} %copy-done.2), channel_id=1, source_target_pairs={{192,0},{497,1},{194,2},{499,3},{196,4},{501,5},{198,6},{503,7},{2... | collective-permute-start | bytes 2654216 | tf_op jit(solution)/shard_map/ppermute | solution.py:279
  86.4 20.3 %collective-permute-start.3 = (bf16[384,1152]{1,0:T(8,128)(2,1)S(1)}, bf16[384,1152]{1,0:T(8,128)(2,1)S(1)}, u32[]{:S(2)}, u32[]{:S(2)}) collective-permute-start(bf16[384,1152]{1,0:T(8,128)(2,1)S(1)} %copy-done.2), channel_id=1, source_target_pairs={{64,0},{113,1},{66,2},{115,3},{68,4},{117,5},{70,6},{119,7},{72,8}... | collective-permute-start | bytes 2654216 | tf_op jit(solution)/shard_map/ppermute | solution.py:279
  88.8 22.3 %collective-permute-start.2 = (bf16[384,1152]{1,0:T(8,128)(2,1)S(1)}, bf16[384,1152]{1,0:T(8,128)(2,1)S(1)}, u32[]{:S(2)}, u32[]{:S(2)}) collective-permute-start(bf16[384,1152]{1,0:T(8,128)(2,1)S(1)} %copy-done.2), channel_id=1, source_target_pairs={{128,0},{385,1},{130,2},{387,3},{132,4},{389,5},{134,6},{391,7},{1... | collective-permute-start | bytes 2654216 | tf_op jit(solution)/shard_map/ppermute | solution.py:279
  101.7 11.3 %collective-permute-start.7 = (bf16[384,1152]{1,0:T(8,128)(2,1)S(1)}, bf16[384,1152]{1,0:T(8,128)(2,1)S(1)}, u32[]{:S(2)}, u32[]{:S(2)}) collective-permute-start(bf16[384,1152]{1,0:T(8,128)(2,1)S(1)} %collective-permute-done.4.d), channel_id=1, source_target_pairs={{0,1},{1,0},{2,3},{3,2},{4,5},{5,4},{6,7},{7,6},{8,9},{9,8},{10,11... | collective-permute-start | bytes 2654216 | tf_op jit(solution)/shard_map/ppermute | solution.py:283
  106.7 6.3 %collective-permute-start.6 = (bf16[384,1152]{1,0:T(8,128)(2,1)S(1)}, bf16[384,1152]{1,0:T(8,128)(2,1)S(1)}, u32[]{:S(2)}, u32[]{:S(2)}) collective-permute-start(bf16[384,1152]{1,0:T(8,128)(2,1)S(1)} %collective-permute-done.3.c), channel_id=1, source_target_pairs={{0,1},{1,0},{2,3},{3,2},{4,5},{5,4},{6,7},{7,6},{8,9},{9,8},{10,11... | collective-permute-start | bytes 2654216 | tf_op jit(solution)/shard_map/ppermute | solution.py:283
  111.1 4.3 %collective-permute-start.5 = (bf16[384,1152]{1,0:T(8,128)(2,1)S(1)}, bf16[384,1152]{1,0:T(8,128)(2,1)S(1)}, u32[]{:S(2)}, u32[]{:S(2)}) collective-permute-start(bf16[384,1152]{1,0:T(8,128)(2,1)S(1)} %collective-permute-done.2.b), channel_id=1, source_target_pairs={{0,1},{1,0},{2,3},{3,2},{4,5},{5,4},{6,7},{7,6},{8,9},{9,8},{10,11... | collective-permute-start | bytes 2654216 | tf_op jit(solution)/shard_map/ppermute | solution.py:283
  115.4 1.2 copy-start.7
  127.9 7.6 %collective-permute-start.8 = (bf16[576,576]{1,0:T(8,128)(2,1)}, bf16[576,576]{1,0:T(8,128)(2,1)}, u32[]{:S(2)}, u32[]{:S(2)}) collective-permute-start(bf16[576,576]{1,0:T(8,128)(2,1)} %get-tuple-element.47), channel_id=1, source_target_pairs={{0,1},{1,0},{2,3},{3,2},{4,5},{5,4},{6,7},{7,6},{8,9},{9,8},{10,11... | collective-permute-start | bytes 1990664 | tf_op jit(solution)/shard_map/ppermute | solution.py:283
  133.5 1.1 copy-start.4
  135.5 2.6 %copy-start.8 = (bf16[64,2,1792]{2,1,0:T(2,128)(2,1)S(1)}, bf16[64,2,1792]{2,1,0:T(2,128)(2,1)}, u32[]{:S(2)}) copy-start(bf16[64,2,1792]{2,1,0:T(2,128)(2,1)} %reshape.104) | copy-start | bytes 1376260
  187.9 11.9 %collective-permute-start.9 = (f32[1,1152]{1,0:T(1,128)S(1)}, f32[1,1152]{1,0:T(1,128)S(1)}, u32[]{:S(2)}, u32[]{:S(2)}) collective-permute-start(f32[1,1152]{1,0:T(1,128)S(1)} %reshape.106), channel_id=1, source_target_pairs={{0,1},{1,0},{2,3},{3,2},{4,5},{5,4},{6,7},{7,6},{8,9},{9,8},{10,11... | collective-permute-start | bytes 13832 | tf_op jit(solution)/shard_map/ppermute | solution.py:283
  192.2 11.3 %copy-start.5 = (bf16[576,1152]{1,0:T(8,128)(2,1)S(1)}, bf16[576,1152]{1,0:T(8,128)(2,1)}, u32[]{:S(2)}) copy-start(bf16[576,1152]{1,0:T(8,128)(2,1)} %copy-done.4) | copy-start | bytes 3981316
  194.2 11.7 %copy-start = (bf16[128,1152]{1,0:T(8,128)(2,1)}, bf16[128,1152]{1,0:T(8,128)(2,1)S(1)}, u32[]{:S(2)}) copy-start(bf16[128,1152]{1,0:T(8,128)(2,1)S(1)} %reshape.107.hidden_grad) | copy-start | bytes 884740
  195.1 12.5 %all-to-all-start.2 = ((bf16[8,2,5184]{2,1,0:T(2,128)(2,1)}), bf16[8,2,5184]{2,1,0:T(2,128)(2,1)S(1)}, u32[]{:S(2)}, u32[]{:S(2)}) async-start(bf16[8,2,5184]{2,1,0:T(2,128)(2,1)} %broadcast_in_dim.18), calls=%async_computation.2 | async-start | bytes 335872 | tf_op jit(solution)/shard_map/all_to_all | solution.py:354
  199.8 7.1 %collective-permute-start.10 = (f32[2,1152]{1,0:T(2,128)S(1)}, f32[2,1152]{1,0:T(2,128)S(1)}, u32[]{:S(2)}, u32[]{:S(2)}) collective-permute-start(f32[2,1152]{1,0:T(2,128)S(1)} %maximum_select_fusion.1), channel_id=1, source_target_pairs={{0,16},{16,0},{32,48},{48,32},{1,17},{17,1},{33,49},{49,33},{2,18}... | collective-permute-start | bytes 27656 | tf_op jit(solution)/shard_map/ppermute | solution.py:362

commit v9 on v8

--- a/solution.py
+++ b/solution.py
@@ -119,58 +119,37 @@
 STEP = (208, 64, 64)
 
 
-def part_copies(ref, half, block, targets):
-    copies = []
-    for section, first, last in SECTIONS:
-        first = first + 16 * half
-        row = first - SECTIONS[section][1] + STEP[section] * half
-        to = pl.multiple_of(block * BLOCK[section] + row, 16)
-        rows = last - first
-        copies.append((ref.at[pl.ds(first, rows)], targets[section].at[pl.ds(to, rows)]))
-    return copies
-
-
-COPIES = 7
-
-
-def start_copies(place, own, near, swapped, targets, sems):
+def assemble(place, own, near, swapped, targets):
     for me in range(2):
 
         @pl.when(place[0] == me)
         def _():
             cls = place[1]
-            pairs = [[] for _ in SECTIONS]
             for section, ref in enumerate(own):
                 to = pl.multiple_of(cls * BLOCK[section], 16)
-                pairs[section].append((ref, targets[section].at[pl.ds(to, BLOCK[section])]))
+                targets[section][pl.ds(to, BLOCK[section]), :] = ref[...]
             for flip, ref, other in zip((2, 1, 3), near, swapped):
                 for half in range(2):
                     source = ref if half == me else other
-                    for section, pair in enumerate(part_copies(source, half, cls ^ flip, targets)):
-                        pairs[section].append(pair)
-            for section in (1, 0, 2):
-                for i, (a, z) in enumerate(pairs[section]):
-                    pltpu.make_async_copy(a, z, sems.at[section * COPIES + i]).start()
-
-
-def wait_copies(section, own, targets, sems):
-    first, last = SECTIONS[section][1:]
-    sizes = [BLOCK[section]] + [last - first, last - first - 16] * 3
-    for i, n in enumerate(sizes):
-        a, z = own[section].at[pl.ds(0, n)], targets[section].at[pl.ds(0, n)]
-        pltpu.make_async_copy(a, z, sems.at[section * COPIES + i]).wait()
+                    for section, first, last in SECTIONS:
+                        skip = 16 * half
+                        row = skip + STEP[section] * half
+                        to = pl.multiple_of((cls ^ flip) * BLOCK[section] + row, 16)
+                        rows = last - first - skip
+                        targets[section][pl.ds(to, rows), :] = source[first + skip : last, :]
 
 
 def temporal_forward_kernel(
     place, sent, factors, own_qkv, own_so, own_out, b, c, d, other_b, other_c, other_d,
     out_keep, out_send, w_so, w_out, w_qkv, q_out, k_out, v_out, probs_out, mixed_out,
-    unit_out, inverse_out, project_out, sems,
+    unit_out, inverse_out, project_out,
 ):
-    own, targets = (own_qkv, own_so, own_out), (w_qkv, w_so, w_out)
-    start_copies(place, own, (b, c, d), (other_b, other_c, other_d), targets, sems)
+    assemble(
+        place, (own_qkv, own_so, own_out), (b, c, d), (other_b, other_c, other_d),
+        (w_qkv, w_so, w_out),
+    )
     tokens, cotangent, mixed_s = sent[:, :D], sent[:, D : 2 * D], sent[:, 2 * D :]
     gate_s, shift, scale, gate_t = (factors[i : i + 1, :] for i in range(4))
-    wait_copies(1, own, targets, sems)
     project = nn(mixed_s, w_so[...])
     project_out[...] = project
     hidden = (tokens.astype(F32) + gate_s * project).astype(BF).astype(F32)
@@ -180,7 +159,6 @@
     unit = centered * inverse
     unit_out[...] = unit
     normed = (unit * (1.0 + scale) + shift).astype(BF)
-    wait_copies(0, own, targets, sems)
     q, k, v = (nt(normed, w_qkv[i * ATT : (i + 1) * ATT, :]).astype(BF) for i in range(3))
     q_out[...], k_out[...], v_out[...] = q, k, v
 
@@ -196,7 +174,6 @@
     first = place[0] == 0
     out_keep[...] = tn(mixed, jnp.where(first, left, right))
     out_send[...] = tn(mixed, jnp.where(first, right, left)).astype(BF)
-    wait_copies(2, own, targets, sems)
 
 
 def temporal_backward_kernel(
@@ -241,15 +218,12 @@
             packed[32 * yhi + 16 : 32 * yhi + 32, D:] = tile
 
 
-def call(kernel, outs, *args, scalars=0, remote=0, scratch=(), flops=10**9):
+def call(kernel, outs, *args, scalars=0, scratch=(), flops=10**9):
     vmem = pl.BlockSpec(memory_space=pltpu.VMEM)
-    specs = [pl.BlockSpec(memory_space=pltpu.SMEM)] * scalars
-    specs += [vmem] * (len(args) - scalars - remote)
-    specs += [pl.BlockSpec(memory_space=pl.ANY)] * remote
     return pl.pallas_call(
         kernel,
         out_shape=[jax.ShapeDtypeStruct(s, d) for s, d in outs],
-        in_specs=specs,
+        in_specs=[pl.BlockSpec(memory_space=pltpu.SMEM)] * scalars + [vmem] * (len(args) - scalars),
         out_specs=[vmem] * len(outs),
         scratch_shapes=list(scratch),
         compiler_params=pltpu.CompilerParams(vmem_limit_bytes=32 * 2**20),
@@ -299,9 +273,9 @@
 
 def gather_weights(w_so, w_qkv, w_out, place, sent):
     shard = jnp.concatenate([w_so, w_out, w_qkv.T, jnp.zeros((3, D), BF)], 0)
-    shard, sent = lax.optimization_barrier((receive(shard, class_source), sent))
+    mine = lax.all_gather(receive(shard, class_source), "z", axis=0, tiled=True)
+    mine, sent = lax.optimization_barrier((mine, sent))
     sent = exchange(sent).reshape(ROWS, 2 * D + ATT)
-    mine = lax.all_gather(shard, "z", axis=0, tiled=True)
     other = swap_cores(mine)
     rows = lambda n: ((n, D), BF)
     own_so, own_out, own_qkv, part = call(
@@ -313,8 +287,8 @@
             pltpu.VMEM((432, D), F32),
         ],
     )
-    part, sent = lax.optimization_barrier((part, sent))
     near = [receive(part, near_source(dx, dy)) for dx, dy in ((1, 0), (0, 1), (1, 1))]
+    near[2], sent = lax.optimization_barrier((near[2], sent))
     return [own_qkv, own_so, own_out] + near + [swap_cores(a) for a in near], sent
 
 
@@ -337,8 +311,7 @@
             rows(D, F32), rows(128, F32), rows(D, F32),
         ],
         place, sent, factors, *weights,
-        scalars=1, remote=len(weights), flops=4 * 10**9,
-        scratch=[pltpu.SemaphoreType.DMA((24,))],
+        scalars=1, flops=4 * 10**9,
     )
     w_so = saved[0]
     out_other = swap_cores(out_send)
@@ -351,6 +324,7 @@
     out_part = back[:, :, D + 640 :].astype(F32).reshape(32, 2, 2, half)
     out_part = jnp.sum(out_part, 0).astype(BF).reshape(1, 2, 9 * ATT)
     out_part = jnp.broadcast_to(out_part, (8, 2, 9 * ATT))
+    out_part, back = lax.optimization_barrier((out_part, back))
     out_part = jnp.sum(lax.all_to_all(out_part, DP, 0, 0, tiled=True).astype(F32), 0)
     out_grad = out_part.reshape(2, 9, ATT).transpose(1, 0, 2).reshape(9, D)
 

time: 209 us -> 199 us (0.952)
  blocking collectives: 86.9 us -> 76.2 us
  waiting for transfers between devices: 16.3 us -> 25 us
  starting transfers between devices: 60.3 us -> 52.4 us
  Pallas kernels: 19.7 us -> 16.1 us
  local copies, waits for them, and re-layouts: 17 us -> 19.6 us
    all_gather x1, blocking collectives: 39.3 us -> 28.4 us  [gather_weights(): mine = lax.all_gather(receive(shard, class_source), 'z', axis=0, tiled=True)]
    all_to_all x1, waiting for transfers between devices: 0.01 us -> 10.2 us  [exchange(): return lax.all_to_all(a, SEQ, 0, 0, tiled=True)]
    all_to_all x1, starting transfers between devices: 23.1 us -> 15.5 us  [exchange(): return lax.all_to_all(a, SEQ, 0, 0, tiled=True)]
    pallas_call x5, Pallas kernels: 19.7 us -> 16.1 us  [call(): pl.pallas_call(kernel, out_shape=[jax.ShapeDtypeStruct(s, d) for s, d in...]
    ppermute x6, waiting for transfers between devices: 4.32 us -> 1.48 us  [swap_cores(): return lax.ppermute(a, 'core', [(0, 1), (1, 0)])]
  transfers between devices with their start and end apart: 13 -> 13, of which waited for: 5 -> 4; matrix products, arithmetic and copies ran while one was open for 5% -> 6% of each run, Pallas kernels for 4% -> 5%
where the time goes in v9:
time: 199 us; the launch traced here: 198 us
  blocking collectives  76.2 us (38%)
  starting transfers between devices  52.4 us (26%)
  waiting for transfers between devices  25 us (13%)
  local copies, waits for them, and re-layouts  19.6 us (10%)
  Pallas kernels  16.1 us (8%)
  other arithmetic  7.4 us (4%)
    all_to_all x1, blocking collectives, exchange(): return lax.all_to_all(a, SEQ, 0, 0, tiled=True)  47.8 us
    all_gather x1, blocking collectives, gather_weights(): mine = lax.all_gather(receive(shard, class_source), 'z', axis=0, tiled=True)  28.4 us
    ppermute x6, starting transfers between devices, swap_cores(): return lax.ppermute(a, 'core', [(0, 1), (1, 0)])  18.9 us
    pallas_call x5, Pallas kernels, call(): pl.pallas_call(kernel, out_shape=[jax.ShapeDtypeStruct(s, d) for s, d in...  16.1 us
    all_to_all x1, starting transfers between devices, exchange(): return lax.all_to_all(a, SEQ, 0, 0, tiled=True)  15.5 us
    ppermute x4, waiting for transfers between devices, receive(): return lax.ppermute(a, AXES, pairs)  13.3 us
    ppermute x4, starting transfers between devices, receive(): return lax.ppermute(a, AXES, pairs)  11.2 us
    all_to_all x1, waiting for transfers between devices, exchange(): return lax.all_to_all(a, SEQ, 0, 0, tiled=True)  10.2 us
  transfers between devices with their start and end apart: 13, of which 4 were waited for; matrix products, arithmetic and copies ran while one was open for 6% of the time, Pallas kernels for 5%

profile of v9, /device:TPU:1, one launch (start us, length us, event | category | flops | bytes accessed | tf_op | source)
XLA Modules:
  0.0 197.6 jit_solution(1499795828437147323)
XLA Ops:
  4.8 1.5 shard_map.102
  6.4 1.6 pad_maximum_fusion.1
  8.0 28.4 %all_gather.3.mine = bf16[384,1152]{1,0:T(8,128)(2,1)S(1)} all-gather(bf16[48,1152]{1,0:T(8,128)(2,1)S(1)} %collective-permute-done), channel_id=1, replica_groups=mesh['x'=4,'ylo'=2,'yhi'=4,'z'=8,'core'=2] {'z'}, dimensions={0}, use_global_device_ids=true | all-gather | bytes 995328 | tf_op jit(solution)/shard_map/all_gather | solution.py:276
  36.4 7.8 %collective-permute-start.1 = (bf16[384,1152]{1,0:T(8,128)(2,1)S(1)}, bf16[384,1152]{1,0:T(8,128)(2,1)S(1)}, u32[]{:S(2)}, u32[]{:S(2)}) collective-permute-start(bf16[384,1152]{1,0:T(8,128)(2,1)S(1)} %all_gather.3.mine), channel_id=1, source_target_pairs={{0,1},{1,0},{2,3},{3,2},{4,5},{5,4},{6,7},{7,6},{8,9},{9,8},{10,11... | collective-permute-start | bytes 2654216 | tf_op jit(solution)/shard_map/ppermute | solution.py:257
  44.1 15.5 %all-to-all-start = ((bf16[64,2,2880]{2,1,0:T(2,128)(2,1)}), bf16[64,2,2880]{2,1,0:T(2,128)(2,1)}, u32[]{:S(2)}, u32[]{:S(2)}) async-start(bf16[64,2,2880]{2,1,0:T(2,128)(2,1)} %pad_maximum_fusion.1), calls=%async_computation | async-start | bytes 1507328 | tf_op jit(solution)/shard_map/all_to_all | solution.py:235
  59.7 2.2 %shard_map.103 = (bf16[144,1152]{1,0:T(8,128)(2,1)S(1)}, bf16[144,1152]{1,0:T(8,128)(2,1)S(1)}, bf16[432,1152]{1,0:T(8,128)(2,1)S(1)}, bf16[384,1152]{1,0:T(8,128)(2,1)}) custom-call(s32[2]{0:T(128)S(1)} %pad_add_fusion.place, bf16[384,1152]{1,0:T(8,128)(2,1)S(1)} %all_gather.3.mine, bf16[384,1152]{1,0:T(8,128)(2,1)S(1)} %collective-permute-done.1.other), custom_call_target="tpu_custom_call" | custom-call | flops 1000000000 | bytes 10000000 | tf_op jit(solution)/shard_map/pallas_call | solution.py:223
  62.9 2.0 %collective-permute-start.2 = (bf16[384,1152]{1,0:T(8,128)(2,1)}, bf16[384,1152]{1,0:T(8,128)(2,1)S(1)}, u32[]{:S(2)}, u32[]{:S(2)}) collective-permute-start(bf16[384,1152]{1,0:T(8,128)(2,1)} %get-tuple-element.30), channel_id=1, source_target_pairs={{192,0},{497,1},{194,2},{499,3},{196,4},{501,5},{198,6},{503,7},{2... | collective-permute-start | bytes 2654216 | tf_op jit(solution)/shard_map/ppermute | solution.py:253
  64.9 3.8 %collective-permute-start.4 = (bf16[384,1152]{1,0:T(8,128)(2,1)}, bf16[384,1152]{1,0:T(8,128)(2,1)}, u32[]{:S(2)}, u32[]{:S(2)}) collective-permute-start(bf16[384,1152]{1,0:T(8,128)(2,1)} %get-tuple-element.30), channel_id=1, source_target_pairs={{64,0},{113,1},{66,2},{115,3},{68,4},{117,5},{70,6},{119,7},{72,8}... | collective-permute-start | bytes 2654216 | tf_op jit(solution)/shard_map/ppermute | solution.py:253
  68.7 4.7 %collective-permute-start.3 = (bf16[384,1152]{1,0:T(8,128)(2,1)}, bf16[384,1152]{1,0:T(8,128)(2,1)}, u32[]{:S(2)}, u32[]{:S(2)}) collective-permute-start(bf16[384,1152]{1,0:T(8,128)(2,1)} %get-tuple-element.30), channel_id=1, source_target_pairs={{128,0},{385,1},{130,2},{387,3},{132,4},{389,5},{134,6},{391,7},{1... | collective-permute-start | bytes 2654216 | tf_op jit(solution)/shard_map/ppermute | solution.py:253
  73.4 10.2 %all-to-all-done = bf16[64,2,2880]{2,1,0:T(2,128)(2,1)} async-done(((bf16[64,2,2880]{2,1,0:T(2,128)(2,1)}), bf16[64,2,2880]{2,1,0:T(2,128)(2,1)}, u32[]{:S(2)}, u32[]{:S(2)}) %all-to-all-start) | async-done | bytes 737312 | tf_op jit(solution)/shard_map/all_to_all | solution.py:235
  83.7 2.2 %reshape.103.sent = bf16[128,2880]{1,0:T(8,128)(2,1)S(1)} reshape(bf16[64,2,2880]{2,1,0:T(2,128)(2,1)} %all-to-all-done) | data formatting | bytes 1474560 | tf_op jit(solution)/shard_map/reshape | solution.py:278
  85.9 3.1 %collective-permute-done.2.d = bf16[384,1152]{1,0:T(8,128)(2,1)S(1)} collective-permute-done((bf16[384,1152]{1,0:T(8,128)(2,1)}, bf16[384,1152]{1,0:T(8,128)(2,1)S(1)}, u32[]{:S(2)}, u32[]{:S(2)}) %collective-permute-start.2) | collective-permute-done | bytes 884768 | tf_op jit(solution)/shard_map/ppermute | solution.py:253
  89.0 10.1 %collective-permute-done.4.c = bf16[384,1152]{1,0:T(8,128)(2,1)} collective-permute-done((bf16[384,1152]{1,0:T(8,128)(2,1)}, bf16[384,1152]{1,0:T(8,128)(2,1)}, u32[]{:S(2)}, u32[]{:S(2)}) %collective-permute-start.4) | collective-permute-done | bytes 884768 | tf_op jit(solution)/shard_map/ppermute | solution.py:253
  99.2 1.9 collective-permute-start.6
  101.1 2.4 %collective-permute-start.5 = (bf16[384,1152]{1,0:T(8,128)(2,1)}, bf16[384,1152]{1,0:T(8,128)(2,1)S(1)}, u32[]{:S(2)}, u32[]{:S(2)}) collective-permute-start(bf16[384,1152]{1,0:T(8,128)(2,1)} %collective-permute-done.3.b), channel_id=1, source_target_pairs={{0,1},{1,0},{2,3},{3,2},{4,5},{5,4},{6,7},{7,6},{8,9},{9,8},{10,11... | collective-permute-start | bytes 2654216 | tf_op jit(solution)/shard_map/ppermute | solution.py:257
  103.5 1.9 collective-permute-start.7
  106.4 1.5 collective-permute-done.7.other_d
  107.8 1.2 copy-done.2
  109.0 1.2 copy-done.7
  110.2 6.7 %shard_map.104 = (f32[576,576]{1,0:T(8,128)S(1)}, bf16[576,576]{1,0:T(8,128)(2,1)}, bf16[576,1152]{1,0:T(8,128)(2,1)S(1)}, bf16[576,1152]{1,0:T(8,128)(2,1)S(1)}...) custom-call(s32[2]{0:T(128)S(1)} %pad_add_fusion.place, ...), custom_call_target="tpu_custom_call" | custom-call | flops 4000000000 | bytes 10000000 | tf_op jit(solution)/shard_map/pallas_call | solution.py:223
  116.9 2.2 %collective-permute-start.8 = (bf16[576,576]{1,0:T(8,128)(2,1)}, bf16[576,576]{1,0:T(8,128)(2,1)}, u32[]{:S(2)}, u32[]{:S(2)}) collective-permute-start(bf16[576,576]{1,0:T(8,128)(2,1)} %get-tuple-element.49), channel_id=1, source_target_pairs={{0,1},{1,0},{2,3},{3,2},{4,5},{5,4},{6,7},{7,6},{8,9},{9,8},{10,11... | collective-permute-start | bytes 1990664 | tf_op jit(solution)/shard_map/ppermute | solution.py:257
  119.1 3.3 %shard_map.105 = bf16[128,1792]{1,0:T(8,128)(2,1)S(1)} custom-call(bf16[128,2880]{1,0:T(8,128)(2,1)S(1)} %reshape.103.sent, f32[4,1152]{1,0:T(4,128)S(1)} %bitcast.20, bf16[576,1152]{1,0:T(8,128)(2,1)S(1)} %get-tuple-element.37.w_so, bf16[576,1152]{1,0:T(8,128)(2,1)S(1)} %get-tuple-element.38.w_out, bf16[1728,1152]{1,0:T(8,128)(2,1)S(1)} %get-tuple-element.39.w_qkv, ...), custom_call_target="tpu_custom_call" | custom-call | flops 4000000000 | bytes 10000000 | tf_op jit(solution)/shard_map/pallas_call | solution.py:223
  122.4 1.1 copy-done.4
  124.5 1.3 add_convert_fusion
  125.8 1.3 reshape.105
  128.1 47.8 %all_to_all.15 = bf16[64,2,4384]{2,1,0:T(2,128)(2,1)} all-to-all(bf16[64,2,4384]{2,1,0:T(2,128)(2,1)S(1)} %pad_maximum_fusion), channel_id=1, replica_groups=mesh['x'=4,'ylo'=2,'yhi'=4,'z'=8,'core'=2] {'yhi','z','core'}, dimensions={0} | all-to-all | bytes 2244608 | tf_op jit(solution)/shard_map/all_to_all | solution.py:235
  175.9 1.6 slice.12
  180.1 2.7 %collective-permute-start.9 = (f32[1,1152]{1,0:T(1,128)S(1)}, f32[1,1152]{1,0:T(1,128)S(1)}, u32[]{:S(2)}, u32[]{:S(2)}) collective-permute-start(f32[1,1152]{1,0:T(1,128)S(1)} %reshape.108), channel_id=1, source_target_pairs={{0,1},{1,0},{2,3},{3,2},{4,5},{5,4},{6,7},{7,6},{8,9},{9,8},{10,11... | collective-permute-start | bytes 13832 | tf_op jit(solution)/shard_map/ppermute | solution.py:257
  182.8 1.9 slice.11
  185.8 3.4 %all-to-all-start.2 = ((bf16[8,2,5184]{2,1,0:T(2,128)(2,1)}), bf16[8,2,5184]{2,1,0:T(2,128)(2,1)S(1)}, u32[]{:S(2)}, u32[]{:S(2)}) async-start(bf16[8,2,5184]{2,1,0:T(2,128)(2,1)} %broadcast_in_dim.16), calls=%async_computation.2 | async-start | bytes 335872 | tf_op jit(solution)/shard_map/all_to_all | solution.py:328
  189.2 3.4 %collective-permute-start.10 = (f32[2,1152]{1,0:T(2,128)S(1)}, f32[2,1152]{1,0:T(2,128)S(1)}, u32[]{:S(2)}, u32[]{:S(2)}) collective-permute-start(f32[2,1152]{1,0:T(2,128)S(1)} %maximum_select_fusion.1), channel_id=1, source_target_pairs={{0,16},{16,0},{32,48},{48,32},{1,17},{17,1},{33,49},{49,33},{2,18}... | collective-permute-start | bytes 27656 | tf_op jit(solution)/shard_map/ppermute | solution.py:336
  192.6 2.4 %shard_map.106 = bf16[128,1728]{1,0:T(8,128)(2,1)S(1)} custom-call(bf16[128,1728]{1,0:T(8,128)(2,1)S(1)} %bitcast.16, bf16[128,1152]{1,0:T(8,128)(2,1)S(1)} %reshape.109.hidden_grad, f32[4,1152]{1,0:T(4,128)S(1)} %bitcast.21, bf16[576,1152]{1,0:T(8,128)(2,1)S(1)} %copy-done.5), custom_call_target="tpu_custom_call" | custom-call | flops 1000000000 | bytes 10000000 | tf_op jit(solution)/shard_map/pallas_call | solution.py:223
  (50 shorter events, 14.5 us)
Async XLA Ops:
  0.6 3.9 %copy-start.9 = (bf16[1,1,128,1728]{2,3,1,0:T(8,128)(2,1)S(1)}, bf16[1,1,128,1728]{2,3,1,0:T(8,128)(2,1)}, u32[]{:S(2)}) copy-start(bf16[1,1,128,1728]{2,3,1,0:T(8,128)(2,1)} %param.8) | copy-start | bytes 1327108
  1.7 6.3 %collective-permute-start = (bf16[48,1152]{1,0:T(8,128)(2,1)S(1)}, bf16[48,1152]{1,0:T(8,128)(2,1)S(1)}, u32[]{:S(2)}, u32[]{:S(2)}) collective-permute-start(bf16[48,1152]{1,0:T(8,128)(2,1)S(1)} %maximum_maximum_fusion), channel_id=1, source_target_pairs={{0,0},{1,1},{2,2},{3,3},{4,4},{5,5},{6,6},{7,7},{8,8},{9,9},{10,10... | collective-permute-start | bytes 331784 | tf_op jit(solution)/shard_map/ppermute | solution.py:253
  36.4 23.3 %collective-permute-start.1 = (bf16[384,1152]{1,0:T(8,128)(2,1)S(1)}, bf16[384,1152]{1,0:T(8,128)(2,1)S(1)}, u32[]{:S(2)}, u32[]{:S(2)}) collective-permute-start(bf16[384,1152]{1,0:T(8,128)(2,1)S(1)} %all_gather.3.mine), channel_id=1, source_target_pairs={{0,1},{1,0},{2,3},{3,2},{4,5},{5,4},{6,7},{7,6},{8,9},{9,8},{10,11... | collective-permute-start | bytes 2654216 | tf_op jit(solution)/shard_map/ppermute | solution.py:257
  44.1 39.5 %all-to-all-start = ((bf16[64,2,2880]{2,1,0:T(2,128)(2,1)}), bf16[64,2,2880]{2,1,0:T(2,128)(2,1)}, u32[]{:S(2)}, u32[]{:S(2)}) async-start(bf16[64,2,2880]{2,1,0:T(2,128)(2,1)} %pad_maximum_fusion.1), calls=%async_computation | async-start | bytes 1507328 | tf_op jit(solution)/shard_map/all_to_all | solution.py:235
  61.9 1.0 copy-start.6
  62.9 45.0 %copy-start.3 = (f32[1,4,1152]{2,1,0:T(4,128)S(1)}, f32[1,4,1152]{2,1,0:T(4,128)}, u32[]{:S(2)}) copy-start(f32[1,4,1152]{2,1,0:T(4,128)} %param.12) | copy-start | bytes 55300
  62.9 26.2 %collective-permute-start.2 = (bf16[384,1152]{1,0:T(8,128)(2,1)}, bf16[384,1152]{1,0:T(8,128)(2,1)S(1)}, u32[]{:S(2)}, u32[]{:S(2)}) collective-permute-start(bf16[384,1152]{1,0:T(8,128)(2,1)} %get-tuple-element.30), channel_id=1, source_target_pairs={{192,0},{497,1},{194,2},{499,3},{196,4},{501,5},{198,6},{503,7},{2... | collective-permute-start | bytes 2654216 | tf_op jit(solution)/shard_map/ppermute | solution.py:253
  64.9 34.3 %collective-permute-start.4 = (bf16[384,1152]{1,0:T(8,128)(2,1)}, bf16[384,1152]{1,0:T(8,128)(2,1)}, u32[]{:S(2)}, u32[]{:S(2)}) collective-permute-start(bf16[384,1152]{1,0:T(8,128)(2,1)} %get-tuple-element.30), channel_id=1, source_target_pairs={{64,0},{113,1},{66,2},{115,3},{68,4},{117,5},{70,6},{119,7},{72,8}... | collective-permute-start | bytes 2654216 | tf_op jit(solution)/shard_map/ppermute | solution.py:253
  68.7 32.3 %collective-permute-start.3 = (bf16[384,1152]{1,0:T(8,128)(2,1)}, bf16[384,1152]{1,0:T(8,128)(2,1)}, u32[]{:S(2)}, u32[]{:S(2)}) collective-permute-start(bf16[384,1152]{1,0:T(8,128)(2,1)} %get-tuple-element.30), channel_id=1, source_target_pairs={{128,0},{385,1},{130,2},{387,3},{132,4},{389,5},{134,6},{391,7},{1... | collective-permute-start | bytes 2654216 | tf_op jit(solution)/shard_map/ppermute | solution.py:253
  99.2 7.2 %collective-permute-start.6 = (bf16[384,1152]{1,0:T(8,128)(2,1)}, bf16[384,1152]{1,0:T(8,128)(2,1)S(1)}, u32[]{:S(2)}, u32[]{:S(2)}) collective-permute-start(bf16[384,1152]{1,0:T(8,128)(2,1)} %collective-permute-done.4.c), channel_id=1, source_target_pairs={{0,1},{1,0},{2,3},{3,2},{4,5},{5,4},{6,7},{7,6},{8,9},{9,8},{10,11... | collective-permute-start | bytes 2654216 | tf_op jit(solution)/shard_map/ppermute | solution.py:257
  101.1 5.3 %collective-permute-start.5 = (bf16[384,1152]{1,0:T(8,128)(2,1)}, bf16[384,1152]{1,0:T(8,128)(2,1)S(1)}, u32[]{:S(2)}, u32[]{:S(2)}) collective-permute-start(bf16[384,1152]{1,0:T(8,128)(2,1)} %collective-permute-done.3.b), channel_id=1, source_target_pairs={{0,1},{1,0},{2,3},{3,2},{4,5},{5,4},{6,7},{7,6},{8,9},{9,8},{10,11... | collective-permute-start | bytes 2654216 | tf_op jit(solution)/shard_map/ppermute | solution.py:257
  103.5 4.3 %collective-permute-start.7 = (bf16[384,1152]{1,0:T(8,128)(2,1)S(1)}, bf16[384,1152]{1,0:T(8,128)(2,1)S(1)}, u32[]{:S(2)}, u32[]{:S(2)}) collective-permute-start(bf16[384,1152]{1,0:T(8,128)(2,1)S(1)} %collective-permute-done.2.d), channel_id=1, source_target_pairs={{0,1},{1,0},{2,3},{3,2},{4,5},{5,4},{6,7},{7,6},{8,9},{9,8},{10,11... | collective-permute-start | bytes 2654216 | tf_op jit(solution)/shard_map/ppermute | solution.py:257
  105.4 0.9 copy-start.1
  107.8 1.2 copy-start.2
  109.0 1.2 copy-start.7
  116.9 7.6 %collective-permute-start.8 = (bf16[576,576]{1,0:T(8,128)(2,1)}, bf16[576,576]{1,0:T(8,128)(2,1)}, u32[]{:S(2)}, u32[]{:S(2)}) collective-permute-start(bf16[576,576]{1,0:T(8,128)(2,1)} %get-tuple-element.49), channel_id=1, source_target_pairs={{0,1},{1,0},{2,3},{3,2},{4,5},{5,4},{6,7},{7,6},{8,9},{9,8},{10,11... | collective-permute-start | bytes 1990664 | tf_op jit(solution)/shard_map/ppermute | solution.py:257
  122.4 1.1 copy-start.4
  124.5 2.6 %copy-start.8 = (bf16[64,2,1792]{2,1,0:T(2,128)(2,1)S(1)}, bf16[64,2,1792]{2,1,0:T(2,128)(2,1)}, u32[]{:S(2)}) copy-start(bf16[64,2,1792]{2,1,0:T(2,128)(2,1)} %reshape.104) | copy-start | bytes 1376260
  177.4 15.2 %copy-start.5 = (bf16[576,1152]{1,0:T(8,128)(2,1)S(1)}, bf16[576,1152]{1,0:T(8,128)(2,1)}, u32[]{:S(2)}) copy-start(bf16[576,1152]{1,0:T(8,128)(2,1)} %copy-done.4) | copy-start | bytes 3981316
  180.1 9.1 %collective-permute-start.9 = (f32[1,1152]{1,0:T(1,128)S(1)}, f32[1,1152]{1,0:T(1,128)S(1)}, u32[]{:S(2)}, u32[]{:S(2)}) collective-permute-start(f32[1,1152]{1,0:T(1,128)S(1)} %reshape.108), channel_id=1, source_target_pairs={{0,1},{1,0},{2,3},{3,2},{4,5},{5,4},{6,7},{7,6},{8,9},{9,8},{10,11... | collective-permute-start | bytes 13832 | tf_op jit(solution)/shard_map/ppermute | solution.py:257
  185.8 9.2 %copy-start = (bf16[128,1152]{1,0:T(8,128)(2,1)}, bf16[128,1152]{1,0:T(8,128)(2,1)S(1)}, u32[]{:S(2)}) copy-start(bf16[128,1152]{1,0:T(8,128)(2,1)S(1)} %reshape.109.hidden_grad) | copy-start | bytes 884740
  185.8 10.8 %all-to-all-start.2 = ((bf16[8,2,5184]{2,1,0:T(2,128)(2,1)}), bf16[8,2,5184]{2,1,0:T(2,128)(2,1)S(1)}, u32[]{:S(2)}, u32[]{:S(2)}) async-start(bf16[8,2,5184]{2,1,0:T(2,128)(2,1)} %broadcast_in_dim.16), calls=%async_computation.2 | async-start | bytes 335872 | tf_op jit(solution)/shard_map/all_to_all | solution.py:328
  189.2 6.8 %collective-permute-start.10 = (f32[2,1152]{1,0:T(2,128)S(1)}, f32[2,1152]{1,0:T(2,128)S(1)}, u32[]{:S(2)}, u32[]{:S(2)}) collective-permute-start(f32[2,1152]{1,0:T(2,128)S(1)} %maximum_select_fusion.1), channel_id=1, source_target_pairs={{0,16},{16,0},{32,48},{48,32},{1,17},{17,1},{33,49},{49,33},{2,18}... | collective-permute-start | bytes 27656 | tf_op jit(solution)/shard_map/ppermute | solution.py:336

commit v10 on v9

--- a/solution.py
+++ b/solution.py
@@ -205,17 +205,9 @@
         jnp.sum(d_normed * unit, 0, keepdims=True),
         jnp.sum(cot * project_t, 0, keepdims=True),
     )
-    zeros = jnp.zeros((16, 64), BF)
-    for parity in range(2):
-        rows = [
-            factor_grads[2 * parity + core][:, part * ATT : part * ATT + ATT]
-            for core in range(2)
-            for part in range(2)
-        ]
-        tile = jnp.concatenate([jnp.concatenate(rows * 4, 0).astype(BF), zeros], 1)
-        for yhi in (parity, parity + 2):
-            packed[32 * yhi : 32 * yhi + 16, D:] = tile
-            packed[32 * yhi + 16 : 32 * yhi + 32, D:] = tile
+    tile = jnp.concatenate(factor_grads * 4, 0).astype(BF)
+    for i in range(8):
+        packed[16 * i : 16 * i + 16, D:] = tile
 
 
 def call(kernel, outs, *args, scalars=0, scratch=(), flops=10**9):
@@ -226,7 +218,7 @@
         in_specs=[pl.BlockSpec(memory_space=pltpu.SMEM)] * scalars + [vmem] * (len(args) - scalars),
         out_specs=[vmem] * len(outs),
         scratch_shapes=list(scratch),
-        compiler_params=pltpu.CompilerParams(vmem_limit_bytes=32 * 2**20),
+        compiler_params=pltpu.CompilerParams(vmem_limit_bytes=20 * 2**20),
         cost_estimate=pl.CostEstimate(flops=flops, bytes_accessed=10**7, transcendentals=10**5),
     )(*args)
 
@@ -274,8 +266,6 @@
 def gather_weights(w_so, w_qkv, w_out, place, sent):
     shard = jnp.concatenate([w_so, w_out, w_qkv.T, jnp.zeros((3, D), BF)], 0)
     mine = lax.all_gather(receive(shard, class_source), "z", axis=0, tiled=True)
-    mine, sent = lax.optimization_barrier((mine, sent))
-    sent = exchange(sent).reshape(ROWS, 2 * D + ATT)
     other = swap_cores(mine)
     rows = lambda n: ((n, D), BF)
     own_so, own_out, own_qkv, part = call(
@@ -288,7 +278,8 @@
         ],
     )
     near = [receive(part, near_source(dx, dy)) for dx, dy in ((1, 0), (0, 1), (1, 1))]
-    near[2], sent = lax.optimization_barrier((near[2], sent))
+    sent = exchange(lax.optimization_barrier((part, sent))[1]).reshape(ROWS, 2 * D + ATT)
+    near[1], sent = lax.optimization_barrier((near[1], sent))
     return [own_qkv, own_so, own_out] + near + [swap_cores(a) for a in near], sent
 
 
@@ -315,30 +306,25 @@
     )
     w_so = saved[0]
     out_other = swap_cores(out_send)
-    (packed,) = call(temporal_backward_kernel, [rows(D + 640)], sent, factors, *saved, flops=4 * 10**9)
+    (packed,) = call(temporal_backward_kernel, [rows(2 * D)], sent, factors, *saved, flops=4 * 10**9)
 
     half = 9 * ATT // 2
     out_part = (out_keep + out_other.astype(F32)).astype(BF).reshape(64, 2, half)
-    back = exchange(jnp.concatenate([packed.reshape(64, 2, D + 640), out_part], 2))
-
-    out_part = back[:, :, D + 640 :].astype(F32).reshape(32, 2, 2, half)
+    back = exchange(jnp.concatenate([packed.reshape(64, 2, 2 * D), out_part], 2))
+
+    out_part = back[:, :, 2 * D :].astype(F32).reshape(32, 2, 2, half)
     out_part = jnp.sum(out_part, 0).astype(BF).reshape(1, 2, 9 * ATT)
     out_part = jnp.broadcast_to(out_part, (8, 2, 9 * ATT))
-    out_part, back = lax.optimization_barrier((out_part, back))
     out_part = jnp.sum(lax.all_to_all(out_part, DP, 0, 0, tiled=True).astype(F32), 0)
     out_grad = out_part.reshape(2, 9, ATT).transpose(1, 0, 2).reshape(9, D)
 
     token_grad = back[:, :, :D].reshape(ROWS, D)
-    mine = jnp.sum(back[:, :, D : D + ATT].astype(F32), 0).reshape(1, D)
-    other = swap_cores(mine)
-    rows = jnp.where(core == 0, jnp.concatenate([mine, other]), jnp.concatenate([other, mine]))
-    rows, token_grad = lax.optimization_barrier((rows, token_grad))
-    other = lax.ppermute(rows, "yhi", [(0, 1), (1, 0), (2, 3), (3, 2)])
     (qkv_grad,) = call(
         spatial_backward_kernel, [((ROWS, 3 * ATT), BF)], qkv, token_grad, factors, w_so
     )
-    low = lax.axis_index("yhi") % 2 == 0
-    factor_grad = jnp.where(low, jnp.concatenate([rows, other]), jnp.concatenate([other, rows]))
+    mine = jnp.sum(back[:, :, D : 2 * D].astype(F32), 0)
+    other = swap_cores(mine)
+    factor_grad = jnp.where(core == 0, jnp.concatenate([mine, other]), jnp.concatenate([other, mine]))
     return token_grad[None, None], qkv_grad[None, None], factor_grad[None], out_grad
 
 

time: 199 us -> 206 us (1.035)
  blocking collectives: 76.2 us -> 28.4 us
  waiting for transfers between devices: 25 us -> 59.7 us
  starting transfers between devices: 52.4 us -> 69.9 us
    all_to_all x1 -> x0, blocking collectives: 47.8 us -> none  [exchange(): return lax.all_to_all(a, SEQ, 0, 0, tiled=True)]
    all_to_all x1 -> x2, waiting for transfers between devices: 10.2 us -> 35.3 us  [exchange(): return lax.all_to_all(a, SEQ, 0, 0, tiled=True)]
    all_to_all x1 -> x2, starting transfers between devices: 15.5 us -> 35 us  [exchange(): return lax.all_to_all(a, SEQ, 0, 0, tiled=True)]
    ppermute x4, waiting for transfers between devices: 13.3 us -> 21.7 us  [receive(): return lax.ppermute(a, AXES, pairs)]
    ppermute x1 -> x0, starting transfers between devices: 3.4 us -> none  [body(): other = lax.ppermute(rows, 'yhi', [(0, 1), (1, 0), (2, 3), (3, 2)])]
    unnamed x22 -> x26, local copies, waits for them, and re-layouts: 6.54 us -> 8.32 us
  transfers between devices with their start and end apart: 13 -> 13, of which waited for: 4 -> 4; matrix products, arithmetic and copies ran while one was open for 6% -> 6% of each run, Pallas kernels for 5% -> 3%
where the time goes in v10:
time: 206 us; the launch traced here: 203 us
  starting transfers between devices  69.9 us (34%)
  waiting for transfers between devices  59.7 us (29%)
  blocking collectives  28.4 us (14%)
  local copies, waits for them, and re-layouts  18.6 us (9%)
  Pallas kernels  16.5 us (8%)
  other arithmetic  8.79 us (4%)
    all_to_all x2, waiting for transfers between devices, exchange(): return lax.all_to_all(a, SEQ, 0, 0, tiled=True)  35.3 us
    all_to_all x2, starting transfers between devices, exchange(): return lax.all_to_all(a, SEQ, 0, 0, tiled=True)  35 us
    all_gather x1, blocking collectives, gather_weights(): mine = lax.all_gather(receive(shard, class_source), 'z', axis=0, tiled=True)  28.4 us
    ppermute x4, waiting for transfers between devices, receive(): return lax.ppermute(a, AXES, pairs)  21.7 us
    ppermute x6, starting transfers between devices, swap_cores(): return lax.ppermute(a, 'core', [(0, 1), (1, 0)])  19.6 us
    pallas_call x5, Pallas kernels, call(): pl.pallas_call(kernel, out_shape=[jax.ShapeDtypeStruct(s, d) for s, d in...  16.5 us
    ppermute x4, starting transfers between devices, receive(): return lax.ppermute(a, AXES, pairs)  11.1 us
    unnamed x26, local copies, waits for them, and re-layouts  8.32 us
  transfers between devices with their start and end apart: 13, of which 4 were waited for; matrix products, arithmetic and copies ran while one was open for 6% of the time, Pallas kernels for 3%

profile of v10, /device:TPU:1, one launch (start us, length us, event | category | flops | bytes accessed | tf_op | source)
XLA Modules:
  0.0 202.8 jit_solution(12206856643262965275)
XLA Ops:
  2.5 28.4 %all_gather.3.mine = bf16[384,1152]{1,0:T(8,128)(2,1)S(1)} all-gather(bf16[48,1152]{1,0:T(8,128)(2,1)S(1)} %collective-permute-done), channel_id=1, replica_groups=mesh['x'=4,'ylo'=2,'yhi'=4,'z'=8,'core'=2] {'z'}, dimensions={0}, use_global_device_ids=true | all-gather | bytes 995328 | tf_op jit(solution)/shard_map/all_gather | solution.py:268
  30.8 7.8 %collective-permute-start.1 = (bf16[384,1152]{1,0:T(8,128)(2,1)S(1)}, bf16[384,1152]{1,0:T(8,128)(2,1)S(1)}, u32[]{:S(2)}, u32[]{:S(2)}) collective-permute-start(bf16[384,1152]{1,0:T(8,128)(2,1)S(1)} %all_gather.3.mine), channel_id=1, source_target_pairs={{0,1},{1,0},{2,3},{3,2},{4,5},{5,4},{6,7},{7,6},{8,9},{9,8},{10,11... | collective-permute-start | bytes 2654216 | tf_op jit(solution)/shard_map/ppermute | solution.py:249
  38.9 1.2 copy.25
  40.1 1.5 shard_map.103
  41.8 1.6 pad_maximum_fusion.1
  43.4 2.2 %shard_map.102 = (bf16[144,1152]{1,0:T(8,128)(2,1)S(1)}, bf16[144,1152]{1,0:T(8,128)(2,1)S(1)}, bf16[432,1152]{1,0:T(8,128)(2,1)S(1)}, bf16[384,1152]{1,0:T(8,128)(2,1)}) custom-call(s32[2]{0:T(128)S(1)} %pad_add_fusion.place, bf16[384,1152]{1,0:T(8,128)(2,1)S(1)} %all_gather.3.mine, bf16[384,1152]{1,0:T(8,128)(2,1)S(1)} %collective-permute-done.1.other), custom_call_target="tpu_custom_call" | custom-call | flops 1000000000 | bytes 10000000 | tf_op jit(solution)/shard_map/pallas_call | solution.py:215
  47.3 21.2 %all-to-all-start = ((bf16[64,2,2880]{2,1,0:T(2,128)(2,1)}), bf16[64,2,2880]{2,1,0:T(2,128)(2,1)}, u32[]{:S(2)}, u32[]{:S(2)}) async-start(bf16[64,2,2880]{2,1,0:T(2,128)(2,1)} %pad_maximum_fusion.1), calls=%async_computation | async-start | bytes 1507328 | tf_op jit(solution)/shard_map/all_to_all | solution.py:227
  68.4 1.9 collective-permute-start.4
  70.4 5.9 %collective-permute-start.3 = (bf16[384,1152]{1,0:T(8,128)(2,1)}, bf16[384,1152]{1,0:T(8,128)(2,1)}, u32[]{:S(2)}, u32[]{:S(2)}) collective-permute-start(bf16[384,1152]{1,0:T(8,128)(2,1)} %get-tuple-element.24), channel_id=1, source_target_pairs={{128,0},{385,1},{130,2},{387,3},{132,4},{389,5},{134,6},{391,7},{1... | collective-permute-start | bytes 2654216 | tf_op jit(solution)/shard_map/ppermute | solution.py:245
  76.3 2.6 %collective-permute-start.2 = (bf16[384,1152]{1,0:T(8,128)(2,1)}, bf16[384,1152]{1,0:T(8,128)(2,1)}, u32[]{:S(2)}, u32[]{:S(2)}) collective-permute-start(bf16[384,1152]{1,0:T(8,128)(2,1)} %get-tuple-element.24), channel_id=1, source_target_pairs={{64,0},{113,1},{66,2},{115,3},{68,4},{117,5},{70,6},{119,7},{72,8}... | collective-permute-start | bytes 2654216 | tf_op jit(solution)/shard_map/ppermute | solution.py:245
  78.9 18.6 %collective-permute-done.4.d = bf16[384,1152]{1,0:T(8,128)(2,1)S(1)} collective-permute-done((bf16[384,1152]{1,0:T(8,128)(2,1)}, bf16[384,1152]{1,0:T(8,128)(2,1)S(1)}, u32[]{:S(2)}, u32[]{:S(2)}) %collective-permute-start.4) | collective-permute-done | bytes 884768 | tf_op jit(solution)/shard_map/ppermute | solution.py:245
  97.5 1.9 collective-permute-start.7
  99.4 3.2 %collective-permute-start.5 = (bf16[384,1152]{1,0:T(8,128)(2,1)}, bf16[384,1152]{1,0:T(8,128)(2,1)}, u32[]{:S(2)}, u32[]{:S(2)}) collective-permute-start(bf16[384,1152]{1,0:T(8,128)(2,1)} %collective-permute-done.3.b), channel_id=1, source_target_pairs={{0,1},{1,0},{2,3},{3,2},{4,5},{5,4},{6,7},{7,6},{8,9},{9,8},{10,11... | collective-permute-start | bytes 2654216 | tf_op jit(solution)/shard_map/ppermute | solution.py:249
  102.6 2.2 %reshape.100.sent = bf16[128,2880]{1,0:T(8,128)(2,1)S(1)} reshape(bf16[64,2,2880]{2,1,0:T(2,128)(2,1)} %all-to-all-done) | data formatting | bytes 1474560 | tf_op jit(solution)/shard_map/reshape | solution.py:281
  104.9 3.1 %collective-permute-done.2.c = bf16[384,1152]{1,0:T(8,128)(2,1)} collective-permute-done((bf16[384,1152]{1,0:T(8,128)(2,1)}, bf16[384,1152]{1,0:T(8,128)(2,1)}, u32[]{:S(2)}, u32[]{:S(2)}) %collective-permute-start.2) | collective-permute-done | bytes 884768 | tf_op jit(solution)/shard_map/ppermute | solution.py:245
  108.0 1.9 collective-permute-start.6
  109.9 2.6 %collective-permute-done.6.other_c = bf16[384,1152]{1,0:T(8,128)(2,1)S(1)} collective-permute-done((bf16[384,1152]{1,0:T(8,128)(2,1)}, bf16[384,1152]{1,0:T(8,128)(2,1)S(1)}, u32[]{:S(2)}, u32[]{:S(2)}) %collective-permute-start.6) | collective-permute-done | bytes 884768 | tf_op jit(solution)/shard_map/ppermute | solution.py:249
  112.5 1.2 copy-done.1
  113.7 1.2 copy-done.6
  115.9 7.2 %shard_map.104 = (f32[576,576]{1,0:T(8,128)S(1)}, bf16[576,576]{1,0:T(8,128)(2,1)}, bf16[576,1152]{1,0:T(8,128)(2,1)S(1)}, bf16[576,1152]{1,0:T(8,128)(2,1)S(1)}...) custom-call(s32[2]{0:T(128)S(1)} %pad_add_fusion.place, ...), custom_call_target="tpu_custom_call" | custom-call | flops 4000000000 | bytes 10000000 | tf_op jit(solution)/shard_map/pallas_call | solution.py:215
  123.1 2.2 %collective-permute-start.8 = (bf16[576,576]{1,0:T(8,128)(2,1)}, bf16[576,576]{1,0:T(8,128)(2,1)}, u32[]{:S(2)}, u32[]{:S(2)}) collective-permute-start(bf16[576,576]{1,0:T(8,128)(2,1)} %get-tuple-element.43), channel_id=1, source_target_pairs={{0,1},{1,0},{2,3},{3,2},{4,5},{5,4},{6,7},{7,6},{8,9},{9,8},{10,11... | collective-permute-start | bytes 1990664 | tf_op jit(solution)/shard_map/ppermute | solution.py:249
  125.3 3.2 %shard_map.105 = bf16[128,2304]{1,0:T(8,128)(2,1)S(1)} custom-call(bf16[128,2880]{1,0:T(8,128)(2,1)S(1)} %reshape.100.sent, f32[4,1152]{1,0:T(4,128)S(1)} %bitcast.18, bf16[576,1152]{1,0:T(8,128)(2,1)S(1)} %get-tuple-element.31.w_so, bf16[576,1152]{1,0:T(8,128)(2,1)S(1)} %get-tuple-element.32.w_out, bf16[1728,1152]{1,0:T(8,128)(2,1)S(1)} %get-tuple-element.33.w_qkv, ...), custom_call_target="tpu_custom_call" | custom-call | flops 4000000000 | bytes 10000000 | tf_op jit(solution)/shard_map/pallas_call | solution.py:215
  130.6 1.3 add_convert_fusion
  131.9 1.3 reshape.102
  133.2 2.2 %pad_maximum_fusion = bf16[64,2,4896]{2,1,0:T(2,128)(2,1)} fusion(bf16[64,2,2592]{2,1,0:T(2,128)(2,1)S(1)} %reshape.102, bf16[64,2,2304]{2,1,0:T(2,128)(2,1)S(1)} %copy-done.9), kind=kLoop, calls=%fused_computation.1 | loop fusion | flops 2506752 | bytes 2506752 | tf_op jit(solution)/shard_map/concatenate | solution.py:313
  135.4 13.8 %all-to-all-start.1 = ((bf16[64,2,4896]{2,1,0:T(2,128)(2,1)}), bf16[64,2,4896]{2,1,0:T(2,128)(2,1)}, u32[]{:S(2)}, u32[]{:S(2)}) async-start(bf16[64,2,4896]{2,1,0:T(2,128)(2,1)} %pad_maximum_fusion), calls=%async_computation.1 | async-start | bytes 2555904 | tf_op jit(solution)/shard_map/all_to_all | solution.py:227
  149.3 35.3 %all-to-all-done.1 = bf16[64,2,4896]{2,1,0:T(2,128)(2,1)} async-done(((bf16[64,2,4896]{2,1,0:T(2,128)(2,1)}), bf16[64,2,4896]{2,1,0:T(2,128)(2,1)}, u32[]{:S(2)}, u32[]{:S(2)}) %all-to-all-start.1) | async-done | bytes 1253408 | tf_op jit(solution)/shard_map/all_to_all | solution.py:227
  184.6 1.2 convert_reduce_fusion
  185.8 2.7 %collective-permute-start.9 = (f32[2,1152]{1,0:T(2,128)S(1)}, f32[2,1152]{1,0:T(2,128)S(1)}, u32[]{:S(2)}, u32[]{:S(2)}) collective-permute-start(f32[2,1152]{1,0:T(2,128)S(1)} %convert_reduce_fusion), channel_id=1, source_target_pairs={{0,1},{1,0},{2,3},{3,2},{4,5},{5,4},{6,7},{7,6},{8,9},{9,8},{10,11... | collective-permute-start | bytes 27656 | tf_op jit(solution)/shard_map/ppermute | solution.py:249
  188.5 1.6 slice.14
  191.6 4.2 %all-to-all-start.2 = ((bf16[8,2,5184]{2,1,0:T(2,128)(2,1)}), bf16[8,2,5184]{2,1,0:T(2,128)(2,1)S(1)}, u32[]{:S(2)}, u32[]{:S(2)}) async-start(bf16[8,2,5184]{2,1,0:T(2,128)(2,1)} %broadcast_in_dim.14), calls=%async_computation.2 | async-start | bytes 335872 | tf_op jit(solution)/shard_map/all_to_all | solution.py:318
  197.1 2.4 %shard_map.106 = bf16[128,1728]{1,0:T(8,128)(2,1)S(1)} custom-call(bf16[128,1728]{1,0:T(8,128)(2,1)S(1)} %bitcast.15, bf16[128,1152]{1,0:T(8,128)(2,1)S(1)} %reshape.103.hidden_grad, f32[4,1152]{1,0:T(4,128)S(1)} %bitcast.19, bf16[576,1152]{1,0:T(8,128)(2,1)S(1)} %copy-done.4), custom_call_target="tpu_custom_call" | custom-call | flops 1000000000 | bytes 10000000 | tf_op jit(solution)/shard_map/pallas_call | solution.py:215
  (52 shorter events, 13.1 us)
Async XLA Ops:
  0.6 38.0 %copy-start.10 = (bf16[1,1,128,1152]{3,2,1,0:T(8,128)(2,1)S(1)}, bf16[1,1,128,1152]{3,2,1,0:T(8,128)(2,1)}, u32[]{:S(2)}) copy-start(bf16[1,1,128,1152]{3,2,1,0:T(8,128)(2,1)} %param.7) | copy-start | bytes 884740
  0.6 38.1 %copy-start.11 = (bf16[1,1,128,1152]{3,2,1,0:T(8,128)(2,1)S(1)}, bf16[1,1,128,1152]{3,2,1,0:T(8,128)(2,1)}, u32[]{:S(2)}) copy-start(bf16[1,1,128,1152]{3,2,1,0:T(8,128)(2,1)} %param.13) | copy-start | bytes 884740
  1.8 0.7 collective-permute-start
  30.8 12.5 %collective-permute-start.1 = (bf16[384,1152]{1,0:T(8,128)(2,1)S(1)}, bf16[384,1152]{1,0:T(8,128)(2,1)S(1)}, u32[]{:S(2)}, u32[]{:S(2)}) collective-permute-start(bf16[384,1152]{1,0:T(8,128)(2,1)S(1)} %all_gather.3.mine), channel_id=1, source_target_pairs={{0,1},{1,0},{2,3},{3,2},{4,5},{5,4},{6,7},{7,6},{8,9},{9,8},{10,11... | collective-permute-start | bytes 2654216 | tf_op jit(solution)/shard_map/ppermute | solution.py:249
  45.6 1.0 copy-start.5
  46.5 0.7 copy-start.7
  47.3 65.2 %copy-start.2 = (f32[1,4,1152]{2,1,0:T(4,128)S(1)}, f32[1,4,1152]{2,1,0:T(4,128)}, u32[]{:S(2)}) copy-start(f32[1,4,1152]{2,1,0:T(4,128)} %param.12) | copy-start | bytes 55300
  47.3 55.3 %all-to-all-start = ((bf16[64,2,2880]{2,1,0:T(2,128)(2,1)}), bf16[64,2,2880]{2,1,0:T(2,128)(2,1)}, u32[]{:S(2)}, u32[]{:S(2)}) async-start(bf16[64,2,2880]{2,1,0:T(2,128)(2,1)} %pad_maximum_fusion.1), calls=%async_computation | async-start | bytes 1507328 | tf_op jit(solution)/shard_map/all_to_all | solution.py:227
  68.4 29.1 %collective-permute-start.4 = (bf16[384,1152]{1,0:T(8,128)(2,1)}, bf16[384,1152]{1,0:T(8,128)(2,1)S(1)}, u32[]{:S(2)}, u32[]{:S(2)}) collective-permute-start(bf16[384,1152]{1,0:T(8,128)(2,1)} %get-tuple-element.24), channel_id=1, source_target_pairs={{192,0},{497,1},{194,2},{499,3},{196,4},{501,5},{198,6},{503,7},{2... | collective-permute-start | bytes 2654216 | tf_op jit(solution)/shard_map/ppermute | solution.py:245
  70.4 29.1 %collective-permute-start.3 = (bf16[384,1152]{1,0:T(8,128)(2,1)}, bf16[384,1152]{1,0:T(8,128)(2,1)}, u32[]{:S(2)}, u32[]{:S(2)}) collective-permute-start(bf16[384,1152]{1,0:T(8,128)(2,1)} %get-tuple-element.24), channel_id=1, source_target_pairs={{128,0},{385,1},{130,2},{387,3},{132,4},{389,5},{134,6},{391,7},{1... | collective-permute-start | bytes 2654216 | tf_op jit(solution)/shard_map/ppermute | solution.py:245
  76.3 31.7 %collective-permute-start.2 = (bf16[384,1152]{1,0:T(8,128)(2,1)}, bf16[384,1152]{1,0:T(8,128)(2,1)}, u32[]{:S(2)}, u32[]{:S(2)}) collective-permute-start(bf16[384,1152]{1,0:T(8,128)(2,1)} %get-tuple-element.24), channel_id=1, source_target_pairs={{64,0},{113,1},{66,2},{115,3},{68,4},{117,5},{70,6},{119,7},{72,8}... | collective-permute-start | bytes 2654216 | tf_op jit(solution)/shard_map/ppermute | solution.py:245
  97.5 15.0 %copy-start = (bf16[384,1152]{1,0:T(8,128)(2,1)}, bf16[384,1152]{1,0:T(8,128)(2,1)S(1)}, u32[]{:S(2)}) copy-start(bf16[384,1152]{1,0:T(8,128)(2,1)S(1)} %collective-permute-done.4.d) | copy-start | bytes 2654212
  97.5 12.4 %collective-permute-start.7 = (bf16[384,1152]{1,0:T(8,128)(2,1)S(1)}, bf16[384,1152]{1,0:T(8,128)(2,1)}, u32[]{:S(2)}, u32[]{:S(2)}) collective-permute-start(bf16[384,1152]{1,0:T(8,128)(2,1)S(1)} %collective-permute-done.4.d), channel_id=1, source_target_pairs={{0,1},{1,0},{2,3},{3,2},{4,5},{5,4},{6,7},{7,6},{8,9},{9,8},{10,11... | collective-permute-start | bytes 2654216 | tf_op jit(solution)/shard_map/ppermute | solution.py:249
  99.4 10.5 %collective-permute-start.5 = (bf16[384,1152]{1,0:T(8,128)(2,1)}, bf16[384,1152]{1,0:T(8,128)(2,1)}, u32[]{:S(2)}, u32[]{:S(2)}) collective-permute-start(bf16[384,1152]{1,0:T(8,128)(2,1)} %collective-permute-done.3.b), channel_id=1, source_target_pairs={{0,1},{1,0},{2,3},{3,2},{4,5},{5,4},{6,7},{7,6},{8,9},{9,8},{10,11... | collective-permute-start | bytes 2654216 | tf_op jit(solution)/shard_map/ppermute | solution.py:249
  108.0 4.5 %collective-permute-start.6 = (bf16[384,1152]{1,0:T(8,128)(2,1)}, bf16[384,1152]{1,0:T(8,128)(2,1)S(1)}, u32[]{:S(2)}, u32[]{:S(2)}) collective-permute-start(bf16[384,1152]{1,0:T(8,128)(2,1)} %collective-permute-done.2.c), channel_id=1, source_target_pairs={{0,1},{1,0},{2,3},{3,2},{4,5},{5,4},{6,7},{7,6},{8,9},{9,8},{10,11... | collective-permute-start | bytes 2654216 | tf_op jit(solution)/shard_map/ppermute | solution.py:249
  112.5 1.2 copy-start.1
  113.7 1.2 copy-start.6
  114.9 1.0 copy-start.8
  123.1 7.5 %collective-permute-start.8 = (bf16[576,576]{1,0:T(8,128)(2,1)}, bf16[576,576]{1,0:T(8,128)(2,1)}, u32[]{:S(2)}, u32[]{:S(2)}) collective-permute-start(bf16[576,576]{1,0:T(8,128)(2,1)} %get-tuple-element.43), channel_id=1, source_target_pairs={{0,1},{1,0},{2,3},{3,2},{4,5},{5,4},{6,7},{7,6},{8,9},{9,8},{10,11... | collective-permute-start | bytes 1990664 | tf_op jit(solution)/shard_map/ppermute | solution.py:249
  128.5 1.1 copy-start.3
  130.6 2.6 %copy-start.9 = (bf16[64,2,2304]{2,1,0:T(2,128)(2,1)S(1)}, bf16[64,2,2304]{2,1,0:T(2,128)(2,1)}, u32[]{:S(2)}) copy-start(bf16[64,2,2304]{2,1,0:T(2,128)(2,1)} %reshape.101) | copy-start | bytes 1769476
  135.4 49.2 %all-to-all-start.1 = ((bf16[64,2,4896]{2,1,0:T(2,128)(2,1)}), bf16[64,2,4896]{2,1,0:T(2,128)(2,1)}, u32[]{:S(2)}, u32[]{:S(2)}) async-start(bf16[64,2,4896]{2,1,0:T(2,128)(2,1)} %pad_maximum_fusion), calls=%async_computation.1 | async-start | bytes 2555904 | tf_op jit(solution)/shard_map/all_to_all | solution.py:227
  185.8 15.4 %collective-permute-start.9 = (f32[2,1152]{1,0:T(2,128)S(1)}, f32[2,1152]{1,0:T(2,128)S(1)}, u32[]{:S(2)}, u32[]{:S(2)}) collective-permute-start(f32[2,1152]{1,0:T(2,128)S(1)} %convert_reduce_fusion), channel_id=1, source_target_pairs={{0,1},{1,0},{2,3},{3,2},{4,5},{5,4},{6,7},{7,6},{8,9},{9,8},{10,11... | collective-permute-start | bytes 27656 | tf_op jit(solution)/shard_map/ppermute | solution.py:249
  190.1 7.0 %copy-start.4 = (bf16[576,1152]{1,0:T(8,128)(2,1)S(1)}, bf16[576,1152]{1,0:T(8,128)(2,1)}, u32[]{:S(2)}) copy-start(bf16[576,1152]{1,0:T(8,128)(2,1)} %copy-done.3) | copy-start | bytes 3981316
  191.6 10.2 %all-to-all-start.2 = ((bf16[8,2,5184]{2,1,0:T(2,128)(2,1)}), bf16[8,2,5184]{2,1,0:T(2,128)(2,1)S(1)}, u32[]{:S(2)}, u32[]{:S(2)}) async-start(bf16[8,2,5184]{2,1,0:T(2,128)(2,1)} %broadcast_in_dim.14), calls=%async_computation.2 | async-start | bytes 335872 | tf_op jit(solution)/shard_map/all_to_all | solution.py:318

commit v11 on v10

--- a/solution.py
+++ b/solution.py
@@ -218,7 +218,7 @@
         in_specs=[pl.BlockSpec(memory_space=pltpu.SMEM)] * scalars + [vmem] * (len(args) - scalars),
         out_specs=[vmem] * len(outs),
         scratch_shapes=list(scratch),
-        compiler_params=pltpu.CompilerParams(vmem_limit_bytes=20 * 2**20),
+        compiler_params=pltpu.CompilerParams(vmem_limit_bytes=32 * 2**20),
         cost_estimate=pl.CostEstimate(flops=flops, bytes_accessed=10**7, transcendentals=10**5),
     )(*args)
 
@@ -265,7 +265,8 @@
 
 def gather_weights(w_so, w_qkv, w_out, place, sent):
     shard = jnp.concatenate([w_so, w_out, w_qkv.T, jnp.zeros((3, D), BF)], 0)
-    mine = lax.all_gather(receive(shard, class_source), "z", axis=0, tiled=True)
+    shard, sent = lax.optimization_barrier((receive(shard, class_source), sent))
+    mine = lax.all_gather(shard, "z", axis=0, tiled=True)
     other = swap_cores(mine)
     rows = lambda n: ((n, D), BF)
     own_so, own_out, own_qkv, part = call(
@@ -277,9 +278,9 @@
             pltpu.VMEM((432, D), F32),
         ],
     )
+    part, sent = lax.optimization_barrier((part, sent))
     near = [receive(part, near_source(dx, dy)) for dx, dy in ((1, 0), (0, 1), (1, 1))]
-    sent = exchange(lax.optimization_barrier((part, sent))[1]).reshape(ROWS, 2 * D + ATT)
-    near[1], sent = lax.optimization_barrier((near[1], sent))
+    sent = exchange(sent).reshape(ROWS, 2 * D + ATT)
     return [own_qkv, own_so, own_out] + near + [swap_cores(a) for a in near], sent
 
 

time: 206 us -> 200 us (0.971)
  waiting for transfers between devices: 59.7 us -> 52.9 us
    all_to_all x2, starting transfers between devices: 35 us -> 19.4 us  [exchange(): return lax.all_to_all(a, SEQ, 0, 0, tiled=True)]
    ppermute x4, waiting for transfers between devices: 21.7 us -> 11.5 us  [receive(): return lax.ppermute(a, AXES, pairs)]
    all_to_all x1, starting transfers between devices: 4.16 us -> 11.7 us  [body(): lax.all_to_all(out_part, DP, 0, 0, tiled=True).astype(F32)]
    ppermute x4, starting transfers between devices: 11.1 us -> 17 us  [receive(): return lax.ppermute(a, AXES, pairs)]
    all_to_all x2, waiting for transfers between devices: 35.3 us -> 39.4 us  [exchange(): return lax.all_to_all(a, SEQ, 0, 0, tiled=True)]
    unnamed x26 -> x28, local copies, waits for them, and re-layouts: 8.32 us -> 8.06 us
  transfers between devices with their start and end apart: 13 -> 13, of which waited for: 4 -> 4; matrix products, arithmetic and copies ran while one was open for 6% -> 7% of each run, Pallas kernels for 3% -> 4%
where the time goes in v11:
time: 200 us; the launch traced here: 196 us
  starting transfers between devices  69.3 us (35%)
  waiting for transfers between devices  52.9 us (26%)
  blocking collectives  28.4 us (14%)
  local copies, waits for them, and re-layouts  20.3 us (10%)
  Pallas kernels  15.8 us (8%)
  other arithmetic  8.77 us (4%)
    all_to_all x2, waiting for transfers between devices, exchange(): return lax.all_to_all(a, SEQ, 0, 0, tiled=True)  39.4 us
    all_gather x1, blocking collectives, gather_weights(): mine = lax.all_gather(shard, 'z', axis=0, tiled=True)  28.4 us
    ppermute x6, starting transfers between devices, swap_cores(): return lax.ppermute(a, 'core', [(0, 1), (1, 0)])  21 us
    all_to_all x2, starting transfers between devices, exchange(): return lax.all_to_all(a, SEQ, 0, 0, tiled=True)  19.4 us
    ppermute x4, starting transfers between devices, receive(): return lax.ppermute(a, AXES, pairs)  17 us
    pallas_call x5, Pallas kernels, call(): pl.pallas_call(kernel, out_shape=[jax.ShapeDtypeStruct(s, d) for s, d in...  15.8 us
    all_to_all x1, starting transfers between devices, body(): lax.all_to_all(out_part, DP, 0, 0, tiled=True).astype(F32)  11.7 us
    ppermute x4, waiting for transfers between devices, receive(): return lax.ppermute(a, AXES, pairs)  11.5 us
  transfers between devices with their start and end apart: 13, of which 4 were waited for; matrix products, arithmetic and copies ran while one was open for 7% of the time, Pallas kernels for 4%

profile of v11, /device:TPU:1, one launch (start us, length us, event | category | flops | bytes accessed | tf_op | source)
XLA Modules:
  0.0 196.5 jit_solution(8486647763443392134)
XLA Ops:
  4.8 1.5 shard_map.102
  6.4 1.6 pad_maximum_fusion.1
  8.0 28.4 %all_gather.3.mine = bf16[384,1152]{1,0:T(8,128)(2,1)S(1)} all-gather(bf16[48,1152]{1,0:T(8,128)(2,1)S(1)} %collective-permute-done), channel_id=1, replica_groups=mesh['x'=4,'ylo'=2,'yhi'=4,'z'=8,'core'=2] {'z'}, dimensions={0}, use_global_device_ids=true | all-gather | bytes 995328 | tf_op jit(solution)/shard_map/all_gather | solution.py:269
  36.4 7.8 %collective-permute-start.1 = (bf16[384,1152]{1,0:T(8,128)(2,1)S(1)}, bf16[384,1152]{1,0:T(8,128)(2,1)S(1)}, u32[]{:S(2)}, u32[]{:S(2)}) collective-permute-start(bf16[384,1152]{1,0:T(8,128)(2,1)S(1)} %all_gather.3.mine), channel_id=1, source_target_pairs={{0,1},{1,0},{2,3},{3,2},{4,5},{5,4},{6,7},{7,6},{8,9},{9,8},{10,11... | collective-permute-start | bytes 2654216 | tf_op jit(solution)/shard_map/ppermute | solution.py:249
  44.2 1.9 collective-permute-done.1.other
  46.2 1.3 shard_map.103
  49.9 11.3 %collective-permute-start.4 = (bf16[384,1152]{1,0:T(8,128)(2,1)S(1)}, bf16[384,1152]{1,0:T(8,128)(2,1)S(1)}, u32[]{:S(2)}, u32[]{:S(2)}) collective-permute-start(bf16[384,1152]{1,0:T(8,128)(2,1)S(1)} %get-tuple-element.32), channel_id=1, source_target_pairs={{192,0},{497,1},{194,2},{499,3},{196,4},{501,5},{198,6},{503,7},{2... | collective-permute-start | bytes 2654216 | tf_op jit(solution)/shard_map/ppermute | solution.py:245
  61.2 3.2 %collective-permute-start.3 = (bf16[384,1152]{1,0:T(8,128)(2,1)S(1)}, bf16[384,1152]{1,0:T(8,128)(2,1)}, u32[]{:S(2)}, u32[]{:S(2)}) collective-permute-start(bf16[384,1152]{1,0:T(8,128)(2,1)S(1)} %get-tuple-element.32), channel_id=1, source_target_pairs={{64,0},{113,1},{66,2},{115,3},{68,4},{117,5},{70,6},{119,7},{72,8}... | collective-permute-start | bytes 2654216 | tf_op jit(solution)/shard_map/ppermute | solution.py:245
  64.4 1.9 collective-permute-start.2
  66.3 9.6 %all-to-all-start = ((bf16[64,2,2880]{2,1,0:T(2,128)(2,1)}), bf16[64,2,2880]{2,1,0:T(2,128)(2,1)}, u32[]{:S(2)}, u32[]{:S(2)}) async-start(bf16[64,2,2880]{2,1,0:T(2,128)(2,1)} %pad_maximum_fusion.1), calls=%async_computation | async-start | bytes 1507328 | tf_op jit(solution)/shard_map/all_to_all | solution.py:227
  75.9 2.4 %collective-permute-start.7 = (bf16[384,1152]{1,0:T(8,128)(2,1)S(1)}, bf16[384,1152]{1,0:T(8,128)(2,1)}, u32[]{:S(2)}, u32[]{:S(2)}) collective-permute-start(bf16[384,1152]{1,0:T(8,128)(2,1)S(1)} %collective-permute-done.4.d), channel_id=1, source_target_pairs={{0,1},{1,0},{2,3},{3,2},{4,5},{5,4},{6,7},{7,6},{8,9},{9,8},{10,11... | collective-permute-start | bytes 2654216 | tf_op jit(solution)/shard_map/ppermute | solution.py:249
  78.4 11.5 %collective-permute-done.3.c = bf16[384,1152]{1,0:T(8,128)(2,1)} collective-permute-done((bf16[384,1152]{1,0:T(8,128)(2,1)S(1)}, bf16[384,1152]{1,0:T(8,128)(2,1)}, u32[]{:S(2)}, u32[]{:S(2)}) %collective-permute-start.3) | collective-permute-done | bytes 884768 | tf_op jit(solution)/shard_map/ppermute | solution.py:245
  89.9 4.8 %collective-permute-start.6 = (bf16[384,1152]{1,0:T(8,128)(2,1)}, bf16[384,1152]{1,0:T(8,128)(2,1)}, u32[]{:S(2)}, u32[]{:S(2)}) collective-permute-start(bf16[384,1152]{1,0:T(8,128)(2,1)} %collective-permute-done.3.c), channel_id=1, source_target_pairs={{0,1},{1,0},{2,3},{3,2},{4,5},{5,4},{6,7},{7,6},{8,9},{9,8},{10,11... | collective-permute-start | bytes 2654216 | tf_op jit(solution)/shard_map/ppermute | solution.py:249
  94.7 2.1 %collective-permute-start.5 = (bf16[384,1152]{1,0:T(8,128)(2,1)}, bf16[384,1152]{1,0:T(8,128)(2,1)}, u32[]{:S(2)}, u32[]{:S(2)}) collective-permute-start(bf16[384,1152]{1,0:T(8,128)(2,1)} %collective-permute-done.2.b), channel_id=1, source_target_pairs={{0,1},{1,0},{2,3},{3,2},{4,5},{5,4},{6,7},{7,6},{8,9},{9,8},{10,11... | collective-permute-start | bytes 2654216 | tf_op jit(solution)/shard_map/ppermute | solution.py:249
  96.8 3.8 %all-to-all-done = bf16[64,2,2880]{2,1,0:T(2,128)(2,1)} async-done(((bf16[64,2,2880]{2,1,0:T(2,128)(2,1)}), bf16[64,2,2880]{2,1,0:T(2,128)(2,1)}, u32[]{:S(2)}, u32[]{:S(2)}) %all-to-all-start) | async-done | bytes 737312 | tf_op jit(solution)/shard_map/all_to_all | solution.py:227
  100.6 2.2 %reshape.100.sent = bf16[128,2880]{1,0:T(8,128)(2,1)S(1)} reshape(bf16[64,2,2880]{2,1,0:T(2,128)(2,1)} %all-to-all-done) | data formatting | bytes 1474560 | tf_op jit(solution)/shard_map/reshape | solution.py:283
  102.9 1.2 copy-done.1
  104.1 1.2 copy-done.6
  106.3 7.5 %shard_map.104 = (f32[576,576]{1,0:T(8,128)S(1)}, bf16[576,576]{1,0:T(8,128)(2,1)}, bf16[576,1152]{1,0:T(8,128)(2,1)S(1)}, bf16[576,1152]{1,0:T(8,128)(2,1)S(1)}...) custom-call(s32[2]{0:T(128)S(1)} %pad_add_fusion.place, ...), custom_call_target="tpu_custom_call" | custom-call | flops 4000000000 | bytes 10000000 | tf_op jit(solution)/shard_map/pallas_call | solution.py:215
  113.7 2.1 %collective-permute-start.8 = (bf16[576,576]{1,0:T(8,128)(2,1)}, bf16[576,576]{1,0:T(8,128)(2,1)}, u32[]{:S(2)}, u32[]{:S(2)}) collective-permute-start(bf16[576,576]{1,0:T(8,128)(2,1)} %get-tuple-element.45), channel_id=1, source_target_pairs={{0,1},{1,0},{2,3},{3,2},{4,5},{5,4},{6,7},{7,6},{8,9},{9,8},{10,11... | collective-permute-start | bytes 1990664 | tf_op jit(solution)/shard_map/ppermute | solution.py:249
  115.8 3.2 %shard_map.105 = bf16[128,2304]{1,0:T(8,128)(2,1)S(1)} custom-call(bf16[128,2880]{1,0:T(8,128)(2,1)S(1)} %reshape.100.sent, f32[4,1152]{1,0:T(4,128)S(1)} %bitcast.18, bf16[576,1152]{1,0:T(8,128)(2,1)S(1)} %get-tuple-element.33.w_so, bf16[576,1152]{1,0:T(8,128)(2,1)S(1)} %get-tuple-element.34.w_out, bf16[1728,1152]{1,0:T(8,128)(2,1)S(1)} %get-tuple-element.35.w_qkv, ...), custom_call_target="tpu_custom_call" | custom-call | flops 4000000000 | bytes 10000000 | tf_op jit(solution)/shard_map/pallas_call | solution.py:215
  121.1 1.3 add_convert_fusion
  122.5 1.3 reshape.102
  123.8 2.2 %pad_maximum_fusion = bf16[64,2,4896]{2,1,0:T(2,128)(2,1)} fusion(bf16[64,2,2592]{2,1,0:T(2,128)(2,1)S(1)} %reshape.102, bf16[64,2,2304]{2,1,0:T(2,128)(2,1)S(1)} %copy-done.11), kind=kLoop, calls=%fused_computation.1 | loop fusion | flops 2506752 | bytes 2506752 | tf_op jit(solution)/shard_map/concatenate | solution.py:314
  126.0 9.8 %all-to-all-start.1 = ((bf16[64,2,4896]{2,1,0:T(2,128)(2,1)}), bf16[64,2,4896]{2,1,0:T(2,128)(2,1)}, u32[]{:S(2)}, u32[]{:S(2)}) async-start(bf16[64,2,4896]{2,1,0:T(2,128)(2,1)} %pad_maximum_fusion), calls=%async_computation.1 | async-start | bytes 2555904 | tf_op jit(solution)/shard_map/all_to_all | solution.py:227
  135.8 35.6 %all-to-all-done.1 = bf16[64,2,4896]{2,1,0:T(2,128)(2,1)} async-done(((bf16[64,2,4896]{2,1,0:T(2,128)(2,1)}), bf16[64,2,4896]{2,1,0:T(2,128)(2,1)}, u32[]{:S(2)}, u32[]{:S(2)}) %all-to-all-start.1) | async-done | bytes 1253408 | tf_op jit(solution)/shard_map/all_to_all | solution.py:227
  171.4 1.2 convert_reduce_fusion
  172.6 1.9 collective-permute-start.9
  174.6 1.6 slice.14
  177.6 11.7 %all-to-all-start.2 = ((bf16[8,2,5184]{2,1,0:T(2,128)(2,1)}), bf16[8,2,5184]{2,1,0:T(2,128)(2,1)S(1)}, u32[]{:S(2)}, u32[]{:S(2)}) async-start(bf16[8,2,5184]{2,1,0:T(2,128)(2,1)} %broadcast_in_dim.14), calls=%async_computation.2 | async-start | bytes 335872 | tf_op jit(solution)/shard_map/all_to_all | solution.py:319
  189.4 1.2 slice.12
  190.7 2.4 %shard_map.106 = bf16[128,1728]{1,0:T(8,128)(2,1)S(1)} custom-call(bf16[128,1728]{1,0:T(8,128)(2,1)S(1)} %bitcast.15, bf16[128,1152]{1,0:T(8,128)(2,1)S(1)} %reshape.103.hidden_grad, f32[4,1152]{1,0:T(4,128)S(1)} %bitcast.19, bf16[576,1152]{1,0:T(8,128)(2,1)S(1)} %copy-done.4), custom_call_target="tpu_custom_call" | custom-call | flops 1000000000 | bytes 10000000 | tf_op jit(solution)/shard_map/pallas_call | solution.py:215
  (54 shorter events, 14.8 us)
Async XLA Ops:
  0.6 3.9 %copy-start.12 = (bf16[1,1,128,1728]{2,3,1,0:T(8,128)(2,1)S(1)}, bf16[1,1,128,1728]{2,3,1,0:T(8,128)(2,1)}, u32[]{:S(2)}) copy-start(bf16[1,1,128,1728]{2,3,1,0:T(8,128)(2,1)} %param.8) | copy-start | bytes 1327108
  1.7 6.3 %collective-permute-start = (bf16[48,1152]{1,0:T(8,128)(2,1)S(1)}, bf16[48,1152]{1,0:T(8,128)(2,1)S(1)}, u32[]{:S(2)}, u32[]{:S(2)}) collective-permute-start(bf16[48,1152]{1,0:T(8,128)(2,1)S(1)} %maximum_maximum_fusion), channel_id=1, source_target_pairs={{0,0},{1,1},{2,2},{3,3},{4,4},{5,5},{6,6},{7,7},{8,8},{9,9},{10,10... | collective-permute-start | bytes 331784 | tf_op jit(solution)/shard_map/ppermute | solution.py:245
  36.4 9.8 %collective-permute-start.1 = (bf16[384,1152]{1,0:T(8,128)(2,1)S(1)}, bf16[384,1152]{1,0:T(8,128)(2,1)S(1)}, u32[]{:S(2)}, u32[]{:S(2)}) collective-permute-start(bf16[384,1152]{1,0:T(8,128)(2,1)S(1)} %all_gather.3.mine), channel_id=1, source_target_pairs={{0,1},{1,0},{2,3},{3,2},{4,5},{5,4},{6,7},{7,6},{8,9},{9,8},{10,11... | collective-permute-start | bytes 2654216 | tf_op jit(solution)/shard_map/ppermute | solution.py:249
  47.4 1.0 copy-start.5
  48.4 0.7 copy-start.7
  49.1 0.8 copy-start.9
  49.9 53.0 %copy-start.2 = (f32[1,4,1152]{2,1,0:T(4,128)S(1)}, f32[1,4,1152]{2,1,0:T(4,128)}, u32[]{:S(2)}) copy-start(f32[1,4,1152]{2,1,0:T(4,128)} %param.12) | copy-start | bytes 55300
  49.9 26.0 %collective-permute-start.4 = (bf16[384,1152]{1,0:T(8,128)(2,1)S(1)}, bf16[384,1152]{1,0:T(8,128)(2,1)S(1)}, u32[]{:S(2)}, u32[]{:S(2)}) collective-permute-start(bf16[384,1152]{1,0:T(8,128)(2,1)S(1)} %get-tuple-element.32), channel_id=1, source_target_pairs={{192,0},{497,1},{194,2},{499,3},{196,4},{501,5},{198,6},{503,7},{2... | collective-permute-start | bytes 2654216 | tf_op jit(solution)/shard_map/ppermute | solution.py:245
  61.2 28.7 %collective-permute-start.3 = (bf16[384,1152]{1,0:T(8,128)(2,1)S(1)}, bf16[384,1152]{1,0:T(8,128)(2,1)}, u32[]{:S(2)}, u32[]{:S(2)}) collective-permute-start(bf16[384,1152]{1,0:T(8,128)(2,1)S(1)} %get-tuple-element.32), channel_id=1, source_target_pairs={{64,0},{113,1},{66,2},{115,3},{68,4},{117,5},{70,6},{119,7},{72,8}... | collective-permute-start | bytes 2654216 | tf_op jit(solution)/shard_map/ppermute | solution.py:245
  64.4 30.3 %collective-permute-start.2 = (bf16[384,1152]{1,0:T(8,128)(2,1)S(1)}, bf16[384,1152]{1,0:T(8,128)(2,1)}, u32[]{:S(2)}, u32[]{:S(2)}) collective-permute-start(bf16[384,1152]{1,0:T(8,128)(2,1)S(1)} %get-tuple-element.32), channel_id=1, source_target_pairs={{128,0},{385,1},{130,2},{387,3},{132,4},{389,5},{134,6},{391,7},{1... | collective-permute-start | bytes 2654216 | tf_op jit(solution)/shard_map/ppermute | solution.py:245
  66.3 34.3 %all-to-all-start = ((bf16[64,2,2880]{2,1,0:T(2,128)(2,1)}), bf16[64,2,2880]{2,1,0:T(2,128)(2,1)}, u32[]{:S(2)}, u32[]{:S(2)}) async-start(bf16[64,2,2880]{2,1,0:T(2,128)(2,1)} %pad_maximum_fusion.1), calls=%async_computation | async-start | bytes 1507328 | tf_op jit(solution)/shard_map/all_to_all | solution.py:227
  75.9 26.9 %copy-start = (bf16[384,1152]{1,0:T(8,128)(2,1)}, bf16[384,1152]{1,0:T(8,128)(2,1)S(1)}, u32[]{:S(2)}) copy-start(bf16[384,1152]{1,0:T(8,128)(2,1)S(1)} %collective-permute-done.4.d) | copy-start | bytes 2654212
  75.9 26.9 %collective-permute-start.7 = (bf16[384,1152]{1,0:T(8,128)(2,1)S(1)}, bf16[384,1152]{1,0:T(8,128)(2,1)}, u32[]{:S(2)}, u32[]{:S(2)}) collective-permute-start(bf16[384,1152]{1,0:T(8,128)(2,1)S(1)} %collective-permute-done.4.d), channel_id=1, source_target_pairs={{0,1},{1,0},{2,3},{3,2},{4,5},{5,4},{6,7},{7,6},{8,9},{9,8},{10,11... | collective-permute-start | bytes 2654216 | tf_op jit(solution)/shard_map/ppermute | solution.py:249
  89.9 13.0 %collective-permute-start.6 = (bf16[384,1152]{1,0:T(8,128)(2,1)}, bf16[384,1152]{1,0:T(8,128)(2,1)}, u32[]{:S(2)}, u32[]{:S(2)}) collective-permute-start(bf16[384,1152]{1,0:T(8,128)(2,1)} %collective-permute-done.3.c), channel_id=1, source_target_pairs={{0,1},{1,0},{2,3},{3,2},{4,5},{5,4},{6,7},{7,6},{8,9},{9,8},{10,11... | collective-permute-start | bytes 2654216 | tf_op jit(solution)/shard_map/ppermute | solution.py:249
  94.7 8.2 %copy-start.8 = (bf16[144,1152]{1,0:T(8,128)(2,1)S(1)}, bf16[144,1152]{1,0:T(8,128)(2,1)}, u32[]{:S(2)}) copy-start(bf16[144,1152]{1,0:T(8,128)(2,1)} %copy-done.7) | copy-start | bytes 995332
  94.7 8.1 %collective-permute-start.5 = (bf16[384,1152]{1,0:T(8,128)(2,1)}, bf16[384,1152]{1,0:T(8,128)(2,1)}, u32[]{:S(2)}, u32[]{:S(2)}) collective-permute-start(bf16[384,1152]{1,0:T(8,128)(2,1)} %collective-permute-done.2.b), channel_id=1, source_target_pairs={{0,1},{1,0},{2,3},{3,2},{4,5},{5,4},{6,7},{7,6},{8,9},{9,8},{10,11... | collective-permute-start | bytes 2654216 | tf_op jit(solution)/shard_map/ppermute | solution.py:249
  102.9 1.2 copy-start.1
  104.1 1.2 copy-start.6
  105.3 1.0 copy-start.10
  113.7 7.4 %collective-permute-start.8 = (bf16[576,576]{1,0:T(8,128)(2,1)}, bf16[576,576]{1,0:T(8,128)(2,1)}, u32[]{:S(2)}, u32[]{:S(2)}) collective-permute-start(bf16[576,576]{1,0:T(8,128)(2,1)} %get-tuple-element.45), channel_id=1, source_target_pairs={{0,1},{1,0},{2,3},{3,2},{4,5},{5,4},{6,7},{7,6},{8,9},{9,8},{10,11... | collective-permute-start | bytes 1990664 | tf_op jit(solution)/shard_map/ppermute | solution.py:249
  119.0 1.1 copy-start.3
  121.1 2.6 %copy-start.11 = (bf16[64,2,2304]{2,1,0:T(2,128)(2,1)S(1)}, bf16[64,2,2304]{2,1,0:T(2,128)(2,1)}, u32[]{:S(2)}) copy-start(bf16[64,2,2304]{2,1,0:T(2,128)(2,1)} %reshape.101) | copy-start | bytes 1769476
  126.0 45.4 %all-to-all-start.1 = ((bf16[64,2,4896]{2,1,0:T(2,128)(2,1)}), bf16[64,2,4896]{2,1,0:T(2,128)(2,1)}, u32[]{:S(2)}, u32[]{:S(2)}) async-start(bf16[64,2,4896]{2,1,0:T(2,128)(2,1)} %pad_maximum_fusion), calls=%async_computation.1 | async-start | bytes 2555904 | tf_op jit(solution)/shard_map/all_to_all | solution.py:227
  172.6 22.2 %collective-permute-start.9 = (f32[2,1152]{1,0:T(2,128)S(1)}, f32[2,1152]{1,0:T(2,128)S(1)}, u32[]{:S(2)}, u32[]{:S(2)}) collective-permute-start(f32[2,1152]{1,0:T(2,128)S(1)} %convert_reduce_fusion), channel_id=1, source_target_pairs={{0,1},{1,0},{2,3},{3,2},{4,5},{5,4},{6,7},{7,6},{8,9},{9,8},{10,11... | collective-permute-start | bytes 27656 | tf_op jit(solution)/shard_map/ppermute | solution.py:249
  176.1 14.5 %copy-start.4 = (bf16[576,1152]{1,0:T(8,128)(2,1)S(1)}, bf16[576,1152]{1,0:T(8,128)(2,1)}, u32[]{:S(2)}) copy-start(bf16[576,1152]{1,0:T(8,128)(2,1)} %copy-done.3) | copy-start | bytes 3981316
  177.6 17.8 %all-to-all-start.2 = ((bf16[8,2,5184]{2,1,0:T(2,128)(2,1)}), bf16[8,2,5184]{2,1,0:T(2,128)(2,1)S(1)}, u32[]{:S(2)}, u32[]{:S(2)}) async-start(bf16[8,2,5184]{2,1,0:T(2,128)(2,1)} %broadcast_in_dim.14), calls=%async_computation.2 | async-start | bytes 335872 | tf_op jit(solution)/shard_map/all_to_all | solution.py:319

commit v12 on v11

--- a/solution.py
+++ b/solution.py
@@ -119,36 +119,52 @@
 STEP = (208, 64, 64)
 
 
-def assemble(place, own, near, swapped, targets):
+COPIES = 6
+
+
+def start_copies(place, near, swapped, targets, sems):
     for me in range(2):
 
         @pl.when(place[0] == me)
         def _():
-            cls = place[1]
-            for section, ref in enumerate(own):
-                to = pl.multiple_of(cls * BLOCK[section], 16)
-                targets[section][pl.ds(to, BLOCK[section]), :] = ref[...]
-            for flip, ref, other in zip((2, 1, 3), near, swapped):
-                for half in range(2):
-                    source = ref if half == me else other
-                    for section, first, last in SECTIONS:
+            for section, first, last in (SECTIONS[1], SECTIONS[0], SECTIONS[2]):
+                for i, (flip, ref, other) in enumerate(zip((2, 1, 3), near, swapped)):
+                    for half in range(2):
+                        source = ref if half == me else other
                         skip = 16 * half
                         row = skip + STEP[section] * half
-                        to = pl.multiple_of((cls ^ flip) * BLOCK[section] + row, 16)
+                        to = pl.multiple_of((place[1] ^ flip) * BLOCK[section] + row, 16)
                         rows = last - first - skip
-                        targets[section][pl.ds(to, rows), :] = source[first + skip : last, :]
+                        pltpu.make_async_copy(
+                            source.at[pl.ds(first + skip, rows)],
+                            targets[section].at[pl.ds(to, rows)],
+                            sems.at[section * COPIES + 2 * i + half],
+                        ).start()
+
+
+def wait_copies(section, near, targets, sems):
+    first, last = SECTIONS[section][1:]
+    for i in range(3):
+        for half in range(2):
+            rows = pl.ds(0, last - first - 16 * half)
+            sem = sems.at[section * COPIES + 2 * i + half]
+            pltpu.make_async_copy(near[i].at[rows], targets[section].at[rows], sem).wait()
 
 
 def temporal_forward_kernel(
     place, sent, factors, own_qkv, own_so, own_out, b, c, d, other_b, other_c, other_d,
     out_keep, out_send, w_so, w_out, w_qkv, q_out, k_out, v_out, probs_out, mixed_out,
-    unit_out, inverse_out, project_out,
+    unit_out, inverse_out, project_out, cot_out, sems,
 ):
-    assemble(
-        place, (own_qkv, own_so, own_out), (b, c, d), (other_b, other_c, other_d),
-        (w_qkv, w_so, w_out),
-    )
-    tokens, cotangent, mixed_s = sent[:, :D], sent[:, D : 2 * D], sent[:, 2 * D :]
+    near, targets = (b, c, d), (w_qkv, w_so, w_out)
+    start_copies(place, near, (other_b, other_c, other_d), targets, sems)
+    for section, ref in enumerate((own_qkv, own_so, own_out)):
+        to = pl.multiple_of(place[1] * BLOCK[section], 16)
+        targets[section][pl.ds(to, BLOCK[section]), :] = ref[...]
+    received = sent[...].reshape(ROWS, 2 * D + ATT)
+    tokens, cotangent, mixed_s = received[:, :D], received[:, D : 2 * D], received[:, 2 * D :]
+    cot_out[...] = cotangent
+    wait_copies(1, near, targets, sems)
     gate_s, shift, scale, gate_t = (factors[i : i + 1, :] for i in range(4))
     project = nn(mixed_s, w_so[...])
     project_out[...] = project
@@ -159,6 +175,7 @@
     unit = centered * inverse
     unit_out[...] = unit
     normed = (unit * (1.0 + scale) + shift).astype(BF)
+    wait_copies(0, near, targets, sems)
     q, k, v = (nt(normed, w_qkv[i * ATT : (i + 1) * ATT, :]).astype(BF) for i in range(3))
     q_out[...], k_out[...], v_out[...] = q, k, v
 
@@ -170,17 +187,25 @@
     mixed_out[...] = mixed
 
     scaled = (cotangent.astype(F32) * gate_t).astype(BF)
+    source = lax.broadcasted_iota(jnp.int32, (ATT, ATT), 0)
+    target = lax.broadcasted_iota(jnp.int32, (ATT, ATT), 1)
+    order = jnp.where(source == (target & 63) * 9 + (target >> 6), 1.0, 0.0).astype(BF)
+    ordered = nn(mixed, order).astype(BF)
     left, right = scaled[:, :ATT], scaled[:, ATT:]
     first = place[0] == 0
-    out_keep[...] = tn(mixed, jnp.where(first, left, right))
-    out_send[...] = tn(mixed, jnp.where(first, right, left)).astype(BF)
+    keep = tn(ordered, jnp.where(first, left, right))
+    send = tn(ordered, jnp.where(first, right, left)).astype(BF)
+    for j in range(9):
+        out_keep[:, ATT * j : ATT * j + ATT] = keep[64 * j : 64 * j + 64]
+        out_send[:, ATT * j : ATT * j + ATT] = send[64 * j : 64 * j + 64]
+    wait_copies(2, near, targets, sems)
 
 
 def temporal_backward_kernel(
-    sent, factors, w_so, w_out, w_qkv, q, k, v, probs, mixed, unit, inverse, project, packed
+    factors, w_so, w_out, w_qkv, q, k, v, probs, mixed, unit, inverse, project, cotangent, packed
 ):
     scale, gate_t = factors[2:3, :], factors[3:4, :]
-    cot = sent[:, D : 2 * D].astype(F32)
+    cot = cotangent[...].astype(F32)
     scaled = (cot * gate_t).astype(BF)
     masks = head_masks()
     q, k, v, probs = q[...], k[...], v[...], probs[...]
@@ -210,12 +235,36 @@
         packed[16 * i : 16 * i + 16, D:] = tile
 
 
-def call(kernel, outs, *args, scalars=0, scratch=(), flops=10**9):
+HALF = 9 * ATT // 2
+
+
+def pack_kernel(packed, out_keep, out_other, out):
+    out[:, :, : 2 * D] = packed[...].reshape(64, 2, 2 * D)
+    pair = (out_keep[...] + out_other[...].astype(F32)).astype(BF)
+    out[:, 0, 2 * D :] = pair[:, :HALF]
+    out[:, 1, 2 * D :] = pair[:, HALF:]
+
+
+def unpack_kernel(back, token_grad, out_part, factor_part):
+    token_grad[...] = back[:, :, :D].reshape(ROWS, D)
+    first = lax.broadcasted_iota(jnp.int32, (64, HALF), 0) & 1 == 0
+    for r in range(2):
+        factor_part[r : r + 1, :] = jnp.sum(back[:, r, D : 2 * D].astype(F32), 0, keepdims=True)
+        rows = back[:, r, 2 * D :].astype(F32)
+        for core in range(2):
+            total = jnp.sum(jnp.where(first == (core == 0), rows, 0.0), 0, keepdims=True)
+            for copy in range(8):
+                out_part[copy, core : core + 1, HALF * r : HALF * r + HALF] = total
+
+
+def call(kernel, outs, *args, scalars=0, hbm=0, scratch=(), flops=10**9):
     vmem = pl.BlockSpec(memory_space=pltpu.VMEM)
+    specs = [pl.BlockSpec(memory_space=pltpu.SMEM)] * scalars
+    specs += [vmem] * (len(args) - scalars - hbm) + [pl.BlockSpec(memory_space=pltpu.HBM)] * hbm
     return pl.pallas_call(
         kernel,
         out_shape=[jax.ShapeDtypeStruct(s, d) for s, d in outs],
-        in_specs=[pl.BlockSpec(memory_space=pltpu.SMEM)] * scalars + [vmem] * (len(args) - scalars),
+        in_specs=specs,
         out_specs=[vmem] * len(outs),
         scratch_shapes=list(scratch),
         compiler_params=pltpu.CompilerParams(vmem_limit_bytes=32 * 2**20),
@@ -280,7 +329,7 @@
     )
     part, sent = lax.optimization_barrier((part, sent))
     near = [receive(part, near_source(dx, dy)) for dx, dy in ((1, 0), (0, 1), (1, 1))]
-    sent = exchange(sent).reshape(ROWS, 2 * D + ATT)
+    sent = exchange(sent)
     return [own_qkv, own_so, own_out] + near + [swap_cores(a) for a in near], sent
 
 
@@ -298,32 +347,33 @@
     out_keep, out_send, *saved = call(
         temporal_forward_kernel,
         [
-            ((ATT, ATT), F32), ((ATT, ATT), BF), ((ATT, D), BF), ((ATT, D), BF), ((3 * ATT, D), BF),
+            ((64, 2 * HALF), F32), ((64, 2 * HALF), BF),
+            ((ATT, D), BF), ((ATT, D), BF), ((3 * ATT, D), BF),
             rows(ATT), rows(ATT), rows(ATT), ((HEADS * ROWS, ROWS), F32), rows(ATT),
-            rows(D, F32), rows(128, F32), rows(D, F32),
+            rows(D, F32), rows(128, F32), rows(D, F32), rows(D),
         ],
         place, sent, factors, *weights,
-        scalars=1, flops=4 * 10**9,
+        scalars=1, hbm=6, flops=4 * 10**9,
+        scratch=[pltpu.SemaphoreType.DMA((3 * COPIES,))],
     )
     w_so = saved[0]
     out_other = swap_cores(out_send)
-    (packed,) = call(temporal_backward_kernel, [rows(2 * D)], sent, factors, *saved, flops=4 * 10**9)
-
-    half = 9 * ATT // 2
-    out_part = (out_keep + out_other.astype(F32)).astype(BF).reshape(64, 2, half)
-    back = exchange(jnp.concatenate([packed.reshape(64, 2, 2 * D), out_part], 2))
-
-    out_part = back[:, :, 2 * D :].astype(F32).reshape(32, 2, 2, half)
-    out_part = jnp.sum(out_part, 0).astype(BF).reshape(1, 2, 9 * ATT)
-    out_part = jnp.broadcast_to(out_part, (8, 2, 9 * ATT))
-    out_part = jnp.sum(lax.all_to_all(out_part, DP, 0, 0, tiled=True).astype(F32), 0)
+    (packed,) = call(temporal_backward_kernel, [rows(2 * D)], factors, *saved, flops=4 * 10**9)
+
+    (packed,) = call(
+        pack_kernel, [((64, 2, 2 * D + HALF), BF)], packed, out_keep, out_other, flops=10**8
+    )
+    token_grad, out_part, mine = call(
+        unpack_kernel,
+        [rows(D), ((8, 2, 2 * HALF), F32), ((2, D), F32)],
+        exchange(packed), flops=10**8,
+    )
+    out_part = jnp.sum(lax.all_to_all(out_part, DP, 0, 0, tiled=True), 0)
     out_grad = out_part.reshape(2, 9, ATT).transpose(1, 0, 2).reshape(9, D)
 
-    token_grad = back[:, :, :D].reshape(ROWS, D)
     (qkv_grad,) = call(
         spatial_backward_kernel, [((ROWS, 3 * ATT), BF)], qkv, token_grad, factors, w_so
     )
-    mine = jnp.sum(back[:, :, D : 2 * D].astype(F32), 0)
     other = swap_cores(mine)
     factor_grad = jnp.where(core == 0, jnp.concatenate([mine, other]), jnp.concatenate([other, mine]))
     return token_grad[None, None], qkv_grad[None, None], factor_grad[None], out_grad

time: 200 us -> 185 us (0.925)
  the two profiles are of different devices: /device:TPU:1 before, /device:TPU:169 now
where the time goes in v12:
time: 185 us; the launch traced here: 184 us
  blocking collectives  70.9 us (38%)
  starting transfers between devices  63.4 us (34%)
  Pallas kernels  19 us (10%)
  waiting for transfers between devices  16.9 us (9%)
  local copies, waits for them, and re-layouts  9.18 us (5%)
  other arithmetic  3.41 us (2%)
    all_to_all x1, blocking collectives, exchange(): return lax.all_to_all(a, SEQ, 0, 0, tiled=True)  47.1 us
    ppermute x6, starting transfers between devices, swap_cores(): return lax.ppermute(a, 'core', [(0, 1), (1, 0)])  26.1 us
    all_gather x1, blocking collectives, gather_weights(): mine = lax.all_gather(shard, 'z', axis=0, tiled=True)  23.9 us
    pallas_call x7, Pallas kernels, call(): pl.pallas_call(kernel, out_shape=[jax.ShapeDtypeStruct(s, d) for s, d in...  19 us
    all_to_all x1, waiting for transfers between devices, exchange(): return lax.all_to_all(a, SEQ, 0, 0, tiled=True)  14.5 us
    all_to_all x1, starting transfers between devices, exchange(): return lax.all_to_all(a, SEQ, 0, 0, tiled=True)  13.5 us
    ppermute x4, starting transfers between devices, receive(): return lax.ppermute(a, AXES, pairs)  12.1 us
    all_to_all x1, starting transfers between devices, body(): out_part = jnp.sum(lax.all_to_all(out_part, DP, 0, 0, tiled=True), 0)  11.7 us
  transfers between devices with their start and end apart: 12, of which 3 were waited for; matrix products, arithmetic and copies ran while one was open for 3% of the time, Pallas kernels for 4%

profile of v12, /device:TPU:169, one launch (start us, length us, event | category | flops | bytes accessed | tf_op | source)
XLA Modules:
  0.0 183.7 jit_solution(14999494408126861617)
XLA Ops:
  0.7 1.0 maximum_maximum_fusion
  1.7 3.7 %collective-permute-start = (bf16[48,1152]{1,0:T(8,128)(2,1)S(1)}, bf16[48,1152]{1,0:T(8,128)(2,1)S(1)}, u32[]{:S(2)}, u32[]{:S(2)}) collective-permute-start(bf16[48,1152]{1,0:T(8,128)(2,1)S(1)} %maximum_maximum_fusion), channel_id=1, source_target_pairs={{0,0},{1,1},{2,2},{3,3},{4,4},{5,5},{6,6},{7,7},{8,8},{9,9},{10,10... | collective-permute-start | bytes 331784 | tf_op jit(solution)/shard_map/ppermute | solution.py:294
  5.4 1.1 concatenate.38
  6.5 1.1 concatenate.39
  7.8 1.5 shard_map.102
  9.4 1.6 pad_maximum_fusion
  11.5 23.9 %all_gather.3.mine = bf16[384,1152]{1,0:T(8,128)(2,1)S(1)} all-gather(bf16[48,1152]{1,0:T(8,128)(2,1)S(1)} %collective-permute-done), channel_id=1, replica_groups=mesh['x'=4,'ylo'=2,'yhi'=4,'z'=8,'core'=2] {'z'}, dimensions={0}, use_global_device_ids=true | all-gather | bytes 995328 | tf_op jit(solution)/shard_map/all_gather | solution.py:318
  35.3 11.2 %collective-permute-start.1 = (bf16[384,1152]{1,0:T(8,128)(2,1)S(1)}, bf16[384,1152]{1,0:T(8,128)(2,1)S(1)}, u32[]{:S(2)}, u32[]{:S(2)}) collective-permute-start(bf16[384,1152]{1,0:T(8,128)(2,1)S(1)} %all_gather.3.mine), channel_id=1, source_target_pairs={{0,1},{1,0},{2,3},{3,2},{4,5},{5,4},{6,7},{7,6},{8,9},{9,8},{10,11... | collective-permute-start | bytes 2654216 | tf_op jit(solution)/shard_map/ppermute | solution.py:298
  46.6 1.9 %collective-permute-done.1.other = bf16[384,1152]{1,0:T(8,128)(2,1)S(1)} collective-permute-done((bf16[384,1152]{1,0:T(8,128)(2,1)S(1)}, bf16[384,1152]{1,0:T(8,128)(2,1)S(1)}, u32[]{:S(2)}, u32[]{:S(2)}) %collective-permute-start.1) | collective-permute-done | bytes 884768 | tf_op jit(solution)/shard_map/ppermute | solution.py:298
  48.5 2.2 %shard_map.103 = (bf16[144,1152]{1,0:T(8,128)(2,1)S(1)}, bf16[144,1152]{1,0:T(8,128)(2,1)S(1)}, bf16[432,1152]{1,0:T(8,128)(2,1)S(1)}, bf16[384,1152]{1,0:T(8,128)(2,1)}) custom-call(s32[2]{0:T(128)S(1)} %pad_add_fusion.place, bf16[384,1152]{1,0:T(8,128)(2,1)S(1)} %all_gather.3.mine, bf16[384,1152]{1,0:T(8,128)(2,1)S(1)} %collective-permute-done.1.other), custom_call_target="tpu_custom_call" | custom-call | flops 1000000000 | bytes 10000000 | tf_op jit(solution)/shard_map/pallas_call | solution.py:264
  50.7 1.0 copy-done.4
  52.4 2.0 %collective-permute-start.4 = (bf16[384,1152]{1,0:T(8,128)(2,1)}, bf16[384,1152]{1,0:T(8,128)(2,1)S(1)}, u32[]{:S(2)}, u32[]{:S(2)}) collective-permute-start(bf16[384,1152]{1,0:T(8,128)(2,1)} %get-tuple-element.36), channel_id=1, source_target_pairs={{192,0},{497,1},{194,2},{499,3},{196,4},{501,5},{198,6},{503,7},{2... | collective-permute-start | bytes 2654216 | tf_op jit(solution)/shard_map/ppermute | solution.py:294
  54.5 2.4 %collective-permute-start.3 = (bf16[384,1152]{1,0:T(8,128)(2,1)}, bf16[384,1152]{1,0:T(8,128)(2,1)S(1)}, u32[]{:S(2)}, u32[]{:S(2)}) collective-permute-start(bf16[384,1152]{1,0:T(8,128)(2,1)} %get-tuple-element.36), channel_id=1, source_target_pairs={{64,0},{113,1},{66,2},{115,3},{68,4},{117,5},{70,6},{119,7},{72,8}... | collective-permute-start | bytes 2654216 | tf_op jit(solution)/shard_map/ppermute | solution.py:294
  56.8 4.0 %collective-permute-start.2 = (bf16[384,1152]{1,0:T(8,128)(2,1)}, bf16[384,1152]{1,0:T(8,128)(2,1)}, u32[]{:S(2)}, u32[]{:S(2)}) collective-permute-start(bf16[384,1152]{1,0:T(8,128)(2,1)} %get-tuple-element.36), channel_id=1, source_target_pairs={{128,0},{385,1},{130,2},{387,3},{132,4},{389,5},{134,6},{391,7},{1... | collective-permute-start | bytes 2654216 | tf_op jit(solution)/shard_map/ppermute | solution.py:294
  60.9 13.5 %all-to-all-start = ((bf16[64,2,2880]{2,1,0:T(2,128)(2,1)}), bf16[64,2,2880]{2,1,0:T(2,128)(2,1)S(1)}, u32[]{:S(2)}, u32[]{:S(2)}) async-start(bf16[64,2,2880]{2,1,0:T(2,128)(2,1)} %pad_maximum_fusion), calls=%async_computation | async-start | bytes 1507328 | tf_op jit(solution)/shard_map/all_to_all | solution.py:276
  74.4 2.3 %collective-permute-start.7 = (bf16[384,1152]{1,0:T(8,128)(2,1)S(1)}, bf16[384,1152]{1,0:T(8,128)(2,1)}, u32[]{:S(2)}, u32[]{:S(2)}) collective-permute-start(bf16[384,1152]{1,0:T(8,128)(2,1)S(1)} %collective-permute-done.4.d), channel_id=1, source_target_pairs={{0,1},{1,0},{2,3},{3,2},{4,5},{5,4},{6,7},{7,6},{8,9},{9,8},{10,11... | collective-permute-start | bytes 2654216 | tf_op jit(solution)/shard_map/ppermute | solution.py:298
  76.7 3.1 %collective-permute-start.6 = (bf16[384,1152]{1,0:T(8,128)(2,1)S(1)}, bf16[384,1152]{1,0:T(8,128)(2,1)}, u32[]{:S(2)}, u32[]{:S(2)}) collective-permute-start(bf16[384,1152]{1,0:T(8,128)(2,1)S(1)} %collective-permute-done.3.c), channel_id=1, source_target_pairs={{0,1},{1,0},{2,3},{3,2},{4,5},{5,4},{6,7},{7,6},{8,9},{9,8},{10,11... | collective-permute-start | bytes 2654216 | tf_op jit(solution)/shard_map/ppermute | solution.py:298
  79.8 1.9 %collective-permute-start.5 = (bf16[384,1152]{1,0:T(8,128)(2,1)}, bf16[384,1152]{1,0:T(8,128)(2,1)}, u32[]{:S(2)}, u32[]{:S(2)}) collective-permute-start(bf16[384,1152]{1,0:T(8,128)(2,1)} %collective-permute-done.2.b), channel_id=1, source_target_pairs={{0,1},{1,0},{2,3},{3,2},{4,5},{5,4},{6,7},{7,6},{8,9},{9,8},{10,11... | collective-permute-start | bytes 2654216 | tf_op jit(solution)/shard_map/ppermute | solution.py:298
  81.8 14.5 %all-to-all-done.sent = bf16[64,2,2880]{2,1,0:T(2,128)(2,1)S(1)} async-done(((bf16[64,2,2880]{2,1,0:T(2,128)(2,1)}), bf16[64,2,2880]{2,1,0:T(2,128)(2,1)S(1)}, u32[]{:S(2)}, u32[]{:S(2)}) %all-to-all-start) | async-done | bytes 737312 | tf_op jit(solution)/shard_map/all_to_all | solution.py:276
  96.3 1.2 copy-done.5
  97.5 1.0 copy-done.7
  98.5 7.0 %shard_map.104 = (f32[64,5184]{1,0:T(8,128)S(1)}, bf16[64,5184]{1,0:T(8,128)(2,1)S(1)}, bf16[576,1152]{1,0:T(8,128)(2,1)S(1)}, bf16[576,1152]{1,0:T(8,128)(2,1)S...) custom-call(s32[2]{0:T(128)S(1)} %pad_add_fusion.place, ...), custom_call_target="tpu_custom_call" | custom-call | flops 4000000000 | bytes 10000000 | tf_op jit(solution)/shard_map/pallas_call | solution.py:264
  105.5 2.9 %collective-permute-start.8 = (bf16[64,5184]{1,0:T(8,128)(2,1)S(1)}, bf16[64,5184]{1,0:T(8,128)(2,1)S(1)}, u32[]{:S(2)}, u32[]{:S(2)}) collective-permute-start(bf16[64,5184]{1,0:T(8,128)(2,1)S(1)} %get-tuple-element.50), channel_id=1, source_target_pairs={{0,1},{1,0},{2,3},{3,2},{4,5},{5,4},{6,7},{7,6},{8,9},{9,8},{10,11... | collective-permute-start | bytes 1990664 | tf_op jit(solution)/shard_map/ppermute | solution.py:298
  108.5 3.2 %shard_map.105.packed = bf16[128,2304]{1,0:T(8,128)(2,1)S(1)} custom-call(f32[4,1152]{1,0:T(4,128)S(1)} %bitcast.20, bf16[576,1152]{1,0:T(8,128)(2,1)S(1)} %get-tuple-element.37.w_so, bf16[576,1152]{1,0:T(8,128)(2,1)S(1)} %get-tuple-element.38.w_out, bf16[1728,1152]{1,0:T(8,128)(2,1)S(1)} %get-tuple-element.39.w_qkv, ...), custom_call_target="tpu_custom_call" | custom-call | flops 4000000000 | bytes 10000000 | tf_op jit(solution)/shard_map/pallas_call | solution.py:264
  112.3 47.1 %all_to_all.15.back = bf16[64,2,4896]{2,1,0:T(2,128)(2,1)S(1)} all-to-all(bf16[64,2,4896]{2,1,0:T(2,128)(2,1)S(1)} %shard_map.106), channel_id=1, replica_groups=mesh['x'=4,'ylo'=2,'yhi'=4,'z'=8,'core'=2] {'yhi','z','core'}, dimensions={0} | all-to-all | bytes 2506752 | tf_op jit(solution)/shard_map/all_to_all | solution.py:276
  159.4 2.1 %shard_map.107 = (bf16[128,1152]{1,0:T(8,128)(2,1)}, f32[8,2,5184]{2,1,0:T(2,128)}, f32[2,1152]{1,0:T(2,128)S(1)}) custom-call(bf16[64,2,4896]{2,1,0:T(2,128)(2,1)S(1)} %all_to_all.15.back), custom_call_target="tpu_custom_call" | custom-call | flops 100000000 | bytes 10000000 | tf_op jit(solution)/shard_map/pallas_call | solution.py:264
  161.5 11.7 %all-to-all-start.2 = ((f32[8,2,5184]{2,1,0:T(2,128)}), f32[8,2,5184]{2,1,0:T(2,128)S(1)}, u32[]{:S(2)}, u32[]{:S(2)}) async-start(f32[8,2,5184]{2,1,0:T(2,128)} %get-tuple-element.53), calls=%async_computation.2 | async-start | bytes 671744 | tf_op jit(solution)/shard_map/all_to_all | solution.py:371
  173.2 4.6 %collective-permute-start.9 = (f32[2,1152]{1,0:T(2,128)S(1)}, f32[2,1152]{1,0:T(2,128)S(1)}, u32[]{:S(2)}, u32[]{:S(2)}) collective-permute-start(f32[2,1152]{1,0:T(2,128)S(1)} %get-tuple-element.52), channel_id=1, source_target_pairs={{0,1},{1,0},{2,3},{3,2},{4,5},{5,4},{6,7},{7,6},{8,9},{9,8},{10,11... | collective-permute-start | bytes 27656 | tf_op jit(solution)/shard_map/ppermute | solution.py:298
  177.8 1.0 copy-done
  178.8 2.4 %shard_map.108 = bf16[128,1728]{1,0:T(8,128)(2,1)S(1)} custom-call(bf16[128,1728]{1,0:T(8,128)(2,1)S(1)} %bitcast.15, bf16[128,1152]{1,0:T(8,128)(2,1)S(1)} %copy-done, f32[4,1152]{1,0:T(4,128)S(1)} %bitcast.21, bf16[576,1152]{1,0:T(8,128)(2,1)S(1)} %copy-done.3), custom_call_target="tpu_custom_call" | custom-call | flops 1000000000 | bytes 10000000 | tf_op jit(solution)/shard_map/pallas_call | solution.py:264
  181.1 1.0 copy.17
  183.0 0.7 reshape.76
  (34 shorter events, 3.1 us)
Async XLA Ops:
  0.6 7.0 %copy-start.8 = (bf16[1,1,128,1728]{2,3,1,0:T(8,128)(2,1)S(1)}, bf16[1,1,128,1728]{2,3,1,0:T(8,128)(2,1)}, u32[]{:S(2)}) copy-start(bf16[1,1,128,1728]{2,3,1,0:T(8,128)(2,1)} %param.8) | copy-start | bytes 1327108
  1.7 9.7 %collective-permute-start = (bf16[48,1152]{1,0:T(8,128)(2,1)S(1)}, bf16[48,1152]{1,0:T(8,128)(2,1)S(1)}, u32[]{:S(2)}, u32[]{:S(2)}) collective-permute-start(bf16[48,1152]{1,0:T(8,128)(2,1)S(1)} %maximum_maximum_fusion), channel_id=1, source_target_pairs={{0,0},{1,1},{2,2},{3,3},{4,4},{5,5},{6,6},{7,7},{8,8},{9,9},{10,10... | collective-permute-start | bytes 331784 | tf_op jit(solution)/shard_map/ppermute | solution.py:294
  35.3 13.2 %collective-permute-start.1 = (bf16[384,1152]{1,0:T(8,128)(2,1)S(1)}, bf16[384,1152]{1,0:T(8,128)(2,1)S(1)}, u32[]{:S(2)}, u32[]{:S(2)}) collective-permute-start(bf16[384,1152]{1,0:T(8,128)(2,1)S(1)} %all_gather.3.mine), channel_id=1, source_target_pairs={{0,1},{1,0},{2,3},{3,2},{4,5},{5,4},{6,7},{7,6},{8,9},{9,8},{10,11... | collective-permute-start | bytes 2654216 | tf_op jit(solution)/shard_map/ppermute | solution.py:298
  50.7 1.0 copy-start.4
  51.7 0.7 copy-start.6
  52.4 43.9 %copy-start.1 = (f32[1,4,1152]{2,1,0:T(4,128)S(1)}, f32[1,4,1152]{2,1,0:T(4,128)}, u32[]{:S(2)}) copy-start(f32[1,4,1152]{2,1,0:T(4,128)} %param.12) | copy-start | bytes 55300
  52.4 22.0 %collective-permute-start.4 = (bf16[384,1152]{1,0:T(8,128)(2,1)}, bf16[384,1152]{1,0:T(8,128)(2,1)S(1)}, u32[]{:S(2)}, u32[]{:S(2)}) collective-permute-start(bf16[384,1152]{1,0:T(8,128)(2,1)} %get-tuple-element.36), channel_id=1, source_target_pairs={{192,0},{497,1},{194,2},{499,3},{196,4},{501,5},{198,6},{503,7},{2... | collective-permute-start | bytes 2654216 | tf_op jit(solution)/shard_map/ppermute | solution.py:294
  54.5 22.2 %collective-permute-start.3 = (bf16[384,1152]{1,0:T(8,128)(2,1)}, bf16[384,1152]{1,0:T(8,128)(2,1)S(1)}, u32[]{:S(2)}, u32[]{:S(2)}) collective-permute-start(bf16[384,1152]{1,0:T(8,128)(2,1)} %get-tuple-element.36), channel_id=1, source_target_pairs={{64,0},{113,1},{66,2},{115,3},{68,4},{117,5},{70,6},{119,7},{72,8}... | collective-permute-start | bytes 2654216 | tf_op jit(solution)/shard_map/ppermute | solution.py:294
  56.8 23.0 %collective-permute-start.2 = (bf16[384,1152]{1,0:T(8,128)(2,1)}, bf16[384,1152]{1,0:T(8,128)(2,1)}, u32[]{:S(2)}, u32[]{:S(2)}) collective-permute-start(bf16[384,1152]{1,0:T(8,128)(2,1)} %get-tuple-element.36), channel_id=1, source_target_pairs={{128,0},{385,1},{130,2},{387,3},{132,4},{389,5},{134,6},{391,7},{1... | collective-permute-start | bytes 2654216 | tf_op jit(solution)/shard_map/ppermute | solution.py:294
  60.9 35.4 %all-to-all-start = ((bf16[64,2,2880]{2,1,0:T(2,128)(2,1)}), bf16[64,2,2880]{2,1,0:T(2,128)(2,1)S(1)}, u32[]{:S(2)}, u32[]{:S(2)}) async-start(bf16[64,2,2880]{2,1,0:T(2,128)(2,1)} %pad_maximum_fusion), calls=%async_computation | async-start | bytes 1507328 | tf_op jit(solution)/shard_map/all_to_all | solution.py:276
  74.4 21.9 %collective-permute-start.7 = (bf16[384,1152]{1,0:T(8,128)(2,1)S(1)}, bf16[384,1152]{1,0:T(8,128)(2,1)}, u32[]{:S(2)}, u32[]{:S(2)}) collective-permute-start(bf16[384,1152]{1,0:T(8,128)(2,1)S(1)} %collective-permute-done.4.d), channel_id=1, source_target_pairs={{0,1},{1,0},{2,3},{3,2},{4,5},{5,4},{6,7},{7,6},{8,9},{9,8},{10,11... | collective-permute-start | bytes 2654216 | tf_op jit(solution)/shard_map/ppermute | solution.py:298
  76.7 19.6 %collective-permute-start.6 = (bf16[384,1152]{1,0:T(8,128)(2,1)S(1)}, bf16[384,1152]{1,0:T(8,128)(2,1)}, u32[]{:S(2)}, u32[]{:S(2)}) collective-permute-start(bf16[384,1152]{1,0:T(8,128)(2,1)S(1)} %collective-permute-done.3.c), channel_id=1, source_target_pairs={{0,1},{1,0},{2,3},{3,2},{4,5},{5,4},{6,7},{7,6},{8,9},{9,8},{10,11... | collective-permute-start | bytes 2654216 | tf_op jit(solution)/shard_map/ppermute | solution.py:298
  79.8 16.5 %collective-permute-start.5 = (bf16[384,1152]{1,0:T(8,128)(2,1)}, bf16[384,1152]{1,0:T(8,128)(2,1)}, u32[]{:S(2)}, u32[]{:S(2)}) collective-permute-start(bf16[384,1152]{1,0:T(8,128)(2,1)} %collective-permute-done.2.b), channel_id=1, source_target_pairs={{0,1},{1,0},{2,3},{3,2},{4,5},{5,4},{6,7},{7,6},{8,9},{9,8},{10,11... | collective-permute-start | bytes 2654216 | tf_op jit(solution)/shard_map/ppermute | solution.py:298
  96.3 1.2 copy-start.5
  97.5 1.0 copy-start.7
  105.5 6.2 %copy-start.2 = (bf16[576,1152]{1,0:T(8,128)(2,1)}, bf16[576,1152]{1,0:T(8,128)(2,1)S(1)}, u32[]{:S(2)}) copy-start(bf16[576,1152]{1,0:T(8,128)(2,1)S(1)} %get-tuple-element.37.w_so) | copy-start | bytes 3981316
  105.5 6.2 %collective-permute-start.8 = (bf16[64,5184]{1,0:T(8,128)(2,1)S(1)}, bf16[64,5184]{1,0:T(8,128)(2,1)S(1)}, u32[]{:S(2)}, u32[]{:S(2)}) collective-permute-start(bf16[64,5184]{1,0:T(8,128)(2,1)S(1)} %get-tuple-element.50), channel_id=1, source_target_pairs={{0,1},{1,0},{2,3},{3,2},{4,5},{5,4},{6,7},{7,6},{8,9},{9,8},{10,11... | collective-permute-start | bytes 1990664 | tf_op jit(solution)/shard_map/ppermute | solution.py:298
  159.4 18.4 %copy-start.3 = (bf16[576,1152]{1,0:T(8,128)(2,1)S(1)}, bf16[576,1152]{1,0:T(8,128)(2,1)}, u32[]{:S(2)}) copy-start(bf16[576,1152]{1,0:T(8,128)(2,1)} %copy-done.2) | copy-start | bytes 3981316
  161.5 21.3 %all-to-all-start.2 = ((f32[8,2,5184]{2,1,0:T(2,128)}), f32[8,2,5184]{2,1,0:T(2,128)S(1)}, u32[]{:S(2)}, u32[]{:S(2)}) async-start(f32[8,2,5184]{2,1,0:T(2,128)} %get-tuple-element.53), calls=%async_computation.2 | async-start | bytes 671744 | tf_op jit(solution)/shard_map/all_to_all | solution.py:371
  173.2 8.9 %collective-permute-start.9 = (f32[2,1152]{1,0:T(2,128)S(1)}, f32[2,1152]{1,0:T(2,128)S(1)}, u32[]{:S(2)}, u32[]{:S(2)}) collective-permute-start(f32[2,1152]{1,0:T(2,128)S(1)} %get-tuple-element.52), channel_id=1, source_target_pairs={{0,1},{1,0},{2,3},{3,2},{4,5},{5,4},{6,7},{7,6},{8,9},{9,8},{10,11... | collective-permute-start | bytes 27656 | tf_op jit(solution)/shard_map/ppermute | solution.py:298
  177.8 1.0 copy-start

commit v13 on v12

--- a/solution.py
+++ b/solution.py
@@ -119,10 +119,17 @@
 STEP = (208, 64, 64)
 
 
-COPIES = 6
-
-
-def start_copies(place, near, swapped, targets, sems):
+COPIES = 7
+
+
+def start_copies(place, own, near, swapped, targets, sems):
+    for section in (1, 0, 2):
+        to = pl.multiple_of(place[1] * BLOCK[section], 16)
+        pltpu.make_async_copy(
+            own[section],
+            targets[section].at[pl.ds(to, BLOCK[section])],
+            sems.at[section * COPIES + 6],
+        ).start()
     for me in range(2):
 
         @pl.when(place[0] == me)
@@ -142,13 +149,15 @@
                         ).start()
 
 
-def wait_copies(section, near, targets, sems):
+def wait_copies(section, own, near, targets, sems):
     first, last = SECTIONS[section][1:]
     for i in range(3):
         for half in range(2):
             rows = pl.ds(0, last - first - 16 * half)
             sem = sems.at[section * COPIES + 2 * i + half]
             pltpu.make_async_copy(near[i].at[rows], targets[section].at[rows], sem).wait()
+    rows, sem = pl.ds(0, BLOCK[section]), sems.at[section * COPIES + 6]
+    pltpu.make_async_copy(own[section], targets[section].at[rows], sem).wait()
 
 
 def temporal_forward_kernel(
@@ -156,15 +165,12 @@
     out_keep, out_send, w_so, w_out, w_qkv, q_out, k_out, v_out, probs_out, mixed_out,
     unit_out, inverse_out, project_out, cot_out, sems,
 ):
-    near, targets = (b, c, d), (w_qkv, w_so, w_out)
-    start_copies(place, near, (other_b, other_c, other_d), targets, sems)
-    for section, ref in enumerate((own_qkv, own_so, own_out)):
-        to = pl.multiple_of(place[1] * BLOCK[section], 16)
-        targets[section][pl.ds(to, BLOCK[section]), :] = ref[...]
+    own, near, targets = (own_qkv, own_so, own_out), (b, c, d), (w_qkv, w_so, w_out)
+    start_copies(place, own, near, (other_b, other_c, other_d), targets, sems)
     received = sent[...].reshape(ROWS, 2 * D + ATT)
     tokens, cotangent, mixed_s = received[:, :D], received[:, D : 2 * D], received[:, 2 * D :]
     cot_out[...] = cotangent
-    wait_copies(1, near, targets, sems)
+    wait_copies(1, own, near, targets, sems)
     gate_s, shift, scale, gate_t = (factors[i : i + 1, :] for i in range(4))
     project = nn(mixed_s, w_so[...])
     project_out[...] = project
@@ -175,7 +181,7 @@
     unit = centered * inverse
     unit_out[...] = unit
     normed = (unit * (1.0 + scale) + shift).astype(BF)
-    wait_copies(0, near, targets, sems)
+    wait_copies(0, own, near, targets, sems)
     q, k, v = (nt(normed, w_qkv[i * ATT : (i + 1) * ATT, :]).astype(BF) for i in range(3))
     q_out[...], k_out[...], v_out[...] = q, k, v
 
@@ -198,7 +204,7 @@
     for j in range(9):
         out_keep[:, ATT * j : ATT * j + ATT] = keep[64 * j : 64 * j + 64]
         out_send[:, ATT * j : ATT * j + ATT] = send[64 * j : 64 * j + 64]
-    wait_copies(2, near, targets, sems)
+    wait_copies(2, own, near, targets, sems)
 
 
 def temporal_backward_kernel(
@@ -230,27 +236,37 @@
         jnp.sum(d_normed * unit, 0, keepdims=True),
         jnp.sum(cot * project_t, 0, keepdims=True),
     )
-    tile = jnp.concatenate(factor_grads * 4, 0).astype(BF)
-    for i in range(8):
-        packed[16 * i : 16 * i + 16, D:] = tile
+    zeros = jnp.zeros((16, 64), BF)
+    for parity in range(2):
+        rows = [
+            factor_grads[2 * parity + core][:, part * ATT : part * ATT + ATT]
+            for core in range(2)
+            for part in range(2)
+        ]
+        tile = jnp.concatenate([jnp.concatenate(rows * 4, 0).astype(BF), zeros], 1)
+        for yhi in (parity, parity + 2):
+            packed[32 * yhi : 32 * yhi + 16, D:] = tile
+            packed[32 * yhi + 16 : 32 * yhi + 32, D:] = tile
 
 
 HALF = 9 * ATT // 2
+HEAD = D + 640
 
 
 def pack_kernel(packed, out_keep, out_other, out):
-    out[:, :, : 2 * D] = packed[...].reshape(64, 2, 2 * D)
+    out[:, :, :HEAD] = packed[...].reshape(64, 2, HEAD)
     pair = (out_keep[...] + out_other[...].astype(F32)).astype(BF)
-    out[:, 0, 2 * D :] = pair[:, :HALF]
-    out[:, 1, 2 * D :] = pair[:, HALF:]
+    out[:, 0, HEAD:] = pair[:, :HALF]
+    out[:, 1, HEAD:] = pair[:, HALF:]
 
 
 def unpack_kernel(back, token_grad, out_part, factor_part):
     token_grad[...] = back[:, :, :D].reshape(ROWS, D)
     first = lax.broadcasted_iota(jnp.int32, (64, HALF), 0) & 1 == 0
     for r in range(2):
-        factor_part[r : r + 1, :] = jnp.sum(back[:, r, D : 2 * D].astype(F32), 0, keepdims=True)
-        rows = back[:, r, 2 * D :].astype(F32)
+        half_row = jnp.sum(back[:, r, D : D + ATT].astype(F32), 0, keepdims=True)
+        factor_part[:, ATT * r : ATT * r + ATT] = half_row
+        rows = back[:, r, HEAD:].astype(F32)
         for core in range(2):
             total = jnp.sum(jnp.where(first == (core == 0), rows, 0.0), 0, keepdims=True)
             for copy in range(8):
@@ -298,10 +314,16 @@
     return lax.ppermute(a, "core", [(0, 1), (1, 0)])
 
 
+SENDERS = (
+    ((0, 0), (1, 2), (0, 1), (3, 3), (1, 1), (0, 3), (3, 0), (0, 2)),
+    ((0, 5), (1, 7), (0, 4), (1, 6), (1, 4), (2, 6), (1, 5), (2, 7)),
+    ((1, 0), (2, 2), (3, 1), (1, 3), (2, 1), (2, 3), (2, 0), (3, 2)),
+    ((3, 5), (0, 7), (2, 4), (0, 6), (3, 4), (3, 6), (2, 5), (3, 7)),
+)
+
+
 def class_source(x, y, z, core):
-    ylo, yhi = y % 2, y // 2
-    cls = (x % 2) * 2 + ylo
-    return (x // 2) * 2 + yhi // 2, cls * 2 + yhi % 2, z
+    return *SENDERS[x][y], z
 
 
 def near_source(dx, dy):
@@ -353,19 +375,19 @@
             rows(D, F32), rows(128, F32), rows(D, F32), rows(D),
         ],
         place, sent, factors, *weights,
-        scalars=1, hbm=6, flops=4 * 10**9,
+        scalars=1, hbm=9, flops=4 * 10**9,
         scratch=[pltpu.SemaphoreType.DMA((3 * COPIES,))],
     )
     w_so = saved[0]
     out_other = swap_cores(out_send)
-    (packed,) = call(temporal_backward_kernel, [rows(2 * D)], factors, *saved, flops=4 * 10**9)
+    (packed,) = call(temporal_backward_kernel, [rows(HEAD)], factors, *saved, flops=4 * 10**9)
 
     (packed,) = call(
-        pack_kernel, [((64, 2, 2 * D + HALF), BF)], packed, out_keep, out_other, flops=10**8
+        pack_kernel, [((64, 2, HEAD + HALF), BF)], packed, out_keep, out_other, flops=10**8
     )
     token_grad, out_part, mine = call(
         unpack_kernel,
-        [rows(D), ((8, 2, 2 * HALF), F32), ((2, D), F32)],
+        [rows(D), ((8, 2, 2 * HALF), F32), ((1, D), F32)],
         exchange(packed), flops=10**8,
     )
     out_part = jnp.sum(lax.all_to_all(out_part, DP, 0, 0, tiled=True), 0)
@@ -375,7 +397,10 @@
         spatial_backward_kernel, [((ROWS, 3 * ATT), BF)], qkv, token_grad, factors, w_so
     )
     other = swap_cores(mine)
-    factor_grad = jnp.where(core == 0, jnp.concatenate([mine, other]), jnp.concatenate([other, mine]))
+    mine = jnp.where(core == 0, jnp.concatenate([mine, other]), jnp.concatenate([other, mine]))
+    other = lax.ppermute(mine, "yhi", [(0, 1), (1, 0), (2, 3), (3, 2)])
+    low = lax.axis_index("yhi") % 2 == 0
+    factor_grad = jnp.where(low, jnp.concatenate([mine, other]), jnp.concatenate([other, mine]))
     return token_grad[None, None], qkv_grad[None, None], factor_grad[None], out_grad
 
 

time: 185 us -> 195 us (1.054)
  the two profiles are of different devices: /device:TPU:169 before, /device:TPU:1 now
where the time goes in v13:
time: 195 us; the launch traced here: 191 us
  starting transfers between devices  68.5 us (35%)
  waiting for transfers between devices  58.4 us (30%)
  blocking collectives  28.4 us (15%)
  Pallas kernels  20.4 us (10%)
  local copies, waits for them, and re-layouts  10.9 us (6%)
  other arithmetic  3.43 us (2%)
    all_to_all x2, waiting for transfers between devices, exchange(): return lax.all_to_all(a, SEQ, 0, 0, tiled=True)  41.6 us
    all_gather x1, blocking collectives, gather_weights(): mine = lax.all_gather(shard, 'z', axis=0, tiled=True)  28.4 us
    pallas_call x7, Pallas kernels, call(): pl.pallas_call(kernel, out_shape=[jax.ShapeDtypeStruct(s, d) for s, d in...  20.4 us
    ppermute x6, starting transfers between devices, swap_cores(): return lax.ppermute(a, 'core', [(0, 1), (1, 0)])  20 us
    all_to_all x2, starting transfers between devices, exchange(): return lax.all_to_all(a, SEQ, 0, 0, tiled=True)  18.2 us
    ppermute x4, starting transfers between devices, receive(): return lax.ppermute(a, AXES, pairs)  16.1 us
    ppermute x4, waiting for transfers between devices, receive(): return lax.ppermute(a, AXES, pairs)  12.1 us
    all_to_all x1, starting transfers between devices, body(): out_part = jnp.sum(lax.all_to_all(out_part, DP, 0, 0, tiled=True), 0)  10.5 us
  transfers between devices with their start and end apart: 14, of which 6 were waited for; matrix products, arithmetic and copies ran while one was open for 3% of the time, Pallas kernels for 4%

profile of v13, /device:TPU:1, one launch (start us, length us, event | category | flops | bytes accessed | tf_op | source)
XLA Modules:
  0.0 191.0 jit_solution(11602128406751793345)
XLA Ops:
  0.7 1.0 maximum_maximum_fusion
  2.4 1.1 concatenate.62
  3.5 1.1 concatenate.63
  4.8 1.5 shard_map.102
  6.4 1.6 pad_maximum_fusion
  8.0 28.4 %all_gather.3.mine = bf16[384,1152]{1,0:T(8,128)(2,1)S(1)} all-gather(bf16[48,1152]{1,0:T(8,128)(2,1)S(1)} %collective-permute-done), channel_id=1, replica_groups=mesh['x'=4,'ylo'=2,'yhi'=4,'z'=8,'core'=2] {'z'}, dimensions={0}, use_global_device_ids=true | all-gather | bytes 995328 | tf_op jit(solution)/shard_map/all_gather | solution.py:340
  36.4 7.8 %collective-permute-start.1 = (bf16[384,1152]{1,0:T(8,128)(2,1)S(1)}, bf16[384,1152]{1,0:T(8,128)(2,1)S(1)}, u32[]{:S(2)}, u32[]{:S(2)}) collective-permute-start(bf16[384,1152]{1,0:T(8,128)(2,1)S(1)} %all_gather.3.mine), channel_id=1, source_target_pairs={{0,1},{1,0},{2,3},{3,2},{4,5},{5,4},{6,7},{7,6},{8,9},{9,8},{10,11... | collective-permute-start | bytes 2654216 | tf_op jit(solution)/shard_map/ppermute | solution.py:314
  44.2 1.9 %collective-permute-done.1.other = bf16[384,1152]{1,0:T(8,128)(2,1)S(1)} collective-permute-done((bf16[384,1152]{1,0:T(8,128)(2,1)S(1)}, bf16[384,1152]{1,0:T(8,128)(2,1)S(1)}, u32[]{:S(2)}, u32[]{:S(2)}) %collective-permute-start.1) | collective-permute-done | bytes 884768 | tf_op jit(solution)/shard_map/ppermute | solution.py:314
  46.2 2.2 %shard_map.103 = (bf16[144,1152]{1,0:T(8,128)(2,1)S(1)}, bf16[144,1152]{1,0:T(8,128)(2,1)S(1)}, bf16[432,1152]{1,0:T(8,128)(2,1)S(1)}, bf16[384,1152]{1,0:T(8,128)(2,1)}) custom-call(s32[2]{0:T(128)S(1)} %pad_add_fusion.place, bf16[384,1152]{1,0:T(8,128)(2,1)S(1)} %all_gather.3.mine, bf16[384,1152]{1,0:T(8,128)(2,1)S(1)} %collective-permute-done.1.other), custom_call_target="tpu_custom_call" | custom-call | flops 1000000000 | bytes 10000000 | tf_op jit(solution)/shard_map/pallas_call | solution.py:280
  50.8 10.3 %collective-permute-start.4 = (bf16[384,1152]{1,0:T(8,128)(2,1)}, bf16[384,1152]{1,0:T(8,128)(2,1)S(1)}, u32[]{:S(2)}, u32[]{:S(2)}) collective-permute-start(bf16[384,1152]{1,0:T(8,128)(2,1)} %get-tuple-element.36), channel_id=1, source_target_pairs={{192,0},{497,1},{194,2},{499,3},{196,4},{501,5},{198,6},{503,7},{2... | collective-permute-start | bytes 2654216 | tf_op jit(solution)/shard_map/ppermute | solution.py:310
  61.1 1.9 %collective-permute-start.3 = (bf16[384,1152]{1,0:T(8,128)(2,1)}, bf16[384,1152]{1,0:T(8,128)(2,1)S(1)}, u32[]{:S(2)}, u32[]{:S(2)}) collective-permute-start(bf16[384,1152]{1,0:T(8,128)(2,1)} %get-tuple-element.36), channel_id=1, source_target_pairs={{64,0},{113,1},{66,2},{115,3},{68,4},{117,5},{70,6},{119,7},{72,8}... | collective-permute-start | bytes 2654216 | tf_op jit(solution)/shard_map/ppermute | solution.py:310
  63.1 3.1 %collective-permute-start.2 = (bf16[384,1152]{1,0:T(8,128)(2,1)}, bf16[384,1152]{1,0:T(8,128)(2,1)}, u32[]{:S(2)}, u32[]{:S(2)}) collective-permute-start(bf16[384,1152]{1,0:T(8,128)(2,1)} %get-tuple-element.36), channel_id=1, source_target_pairs={{128,0},{385,1},{130,2},{387,3},{132,4},{389,5},{134,6},{391,7},{1... | collective-permute-start | bytes 2654216 | tf_op jit(solution)/shard_map/ppermute | solution.py:310
  66.2 9.5 %all-to-all-start = ((bf16[64,2,2880]{2,1,0:T(2,128)(2,1)}), bf16[64,2,2880]{2,1,0:T(2,128)(2,1)S(1)}, u32[]{:S(2)}, u32[]{:S(2)}) async-start(bf16[64,2,2880]{2,1,0:T(2,128)(2,1)} %pad_maximum_fusion), calls=%async_computation | async-start | bytes 1507328 | tf_op jit(solution)/shard_map/all_to_all | solution.py:292
  75.8 2.4 %collective-permute-start.7 = (bf16[384,1152]{1,0:T(8,128)(2,1)S(1)}, bf16[384,1152]{1,0:T(8,128)(2,1)}, u32[]{:S(2)}, u32[]{:S(2)}) collective-permute-start(bf16[384,1152]{1,0:T(8,128)(2,1)S(1)} %collective-permute-done.4.d), channel_id=1, source_target_pairs={{0,1},{1,0},{2,3},{3,2},{4,5},{5,4},{6,7},{7,6},{8,9},{9,8},{10,11... | collective-permute-start | bytes 2654216 | tf_op jit(solution)/shard_map/ppermute | solution.py:314
  78.1 12.1 %collective-permute-done.3.c = bf16[384,1152]{1,0:T(8,128)(2,1)S(1)} collective-permute-done((bf16[384,1152]{1,0:T(8,128)(2,1)}, bf16[384,1152]{1,0:T(8,128)(2,1)S(1)}, u32[]{:S(2)}, u32[]{:S(2)}) %collective-permute-start.3) | collective-permute-done | bytes 884768 | tf_op jit(solution)/shard_map/ppermute | solution.py:310
  90.2 3.1 %collective-permute-start.6 = (bf16[384,1152]{1,0:T(8,128)(2,1)S(1)}, bf16[384,1152]{1,0:T(8,128)(2,1)}, u32[]{:S(2)}, u32[]{:S(2)}) collective-permute-start(bf16[384,1152]{1,0:T(8,128)(2,1)S(1)} %collective-permute-done.3.c), channel_id=1, source_target_pairs={{0,1},{1,0},{2,3},{3,2},{4,5},{5,4},{6,7},{7,6},{8,9},{9,8},{10,11... | collective-permute-start | bytes 2654216 | tf_op jit(solution)/shard_map/ppermute | solution.py:314
  93.3 1.9 %collective-permute-start.5 = (bf16[384,1152]{1,0:T(8,128)(2,1)}, bf16[384,1152]{1,0:T(8,128)(2,1)}, u32[]{:S(2)}, u32[]{:S(2)}) collective-permute-start(bf16[384,1152]{1,0:T(8,128)(2,1)} %collective-permute-done.2.b), channel_id=1, source_target_pairs={{0,1},{1,0},{2,3},{3,2},{4,5},{5,4},{6,7},{7,6},{8,9},{9,8},{10,11... | collective-permute-start | bytes 2654216 | tf_op jit(solution)/shard_map/ppermute | solution.py:314
  95.2 8.2 %all-to-all-done.sent = bf16[64,2,2880]{2,1,0:T(2,128)(2,1)S(1)} async-done(((bf16[64,2,2880]{2,1,0:T(2,128)(2,1)}), bf16[64,2,2880]{2,1,0:T(2,128)(2,1)S(1)}, u32[]{:S(2)}, u32[]{:S(2)}) %all-to-all-start) | async-done | bytes 737312 | tf_op jit(solution)/shard_map/all_to_all | solution.py:292
  103.5 1.2 copy-done.5
  106.6 7.6 %shard_map.104 = (f32[64,5184]{1,0:T(8,128)S(1)}, bf16[64,5184]{1,0:T(8,128)(2,1)S(1)}, bf16[576,1152]{1,0:T(8,128)(2,1)S(1)}, bf16[576,1152]{1,0:T(8,128)(2,1)S...) custom-call(s32[2]{0:T(128)S(1)} %pad_add_fusion.place, ...), custom_call_target="tpu_custom_call" | custom-call | flops 4000000000 | bytes 10000000 | tf_op jit(solution)/shard_map/pallas_call | solution.py:280
  114.2 2.9 %collective-permute-start.8 = (bf16[64,5184]{1,0:T(8,128)(2,1)S(1)}, bf16[64,5184]{1,0:T(8,128)(2,1)S(1)}, u32[]{:S(2)}, u32[]{:S(2)}) collective-permute-start(bf16[64,5184]{1,0:T(8,128)(2,1)S(1)} %get-tuple-element.50), channel_id=1, source_target_pairs={{0,1},{1,0},{2,3},{3,2},{4,5},{5,4},{6,7},{7,6},{8,9},{9,8},{10,11... | collective-permute-start | bytes 1990664 | tf_op jit(solution)/shard_map/ppermute | solution.py:314
  117.1 3.3 %shard_map.105.packed = bf16[128,1792]{1,0:T(8,128)(2,1)S(1)} custom-call(f32[4,1152]{1,0:T(4,128)S(1)} %bitcast.20, bf16[576,1152]{1,0:T(8,128)(2,1)S(1)} %get-tuple-element.37.w_so, bf16[576,1152]{1,0:T(8,128)(2,1)S(1)} %get-tuple-element.38.w_out, bf16[1728,1152]{1,0:T(8,128)(2,1)S(1)} %get-tuple-element.39.w_qkv, ...), custom_call_target="tpu_custom_call" | custom-call | flops 4000000000 | bytes 10000000 | tf_op jit(solution)/shard_map/pallas_call | solution.py:280
  120.5 1.6 shard_map.106
  122.0 8.6 %all-to-all-start.1 = ((bf16[64,2,4384]{2,1,0:T(2,128)(2,1)}), bf16[64,2,4384]{2,1,0:T(2,128)(2,1)S(1)}, u32[]{:S(2)}, u32[]{:S(2)}) async-start(bf16[64,2,4384]{2,1,0:T(2,128)(2,1)} %shard_map.106), calls=%async_computation.1 | async-start | bytes 2293760 | tf_op jit(solution)/shard_map/all_to_all | solution.py:292
  130.7 33.4 %all-to-all-done.1.back = bf16[64,2,4384]{2,1,0:T(2,128)(2,1)S(1)} async-done(((bf16[64,2,4384]{2,1,0:T(2,128)(2,1)}), bf16[64,2,4384]{2,1,0:T(2,128)(2,1)S(1)}, u32[]{:S(2)}, u32[]{:S(2)}) %all-to-all-start.1) | async-done | bytes 1122336 | tf_op jit(solution)/shard_map/all_to_all | solution.py:292
  164.1 1.9 shard_map.107
  166.0 1.9 collective-permute-start.9
  168.9 2.4 %shard_map.108 = bf16[128,1728]{1,0:T(8,128)(2,1)S(1)} custom-call(bf16[128,1728]{1,0:T(8,128)(2,1)S(1)} %bitcast.16, bf16[128,1152]{1,0:T(8,128)(2,1)S(1)} %copy-done, f32[4,1152]{1,0:T(4,128)S(1)} %bitcast.21, bf16[576,1152]{1,0:T(8,128)(2,1)S(1)} %copy-done.3), custom_call_target="tpu_custom_call" | custom-call | flops 1000000000 | bytes 10000000 | tf_op jit(solution)/shard_map/pallas_call | solution.py:280
  172.2 10.5 %all-to-all-start.2 = ((f32[8,2,5184]{2,1,0:T(2,128)}), f32[8,2,5184]{2,1,0:T(2,128)S(1)}, u32[]{:S(2)}, u32[]{:S(2)}) async-start(f32[8,2,5184]{2,1,0:T(2,128)} %get-tuple-element.53), calls=%async_computation.2 | async-start | bytes 671744 | tf_op jit(solution)/shard_map/all_to_all | solution.py:393
  182.8 3.8 %collective-permute-start.10 = (f32[2,1152]{1,0:T(2,128)S(1)}, f32[2,1152]{1,0:T(2,128)S(1)}, u32[]{:S(2)}, u32[]{:S(2)}) collective-permute-start(f32[2,1152]{1,0:T(2,128)S(1)} %maximum_select_fusion.1), channel_id=1, source_target_pairs={{0,16},{16,0},{32,48},{48,32},{1,17},{17,1},{33,49},{49,33},{2,18}... | collective-permute-start | bytes 27656 | tf_op jit(solution)/shard_map/ppermute | solution.py:401
  186.6 1.8 collective-permute-done.10
  189.0 1.0 all-to-all-done.2
  (43 shorter events, 9.1 us)
Async XLA Ops:
  0.6 3.9 %copy-start.10 = (bf16[1,1,128,1728]{2,3,1,0:T(8,128)(2,1)S(1)}, bf16[1,1,128,1728]{2,3,1,0:T(8,128)(2,1)}, u32[]{:S(2)}) copy-start(bf16[1,1,128,1728]{2,3,1,0:T(8,128)(2,1)} %param.8) | copy-start | bytes 1327108
  1.7 6.3 %collective-permute-start = (bf16[48,1152]{1,0:T(8,128)(2,1)S(1)}, bf16[48,1152]{1,0:T(8,128)(2,1)S(1)}, u32[]{:S(2)}, u32[]{:S(2)}) collective-permute-start(bf16[48,1152]{1,0:T(8,128)(2,1)S(1)} %maximum_maximum_fusion), channel_id=1, source_target_pairs={{0,0},{1,1},{2,2},{3,3},{4,4},{5,5},{6,6},{7,7},{8,8},{9,9},{10,10... | collective-permute-start | bytes 331784 | tf_op jit(solution)/shard_map/ppermute | solution.py:310
  36.4 9.8 %collective-permute-start.1 = (bf16[384,1152]{1,0:T(8,128)(2,1)S(1)}, bf16[384,1152]{1,0:T(8,128)(2,1)S(1)}, u32[]{:S(2)}, u32[]{:S(2)}) collective-permute-start(bf16[384,1152]{1,0:T(8,128)(2,1)S(1)} %all_gather.3.mine), channel_id=1, source_target_pairs={{0,1},{1,0},{2,3},{3,2},{4,5},{5,4},{6,7},{7,6},{8,9},{9,8},{10,11... | collective-permute-start | bytes 2654216 | tf_op jit(solution)/shard_map/ppermute | solution.py:314
  48.4 1.0 copy-start.4
  49.3 0.7 copy-start.6
  50.1 0.7 copy-start.8
  50.8 52.7 %copy-start.1 = (f32[1,4,1152]{2,1,0:T(4,128)S(1)}, f32[1,4,1152]{2,1,0:T(4,128)}, u32[]{:S(2)}) copy-start(f32[1,4,1152]{2,1,0:T(4,128)} %param.12) | copy-start | bytes 55300
  50.8 25.0 %collective-permute-start.4 = (bf16[384,1152]{1,0:T(8,128)(2,1)}, bf16[384,1152]{1,0:T(8,128)(2,1)S(1)}, u32[]{:S(2)}, u32[]{:S(2)}) collective-permute-start(bf16[384,1152]{1,0:T(8,128)(2,1)} %get-tuple-element.36), channel_id=1, source_target_pairs={{192,0},{497,1},{194,2},{499,3},{196,4},{501,5},{198,6},{503,7},{2... | collective-permute-start | bytes 2654216 | tf_op jit(solution)/shard_map/ppermute | solution.py:310
  61.1 29.1 %collective-permute-start.3 = (bf16[384,1152]{1,0:T(8,128)(2,1)}, bf16[384,1152]{1,0:T(8,128)(2,1)S(1)}, u32[]{:S(2)}, u32[]{:S(2)}) collective-permute-start(bf16[384,1152]{1,0:T(8,128)(2,1)} %get-tuple-element.36), channel_id=1, source_target_pairs={{64,0},{113,1},{66,2},{115,3},{68,4},{117,5},{70,6},{119,7},{72,8}... | collective-permute-start | bytes 2654216 | tf_op jit(solution)/shard_map/ppermute | solution.py:310
  63.1 30.2 %collective-permute-start.2 = (bf16[384,1152]{1,0:T(8,128)(2,1)}, bf16[384,1152]{1,0:T(8,128)(2,1)}, u32[]{:S(2)}, u32[]{:S(2)}) collective-permute-start(bf16[384,1152]{1,0:T(8,128)(2,1)} %get-tuple-element.36), channel_id=1, source_target_pairs={{128,0},{385,1},{130,2},{387,3},{132,4},{389,5},{134,6},{391,7},{1... | collective-permute-start | bytes 2654216 | tf_op jit(solution)/shard_map/ppermute | solution.py:310
  66.2 37.2 %all-to-all-start = ((bf16[64,2,2880]{2,1,0:T(2,128)(2,1)}), bf16[64,2,2880]{2,1,0:T(2,128)(2,1)S(1)}, u32[]{:S(2)}, u32[]{:S(2)}) async-start(bf16[64,2,2880]{2,1,0:T(2,128)(2,1)} %pad_maximum_fusion), calls=%async_computation | async-start | bytes 1507328 | tf_op jit(solution)/shard_map/all_to_all | solution.py:292
  75.8 27.7 %collective-permute-start.7 = (bf16[384,1152]{1,0:T(8,128)(2,1)S(1)}, bf16[384,1152]{1,0:T(8,128)(2,1)}, u32[]{:S(2)}, u32[]{:S(2)}) collective-permute-start(bf16[384,1152]{1,0:T(8,128)(2,1)S(1)} %collective-permute-done.4.d), channel_id=1, source_target_pairs={{0,1},{1,0},{2,3},{3,2},{4,5},{5,4},{6,7},{7,6},{8,9},{9,8},{10,11... | collective-permute-start | bytes 2654216 | tf_op jit(solution)/shard_map/ppermute | solution.py:314
  90.2 13.3 %collective-permute-start.6 = (bf16[384,1152]{1,0:T(8,128)(2,1)S(1)}, bf16[384,1152]{1,0:T(8,128)(2,1)}, u32[]{:S(2)}, u32[]{:S(2)}) collective-permute-start(bf16[384,1152]{1,0:T(8,128)(2,1)S(1)} %collective-permute-done.3.c), channel_id=1, source_target_pairs={{0,1},{1,0},{2,3},{3,2},{4,5},{5,4},{6,7},{7,6},{8,9},{9,8},{10,11... | collective-permute-start | bytes 2654216 | tf_op jit(solution)/shard_map/ppermute | solution.py:314
  93.3 10.2 %collective-permute-start.5 = (bf16[384,1152]{1,0:T(8,128)(2,1)}, bf16[384,1152]{1,0:T(8,128)(2,1)}, u32[]{:S(2)}, u32[]{:S(2)}) collective-permute-start(bf16[384,1152]{1,0:T(8,128)(2,1)} %collective-permute-done.2.b), channel_id=1, source_target_pairs={{0,1},{1,0},{2,3},{3,2},{4,5},{5,4},{6,7},{7,6},{8,9},{9,8},{10,11... | collective-permute-start | bytes 2654216 | tf_op jit(solution)/shard_map/ppermute | solution.py:314
  103.5 1.2 copy-start.5
  104.7 1.0 copy-start.7
  105.7 1.0 copy-start.9
  114.2 6.3 %copy-start.2 = (bf16[576,1152]{1,0:T(8,128)(2,1)}, bf16[576,1152]{1,0:T(8,128)(2,1)S(1)}, u32[]{:S(2)}) copy-start(bf16[576,1152]{1,0:T(8,128)(2,1)S(1)} %get-tuple-element.37.w_so) | copy-start | bytes 3981316
  114.2 6.3 %collective-permute-start.8 = (bf16[64,5184]{1,0:T(8,128)(2,1)S(1)}, bf16[64,5184]{1,0:T(8,128)(2,1)S(1)}, u32[]{:S(2)}, u32[]{:S(2)}) collective-permute-start(bf16[64,5184]{1,0:T(8,128)(2,1)S(1)} %get-tuple-element.50), channel_id=1, source_target_pairs={{0,1},{1,0},{2,3},{3,2},{4,5},{5,4},{6,7},{7,6},{8,9},{9,8},{10,11... | collective-permute-start | bytes 1990664 | tf_op jit(solution)/shard_map/ppermute | solution.py:314
  122.0 45.9 %copy-start.3 = (bf16[576,1152]{1,0:T(8,128)(2,1)S(1)}, bf16[576,1152]{1,0:T(8,128)(2,1)}, u32[]{:S(2)}) copy-start(bf16[576,1152]{1,0:T(8,128)(2,1)} %copy-done.2) | copy-start | bytes 3981316
  122.0 42.1 %all-to-all-start.1 = ((bf16[64,2,4384]{2,1,0:T(2,128)(2,1)}), bf16[64,2,4384]{2,1,0:T(2,128)(2,1)S(1)}, u32[]{:S(2)}, u32[]{:S(2)}) async-start(bf16[64,2,4384]{2,1,0:T(2,128)(2,1)} %shard_map.106), calls=%async_computation.1 | async-start | bytes 2293760 | tf_op jit(solution)/shard_map/all_to_all | solution.py:292
  166.0 16.7 %collective-permute-start.9 = (f32[1,1152]{1,0:T(1,128)S(1)}, f32[1,1152]{1,0:T(1,128)S(1)}, u32[]{:S(2)}, u32[]{:S(2)}) collective-permute-start(f32[1,1152]{1,0:T(1,128)S(1)} %get-tuple-element.52), channel_id=1, source_target_pairs={{0,1},{1,0},{2,3},{3,2},{4,5},{5,4},{6,7},{7,6},{8,9},{9,8},{10,11... | collective-permute-start | bytes 13832 | tf_op jit(solution)/shard_map/ppermute | solution.py:314
  167.9 1.0 copy-start
  172.2 17.8 %all-to-all-start.2 = ((f32[8,2,5184]{2,1,0:T(2,128)}), f32[8,2,5184]{2,1,0:T(2,128)S(1)}, u32[]{:S(2)}, u32[]{:S(2)}) async-start(f32[8,2,5184]{2,1,0:T(2,128)} %get-tuple-element.53), calls=%async_computation.2 | async-start | bytes 671744 | tf_op jit(solution)/shard_map/all_to_all | solution.py:393
  182.8 5.6 %collective-permute-start.10 = (f32[2,1152]{1,0:T(2,128)S(1)}, f32[2,1152]{1,0:T(2,128)S(1)}, u32[]{:S(2)}, u32[]{:S(2)}) collective-permute-start(f32[2,1152]{1,0:T(2,128)S(1)} %maximum_select_fusion.1), channel_id=1, source_target_pairs={{0,16},{16,0},{32,48},{48,32},{1,17},{17,1},{33,49},{49,33},{2,18}... | collective-permute-start | bytes 27656 | tf_op jit(solution)/shard_map/ppermute | solution.py:401

commit v14 on v12

--- a/solution.py
+++ b/solution.py
@@ -95,7 +95,7 @@
     out[:, 2 * ATT :] = d_v
 
 
-def compact_kernel(place, mine, other, own_so, own_out, own_qkv, part, both, so, out, qkv):
+def compact_kernel(place, mine, other, own, part, both, so, out, qkv):
     core = place[0]
     both[core] = mine[...]
     both[1 - core] = other[...]
@@ -104,18 +104,19 @@
         so[9 * i : 9 * i + 9, :] = shard[:9]
         out[9 * i : 9 * i + 9, :] = shard[9:18]
         qkv[27 * i : 27 * i + 27, :] = shard[18:45]
-    own_so[...] = so[...].astype(BF)
-    own_out[...] = out[...].astype(BF)
-    own_qkv[...] = qkv[...].astype(BF)
+    own[OWN[1] : OWN[1] + 144, :] = so[...].astype(BF)
+    own[OWN[2] : OWN[2] + 144, :] = out[...].astype(BF)
+    own[OWN[0] : OWN[0] + 432, :] = qkv[...].astype(BF)
     at_qkv = pl.multiple_of(core * 208, 16)
     at = pl.multiple_of(core * 64, 16)
-    part[0:224, :] = own_qkv[pl.ds(at_qkv, 224), :]
-    part[224:304, :] = own_so[pl.ds(at, 80), :]
-    part[304:384, :] = own_out[pl.ds(at, 80), :]
+    part[0:224, :] = own[pl.ds(OWN[0] + at_qkv, 224), :]
+    part[224:304, :] = own[pl.ds(OWN[1] + at, 80), :]
+    part[304:384, :] = own[pl.ds(OWN[2] + at, 80), :]
 
 
 SECTIONS = ((0, 0, 224), (1, 224, 304), (2, 304, 384))
 BLOCK = (432, 144, 144)
+OWN = (288, 0, 144)
 STEP = (208, 64, 64)
 
 
@@ -152,15 +153,15 @@
 
 
 def temporal_forward_kernel(
-    place, sent, factors, own_qkv, own_so, own_out, b, c, d, other_b, other_c, other_d,
+    place, sent, factors, own, b, c, d, other_b, other_c, other_d,
     out_keep, out_send, w_so, w_out, w_qkv, q_out, k_out, v_out, probs_out, mixed_out,
     unit_out, inverse_out, project_out, cot_out, sems,
 ):
     near, targets = (b, c, d), (w_qkv, w_so, w_out)
     start_copies(place, near, (other_b, other_c, other_d), targets, sems)
-    for section, ref in enumerate((own_qkv, own_so, own_out)):
-        to = pl.multiple_of(place[1] * BLOCK[section], 16)
-        targets[section][pl.ds(to, BLOCK[section]), :] = ref[...]
+    for section, rows in enumerate(BLOCK):
+        to = pl.multiple_of(place[1] * rows, 16)
+        targets[section][pl.ds(to, rows), :] = own[OWN[section] : OWN[section] + rows, :]
     received = sent[...].reshape(ROWS, 2 * D + ATT)
     tokens, cotangent, mixed_s = received[:, :D], received[:, D : 2 * D], received[:, 2 * D :]
     cot_out[...] = cotangent
@@ -298,10 +299,16 @@
     return lax.ppermute(a, "core", [(0, 1), (1, 0)])
 
 
+SENDERS = (
+    ((0, 0), (1, 2), (0, 1), (3, 3), (1, 1), (0, 3), (3, 0), (0, 2)),
+    ((0, 5), (1, 7), (0, 4), (1, 6), (1, 4), (2, 6), (1, 5), (2, 7)),
+    ((1, 0), (2, 2), (3, 1), (1, 3), (2, 1), (2, 3), (2, 0), (3, 2)),
+    ((3, 5), (0, 7), (2, 4), (0, 6), (3, 4), (3, 6), (2, 5), (3, 7)),
+)
+
+
 def class_source(x, y, z, core):
-    ylo, yhi = y % 2, y // 2
-    cls = (x % 2) * 2 + ylo
-    return (x // 2) * 2 + yhi // 2, cls * 2 + yhi % 2, z
+    return *SENDERS[x][y], z
 
 
 def near_source(dx, dy):
@@ -318,8 +325,8 @@
     mine = lax.all_gather(shard, "z", axis=0, tiled=True)
     other = swap_cores(mine)
     rows = lambda n: ((n, D), BF)
-    own_so, own_out, own_qkv, part = call(
-        compact_kernel, [rows(144), rows(144), rows(432), rows(384)], place, mine, other, scalars=1,
+    own, part = call(
+        compact_kernel, [rows(720), rows(384)], place, mine, other, scalars=1,
         scratch=[
             pltpu.VMEM((2, 384, D), BF),
             pltpu.VMEM((144, D), F32),
@@ -328,9 +335,10 @@
         ],
     )
     part, sent = lax.optimization_barrier((part, sent))
-    near = [receive(part, near_source(dx, dy)) for dx, dy in ((1, 0), (0, 1), (1, 1))]
+    near = [receive(part, near_source(1, 0)), receive(part, near_source(0, 1))]
+    near.append(receive(near[1], near_source(1, 0)))
     sent = exchange(sent)
-    return [own_qkv, own_so, own_out] + near + [swap_cores(a) for a in near], sent
+    return [own] + near + [swap_cores(a) for a in near], sent
 
 
 def body(tokens, qkv, w_so, w_qkv, w_out, factors, cotangent):

time: 185 us -> 195 us (1.054)
  the two profiles are of different devices: /device:TPU:169 before, /device:TPU:105 now
where the time goes in v14:
time: 195 us; the launch traced here: 194 us
  blocking collectives  74.7 us (38%)
  starting transfers between devices  54.2 us (28%)
  waiting for transfers between devices  34.2 us (18%)
  Pallas kernels  19 us (10%)
  local copies, waits for them, and re-layouts  7.95 us (4%)
  other arithmetic  3.4 us (2%)
    all_to_all x1, blocking collectives, exchange(): return lax.all_to_all(a, SEQ, 0, 0, tiled=True)  48.5 us
    all_gather x1, blocking collectives, gather_weights(): mine = lax.all_gather(shard, 'z', axis=0, tiled=True)  26.2 us
    all_to_all x1, waiting for transfers between devices, exchange(): return lax.all_to_all(a, SEQ, 0, 0, tiled=True)  23.6 us
    ppermute x6, starting transfers between devices, swap_cores(): return lax.ppermute(a, 'core', [(0, 1), (1, 0)])  19.8 us
    pallas_call x7, Pallas kernels, call(): pl.pallas_call(kernel, out_shape=[jax.ShapeDtypeStruct(s, d) for s, d in...  19 us
    ppermute x4, starting transfers between devices, receive(): return lax.ppermute(a, AXES, pairs)  13.3 us
    all_to_all x1, starting transfers between devices, exchange(): return lax.all_to_all(a, SEQ, 0, 0, tiled=True)  13 us
    ppermute x4, waiting for transfers between devices, receive(): return lax.ppermute(a, AXES, pairs)  8.36 us
  transfers between devices with their start and end apart: 12, of which 4 were waited for; matrix products, arithmetic and copies ran while one was open for 3% of the time, Pallas kernels for 4%

profile of v14, /device:TPU:105, one launch (start us, length us, event | category | flops | bytes accessed | tf_op | source)
XLA Modules:
  0.0 194.3 jit_solution(13939386008047100664)
XLA Ops:
  0.7 1.0 maximum_maximum_fusion
  1.7 2.6 %collective-permute-start = (bf16[48,1152]{1,0:T(8,128)(2,1)S(1)}, bf16[48,1152]{1,0:T(8,128)(2,1)S(1)}, u32[]{:S(2)}, u32[]{:S(2)}) collective-permute-start(bf16[48,1152]{1,0:T(8,128)(2,1)S(1)} %maximum_maximum_fusion), channel_id=1, source_target_pairs={{0,0},{1,1},{2,2},{3,3},{4,4},{5,5},{6,6},{7,7},{8,8},{9,9},{10,10... | collective-permute-start | bytes 331784 | tf_op jit(solution)/shard_map/ppermute | solution.py:295
  4.3 1.1 concatenate.38
  5.4 1.1 concatenate.39
  6.7 1.5 shard_map.102
  8.3 1.6 pad_maximum_fusion
  9.9 26.2 %all_gather.3.mine = bf16[384,1152]{1,0:T(8,128)(2,1)S(1)} all-gather(bf16[48,1152]{1,0:T(8,128)(2,1)S(1)} %collective-permute-done), channel_id=1, replica_groups=mesh['x'=4,'ylo'=2,'yhi'=4,'z'=8,'core'=2] {'z'}, dimensions={0}, use_global_device_ids=true | all-gather | bytes 995328 | tf_op jit(solution)/shard_map/all_gather | solution.py:325
  36.1 8.6 %collective-permute-start.1 = (bf16[384,1152]{1,0:T(8,128)(2,1)S(1)}, bf16[384,1152]{1,0:T(8,128)(2,1)S(1)}, u32[]{:S(2)}, u32[]{:S(2)}) collective-permute-start(bf16[384,1152]{1,0:T(8,128)(2,1)S(1)} %all_gather.3.mine), channel_id=1, source_target_pairs={{0,1},{1,0},{2,3},{3,2},{4,5},{5,4},{6,7},{7,6},{8,9},{9,8},{10,11... | collective-permute-start | bytes 2654216 | tf_op jit(solution)/shard_map/ppermute | solution.py:299
  44.8 1.9 collective-permute-done.1.other
  46.8 2.2 %shard_map.103 = (bf16[720,1152]{1,0:T(8,128)(2,1)S(1)}, bf16[384,1152]{1,0:T(8,128)(2,1)}) custom-call(s32[2]{0:T(128)S(1)} %pad_add_fusion.place, bf16[384,1152]{1,0:T(8,128)(2,1)S(1)} %all_gather.3.mine, bf16[384,1152]{1,0:T(8,128)(2,1)S(1)} %collective-permute-done.1.other), custom_call_target="tpu_custom_call" | custom-call | flops 1000000000 | bytes 10000000 | tf_op jit(solution)/shard_map/pallas_call | solution.py:265
  48.9 1.2 copy-done.4
  50.2 6.9 %collective-permute-start.3 = (bf16[384,1152]{1,0:T(8,128)(2,1)}, bf16[384,1152]{1,0:T(8,128)(2,1)S(1)}, u32[]{:S(2)}, u32[]{:S(2)}) collective-permute-start(bf16[384,1152]{1,0:T(8,128)(2,1)} %get-tuple-element.32), channel_id=1, source_target_pairs={{64,0},{113,1},{66,2},{115,3},{68,4},{117,5},{70,6},{119,7},{72,8}... | collective-permute-start | bytes 2654216 | tf_op jit(solution)/shard_map/ppermute | solution.py:295
  57.1 1.9 collective-permute-start.2
  59.0 8.4 %collective-permute-done.3.c = bf16[384,1152]{1,0:T(8,128)(2,1)S(1)} collective-permute-done((bf16[384,1152]{1,0:T(8,128)(2,1)}, bf16[384,1152]{1,0:T(8,128)(2,1)S(1)}, u32[]{:S(2)}, u32[]{:S(2)}) %collective-permute-start.3) | collective-permute-done | bytes 884768 | tf_op jit(solution)/shard_map/ppermute | solution.py:295
  67.4 1.9 collective-permute-start.4
  69.3 13.0 %all-to-all-start = ((bf16[64,2,2880]{2,1,0:T(2,128)(2,1)}), bf16[64,2,2880]{2,1,0:T(2,128)(2,1)S(1)}, u32[]{:S(2)}, u32[]{:S(2)}) async-start(bf16[64,2,2880]{2,1,0:T(2,128)(2,1)} %pad_maximum_fusion), calls=%async_computation | async-start | bytes 1507328 | tf_op jit(solution)/shard_map/all_to_all | solution.py:277
  82.3 2.3 %collective-permute-start.6 = (bf16[384,1152]{1,0:T(8,128)(2,1)S(1)}, bf16[384,1152]{1,0:T(8,128)(2,1)}, u32[]{:S(2)}, u32[]{:S(2)}) collective-permute-start(bf16[384,1152]{1,0:T(8,128)(2,1)S(1)} %collective-permute-done.3.c), channel_id=1, source_target_pairs={{0,1},{1,0},{2,3},{3,2},{4,5},{5,4},{6,7},{7,6},{8,9},{9,8},{10,11... | collective-permute-start | bytes 2654216 | tf_op jit(solution)/shard_map/ppermute | solution.py:299
  84.6 2.1 %collective-permute-start.5 = (bf16[384,1152]{1,0:T(8,128)(2,1)S(1)}, bf16[384,1152]{1,0:T(8,128)(2,1)}, u32[]{:S(2)}, u32[]{:S(2)}) collective-permute-start(bf16[384,1152]{1,0:T(8,128)(2,1)S(1)} %collective-permute-done.2.b), channel_id=1, source_target_pairs={{0,1},{1,0},{2,3},{3,2},{4,5},{5,4},{6,7},{7,6},{8,9},{9,8},{10,11... | collective-permute-start | bytes 2654216 | tf_op jit(solution)/shard_map/ppermute | solution.py:299
  86.7 2.3 %collective-permute-start.7 = (bf16[384,1152]{1,0:T(8,128)(2,1)}, bf16[384,1152]{1,0:T(8,128)(2,1)}, u32[]{:S(2)}, u32[]{:S(2)}) collective-permute-start(bf16[384,1152]{1,0:T(8,128)(2,1)} %collective-permute-done.4.d), channel_id=1, source_target_pairs={{0,1},{1,0},{2,3},{3,2},{4,5},{5,4},{6,7},{7,6},{8,9},{9,8},{10,11... | collective-permute-start | bytes 2654216 | tf_op jit(solution)/shard_map/ppermute | solution.py:299
  89.0 23.6 %all-to-all-done.sent = bf16[64,2,2880]{2,1,0:T(2,128)(2,1)S(1)} async-done(((bf16[64,2,2880]{2,1,0:T(2,128)(2,1)}), bf16[64,2,2880]{2,1,0:T(2,128)(2,1)S(1)}, u32[]{:S(2)}, u32[]{:S(2)}) %all-to-all-start) | async-done | bytes 737312 | tf_op jit(solution)/shard_map/all_to_all | solution.py:277
  112.6 1.4 copy-done.5
  114.0 7.0 %shard_map.104 = (f32[64,5184]{1,0:T(8,128)S(1)}, bf16[64,5184]{1,0:T(8,128)(2,1)S(1)}, bf16[576,1152]{1,0:T(8,128)(2,1)S(1)}, bf16[576,1152]{1,0:T(8,128)(2,1)S...) custom-call(s32[2]{0:T(128)S(1)} %pad_add_fusion.place, ...), custom_call_target="tpu_custom_call" | custom-call | flops 4000000000 | bytes 10000000 | tf_op jit(solution)/shard_map/pallas_call | solution.py:265
  121.0 2.7 %collective-permute-start.8 = (bf16[64,5184]{1,0:T(8,128)(2,1)S(1)}, bf16[64,5184]{1,0:T(8,128)(2,1)S(1)}, u32[]{:S(2)}, u32[]{:S(2)}) collective-permute-start(bf16[64,5184]{1,0:T(8,128)(2,1)S(1)} %get-tuple-element.46), channel_id=1, source_target_pairs={{0,1},{1,0},{2,3},{3,2},{4,5},{5,4},{6,7},{7,6},{8,9},{9,8},{10,11... | collective-permute-start | bytes 1990664 | tf_op jit(solution)/shard_map/ppermute | solution.py:299
  123.7 3.2 %shard_map.105.packed = bf16[128,2304]{1,0:T(8,128)(2,1)S(1)} custom-call(f32[4,1152]{1,0:T(4,128)S(1)} %bitcast.20, bf16[576,1152]{1,0:T(8,128)(2,1)S(1)} %get-tuple-element.33.w_so, bf16[576,1152]{1,0:T(8,128)(2,1)S(1)} %get-tuple-element.34.w_out, bf16[1728,1152]{1,0:T(8,128)(2,1)S(1)} %get-tuple-element.35.w_qkv, ...), custom_call_target="tpu_custom_call" | custom-call | flops 4000000000 | bytes 10000000 | tf_op jit(solution)/shard_map/pallas_call | solution.py:265
  127.5 48.5 %all_to_all.15.back = bf16[64,2,4896]{2,1,0:T(2,128)(2,1)S(1)} all-to-all(bf16[64,2,4896]{2,1,0:T(2,128)(2,1)S(1)} %shard_map.106), channel_id=1, replica_groups=mesh['x'=4,'ylo'=2,'yhi'=4,'z'=8,'core'=2] {'yhi','z','core'}, dimensions={0} | all-to-all | bytes 2506752 | tf_op jit(solution)/shard_map/all_to_all | solution.py:277
  176.1 2.1 %shard_map.107 = (bf16[128,1152]{1,0:T(8,128)(2,1)}, f32[8,2,5184]{2,1,0:T(2,128)}, f32[2,1152]{1,0:T(2,128)S(1)}) custom-call(bf16[64,2,4896]{2,1,0:T(2,128)(2,1)S(1)} %all_to_all.15.back), custom_call_target="tpu_custom_call" | custom-call | flops 100000000 | bytes 10000000 | tf_op jit(solution)/shard_map/pallas_call | solution.py:265
  178.2 8.0 %all-to-all-start.2 = ((f32[8,2,5184]{2,1,0:T(2,128)}), f32[8,2,5184]{2,1,0:T(2,128)S(1)}, u32[]{:S(2)}, u32[]{:S(2)}) async-start(f32[8,2,5184]{2,1,0:T(2,128)} %get-tuple-element.49), calls=%async_computation.2 | async-start | bytes 671744 | tf_op jit(solution)/shard_map/all_to_all | solution.py:379
  186.2 1.9 collective-permute-start.9
  188.1 1.0 copy-done
  189.1 2.4 %shard_map.108 = bf16[128,1728]{1,0:T(8,128)(2,1)S(1)} custom-call(bf16[128,1728]{1,0:T(8,128)(2,1)S(1)} %bitcast.15, bf16[128,1152]{1,0:T(8,128)(2,1)S(1)} %copy-done, f32[4,1152]{1,0:T(4,128)S(1)} %bitcast.21, bf16[576,1152]{1,0:T(8,128)(2,1)S(1)} %copy-done.3), custom_call_target="tpu_custom_call" | custom-call | flops 1000000000 | bytes 10000000 | tf_op jit(solution)/shard_map/pallas_call | solution.py:265
  191.4 1.0 copy.17
  193.6 0.7 reshape.76
  (30 shorter events, 2.2 us)
Async XLA Ops:
  0.6 5.8 %copy-start.6 = (bf16[1,1,128,1728]{2,3,1,0:T(8,128)(2,1)S(1)}, bf16[1,1,128,1728]{2,3,1,0:T(8,128)(2,1)}, u32[]{:S(2)}) copy-start(bf16[1,1,128,1728]{2,3,1,0:T(8,128)(2,1)} %param.8) | copy-start | bytes 1327108
  1.7 8.2 %collective-permute-start = (bf16[48,1152]{1,0:T(8,128)(2,1)S(1)}, bf16[48,1152]{1,0:T(8,128)(2,1)S(1)}, u32[]{:S(2)}, u32[]{:S(2)}) collective-permute-start(bf16[48,1152]{1,0:T(8,128)(2,1)S(1)} %maximum_maximum_fusion), channel_id=1, source_target_pairs={{0,0},{1,1},{2,2},{3,3},{4,4},{5,5},{6,6},{7,7},{8,8},{9,9},{10,10... | collective-permute-start | bytes 331784 | tf_op jit(solution)/shard_map/ppermute | solution.py:295
  36.1 10.7 %collective-permute-start.1 = (bf16[384,1152]{1,0:T(8,128)(2,1)S(1)}, bf16[384,1152]{1,0:T(8,128)(2,1)S(1)}, u32[]{:S(2)}, u32[]{:S(2)}) collective-permute-start(bf16[384,1152]{1,0:T(8,128)(2,1)S(1)} %all_gather.3.mine), channel_id=1, source_target_pairs={{0,1},{1,0},{2,3},{3,2},{4,5},{5,4},{6,7},{7,6},{8,9},{9,8},{10,11... | collective-permute-start | bytes 2654216 | tf_op jit(solution)/shard_map/ppermute | solution.py:299
  48.9 1.2 copy-start.4
  50.2 62.4 %copy-start.1 = (f32[1,4,1152]{2,1,0:T(4,128)S(1)}, f32[1,4,1152]{2,1,0:T(4,128)}, u32[]{:S(2)}) copy-start(f32[1,4,1152]{2,1,0:T(4,128)} %param.12) | copy-start | bytes 55300
  50.2 17.2 %collective-permute-start.3 = (bf16[384,1152]{1,0:T(8,128)(2,1)}, bf16[384,1152]{1,0:T(8,128)(2,1)S(1)}, u32[]{:S(2)}, u32[]{:S(2)}) collective-permute-start(bf16[384,1152]{1,0:T(8,128)(2,1)} %get-tuple-element.32), channel_id=1, source_target_pairs={{64,0},{113,1},{66,2},{115,3},{68,4},{117,5},{70,6},{119,7},{72,8}... | collective-permute-start | bytes 2654216 | tf_op jit(solution)/shard_map/ppermute | solution.py:295
  57.1 27.5 %collective-permute-start.2 = (bf16[384,1152]{1,0:T(8,128)(2,1)}, bf16[384,1152]{1,0:T(8,128)(2,1)S(1)}, u32[]{:S(2)}, u32[]{:S(2)}) collective-permute-start(bf16[384,1152]{1,0:T(8,128)(2,1)} %get-tuple-element.32), channel_id=1, source_target_pairs={{128,0},{385,1},{130,2},{387,3},{132,4},{389,5},{134,6},{391,7},{1... | collective-permute-start | bytes 2654216 | tf_op jit(solution)/shard_map/ppermute | solution.py:295
  67.4 19.3 %collective-permute-start.4 = (bf16[384,1152]{1,0:T(8,128)(2,1)S(1)}, bf16[384,1152]{1,0:T(8,128)(2,1)}, u32[]{:S(2)}, u32[]{:S(2)}) collective-permute-start(bf16[384,1152]{1,0:T(8,128)(2,1)S(1)} %collective-permute-done.3.c), channel_id=1, source_target_pairs={{128,0},{385,1},{130,2},{387,3},{132,4},{389,5},{134,6},{391,7},{1... | collective-permute-start | bytes 2654216 | tf_op jit(solution)/shard_map/ppermute | solution.py:295
  69.3 43.2 %all-to-all-start = ((bf16[64,2,2880]{2,1,0:T(2,128)(2,1)}), bf16[64,2,2880]{2,1,0:T(2,128)(2,1)S(1)}, u32[]{:S(2)}, u32[]{:S(2)}) async-start(bf16[64,2,2880]{2,1,0:T(2,128)(2,1)} %pad_maximum_fusion), calls=%async_computation | async-start | bytes 1507328 | tf_op jit(solution)/shard_map/all_to_all | solution.py:277
  82.3 30.2 %collective-permute-start.6 = (bf16[384,1152]{1,0:T(8,128)(2,1)S(1)}, bf16[384,1152]{1,0:T(8,128)(2,1)}, u32[]{:S(2)}, u32[]{:S(2)}) collective-permute-start(bf16[384,1152]{1,0:T(8,128)(2,1)S(1)} %collective-permute-done.3.c), channel_id=1, source_target_pairs={{0,1},{1,0},{2,3},{3,2},{4,5},{5,4},{6,7},{7,6},{8,9},{9,8},{10,11... | collective-permute-start | bytes 2654216 | tf_op jit(solution)/shard_map/ppermute | solution.py:299
  84.6 27.9 %collective-permute-start.5 = (bf16[384,1152]{1,0:T(8,128)(2,1)S(1)}, bf16[384,1152]{1,0:T(8,128)(2,1)}, u32[]{:S(2)}, u32[]{:S(2)}) collective-permute-start(bf16[384,1152]{1,0:T(8,128)(2,1)S(1)} %collective-permute-done.2.b), channel_id=1, source_target_pairs={{0,1},{1,0},{2,3},{3,2},{4,5},{5,4},{6,7},{7,6},{8,9},{9,8},{10,11... | collective-permute-start | bytes 2654216 | tf_op jit(solution)/shard_map/ppermute | solution.py:299
  86.7 25.8 %collective-permute-start.7 = (bf16[384,1152]{1,0:T(8,128)(2,1)}, bf16[384,1152]{1,0:T(8,128)(2,1)}, u32[]{:S(2)}, u32[]{:S(2)}) collective-permute-start(bf16[384,1152]{1,0:T(8,128)(2,1)} %collective-permute-done.4.d), channel_id=1, source_target_pairs={{0,1},{1,0},{2,3},{3,2},{4,5},{5,4},{6,7},{7,6},{8,9},{9,8},{10,11... | collective-permute-start | bytes 2654216 | tf_op jit(solution)/shard_map/ppermute | solution.py:299
  112.6 1.4 copy-start.5
  121.0 5.9 %copy-start.2 = (bf16[576,1152]{1,0:T(8,128)(2,1)}, bf16[576,1152]{1,0:T(8,128)(2,1)S(1)}, u32[]{:S(2)}) copy-start(bf16[576,1152]{1,0:T(8,128)(2,1)S(1)} %get-tuple-element.33.w_so) | copy-start | bytes 3981316
  121.0 5.9 %collective-permute-start.8 = (bf16[64,5184]{1,0:T(8,128)(2,1)S(1)}, bf16[64,5184]{1,0:T(8,128)(2,1)S(1)}, u32[]{:S(2)}, u32[]{:S(2)}) collective-permute-start(bf16[64,5184]{1,0:T(8,128)(2,1)S(1)} %get-tuple-element.46), channel_id=1, source_target_pairs={{0,1},{1,0},{2,3},{3,2},{4,5},{5,4},{6,7},{7,6},{8,9},{9,8},{10,11... | collective-permute-start | bytes 1990664 | tf_op jit(solution)/shard_map/ppermute | solution.py:299
  176.0 12.0 %copy-start.3 = (bf16[576,1152]{1,0:T(8,128)(2,1)S(1)}, bf16[576,1152]{1,0:T(8,128)(2,1)}, u32[]{:S(2)}) copy-start(bf16[576,1152]{1,0:T(8,128)(2,1)} %copy-done.2) | copy-start | bytes 3981316
  178.2 15.2 %all-to-all-start.2 = ((f32[8,2,5184]{2,1,0:T(2,128)}), f32[8,2,5184]{2,1,0:T(2,128)S(1)}, u32[]{:S(2)}, u32[]{:S(2)}) async-start(f32[8,2,5184]{2,1,0:T(2,128)} %get-tuple-element.49), calls=%async_computation.2 | async-start | bytes 671744 | tf_op jit(solution)/shard_map/all_to_all | solution.py:379
  186.2 6.2 %collective-permute-start.9 = (f32[2,1152]{1,0:T(2,128)S(1)}, f32[2,1152]{1,0:T(2,128)S(1)}, u32[]{:S(2)}, u32[]{:S(2)}) collective-permute-start(f32[2,1152]{1,0:T(2,128)S(1)} %get-tuple-element.48), channel_id=1, source_target_pairs={{0,1},{1,0},{2,3},{3,2},{4,5},{5,4},{6,7},{7,6},{8,9},{9,8},{10,11... | collective-permute-start | bytes 27656 | tf_op jit(solution)/shard_map/ppermute | solution.py:299
  188.1 1.0 copy-start

commit v15 on v14

--- a/solution.py
+++ b/solution.py
@@ -323,6 +323,8 @@
     shard = jnp.concatenate([w_so, w_out, w_qkv.T, jnp.zeros((3, D), BF)], 0)
     shard, sent = lax.optimization_barrier((receive(shard, class_source), sent))
     mine = lax.all_gather(shard, "z", axis=0, tiled=True)
+    mine, sent = lax.optimization_barrier((mine, sent))
+    sent = exchange(sent)
     other = swap_cores(mine)
     rows = lambda n: ((n, D), BF)
     own, part = call(
@@ -334,10 +336,8 @@
             pltpu.VMEM((432, D), F32),
         ],
     )
-    part, sent = lax.optimization_barrier((part, sent))
     near = [receive(part, near_source(1, 0)), receive(part, near_source(0, 1))]
     near.append(receive(near[1], near_source(1, 0)))
-    sent = exchange(sent)
     return [own] + near + [swap_cores(a) for a in near], sent
 
 

time: 195 us -> 195 us (level)
  no operation moved by 1% of the time
where the time goes in v15:
time: 195 us; the launch traced here: 194 us
  blocking collectives  74.7 us (38%)
  starting transfers between devices  54.2 us (28%)
  waiting for transfers between devices  34.2 us (18%)
  Pallas kernels  19 us (10%)
  local copies, waits for them, and re-layouts  7.95 us (4%)
  other arithmetic  3.4 us (2%)
    all_to_all x1, blocking collectives, exchange(): return lax.all_to_all(a, SEQ, 0, 0, tiled=True)  48.5 us
    all_gather x1, blocking collectives, gather_weights(): mine = lax.all_gather(shard, 'z', axis=0, tiled=True)  26.2 us
    all_to_all x1, waiting for transfers between devices, exchange(): return lax.all_to_all(a, SEQ, 0, 0, tiled=True)  23.6 us
    ppermute x6, starting transfers between devices, swap_cores(): return lax.ppermute(a, 'core', [(0, 1), (1, 0)])  19.8 us
    pallas_call x7, Pallas kernels, call(): pl.pallas_call(kernel, out_shape=[jax.ShapeDtypeStruct(s, d) for s, d in...  19 us
    ppermute x4, starting transfers between devices, receive(): return lax.ppermute(a, AXES, pairs)  13.3 us
    all_to_all x1, starting transfers between devices, exchange(): return lax.all_to_all(a, SEQ, 0, 0, tiled=True)  13 us
    ppermute x4, waiting for transfers between devices, receive(): return lax.ppermute(a, AXES, pairs)  8.36 us
  transfers between devices with their start and end apart: 12, of which 4 were waited for; matrix products, arithmetic and copies ran while one was open for 3% of the time, Pallas kernels for 4%

profile of v15, /device:TPU:105, one launch (start us, length us, event | category | flops | bytes accessed | tf_op | source)
XLA Modules:
  0.0 194.3 jit_solution(13939386008047100664)
XLA Ops:
  0.7 1.0 maximum_maximum_fusion
  1.7 2.6 %collective-permute-start = (bf16[48,1152]{1,0:T(8,128)(2,1)S(1)}, bf16[48,1152]{1,0:T(8,128)(2,1)S(1)}, u32[]{:S(2)}, u32[]{:S(2)}) collective-permute-start(bf16[48,1152]{1,0:T(8,128)(2,1)S(1)} %maximum_maximum_fusion), channel_id=1, source_target_pairs={{0,0},{1,1},{2,2},{3,3},{4,4},{5,5},{6,6},{7,7},{8,8},{9,9},{10,10... | collective-permute-start | bytes 331784 | tf_op jit(solution)/shard_map/ppermute | solution.py:295
  4.3 1.1 concatenate.38
  5.4 1.1 concatenate.39
  6.7 1.5 shard_map.102
  8.3 1.6 pad_maximum_fusion
  9.9 26.2 %all_gather.3.mine = bf16[384,1152]{1,0:T(8,128)(2,1)S(1)} all-gather(bf16[48,1152]{1,0:T(8,128)(2,1)S(1)} %collective-permute-done), channel_id=1, replica_groups=mesh['x'=4,'ylo'=2,'yhi'=4,'z'=8,'core'=2] {'z'}, dimensions={0}, use_global_device_ids=true | all-gather | bytes 995328 | tf_op jit(solution)/shard_map/all_gather | solution.py:325
  36.1 8.6 %collective-permute-start.1 = (bf16[384,1152]{1,0:T(8,128)(2,1)S(1)}, bf16[384,1152]{1,0:T(8,128)(2,1)S(1)}, u32[]{:S(2)}, u32[]{:S(2)}) collective-permute-start(bf16[384,1152]{1,0:T(8,128)(2,1)S(1)} %all_gather.3.mine), channel_id=1, source_target_pairs={{0,1},{1,0},{2,3},{3,2},{4,5},{5,4},{6,7},{7,6},{8,9},{9,8},{10,11... | collective-permute-start | bytes 2654216 | tf_op jit(solution)/shard_map/ppermute | solution.py:299
  44.8 1.9 collective-permute-done.1.other
  46.8 2.2 %shard_map.103 = (bf16[720,1152]{1,0:T(8,128)(2,1)S(1)}, bf16[384,1152]{1,0:T(8,128)(2,1)}) custom-call(s32[2]{0:T(128)S(1)} %pad_add_fusion.place, bf16[384,1152]{1,0:T(8,128)(2,1)S(1)} %all_gather.3.mine, bf16[384,1152]{1,0:T(8,128)(2,1)S(1)} %collective-permute-done.1.other), custom_call_target="tpu_custom_call" | custom-call | flops 1000000000 | bytes 10000000 | tf_op jit(solution)/shard_map/pallas_call | solution.py:265
  48.9 1.2 copy-done.4
  50.2 6.9 %collective-permute-start.3 = (bf16[384,1152]{1,0:T(8,128)(2,1)}, bf16[384,1152]{1,0:T(8,128)(2,1)S(1)}, u32[]{:S(2)}, u32[]{:S(2)}) collective-permute-start(bf16[384,1152]{1,0:T(8,128)(2,1)} %get-tuple-element.32), channel_id=1, source_target_pairs={{64,0},{113,1},{66,2},{115,3},{68,4},{117,5},{70,6},{119,7},{72,8}... | collective-permute-start | bytes 2654216 | tf_op jit(solution)/shard_map/ppermute | solution.py:295
  57.1 1.9 collective-permute-start.2
  59.0 8.4 %collective-permute-done.3.c = bf16[384,1152]{1,0:T(8,128)(2,1)S(1)} collective-permute-done((bf16[384,1152]{1,0:T(8,128)(2,1)}, bf16[384,1152]{1,0:T(8,128)(2,1)S(1)}, u32[]{:S(2)}, u32[]{:S(2)}) %collective-permute-start.3) | collective-permute-done | bytes 884768 | tf_op jit(solution)/shard_map/ppermute | solution.py:295
  67.4 1.9 collective-permute-start.4
  69.3 13.0 %all-to-all-start = ((bf16[64,2,2880]{2,1,0:T(2,128)(2,1)}), bf16[64,2,2880]{2,1,0:T(2,128)(2,1)S(1)}, u32[]{:S(2)}, u32[]{:S(2)}) async-start(bf16[64,2,2880]{2,1,0:T(2,128)(2,1)} %pad_maximum_fusion), calls=%async_computation | async-start | bytes 1507328 | tf_op jit(solution)/shard_map/all_to_all | solution.py:277
  82.3 2.3 %collective-permute-start.6 = (bf16[384,1152]{1,0:T(8,128)(2,1)S(1)}, bf16[384,1152]{1,0:T(8,128)(2,1)}, u32[]{:S(2)}, u32[]{:S(2)}) collective-permute-start(bf16[384,1152]{1,0:T(8,128)(2,1)S(1)} %collective-permute-done.3.c), channel_id=1, source_target_pairs={{0,1},{1,0},{2,3},{3,2},{4,5},{5,4},{6,7},{7,6},{8,9},{9,8},{10,11... | collective-permute-start | bytes 2654216 | tf_op jit(solution)/shard_map/ppermute | solution.py:299
  84.6 2.1 %collective-permute-start.5 = (bf16[384,1152]{1,0:T(8,128)(2,1)S(1)}, bf16[384,1152]{1,0:T(8,128)(2,1)}, u32[]{:S(2)}, u32[]{:S(2)}) collective-permute-start(bf16[384,1152]{1,0:T(8,128)(2,1)S(1)} %collective-permute-done.2.b), channel_id=1, source_target_pairs={{0,1},{1,0},{2,3},{3,2},{4,5},{5,4},{6,7},{7,6},{8,9},{9,8},{10,11... | collective-permute-start | bytes 2654216 | tf_op jit(solution)/shard_map/ppermute | solution.py:299
  86.7 2.3 %collective-permute-start.7 = (bf16[384,1152]{1,0:T(8,128)(2,1)}, bf16[384,1152]{1,0:T(8,128)(2,1)}, u32[]{:S(2)}, u32[]{:S(2)}) collective-permute-start(bf16[384,1152]{1,0:T(8,128)(2,1)} %collective-permute-done.4.d), channel_id=1, source_target_pairs={{0,1},{1,0},{2,3},{3,2},{4,5},{5,4},{6,7},{7,6},{8,9},{9,8},{10,11... | collective-permute-start | bytes 2654216 | tf_op jit(solution)/shard_map/ppermute | solution.py:299
  89.0 23.6 %all-to-all-done.sent = bf16[64,2,2880]{2,1,0:T(2,128)(2,1)S(1)} async-done(((bf16[64,2,2880]{2,1,0:T(2,128)(2,1)}), bf16[64,2,2880]{2,1,0:T(2,128)(2,1)S(1)}, u32[]{:S(2)}, u32[]{:S(2)}) %all-to-all-start) | async-done | bytes 737312 | tf_op jit(solution)/shard_map/all_to_all | solution.py:277
  112.6 1.4 copy-done.5
  114.0 7.0 %shard_map.104 = (f32[64,5184]{1,0:T(8,128)S(1)}, bf16[64,5184]{1,0:T(8,128)(2,1)S(1)}, bf16[576,1152]{1,0:T(8,128)(2,1)S(1)}, bf16[576,1152]{1,0:T(8,128)(2,1)S...) custom-call(s32[2]{0:T(128)S(1)} %pad_add_fusion.place, ...), custom_call_target="tpu_custom_call" | custom-call | flops 4000000000 | bytes 10000000 | tf_op jit(solution)/shard_map/pallas_call | solution.py:265
  121.0 2.7 %collective-permute-start.8 = (bf16[64,5184]{1,0:T(8,128)(2,1)S(1)}, bf16[64,5184]{1,0:T(8,128)(2,1)S(1)}, u32[]{:S(2)}, u32[]{:S(2)}) collective-permute-start(bf16[64,5184]{1,0:T(8,128)(2,1)S(1)} %get-tuple-element.46), channel_id=1, source_target_pairs={{0,1},{1,0},{2,3},{3,2},{4,5},{5,4},{6,7},{7,6},{8,9},{9,8},{10,11... | collective-permute-start | bytes 1990664 | tf_op jit(solution)/shard_map/ppermute | solution.py:299
  123.7 3.2 %shard_map.105.packed = bf16[128,2304]{1,0:T(8,128)(2,1)S(1)} custom-call(f32[4,1152]{1,0:T(4,128)S(1)} %bitcast.20, bf16[576,1152]{1,0:T(8,128)(2,1)S(1)} %get-tuple-element.33.w_so, bf16[576,1152]{1,0:T(8,128)(2,1)S(1)} %get-tuple-element.34.w_out, bf16[1728,1152]{1,0:T(8,128)(2,1)S(1)} %get-tuple-element.35.w_qkv, ...), custom_call_target="tpu_custom_call" | custom-call | flops 4000000000 | bytes 10000000 | tf_op jit(solution)/shard_map/pallas_call | solution.py:265
  127.5 48.5 %all_to_all.15.back = bf16[64,2,4896]{2,1,0:T(2,128)(2,1)S(1)} all-to-all(bf16[64,2,4896]{2,1,0:T(2,128)(2,1)S(1)} %shard_map.106), channel_id=1, replica_groups=mesh['x'=4,'ylo'=2,'yhi'=4,'z'=8,'core'=2] {'yhi','z','core'}, dimensions={0} | all-to-all | bytes 2506752 | tf_op jit(solution)/shard_map/all_to_all | solution.py:277
  176.1 2.1 %shard_map.107 = (bf16[128,1152]{1,0:T(8,128)(2,1)}, f32[8,2,5184]{2,1,0:T(2,128)}, f32[2,1152]{1,0:T(2,128)S(1)}) custom-call(bf16[64,2,4896]{2,1,0:T(2,128)(2,1)S(1)} %all_to_all.15.back), custom_call_target="tpu_custom_call" | custom-call | flops 100000000 | bytes 10000000 | tf_op jit(solution)/shard_map/pallas_call | solution.py:265
  178.2 8.0 %all-to-all-start.2 = ((f32[8,2,5184]{2,1,0:T(2,128)}), f32[8,2,5184]{2,1,0:T(2,128)S(1)}, u32[]{:S(2)}, u32[]{:S(2)}) async-start(f32[8,2,5184]{2,1,0:T(2,128)} %get-tuple-element.49), calls=%async_computation.2 | async-start | bytes 671744 | tf_op jit(solution)/shard_map/all_to_all | solution.py:379
  186.2 1.9 collective-permute-start.9
  188.1 1.0 copy-done
  189.1 2.4 %shard_map.108 = bf16[128,1728]{1,0:T(8,128)(2,1)S(1)} custom-call(bf16[128,1728]{1,0:T(8,128)(2,1)S(1)} %bitcast.15, bf16[128,1152]{1,0:T(8,128)(2,1)S(1)} %copy-done, f32[4,1152]{1,0:T(4,128)S(1)} %bitcast.21, bf16[576,1152]{1,0:T(8,128)(2,1)S(1)} %copy-done.3), custom_call_target="tpu_custom_call" | custom-call | flops 1000000000 | bytes 10000000 | tf_op jit(solution)/shard_map/pallas_call | solution.py:265
  191.4 1.0 copy.17
  193.6 0.7 reshape.76
  (30 shorter events, 2.2 us)
Async XLA Ops:
  0.6 5.8 %copy-start.6 = (bf16[1,1,128,1728]{2,3,1,0:T(8,128)(2,1)S(1)}, bf16[1,1,128,1728]{2,3,1,0:T(8,128)(2,1)}, u32[]{:S(2)}) copy-start(bf16[1,1,128,1728]{2,3,1,0:T(8,128)(2,1)} %param.8) | copy-start | bytes 1327108
  1.7 8.2 %collective-permute-start = (bf16[48,1152]{1,0:T(8,128)(2,1)S(1)}, bf16[48,1152]{1,0:T(8,128)(2,1)S(1)}, u32[]{:S(2)}, u32[]{:S(2)}) collective-permute-start(bf16[48,1152]{1,0:T(8,128)(2,1)S(1)} %maximum_maximum_fusion), channel_id=1, source_target_pairs={{0,0},{1,1},{2,2},{3,3},{4,4},{5,5},{6,6},{7,7},{8,8},{9,9},{10,10... | collective-permute-start | bytes 331784 | tf_op jit(solution)/shard_map/ppermute | solution.py:295
  36.1 10.7 %collective-permute-start.1 = (bf16[384,1152]{1,0:T(8,128)(2,1)S(1)}, bf16[384,1152]{1,0:T(8,128)(2,1)S(1)}, u32[]{:S(2)}, u32[]{:S(2)}) collective-permute-start(bf16[384,1152]{1,0:T(8,128)(2,1)S(1)} %all_gather.3.mine), channel_id=1, source_target_pairs={{0,1},{1,0},{2,3},{3,2},{4,5},{5,4},{6,7},{7,6},{8,9},{9,8},{10,11... | collective-permute-start | bytes 2654216 | tf_op jit(solution)/shard_map/ppermute | solution.py:299
  48.9 1.2 copy-start.4
  50.2 62.4 %copy-start.1 = (f32[1,4,1152]{2,1,0:T(4,128)S(1)}, f32[1,4,1152]{2,1,0:T(4,128)}, u32[]{:S(2)}) copy-start(f32[1,4,1152]{2,1,0:T(4,128)} %param.12) | copy-start | bytes 55300
  50.2 17.2 %collective-permute-start.3 = (bf16[384,1152]{1,0:T(8,128)(2,1)}, bf16[384,1152]{1,0:T(8,128)(2,1)S(1)}, u32[]{:S(2)}, u32[]{:S(2)}) collective-permute-start(bf16[384,1152]{1,0:T(8,128)(2,1)} %get-tuple-element.32), channel_id=1, source_target_pairs={{64,0},{113,1},{66,2},{115,3},{68,4},{117,5},{70,6},{119,7},{72,8}... | collective-permute-start | bytes 2654216 | tf_op jit(solution)/shard_map/ppermute | solution.py:295
  57.1 27.5 %collective-permute-start.2 = (bf16[384,1152]{1,0:T(8,128)(2,1)}, bf16[384,1152]{1,0:T(8,128)(2,1)S(1)}, u32[]{:S(2)}, u32[]{:S(2)}) collective-permute-start(bf16[384,1152]{1,0:T(8,128)(2,1)} %get-tuple-element.32), channel_id=1, source_target_pairs={{128,0},{385,1},{130,2},{387,3},{132,4},{389,5},{134,6},{391,7},{1... | collective-permute-start | bytes 2654216 | tf_op jit(solution)/shard_map/ppermute | solution.py:295
  67.4 19.3 %collective-permute-start.4 = (bf16[384,1152]{1,0:T(8,128)(2,1)S(1)}, bf16[384,1152]{1,0:T(8,128)(2,1)}, u32[]{:S(2)}, u32[]{:S(2)}) collective-permute-start(bf16[384,1152]{1,0:T(8,128)(2,1)S(1)} %collective-permute-done.3.c), channel_id=1, source_target_pairs={{128,0},{385,1},{130,2},{387,3},{132,4},{389,5},{134,6},{391,7},{1... | collective-permute-start | bytes 2654216 | tf_op jit(solution)/shard_map/ppermute | solution.py:295
  69.3 43.2 %all-to-all-start = ((bf16[64,2,2880]{2,1,0:T(2,128)(2,1)}), bf16[64,2,2880]{2,1,0:T(2,128)(2,1)S(1)}, u32[]{:S(2)}, u32[]{:S(2)}) async-start(bf16[64,2,2880]{2,1,0:T(2,128)(2,1)} %pad_maximum_fusion), calls=%async_computation | async-start | bytes 1507328 | tf_op jit(solution)/shard_map/all_to_all | solution.py:277
  82.3 30.2 %collective-permute-start.6 = (bf16[384,1152]{1,0:T(8,128)(2,1)S(1)}, bf16[384,1152]{1,0:T(8,128)(2,1)}, u32[]{:S(2)}, u32[]{:S(2)}) collective-permute-start(bf16[384,1152]{1,0:T(8,128)(2,1)S(1)} %collective-permute-done.3.c), channel_id=1, source_target_pairs={{0,1},{1,0},{2,3},{3,2},{4,5},{5,4},{6,7},{7,6},{8,9},{9,8},{10,11... | collective-permute-start | bytes 2654216 | tf_op jit(solution)/shard_map/ppermute | solution.py:299
  84.6 27.9 %collective-permute-start.5 = (bf16[384,1152]{1,0:T(8,128)(2,1)S(1)}, bf16[384,1152]{1,0:T(8,128)(2,1)}, u32[]{:S(2)}, u32[]{:S(2)}) collective-permute-start(bf16[384,1152]{1,0:T(8,128)(2,1)S(1)} %collective-permute-done.2.b), channel_id=1, source_target_pairs={{0,1},{1,0},{2,3},{3,2},{4,5},{5,4},{6,7},{7,6},{8,9},{9,8},{10,11... | collective-permute-start | bytes 2654216 | tf_op jit(solution)/shard_map/ppermute | solution.py:299
  86.7 25.8 %collective-permute-start.7 = (bf16[384,1152]{1,0:T(8,128)(2,1)}, bf16[384,1152]{1,0:T(8,128)(2,1)}, u32[]{:S(2)}, u32[]{:S(2)}) collective-permute-start(bf16[384,1152]{1,0:T(8,128)(2,1)} %collective-permute-done.4.d), channel_id=1, source_target_pairs={{0,1},{1,0},{2,3},{3,2},{4,5},{5,4},{6,7},{7,6},{8,9},{9,8},{10,11... | collective-permute-start | bytes 2654216 | tf_op jit(solution)/shard_map/ppermute | solution.py:299
  112.6 1.4 copy-start.5
  121.0 5.9 %copy-start.2 = (bf16[576,1152]{1,0:T(8,128)(2,1)}, bf16[576,1152]{1,0:T(8,128)(2,1)S(1)}, u32[]{:S(2)}) copy-start(bf16[576,1152]{1,0:T(8,128)(2,1)S(1)} %get-tuple-element.33.w_so) | copy-start | bytes 3981316
  121.0 5.9 %collective-permute-start.8 = (bf16[64,5184]{1,0:T(8,128)(2,1)S(1)}, bf16[64,5184]{1,0:T(8,128)(2,1)S(1)}, u32[]{:S(2)}, u32[]{:S(2)}) collective-permute-start(bf16[64,5184]{1,0:T(8,128)(2,1)S(1)} %get-tuple-element.46), channel_id=1, source_target_pairs={{0,1},{1,0},{2,3},{3,2},{4,5},{5,4},{6,7},{7,6},{8,9},{9,8},{10,11... | collective-permute-start | bytes 1990664 | tf_op jit(solution)/shard_map/ppermute | solution.py:299
  176.0 12.0 %copy-start.3 = (bf16[576,1152]{1,0:T(8,128)(2,1)S(1)}, bf16[576,1152]{1,0:T(8,128)(2,1)}, u32[]{:S(2)}) copy-start(bf16[576,1152]{1,0:T(8,128)(2,1)} %copy-done.2) | copy-start | bytes 3981316
  178.2 15.2 %all-to-all-start.2 = ((f32[8,2,5184]{2,1,0:T(2,128)}), f32[8,2,5184]{2,1,0:T(2,128)S(1)}, u32[]{:S(2)}, u32[]{:S(2)}) async-start(f32[8,2,5184]{2,1,0:T(2,128)} %get-tuple-element.49), calls=%async_computation.2 | async-start | bytes 671744 | tf_op jit(solution)/shard_map/all_to_all | solution.py:379
  186.2 6.2 %collective-permute-start.9 = (f32[2,1152]{1,0:T(2,128)S(1)}, f32[2,1152]{1,0:T(2,128)S(1)}, u32[]{:S(2)}, u32[]{:S(2)}) collective-permute-start(f32[2,1152]{1,0:T(2,128)S(1)} %get-tuple-element.48), channel_id=1, source_target_pairs={{0,1},{1,0},{2,3},{3,2},{4,5},{5,4},{6,7},{7,6},{8,9},{9,8},{10,11... | collective-permute-start | bytes 27656 | tf_op jit(solution)/shard_map/ppermute | solution.py:299
  188.1 1.0 copy-start

commit v16 on v15

--- a/solution.py
+++ b/solution.py
@@ -337,6 +337,7 @@
         ],
     )
     near = [receive(part, near_source(1, 0)), receive(part, near_source(0, 1))]
+    near[1], sent = lax.optimization_barrier((near[1], sent))
     near.append(receive(near[1], near_source(1, 0)))
     return [own] + near + [swap_cores(a) for a in near], sent
 

time: 195 us -> 200 us (1.026)
  the two profiles are of different devices: /device:TPU:105 before, /device:TPU:1 now
where the time goes in v16:
time: 200 us; the launch traced here: 197 us
  blocking collectives  74.3 us (37%)
  starting transfers between devices  54.2 us (27%)
  waiting for transfers between devices  32.1 us (16%)
  Pallas kernels  22.5 us (11%)
  local copies, waits for them, and re-layouts  9.27 us (5%)
  other arithmetic  3.37 us (2%)
    all_to_all x1, blocking collectives, exchange(): return lax.all_to_all(a, SEQ, 0, 0, tiled=True)  46 us
    all_gather x1, blocking collectives, gather_weights(): mine = lax.all_gather(shard, 'z', axis=0, tiled=True)  28.4 us
    pallas_call x7, Pallas kernels, call(): pl.pallas_call(kernel, out_shape=[jax.ShapeDtypeStruct(s, d) for s, d in...  22.5 us
    ppermute x6, starting transfers between devices, swap_cores(): return lax.ppermute(a, 'core', [(0, 1), (1, 0)])  18.2 us
    all_to_all x1, waiting for transfers between devices, exchange(): return lax.all_to_all(a, SEQ, 0, 0, tiled=True)  16.4 us
    all_to_all x1, starting transfers between devices, exchange(): return lax.all_to_all(a, SEQ, 0, 0, tiled=True)  15.2 us
    all_to_all x1, starting transfers between devices, body(): out_part = jnp.sum(lax.all_to_all(out_part, DP, 0, 0, tiled=True), 0)  14.4 us
    ppermute x4, waiting for transfers between devices, receive(): return lax.ppermute(a, AXES, pairs)  13.3 us
  transfers between devices with their start and end apart: 12, of which 4 were waited for; matrix products, arithmetic and copies ran while one was open for 3% of the time, Pallas kernels for 5%

profile of v16, /device:TPU:1, one launch (start us, length us, event | category | flops | bytes accessed | tf_op | source)
XLA Modules:
  0.0 196.7 jit_solution(2057331970862626410)
XLA Ops:
  0.7 1.0 maximum_maximum_fusion
  2.4 1.1 concatenate.38
  3.5 1.1 concatenate.39
  4.8 1.5 shard_map.102
  6.4 1.6 pad_maximum_fusion
  8.0 28.4 %all_gather.3.mine = bf16[384,1152]{1,0:T(8,128)(2,1)S(1)} all-gather(bf16[48,1152]{1,0:T(8,128)(2,1)S(1)} %collective-permute-done), channel_id=1, replica_groups=mesh['x'=4,'ylo'=2,'yhi'=4,'z'=8,'core'=2] {'z'}, dimensions={0}, use_global_device_ids=true | all-gather | bytes 995328 | tf_op jit(solution)/shard_map/all_gather | solution.py:325
  36.4 7.8 %collective-permute-start.1 = (bf16[384,1152]{1,0:T(8,128)(2,1)S(1)}, bf16[384,1152]{1,0:T(8,128)(2,1)S(1)}, u32[]{:S(2)}, u32[]{:S(2)}) collective-permute-start(bf16[384,1152]{1,0:T(8,128)(2,1)S(1)} %all_gather.3.mine), channel_id=1, source_target_pairs={{0,1},{1,0},{2,3},{3,2},{4,5},{5,4},{6,7},{7,6},{8,9},{9,8},{10,11... | collective-permute-start | bytes 2654216 | tf_op jit(solution)/shard_map/ppermute | solution.py:299
  44.1 15.2 %all-to-all-start = ((bf16[64,2,2880]{2,1,0:T(2,128)(2,1)}), bf16[64,2,2880]{2,1,0:T(2,128)(2,1)S(1)}, u32[]{:S(2)}, u32[]{:S(2)}) async-start(bf16[64,2,2880]{2,1,0:T(2,128)(2,1)} %pad_maximum_fusion), calls=%async_computation | async-start | bytes 1507328 | tf_op jit(solution)/shard_map/all_to_all | solution.py:277
  59.5 2.2 %shard_map.103 = (bf16[720,1152]{1,0:T(8,128)(2,1)S(1)}, bf16[384,1152]{1,0:T(8,128)(2,1)}) custom-call(s32[2]{0:T(128)S(1)} %pad_add_fusion.place, bf16[384,1152]{1,0:T(8,128)(2,1)S(1)} %all_gather.3.mine, bf16[384,1152]{1,0:T(8,128)(2,1)S(1)} %collective-permute-done.1.other), custom_call_target="tpu_custom_call" | custom-call | flops 1000000000 | bytes 10000000 | tf_op jit(solution)/shard_map/pallas_call | solution.py:265
  61.7 1.2 copy-done.4
  62.9 1.9 collective-permute-start.2
  64.8 1.9 collective-permute-start.3
  66.7 16.4 %all-to-all-done.sent = bf16[64,2,2880]{2,1,0:T(2,128)(2,1)S(1)} async-done(((bf16[64,2,2880]{2,1,0:T(2,128)(2,1)}), bf16[64,2,2880]{2,1,0:T(2,128)(2,1)S(1)}, u32[]{:S(2)}, u32[]{:S(2)}) %all-to-all-start) | async-done | bytes 737312 | tf_op jit(solution)/shard_map/all_to_all | solution.py:277
  83.2 4.6 %collective-permute-done.2.c = bf16[384,1152]{1,0:T(8,128)(2,1)S(1)} collective-permute-done((bf16[384,1152]{1,0:T(8,128)(2,1)}, bf16[384,1152]{1,0:T(8,128)(2,1)S(1)}, u32[]{:S(2)}, u32[]{:S(2)}) %collective-permute-start.2) | collective-permute-done | bytes 884768 | tf_op jit(solution)/shard_map/ppermute | solution.py:295
  87.7 1.9 collective-permute-start.4
  89.6 1.9 collective-permute-start.6
  91.6 2.4 %collective-permute-start.5 = (bf16[384,1152]{1,0:T(8,128)(2,1)S(1)}, bf16[384,1152]{1,0:T(8,128)(2,1)S(1)}, u32[]{:S(2)}, u32[]{:S(2)}) collective-permute-start(bf16[384,1152]{1,0:T(8,128)(2,1)S(1)} %collective-permute-done.3.b), channel_id=1, source_target_pairs={{0,1},{1,0},{2,3},{3,2},{4,5},{5,4},{6,7},{7,6},{8,9},{9,8},{10,11... | collective-permute-start | bytes 2654216 | tf_op jit(solution)/shard_map/ppermute | solution.py:299
  94.0 8.7 %collective-permute-done.4.d = bf16[384,1152]{1,0:T(8,128)(2,1)S(1)} collective-permute-done((bf16[384,1152]{1,0:T(8,128)(2,1)S(1)}, bf16[384,1152]{1,0:T(8,128)(2,1)S(1)}, u32[]{:S(2)}, u32[]{:S(2)}) %collective-permute-start.4) | collective-permute-done | bytes 884768 | tf_op jit(solution)/shard_map/ppermute | solution.py:295
  102.7 1.9 collective-permute-start.7
  104.6 2.4 %collective-permute-done.7.other_d = bf16[384,1152]{1,0:T(8,128)(2,1)S(1)} collective-permute-done((bf16[384,1152]{1,0:T(8,128)(2,1)S(1)}, bf16[384,1152]{1,0:T(8,128)(2,1)S(1)}, u32[]{:S(2)}, u32[]{:S(2)}) %collective-permute-start.7) | collective-permute-done | bytes 884768 | tf_op jit(solution)/shard_map/ppermute | solution.py:299
  107.0 1.4 copy-done.5
  108.5 10.5 %shard_map.104 = (f32[64,5184]{1,0:T(8,128)S(1)}, bf16[64,5184]{1,0:T(8,128)(2,1)S(1)}, bf16[576,1152]{1,0:T(8,128)(2,1)S(1)}, bf16[576,1152]{1,0:T(8,128)(2,1)S...) custom-call(s32[2]{0:T(128)S(1)} %pad_add_fusion.place, ...), custom_call_target="tpu_custom_call" | custom-call | flops 4000000000 | bytes 10000000 | tf_op jit(solution)/shard_map/pallas_call | solution.py:265
  119.0 2.3 %collective-permute-start.8 = (bf16[64,5184]{1,0:T(8,128)(2,1)S(1)}, bf16[64,5184]{1,0:T(8,128)(2,1)S(1)}, u32[]{:S(2)}, u32[]{:S(2)}) collective-permute-start(bf16[64,5184]{1,0:T(8,128)(2,1)S(1)} %get-tuple-element.50), channel_id=1, source_target_pairs={{0,1},{1,0},{2,3},{3,2},{4,5},{5,4},{6,7},{7,6},{8,9},{9,8},{10,11... | collective-permute-start | bytes 1990664 | tf_op jit(solution)/shard_map/ppermute | solution.py:299
  121.2 3.2 %shard_map.105.packed = bf16[128,2304]{1,0:T(8,128)(2,1)S(1)} custom-call(f32[4,1152]{1,0:T(4,128)S(1)} %bitcast.20, bf16[576,1152]{1,0:T(8,128)(2,1)S(1)} %get-tuple-element.37.w_so, bf16[576,1152]{1,0:T(8,128)(2,1)S(1)} %get-tuple-element.38.w_out, bf16[1728,1152]{1,0:T(8,128)(2,1)S(1)} %get-tuple-element.39.w_qkv, ...), custom_call_target="tpu_custom_call" | custom-call | flops 4000000000 | bytes 10000000 | tf_op jit(solution)/shard_map/pallas_call | solution.py:265
  125.1 46.0 %all_to_all.15.back = bf16[64,2,4896]{2,1,0:T(2,128)(2,1)S(1)} all-to-all(bf16[64,2,4896]{2,1,0:T(2,128)(2,1)S(1)} %shard_map.106), channel_id=1, replica_groups=mesh['x'=4,'ylo'=2,'yhi'=4,'z'=8,'core'=2] {'yhi','z','core'}, dimensions={0} | all-to-all | bytes 2506752 | tf_op jit(solution)/shard_map/all_to_all | solution.py:277
  171.0 2.1 %shard_map.107 = (bf16[128,1152]{1,0:T(8,128)(2,1)}, f32[8,2,5184]{2,1,0:T(2,128)}, f32[2,1152]{1,0:T(2,128)S(1)}) custom-call(bf16[64,2,4896]{2,1,0:T(2,128)(2,1)S(1)} %all_to_all.15.back), custom_call_target="tpu_custom_call" | custom-call | flops 100000000 | bytes 10000000 | tf_op jit(solution)/shard_map/pallas_call | solution.py:265
  173.1 14.4 %all-to-all-start.2 = ((f32[8,2,5184]{2,1,0:T(2,128)}), f32[8,2,5184]{2,1,0:T(2,128)S(1)}, u32[]{:S(2)}, u32[]{:S(2)}) async-start(f32[8,2,5184]{2,1,0:T(2,128)} %get-tuple-element.53), calls=%async_computation.2 | async-start | bytes 671744 | tf_op jit(solution)/shard_map/all_to_all | solution.py:380
  187.6 1.9 collective-permute-start.9
  189.5 1.0 copy-done
  190.4 1.3 copy-done.3
  191.8 2.4 %shard_map.108 = bf16[128,1728]{1,0:T(8,128)(2,1)S(1)} custom-call(bf16[128,1728]{1,0:T(8,128)(2,1)S(1)} %bitcast.15, bf16[128,1152]{1,0:T(8,128)(2,1)S(1)} %copy-done, f32[4,1152]{1,0:T(4,128)S(1)} %bitcast.21, bf16[576,1152]{1,0:T(8,128)(2,1)S(1)} %copy-done.3), custom_call_target="tpu_custom_call" | custom-call | flops 1000000000 | bytes 10000000 | tf_op jit(solution)/shard_map/pallas_call | solution.py:265
  194.1 1.0 copy.17
  (30 shorter events, 3.3 us)
Async XLA Ops:
  0.6 3.9 %copy-start.6 = (bf16[1,1,128,1728]{2,3,1,0:T(8,128)(2,1)S(1)}, bf16[1,1,128,1728]{2,3,1,0:T(8,128)(2,1)}, u32[]{:S(2)}) copy-start(bf16[1,1,128,1728]{2,3,1,0:T(8,128)(2,1)} %param.8) | copy-start | bytes 1327108
  1.7 6.2 %collective-permute-start = (bf16[48,1152]{1,0:T(8,128)(2,1)S(1)}, bf16[48,1152]{1,0:T(8,128)(2,1)S(1)}, u32[]{:S(2)}, u32[]{:S(2)}) collective-permute-start(bf16[48,1152]{1,0:T(8,128)(2,1)S(1)} %maximum_maximum_fusion), channel_id=1, source_target_pairs={{0,0},{1,1},{2,2},{3,3},{4,4},{5,5},{6,6},{7,7},{8,8},{9,9},{10,10... | collective-permute-start | bytes 331784 | tf_op jit(solution)/shard_map/ppermute | solution.py:295
  36.4 23.1 %collective-permute-start.1 = (bf16[384,1152]{1,0:T(8,128)(2,1)S(1)}, bf16[384,1152]{1,0:T(8,128)(2,1)S(1)}, u32[]{:S(2)}, u32[]{:S(2)}) collective-permute-start(bf16[384,1152]{1,0:T(8,128)(2,1)S(1)} %all_gather.3.mine), channel_id=1, source_target_pairs={{0,1},{1,0},{2,3},{3,2},{4,5},{5,4},{6,7},{7,6},{8,9},{9,8},{10,11... | collective-permute-start | bytes 2654216 | tf_op jit(solution)/shard_map/ppermute | solution.py:299
  44.1 39.0 %all-to-all-start = ((bf16[64,2,2880]{2,1,0:T(2,128)(2,1)}), bf16[64,2,2880]{2,1,0:T(2,128)(2,1)S(1)}, u32[]{:S(2)}, u32[]{:S(2)}) async-start(bf16[64,2,2880]{2,1,0:T(2,128)(2,1)} %pad_maximum_fusion), calls=%async_computation | async-start | bytes 1507328 | tf_op jit(solution)/shard_map/all_to_all | solution.py:277
  59.5 47.6 %copy-start.1 = (f32[1,4,1152]{2,1,0:T(4,128)S(1)}, f32[1,4,1152]{2,1,0:T(4,128)}, u32[]{:S(2)}) copy-start(f32[1,4,1152]{2,1,0:T(4,128)} %param.12) | copy-start | bytes 55300
  61.7 1.2 copy-start.4
  62.9 24.8 %collective-permute-start.2 = (bf16[384,1152]{1,0:T(8,128)(2,1)}, bf16[384,1152]{1,0:T(8,128)(2,1)S(1)}, u32[]{:S(2)}, u32[]{:S(2)}) collective-permute-start(bf16[384,1152]{1,0:T(8,128)(2,1)} %get-tuple-element.32), channel_id=1, source_target_pairs={{64,0},{113,1},{66,2},{115,3},{68,4},{117,5},{70,6},{119,7},{72,8}... | collective-permute-start | bytes 2654216 | tf_op jit(solution)/shard_map/ppermute | solution.py:295
  64.8 26.8 %collective-permute-start.3 = (bf16[384,1152]{1,0:T(8,128)(2,1)}, bf16[384,1152]{1,0:T(8,128)(2,1)S(1)}, u32[]{:S(2)}, u32[]{:S(2)}) collective-permute-start(bf16[384,1152]{1,0:T(8,128)(2,1)} %get-tuple-element.32), channel_id=1, source_target_pairs={{128,0},{385,1},{130,2},{387,3},{132,4},{389,5},{134,6},{391,7},{1... | collective-permute-start | bytes 2654216 | tf_op jit(solution)/shard_map/ppermute | solution.py:295
  87.7 15.0 %collective-permute-start.4 = (bf16[384,1152]{1,0:T(8,128)(2,1)S(1)}, bf16[384,1152]{1,0:T(8,128)(2,1)S(1)}, u32[]{:S(2)}, u32[]{:S(2)}) collective-permute-start(bf16[384,1152]{1,0:T(8,128)(2,1)S(1)} %collective-permute-done.2.c), channel_id=1, source_target_pairs={{128,0},{385,1},{130,2},{387,3},{132,4},{389,5},{134,6},{391,7},{1... | collective-permute-start | bytes 2654216 | tf_op jit(solution)/shard_map/ppermute | solution.py:295
  89.6 15.0 %collective-permute-start.6 = (bf16[384,1152]{1,0:T(8,128)(2,1)S(1)}, bf16[384,1152]{1,0:T(8,128)(2,1)S(1)}, u32[]{:S(2)}, u32[]{:S(2)}) collective-permute-start(bf16[384,1152]{1,0:T(8,128)(2,1)S(1)} %collective-permute-done.2.c), channel_id=1, source_target_pairs={{0,1},{1,0},{2,3},{3,2},{4,5},{5,4},{6,7},{7,6},{8,9},{9,8},{10,11... | collective-permute-start | bytes 2654216 | tf_op jit(solution)/shard_map/ppermute | solution.py:299
  91.6 13.1 %collective-permute-start.5 = (bf16[384,1152]{1,0:T(8,128)(2,1)S(1)}, bf16[384,1152]{1,0:T(8,128)(2,1)S(1)}, u32[]{:S(2)}, u32[]{:S(2)}) collective-permute-start(bf16[384,1152]{1,0:T(8,128)(2,1)S(1)} %collective-permute-done.3.b), channel_id=1, source_target_pairs={{0,1},{1,0},{2,3},{3,2},{4,5},{5,4},{6,7},{7,6},{8,9},{9,8},{10,11... | collective-permute-start | bytes 2654216 | tf_op jit(solution)/shard_map/ppermute | solution.py:299
  102.7 4.3 %collective-permute-start.7 = (bf16[384,1152]{1,0:T(8,128)(2,1)S(1)}, bf16[384,1152]{1,0:T(8,128)(2,1)S(1)}, u32[]{:S(2)}, u32[]{:S(2)}) collective-permute-start(bf16[384,1152]{1,0:T(8,128)(2,1)S(1)} %collective-permute-done.4.d), channel_id=1, source_target_pairs={{0,1},{1,0},{2,3},{3,2},{4,5},{5,4},{6,7},{7,6},{8,9},{9,8},{10,11... | collective-permute-start | bytes 2654216 | tf_op jit(solution)/shard_map/ppermute | solution.py:299
  107.0 1.4 copy-start.5
  119.0 5.5 %copy-start.2 = (bf16[576,1152]{1,0:T(8,128)(2,1)}, bf16[576,1152]{1,0:T(8,128)(2,1)S(1)}, u32[]{:S(2)}) copy-start(bf16[576,1152]{1,0:T(8,128)(2,1)S(1)} %get-tuple-element.37.w_so) | copy-start | bytes 3981316
  119.0 5.5 %collective-permute-start.8 = (bf16[64,5184]{1,0:T(8,128)(2,1)S(1)}, bf16[64,5184]{1,0:T(8,128)(2,1)S(1)}, u32[]{:S(2)}, u32[]{:S(2)}) collective-permute-start(bf16[64,5184]{1,0:T(8,128)(2,1)S(1)} %get-tuple-element.50), channel_id=1, source_target_pairs={{0,1},{1,0},{2,3},{3,2},{4,5},{5,4},{6,7},{7,6},{8,9},{9,8},{10,11... | collective-permute-start | bytes 1990664 | tf_op jit(solution)/shard_map/ppermute | solution.py:299
  173.1 22.6 %all-to-all-start.2 = ((f32[8,2,5184]{2,1,0:T(2,128)}), f32[8,2,5184]{2,1,0:T(2,128)S(1)}, u32[]{:S(2)}, u32[]{:S(2)}) async-start(f32[8,2,5184]{2,1,0:T(2,128)} %get-tuple-element.53), calls=%async_computation.2 | async-start | bytes 671744 | tf_op jit(solution)/shard_map/all_to_all | solution.py:380
  187.6 7.5 %collective-permute-start.9 = (f32[2,1152]{1,0:T(2,128)S(1)}, f32[2,1152]{1,0:T(2,128)S(1)}, u32[]{:S(2)}, u32[]{:S(2)}) collective-permute-start(f32[2,1152]{1,0:T(2,128)S(1)} %get-tuple-element.52), channel_id=1, source_target_pairs={{0,1},{1,0},{2,3},{3,2},{4,5},{5,4},{6,7},{7,6},{8,9},{9,8},{10,11... | collective-permute-start | bytes 27656 | tf_op jit(solution)/shard_map/ppermute | solution.py:299
  189.5 1.0 copy-start
  190.4 1.3 copy-start.3

commit v17 on v14

--- a/solution.py
+++ b/solution.py
@@ -299,16 +299,10 @@
     return lax.ppermute(a, "core", [(0, 1), (1, 0)])
 
 
-SENDERS = (
-    ((0, 0), (1, 2), (0, 1), (3, 3), (1, 1), (0, 3), (3, 0), (0, 2)),
-    ((0, 5), (1, 7), (0, 4), (1, 6), (1, 4), (2, 6), (1, 5), (2, 7)),
-    ((1, 0), (2, 2), (3, 1), (1, 3), (2, 1), (2, 3), (2, 0), (3, 2)),
-    ((3, 5), (0, 7), (2, 4), (0, 6), (3, 4), (3, 6), (2, 5), (3, 7)),
-)
-
-
 def class_source(x, y, z, core):
-    return *SENDERS[x][y], z
+    ylo, yhi = y % 2, y // 2
+    cls = (x % 2) * 2 + ylo
+    return (x // 2) * 2 + yhi // 2, cls * 2 + yhi % 2, z
 
 
 def near_source(dx, dy):
@@ -335,8 +329,7 @@
         ],
     )
     part, sent = lax.optimization_barrier((part, sent))
-    near = [receive(part, near_source(1, 0)), receive(part, near_source(0, 1))]
-    near.append(receive(near[1], near_source(1, 0)))
+    near = [receive(part, near_source(dx, dy)) for dx, dy in ((1, 0), (0, 1), (1, 1))]
     sent = exchange(sent)
     return [own] + near + [swap_cores(a) for a in near], sent
 

time: 195 us -> 185 us (0.949)
  the two profiles are of different devices: /device:TPU:105 before, /device:TPU:65 now
where the time goes in v17:
time: 185 us; the launch traced here: 184 us
  starting transfers between devices  69.6 us (38%)
  blocking collectives  66.6 us (36%)
  Pallas kernels  18.9 us (10%)
  waiting for transfers between devices  16.6 us (9%)
  local copies, waits for them, and re-layouts  7.96 us (4%)
  other arithmetic  3.4 us (2%)
    all_to_all x1, blocking collectives, exchange(): return lax.all_to_all(a, SEQ, 0, 0, tiled=True)  40.2 us
    all_gather x1, blocking collectives, gather_weights(): mine = lax.all_gather(shard, 'z', axis=0, tiled=True)  26.4 us
    ppermute x6, starting transfers between devices, swap_cores(): return lax.ppermute(a, 'core', [(0, 1), (1, 0)])  24.9 us
    pallas_call x7, Pallas kernels, call(): pl.pallas_call(kernel, out_shape=[jax.ShapeDtypeStruct(s, d) for s, d in...  18.9 us
    all_to_all x1, starting transfers between devices, body(): out_part = jnp.sum(lax.all_to_all(out_part, DP, 0, 0, tiled=True), 0)  18.1 us
    ppermute x4, starting transfers between devices, receive(): return lax.ppermute(a, AXES, pairs)  16.5 us
    ppermute x4, waiting for transfers between devices, receive(): return lax.ppermute(a, AXES, pairs)  10.4 us
    all_to_all x1, starting transfers between devices, exchange(): return lax.all_to_all(a, SEQ, 0, 0, tiled=True)  10.1 us
  transfers between devices with their start and end apart: 12, of which 5 were waited for; matrix products, arithmetic and copies ran while one was open for 3% of the time, Pallas kernels for 4%

profile of v17, /device:TPU:65, one launch (start us, length us, event | category | flops | bytes accessed | tf_op | source)
XLA Modules:
  0.0 184.0 jit_solution(12142008217322441601)
XLA Ops:
  0.7 1.0 maximum_maximum_fusion
  2.4 1.1 concatenate.38
  3.5 1.1 concatenate.39
  4.8 1.5 shard_map.102
  6.4 1.6 pad_maximum_fusion
  8.0 26.4 %all_gather.3.mine = bf16[384,1152]{1,0:T(8,128)(2,1)S(1)} all-gather(bf16[48,1152]{1,0:T(8,128)(2,1)S(1)} %collective-permute-done), channel_id=1, replica_groups=mesh['x'=4,'ylo'=2,'yhi'=4,'z'=8,'core'=2] {'z'}, dimensions={0}, use_global_device_ids=true | all-gather | bytes 995328 | tf_op jit(solution)/shard_map/all_gather | solution.py:319
  34.4 8.1 %collective-permute-start.1 = (bf16[384,1152]{1,0:T(8,128)(2,1)S(1)}, bf16[384,1152]{1,0:T(8,128)(2,1)S(1)}, u32[]{:S(2)}, u32[]{:S(2)}) collective-permute-start(bf16[384,1152]{1,0:T(8,128)(2,1)S(1)} %all_gather.3.mine), channel_id=1, source_target_pairs={{0,1},{1,0},{2,3},{3,2},{4,5},{5,4},{6,7},{7,6},{8,9},{9,8},{10,11... | collective-permute-start | bytes 2654216 | tf_op jit(solution)/shard_map/ppermute | solution.py:299
  42.6 1.9 %collective-permute-done.1.other = bf16[384,1152]{1,0:T(8,128)(2,1)S(1)} collective-permute-done((bf16[384,1152]{1,0:T(8,128)(2,1)S(1)}, bf16[384,1152]{1,0:T(8,128)(2,1)S(1)}, u32[]{:S(2)}, u32[]{:S(2)}) %collective-permute-start.1) | collective-permute-done | bytes 884768 | tf_op jit(solution)/shard_map/ppermute | solution.py:299
  44.5 2.2 %shard_map.103 = (bf16[720,1152]{1,0:T(8,128)(2,1)S(1)}, bf16[384,1152]{1,0:T(8,128)(2,1)}) custom-call(s32[2]{0:T(128)S(1)} %pad_add_fusion.place, bf16[384,1152]{1,0:T(8,128)(2,1)S(1)} %all_gather.3.mine, bf16[384,1152]{1,0:T(8,128)(2,1)S(1)} %collective-permute-done.1.other), custom_call_target="tpu_custom_call" | custom-call | flops 1000000000 | bytes 10000000 | tf_op jit(solution)/shard_map/pallas_call | solution.py:265
  46.7 1.2 copy-done.4
  47.9 10.7 %collective-permute-start.4 = (bf16[384,1152]{1,0:T(8,128)(2,1)}, bf16[384,1152]{1,0:T(8,128)(2,1)S(1)}, u32[]{:S(2)}, u32[]{:S(2)}) collective-permute-start(bf16[384,1152]{1,0:T(8,128)(2,1)} %get-tuple-element.32), channel_id=1, source_target_pairs={{192,0},{497,1},{194,2},{499,3},{196,4},{501,5},{198,6},{503,7},{2... | collective-permute-start | bytes 2654216 | tf_op jit(solution)/shard_map/ppermute | solution.py:295
  58.6 3.2 %collective-permute-start.3 = (bf16[384,1152]{1,0:T(8,128)(2,1)}, bf16[384,1152]{1,0:T(8,128)(2,1)S(1)}, u32[]{:S(2)}, u32[]{:S(2)}) collective-permute-start(bf16[384,1152]{1,0:T(8,128)(2,1)} %get-tuple-element.32), channel_id=1, source_target_pairs={{64,0},{113,1},{66,2},{115,3},{68,4},{117,5},{70,6},{119,7},{72,8}... | collective-permute-start | bytes 2654216 | tf_op jit(solution)/shard_map/ppermute | solution.py:295
  61.9 1.9 %collective-permute-start.2 = (bf16[384,1152]{1,0:T(8,128)(2,1)}, bf16[384,1152]{1,0:T(8,128)(2,1)}, u32[]{:S(2)}, u32[]{:S(2)}) collective-permute-start(bf16[384,1152]{1,0:T(8,128)(2,1)} %get-tuple-element.32), channel_id=1, source_target_pairs={{128,0},{385,1},{130,2},{387,3},{132,4},{389,5},{134,6},{391,7},{1... | collective-permute-start | bytes 2654216 | tf_op jit(solution)/shard_map/ppermute | solution.py:295
  63.8 10.1 %all-to-all-start = ((bf16[64,2,2880]{2,1,0:T(2,128)(2,1)}), bf16[64,2,2880]{2,1,0:T(2,128)(2,1)S(1)}, u32[]{:S(2)}, u32[]{:S(2)}) async-start(bf16[64,2,2880]{2,1,0:T(2,128)(2,1)} %pad_maximum_fusion), calls=%async_computation | async-start | bytes 1507328 | tf_op jit(solution)/shard_map/all_to_all | solution.py:277
  73.9 2.3 %collective-permute-start.7 = (bf16[384,1152]{1,0:T(8,128)(2,1)S(1)}, bf16[384,1152]{1,0:T(8,128)(2,1)}, u32[]{:S(2)}, u32[]{:S(2)}) collective-permute-start(bf16[384,1152]{1,0:T(8,128)(2,1)S(1)} %collective-permute-done.4.d), channel_id=1, source_target_pairs={{0,1},{1,0},{2,3},{3,2},{4,5},{5,4},{6,7},{7,6},{8,9},{9,8},{10,11... | collective-permute-start | bytes 2654216 | tf_op jit(solution)/shard_map/ppermute | solution.py:299
  76.2 10.4 %collective-permute-done.3.c = bf16[384,1152]{1,0:T(8,128)(2,1)S(1)} collective-permute-done((bf16[384,1152]{1,0:T(8,128)(2,1)}, bf16[384,1152]{1,0:T(8,128)(2,1)S(1)}, u32[]{:S(2)}, u32[]{:S(2)}) %collective-permute-start.3) | collective-permute-done | bytes 884768 | tf_op jit(solution)/shard_map/ppermute | solution.py:295
  86.6 8.2 %collective-permute-start.6 = (bf16[384,1152]{1,0:T(8,128)(2,1)S(1)}, bf16[384,1152]{1,0:T(8,128)(2,1)}, u32[]{:S(2)}, u32[]{:S(2)}) collective-permute-start(bf16[384,1152]{1,0:T(8,128)(2,1)S(1)} %collective-permute-done.3.c), channel_id=1, source_target_pairs={{0,1},{1,0},{2,3},{3,2},{4,5},{5,4},{6,7},{7,6},{8,9},{9,8},{10,11... | collective-permute-start | bytes 2654216 | tf_op jit(solution)/shard_map/ppermute | solution.py:299
  94.8 1.9 %collective-permute-start.5 = (bf16[384,1152]{1,0:T(8,128)(2,1)}, bf16[384,1152]{1,0:T(8,128)(2,1)}, u32[]{:S(2)}, u32[]{:S(2)}) collective-permute-start(bf16[384,1152]{1,0:T(8,128)(2,1)} %collective-permute-done.2.b), channel_id=1, source_target_pairs={{0,1},{1,0},{2,3},{3,2},{4,5},{5,4},{6,7},{7,6},{8,9},{9,8},{10,11... | collective-permute-start | bytes 2654216 | tf_op jit(solution)/shard_map/ppermute | solution.py:299
  96.7 2.3 %all-to-all-done.sent = bf16[64,2,2880]{2,1,0:T(2,128)(2,1)S(1)} async-done(((bf16[64,2,2880]{2,1,0:T(2,128)(2,1)}), bf16[64,2,2880]{2,1,0:T(2,128)(2,1)S(1)}, u32[]{:S(2)}, u32[]{:S(2)}) %all-to-all-start) | async-done | bytes 737312 | tf_op jit(solution)/shard_map/all_to_all | solution.py:277
  99.5 1.4 copy-done.5
  100.9 7.0 %shard_map.104 = (f32[64,5184]{1,0:T(8,128)S(1)}, bf16[64,5184]{1,0:T(8,128)(2,1)S(1)}, bf16[576,1152]{1,0:T(8,128)(2,1)S(1)}, bf16[576,1152]{1,0:T(8,128)(2,1)S...) custom-call(s32[2]{0:T(128)S(1)} %pad_add_fusion.place, ...), custom_call_target="tpu_custom_call" | custom-call | flops 4000000000 | bytes 10000000 | tf_op jit(solution)/shard_map/pallas_call | solution.py:265
  108.0 2.6 %collective-permute-start.8 = (bf16[64,5184]{1,0:T(8,128)(2,1)S(1)}, bf16[64,5184]{1,0:T(8,128)(2,1)S(1)}, u32[]{:S(2)}, u32[]{:S(2)}) collective-permute-start(bf16[64,5184]{1,0:T(8,128)(2,1)S(1)} %get-tuple-element.46), channel_id=1, source_target_pairs={{0,1},{1,0},{2,3},{3,2},{4,5},{5,4},{6,7},{7,6},{8,9},{9,8},{10,11... | collective-permute-start | bytes 1990664 | tf_op jit(solution)/shard_map/ppermute | solution.py:299
  110.5 3.2 %shard_map.105.packed = bf16[128,2304]{1,0:T(8,128)(2,1)S(1)} custom-call(f32[4,1152]{1,0:T(4,128)S(1)} %bitcast.20, bf16[576,1152]{1,0:T(8,128)(2,1)S(1)} %get-tuple-element.33.w_so, bf16[576,1152]{1,0:T(8,128)(2,1)S(1)} %get-tuple-element.34.w_out, bf16[1728,1152]{1,0:T(8,128)(2,1)S(1)} %get-tuple-element.35.w_qkv, ...), custom_call_target="tpu_custom_call" | custom-call | flops 4000000000 | bytes 10000000 | tf_op jit(solution)/shard_map/pallas_call | solution.py:265
  114.3 40.2 %all_to_all.15.back = bf16[64,2,4896]{2,1,0:T(2,128)(2,1)S(1)} all-to-all(bf16[64,2,4896]{2,1,0:T(2,128)(2,1)S(1)} %shard_map.106), channel_id=1, replica_groups=mesh['x'=4,'ylo'=2,'yhi'=4,'z'=8,'core'=2] {'yhi','z','core'}, dimensions={0} | all-to-all | bytes 2506752 | tf_op jit(solution)/shard_map/all_to_all | solution.py:277
  154.5 2.1 %shard_map.107 = (bf16[128,1152]{1,0:T(8,128)(2,1)}, f32[8,2,5184]{2,1,0:T(2,128)}, f32[2,1152]{1,0:T(2,128)S(1)}) custom-call(bf16[64,2,4896]{2,1,0:T(2,128)(2,1)S(1)} %all_to_all.15.back), custom_call_target="tpu_custom_call" | custom-call | flops 100000000 | bytes 10000000 | tf_op jit(solution)/shard_map/pallas_call | solution.py:265
  156.6 18.1 %all-to-all-start.2 = ((f32[8,2,5184]{2,1,0:T(2,128)}), f32[8,2,5184]{2,1,0:T(2,128)S(1)}, u32[]{:S(2)}, u32[]{:S(2)}) async-start(f32[8,2,5184]{2,1,0:T(2,128)} %get-tuple-element.49), calls=%async_computation.2 | async-start | bytes 671744 | tf_op jit(solution)/shard_map/all_to_all | solution.py:372
  174.7 1.9 %collective-permute-start.9 = (f32[2,1152]{1,0:T(2,128)S(1)}, f32[2,1152]{1,0:T(2,128)S(1)}, u32[]{:S(2)}, u32[]{:S(2)}) collective-permute-start(f32[2,1152]{1,0:T(2,128)S(1)} %get-tuple-element.48), channel_id=1, source_target_pairs={{0,1},{1,0},{2,3},{3,2},{4,5},{5,4},{6,7},{7,6},{8,9},{9,8},{10,11... | collective-permute-start | bytes 27656 | tf_op jit(solution)/shard_map/ppermute | solution.py:299
  176.6 1.0 copy-done
  177.6 2.3 %shard_map.108 = bf16[128,1728]{1,0:T(8,128)(2,1)S(1)} custom-call(bf16[128,1728]{1,0:T(8,128)(2,1)S(1)} %bitcast.15, bf16[128,1152]{1,0:T(8,128)(2,1)S(1)} %copy-done, f32[4,1152]{1,0:T(4,128)S(1)} %bitcast.21, bf16[576,1152]{1,0:T(8,128)(2,1)S(1)} %copy-done.3), custom_call_target="tpu_custom_call" | custom-call | flops 1000000000 | bytes 10000000 | tf_op jit(solution)/shard_map/pallas_call | solution.py:265
  180.0 1.0 copy.17
  181.5 1.5 all-to-all-done.2
  183.3 0.7 reshape.76
  (30 shorter events, 3.0 us)
Async XLA Ops:
  0.6 3.9 %copy-start.6 = (bf16[1,1,128,1728]{2,3,1,0:T(8,128)(2,1)S(1)}, bf16[1,1,128,1728]{2,3,1,0:T(8,128)(2,1)}, u32[]{:S(2)}) copy-start(bf16[1,1,128,1728]{2,3,1,0:T(8,128)(2,1)} %param.8) | copy-start | bytes 1327108
  1.7 6.3 %collective-permute-start = (bf16[48,1152]{1,0:T(8,128)(2,1)S(1)}, bf16[48,1152]{1,0:T(8,128)(2,1)S(1)}, u32[]{:S(2)}, u32[]{:S(2)}) collective-permute-start(bf16[48,1152]{1,0:T(8,128)(2,1)S(1)} %maximum_maximum_fusion), channel_id=1, source_target_pairs={{0,0},{1,1},{2,2},{3,3},{4,4},{5,5},{6,6},{7,7},{8,8},{9,9},{10,10... | collective-permute-start | bytes 331784 | tf_op jit(solution)/shard_map/ppermute | solution.py:295
  34.4 10.1 %collective-permute-start.1 = (bf16[384,1152]{1,0:T(8,128)(2,1)S(1)}, bf16[384,1152]{1,0:T(8,128)(2,1)S(1)}, u32[]{:S(2)}, u32[]{:S(2)}) collective-permute-start(bf16[384,1152]{1,0:T(8,128)(2,1)S(1)} %all_gather.3.mine), channel_id=1, source_target_pairs={{0,1},{1,0},{2,3},{3,2},{4,5},{5,4},{6,7},{7,6},{8,9},{9,8},{10,11... | collective-permute-start | bytes 2654216 | tf_op jit(solution)/shard_map/ppermute | solution.py:299
  46.7 1.2 copy-start.4
  47.9 51.6 %copy-start.1 = (f32[1,4,1152]{2,1,0:T(4,128)S(1)}, f32[1,4,1152]{2,1,0:T(4,128)}, u32[]{:S(2)}) copy-start(f32[1,4,1152]{2,1,0:T(4,128)} %param.12) | copy-start | bytes 55300
  47.9 26.0 %collective-permute-start.4 = (bf16[384,1152]{1,0:T(8,128)(2,1)}, bf16[384,1152]{1,0:T(8,128)(2,1)S(1)}, u32[]{:S(2)}, u32[]{:S(2)}) collective-permute-start(bf16[384,1152]{1,0:T(8,128)(2,1)} %get-tuple-element.32), channel_id=1, source_target_pairs={{192,0},{497,1},{194,2},{499,3},{196,4},{501,5},{198,6},{503,7},{2... | collective-permute-start | bytes 2654216 | tf_op jit(solution)/shard_map/ppermute | solution.py:295
  58.6 28.0 %collective-permute-start.3 = (bf16[384,1152]{1,0:T(8,128)(2,1)}, bf16[384,1152]{1,0:T(8,128)(2,1)S(1)}, u32[]{:S(2)}, u32[]{:S(2)}) collective-permute-start(bf16[384,1152]{1,0:T(8,128)(2,1)} %get-tuple-element.32), channel_id=1, source_target_pairs={{64,0},{113,1},{66,2},{115,3},{68,4},{117,5},{70,6},{119,7},{72,8}... | collective-permute-start | bytes 2654216 | tf_op jit(solution)/shard_map/ppermute | solution.py:295
  61.9 32.9 %collective-permute-start.2 = (bf16[384,1152]{1,0:T(8,128)(2,1)}, bf16[384,1152]{1,0:T(8,128)(2,1)}, u32[]{:S(2)}, u32[]{:S(2)}) collective-permute-start(bf16[384,1152]{1,0:T(8,128)(2,1)} %get-tuple-element.32), channel_id=1, source_target_pairs={{128,0},{385,1},{130,2},{387,3},{132,4},{389,5},{134,6},{391,7},{1... | collective-permute-start | bytes 2654216 | tf_op jit(solution)/shard_map/ppermute | solution.py:295
  63.8 35.2 %all-to-all-start = ((bf16[64,2,2880]{2,1,0:T(2,128)(2,1)}), bf16[64,2,2880]{2,1,0:T(2,128)(2,1)S(1)}, u32[]{:S(2)}, u32[]{:S(2)}) async-start(bf16[64,2,2880]{2,1,0:T(2,128)(2,1)} %pad_maximum_fusion), calls=%async_computation | async-start | bytes 1507328 | tf_op jit(solution)/shard_map/all_to_all | solution.py:277
  73.9 25.1 %collective-permute-start.7 = (bf16[384,1152]{1,0:T(8,128)(2,1)S(1)}, bf16[384,1152]{1,0:T(8,128)(2,1)}, u32[]{:S(2)}, u32[]{:S(2)}) collective-permute-start(bf16[384,1152]{1,0:T(8,128)(2,1)S(1)} %collective-permute-done.4.d), channel_id=1, source_target_pairs={{0,1},{1,0},{2,3},{3,2},{4,5},{5,4},{6,7},{7,6},{8,9},{9,8},{10,11... | collective-permute-start | bytes 2654216 | tf_op jit(solution)/shard_map/ppermute | solution.py:299
  86.6 12.4 %collective-permute-start.6 = (bf16[384,1152]{1,0:T(8,128)(2,1)S(1)}, bf16[384,1152]{1,0:T(8,128)(2,1)}, u32[]{:S(2)}, u32[]{:S(2)}) collective-permute-start(bf16[384,1152]{1,0:T(8,128)(2,1)S(1)} %collective-permute-done.3.c), channel_id=1, source_target_pairs={{0,1},{1,0},{2,3},{3,2},{4,5},{5,4},{6,7},{7,6},{8,9},{9,8},{10,11... | collective-permute-start | bytes 2654216 | tf_op jit(solution)/shard_map/ppermute | solution.py:299
  94.8 4.7 %collective-permute-start.5 = (bf16[384,1152]{1,0:T(8,128)(2,1)}, bf16[384,1152]{1,0:T(8,128)(2,1)}, u32[]{:S(2)}, u32[]{:S(2)}) collective-permute-start(bf16[384,1152]{1,0:T(8,128)(2,1)} %collective-permute-done.2.b), channel_id=1, source_target_pairs={{0,1},{1,0},{2,3},{3,2},{4,5},{5,4},{6,7},{7,6},{8,9},{9,8},{10,11... | collective-permute-start | bytes 2654216 | tf_op jit(solution)/shard_map/ppermute | solution.py:299
  99.5 1.4 copy-start.5
  107.9 5.8 %copy-start.2 = (bf16[576,1152]{1,0:T(8,128)(2,1)}, bf16[576,1152]{1,0:T(8,128)(2,1)S(1)}, u32[]{:S(2)}) copy-start(bf16[576,1152]{1,0:T(8,128)(2,1)S(1)} %get-tuple-element.33.w_so) | copy-start | bytes 3981316
  108.0 5.8 %collective-permute-start.8 = (bf16[64,5184]{1,0:T(8,128)(2,1)S(1)}, bf16[64,5184]{1,0:T(8,128)(2,1)S(1)}, u32[]{:S(2)}, u32[]{:S(2)}) collective-permute-start(bf16[64,5184]{1,0:T(8,128)(2,1)S(1)} %get-tuple-element.46), channel_id=1, source_target_pairs={{0,1},{1,0},{2,3},{3,2},{4,5},{5,4},{6,7},{7,6},{8,9},{9,8},{10,11... | collective-permute-start | bytes 1990664 | tf_op jit(solution)/shard_map/ppermute | solution.py:299
  154.5 22.1 %copy-start.3 = (bf16[576,1152]{1,0:T(8,128)(2,1)S(1)}, bf16[576,1152]{1,0:T(8,128)(2,1)}, u32[]{:S(2)}) copy-start(bf16[576,1152]{1,0:T(8,128)(2,1)} %copy-done.2) | copy-start | bytes 3981316
  156.6 26.4 %all-to-all-start.2 = ((f32[8,2,5184]{2,1,0:T(2,128)}), f32[8,2,5184]{2,1,0:T(2,128)S(1)}, u32[]{:S(2)}, u32[]{:S(2)}) async-start(f32[8,2,5184]{2,1,0:T(2,128)} %get-tuple-element.49), calls=%async_computation.2 | async-start | bytes 671744 | tf_op jit(solution)/shard_map/all_to_all | solution.py:372
  174.7 6.2 %collective-permute-start.9 = (f32[2,1152]{1,0:T(2,128)S(1)}, f32[2,1152]{1,0:T(2,128)S(1)}, u32[]{:S(2)}, u32[]{:S(2)}) collective-permute-start(f32[2,1152]{1,0:T(2,128)S(1)} %get-tuple-element.48), channel_id=1, source_target_pairs={{0,1},{1,0},{2,3},{3,2},{4,5},{5,4},{6,7},{7,6},{8,9},{9,8},{10,11... | collective-permute-start | bytes 27656 | tf_op jit(solution)/shard_map/ppermute | solution.py:299
  176.6 1.0 copy-start

commit v18 on v14

--- a/solution.py
+++ b/solution.py
@@ -335,8 +335,7 @@
         ],
     )
     part, sent = lax.optimization_barrier((part, sent))
-    near = [receive(part, near_source(1, 0)), receive(part, near_source(0, 1))]
-    near.append(receive(near[1], near_source(1, 0)))
+    near = [receive(part, near_source(dx, dy)) for dx, dy in ((1, 0), (0, 1), (1, 1))]
     sent = exchange(sent)
     return [own] + near + [swap_cores(a) for a in near], sent
 

time: 195 us -> 187 us (0.959)
  the two profiles are of different devices: /device:TPU:105 before, /device:TPU:1 now
where the time goes in v18:
time: 187 us; the launch traced here: 184 us
  blocking collectives  72 us (39%)
  starting transfers between devices  58.2 us (31%)
  waiting for transfers between devices  22.2 us (12%)
  Pallas kernels  18.9 us (10%)
  local copies, waits for them, and re-layouts  7.95 us (4%)
  other arithmetic  3.4 us (2%)
    all_to_all x1, blocking collectives, exchange(): return lax.all_to_all(a, SEQ, 0, 0, tiled=True)  43.6 us
    all_gather x1, blocking collectives, gather_weights(): mine = lax.all_gather(shard, 'z', axis=0, tiled=True)  28.4 us
    ppermute x6, starting transfers between devices, swap_cores(): return lax.ppermute(a, 'core', [(0, 1), (1, 0)])  19.9 us
    pallas_call x7, Pallas kernels, call(): pl.pallas_call(kernel, out_shape=[jax.ShapeDtypeStruct(s, d) for s, d in...  18.9 us
    ppermute x4, starting transfers between devices, receive(): return lax.ppermute(a, AXES, pairs)  16.1 us
    all_to_all x1, starting transfers between devices, body(): out_part = jnp.sum(lax.all_to_all(out_part, DP, 0, 0, tiled=True), 0)  12.7 us
    ppermute x4, waiting for transfers between devices, receive(): return lax.ppermute(a, AXES, pairs)  12.1 us
    all_to_all x1, starting transfers between devices, exchange(): return lax.all_to_all(a, SEQ, 0, 0, tiled=True)  9.53 us
  transfers between devices with their start and end apart: 12, of which 3 were waited for; matrix products, arithmetic and copies ran while one was open for 3% of the time, Pallas kernels for 4%

profile of v18, /device:TPU:1, one launch (start us, length us, event | category | flops | bytes accessed | tf_op | source)
XLA Modules:
  0.0 183.6 jit_solution(9842393181739953827)
XLA Ops:
  0.7 1.0 maximum_maximum_fusion
  1.7 0.7 collective-permute-start
  2.4 1.1 concatenate.38
  3.5 1.1 concatenate.39
  4.8 1.5 shard_map.102
  6.4 1.6 pad_maximum_fusion
  8.0 28.4 %all_gather.3.mine = bf16[384,1152]{1,0:T(8,128)(2,1)S(1)} all-gather(bf16[48,1152]{1,0:T(8,128)(2,1)S(1)} %collective-permute-done), channel_id=1, replica_groups=mesh['x'=4,'ylo'=2,'yhi'=4,'z'=8,'core'=2] {'z'}, dimensions={0}, use_global_device_ids=true | all-gather | bytes 995328 | tf_op jit(solution)/shard_map/all_gather | solution.py:325
  36.4 7.8 %collective-permute-start.1 = (bf16[384,1152]{1,0:T(8,128)(2,1)S(1)}, bf16[384,1152]{1,0:T(8,128)(2,1)S(1)}, u32[]{:S(2)}, u32[]{:S(2)}) collective-permute-start(bf16[384,1152]{1,0:T(8,128)(2,1)S(1)} %all_gather.3.mine), channel_id=1, source_target_pairs={{0,1},{1,0},{2,3},{3,2},{4,5},{5,4},{6,7},{7,6},{8,9},{9,8},{10,11... | collective-permute-start | bytes 2654216 | tf_op jit(solution)/shard_map/ppermute | solution.py:299
  44.2 1.9 %collective-permute-done.1.other = bf16[384,1152]{1,0:T(8,128)(2,1)S(1)} collective-permute-done((bf16[384,1152]{1,0:T(8,128)(2,1)S(1)}, bf16[384,1152]{1,0:T(8,128)(2,1)S(1)}, u32[]{:S(2)}, u32[]{:S(2)}) %collective-permute-start.1) | collective-permute-done | bytes 884768 | tf_op jit(solution)/shard_map/ppermute | solution.py:299
  46.2 2.2 %shard_map.103 = (bf16[720,1152]{1,0:T(8,128)(2,1)S(1)}, bf16[384,1152]{1,0:T(8,128)(2,1)}) custom-call(s32[2]{0:T(128)S(1)} %pad_add_fusion.place, bf16[384,1152]{1,0:T(8,128)(2,1)S(1)} %all_gather.3.mine, bf16[384,1152]{1,0:T(8,128)(2,1)S(1)} %collective-permute-done.1.other), custom_call_target="tpu_custom_call" | custom-call | flops 1000000000 | bytes 10000000 | tf_op jit(solution)/shard_map/pallas_call | solution.py:265
  48.4 1.2 copy-done.4
  49.6 10.3 %collective-permute-start.4 = (bf16[384,1152]{1,0:T(8,128)(2,1)}, bf16[384,1152]{1,0:T(8,128)(2,1)S(1)}, u32[]{:S(2)}, u32[]{:S(2)}) collective-permute-start(bf16[384,1152]{1,0:T(8,128)(2,1)} %get-tuple-element.32), channel_id=1, source_target_pairs={{192,0},{497,1},{194,2},{499,3},{196,4},{501,5},{198,6},{503,7},{2... | collective-permute-start | bytes 2654216 | tf_op jit(solution)/shard_map/ppermute | solution.py:295
  59.9 1.9 %collective-permute-start.3 = (bf16[384,1152]{1,0:T(8,128)(2,1)}, bf16[384,1152]{1,0:T(8,128)(2,1)S(1)}, u32[]{:S(2)}, u32[]{:S(2)}) collective-permute-start(bf16[384,1152]{1,0:T(8,128)(2,1)} %get-tuple-element.32), channel_id=1, source_target_pairs={{64,0},{113,1},{66,2},{115,3},{68,4},{117,5},{70,6},{119,7},{72,8}... | collective-permute-start | bytes 2654216 | tf_op jit(solution)/shard_map/ppermute | solution.py:295
  61.8 3.1 %collective-permute-start.2 = (bf16[384,1152]{1,0:T(8,128)(2,1)}, bf16[384,1152]{1,0:T(8,128)(2,1)}, u32[]{:S(2)}, u32[]{:S(2)}) collective-permute-start(bf16[384,1152]{1,0:T(8,128)(2,1)} %get-tuple-element.32), channel_id=1, source_target_pairs={{128,0},{385,1},{130,2},{387,3},{132,4},{389,5},{134,6},{391,7},{1... | collective-permute-start | bytes 2654216 | tf_op jit(solution)/shard_map/ppermute | solution.py:295
  65.0 9.5 %all-to-all-start = ((bf16[64,2,2880]{2,1,0:T(2,128)(2,1)}), bf16[64,2,2880]{2,1,0:T(2,128)(2,1)S(1)}, u32[]{:S(2)}, u32[]{:S(2)}) async-start(bf16[64,2,2880]{2,1,0:T(2,128)(2,1)} %pad_maximum_fusion), calls=%async_computation | async-start | bytes 1507328 | tf_op jit(solution)/shard_map/all_to_all | solution.py:277
  74.5 2.4 %collective-permute-start.7 = (bf16[384,1152]{1,0:T(8,128)(2,1)S(1)}, bf16[384,1152]{1,0:T(8,128)(2,1)}, u32[]{:S(2)}, u32[]{:S(2)}) collective-permute-start(bf16[384,1152]{1,0:T(8,128)(2,1)S(1)} %collective-permute-done.4.d), channel_id=1, source_target_pairs={{0,1},{1,0},{2,3},{3,2},{4,5},{5,4},{6,7},{7,6},{8,9},{9,8},{10,11... | collective-permute-start | bytes 2654216 | tf_op jit(solution)/shard_map/ppermute | solution.py:299
  76.9 12.1 %collective-permute-done.3.c = bf16[384,1152]{1,0:T(8,128)(2,1)S(1)} collective-permute-done((bf16[384,1152]{1,0:T(8,128)(2,1)}, bf16[384,1152]{1,0:T(8,128)(2,1)S(1)}, u32[]{:S(2)}, u32[]{:S(2)}) %collective-permute-start.3) | collective-permute-done | bytes 884768 | tf_op jit(solution)/shard_map/ppermute | solution.py:295
  89.0 3.1 %collective-permute-start.6 = (bf16[384,1152]{1,0:T(8,128)(2,1)S(1)}, bf16[384,1152]{1,0:T(8,128)(2,1)}, u32[]{:S(2)}, u32[]{:S(2)}) collective-permute-start(bf16[384,1152]{1,0:T(8,128)(2,1)S(1)} %collective-permute-done.3.c), channel_id=1, source_target_pairs={{0,1},{1,0},{2,3},{3,2},{4,5},{5,4},{6,7},{7,6},{8,9},{9,8},{10,11... | collective-permute-start | bytes 2654216 | tf_op jit(solution)/shard_map/ppermute | solution.py:299
  92.1 1.9 %collective-permute-start.5 = (bf16[384,1152]{1,0:T(8,128)(2,1)}, bf16[384,1152]{1,0:T(8,128)(2,1)}, u32[]{:S(2)}, u32[]{:S(2)}) collective-permute-start(bf16[384,1152]{1,0:T(8,128)(2,1)} %collective-permute-done.2.b), channel_id=1, source_target_pairs={{0,1},{1,0},{2,3},{3,2},{4,5},{5,4},{6,7},{7,6},{8,9},{9,8},{10,11... | collective-permute-start | bytes 2654216 | tf_op jit(solution)/shard_map/ppermute | solution.py:299
  94.0 8.2 %all-to-all-done.sent = bf16[64,2,2880]{2,1,0:T(2,128)(2,1)S(1)} async-done(((bf16[64,2,2880]{2,1,0:T(2,128)(2,1)}), bf16[64,2,2880]{2,1,0:T(2,128)(2,1)S(1)}, u32[]{:S(2)}, u32[]{:S(2)}) %all-to-all-start) | async-done | bytes 737312 | tf_op jit(solution)/shard_map/all_to_all | solution.py:277
  102.3 1.4 copy-done.5
  103.7 7.0 %shard_map.104 = (f32[64,5184]{1,0:T(8,128)S(1)}, bf16[64,5184]{1,0:T(8,128)(2,1)S(1)}, bf16[576,1152]{1,0:T(8,128)(2,1)S(1)}, bf16[576,1152]{1,0:T(8,128)(2,1)S...) custom-call(s32[2]{0:T(128)S(1)} %pad_add_fusion.place, ...), custom_call_target="tpu_custom_call" | custom-call | flops 4000000000 | bytes 10000000 | tf_op jit(solution)/shard_map/pallas_call | solution.py:265
  110.7 2.9 %collective-permute-start.8 = (bf16[64,5184]{1,0:T(8,128)(2,1)S(1)}, bf16[64,5184]{1,0:T(8,128)(2,1)S(1)}, u32[]{:S(2)}, u32[]{:S(2)}) collective-permute-start(bf16[64,5184]{1,0:T(8,128)(2,1)S(1)} %get-tuple-element.46), channel_id=1, source_target_pairs={{0,1},{1,0},{2,3},{3,2},{4,5},{5,4},{6,7},{7,6},{8,9},{9,8},{10,11... | collective-permute-start | bytes 1990664 | tf_op jit(solution)/shard_map/ppermute | solution.py:299
  113.6 3.2 %shard_map.105.packed = bf16[128,2304]{1,0:T(8,128)(2,1)S(1)} custom-call(f32[4,1152]{1,0:T(4,128)S(1)} %bitcast.20, bf16[576,1152]{1,0:T(8,128)(2,1)S(1)} %get-tuple-element.33.w_so, bf16[576,1152]{1,0:T(8,128)(2,1)S(1)} %get-tuple-element.34.w_out, bf16[1728,1152]{1,0:T(8,128)(2,1)S(1)} %get-tuple-element.35.w_qkv, ...), custom_call_target="tpu_custom_call" | custom-call | flops 4000000000 | bytes 10000000 | tf_op jit(solution)/shard_map/pallas_call | solution.py:265
  117.4 43.6 %all_to_all.15.back = bf16[64,2,4896]{2,1,0:T(2,128)(2,1)S(1)} all-to-all(bf16[64,2,4896]{2,1,0:T(2,128)(2,1)S(1)} %shard_map.106), channel_id=1, replica_groups=mesh['x'=4,'ylo'=2,'yhi'=4,'z'=8,'core'=2] {'yhi','z','core'}, dimensions={0} | all-to-all | bytes 2506752 | tf_op jit(solution)/shard_map/all_to_all | solution.py:277
  161.0 2.1 %shard_map.107 = (bf16[128,1152]{1,0:T(8,128)(2,1)}, f32[8,2,5184]{2,1,0:T(2,128)}, f32[2,1152]{1,0:T(2,128)S(1)}) custom-call(bf16[64,2,4896]{2,1,0:T(2,128)(2,1)S(1)} %all_to_all.15.back), custom_call_target="tpu_custom_call" | custom-call | flops 100000000 | bytes 10000000 | tf_op jit(solution)/shard_map/pallas_call | solution.py:265
  163.1 12.7 %all-to-all-start.2 = ((f32[8,2,5184]{2,1,0:T(2,128)}), f32[8,2,5184]{2,1,0:T(2,128)S(1)}, u32[]{:S(2)}, u32[]{:S(2)}) async-start(f32[8,2,5184]{2,1,0:T(2,128)} %get-tuple-element.49), calls=%async_computation.2 | async-start | bytes 671744 | tf_op jit(solution)/shard_map/all_to_all | solution.py:378
  175.8 1.9 %collective-permute-start.9 = (f32[2,1152]{1,0:T(2,128)S(1)}, f32[2,1152]{1,0:T(2,128)S(1)}, u32[]{:S(2)}, u32[]{:S(2)}) collective-permute-start(f32[2,1152]{1,0:T(2,128)S(1)} %get-tuple-element.48), channel_id=1, source_target_pairs={{0,1},{1,0},{2,3},{3,2},{4,5},{5,4},{6,7},{7,6},{8,9},{9,8},{10,11... | collective-permute-start | bytes 27656 | tf_op jit(solution)/shard_map/ppermute | solution.py:299
  177.7 1.0 copy-done
  178.7 2.4 %shard_map.108 = bf16[128,1728]{1,0:T(8,128)(2,1)S(1)} custom-call(bf16[128,1728]{1,0:T(8,128)(2,1)S(1)} %bitcast.15, bf16[128,1152]{1,0:T(8,128)(2,1)S(1)} %copy-done, f32[4,1152]{1,0:T(4,128)S(1)} %bitcast.21, bf16[576,1152]{1,0:T(8,128)(2,1)S(1)} %copy-done.3), custom_call_target="tpu_custom_call" | custom-call | flops 1000000000 | bytes 10000000 | tf_op jit(solution)/shard_map/pallas_call | solution.py:265
  181.0 1.0 copy.17
  182.9 0.7 reshape.76
  (30 shorter events, 1.9 us)
Async XLA Ops:
  0.6 3.9 %copy-start.6 = (bf16[1,1,128,1728]{2,3,1,0:T(8,128)(2,1)S(1)}, bf16[1,1,128,1728]{2,3,1,0:T(8,128)(2,1)}, u32[]{:S(2)}) copy-start(bf16[1,1,128,1728]{2,3,1,0:T(8,128)(2,1)} %param.8) | copy-start | bytes 1327108
  1.7 6.3 %collective-permute-start = (bf16[48,1152]{1,0:T(8,128)(2,1)S(1)}, bf16[48,1152]{1,0:T(8,128)(2,1)S(1)}, u32[]{:S(2)}, u32[]{:S(2)}) collective-permute-start(bf16[48,1152]{1,0:T(8,128)(2,1)S(1)} %maximum_maximum_fusion), channel_id=1, source_target_pairs={{0,0},{1,1},{2,2},{3,3},{4,4},{5,5},{6,6},{7,7},{8,8},{9,9},{10,10... | collective-permute-start | bytes 331784 | tf_op jit(solution)/shard_map/ppermute | solution.py:295
  36.4 9.8 %collective-permute-start.1 = (bf16[384,1152]{1,0:T(8,128)(2,1)S(1)}, bf16[384,1152]{1,0:T(8,128)(2,1)S(1)}, u32[]{:S(2)}, u32[]{:S(2)}) collective-permute-start(bf16[384,1152]{1,0:T(8,128)(2,1)S(1)} %all_gather.3.mine), channel_id=1, source_target_pairs={{0,1},{1,0},{2,3},{3,2},{4,5},{5,4},{6,7},{7,6},{8,9},{9,8},{10,11... | collective-permute-start | bytes 2654216 | tf_op jit(solution)/shard_map/ppermute | solution.py:299
  48.4 1.2 copy-start.4
  49.6 52.7 %copy-start.1 = (f32[1,4,1152]{2,1,0:T(4,128)S(1)}, f32[1,4,1152]{2,1,0:T(4,128)}, u32[]{:S(2)}) copy-start(f32[1,4,1152]{2,1,0:T(4,128)} %param.12) | copy-start | bytes 55300
  49.6 24.9 %collective-permute-start.4 = (bf16[384,1152]{1,0:T(8,128)(2,1)}, bf16[384,1152]{1,0:T(8,128)(2,1)S(1)}, u32[]{:S(2)}, u32[]{:S(2)}) collective-permute-start(bf16[384,1152]{1,0:T(8,128)(2,1)} %get-tuple-element.32), channel_id=1, source_target_pairs={{192,0},{497,1},{194,2},{499,3},{196,4},{501,5},{198,6},{503,7},{2... | collective-permute-start | bytes 2654216 | tf_op jit(solution)/shard_map/ppermute | solution.py:295
  59.9 29.1 %collective-permute-start.3 = (bf16[384,1152]{1,0:T(8,128)(2,1)}, bf16[384,1152]{1,0:T(8,128)(2,1)S(1)}, u32[]{:S(2)}, u32[]{:S(2)}) collective-permute-start(bf16[384,1152]{1,0:T(8,128)(2,1)} %get-tuple-element.32), channel_id=1, source_target_pairs={{64,0},{113,1},{66,2},{115,3},{68,4},{117,5},{70,6},{119,7},{72,8}... | collective-permute-start | bytes 2654216 | tf_op jit(solution)/shard_map/ppermute | solution.py:295
  61.8 30.2 %collective-permute-start.2 = (bf16[384,1152]{1,0:T(8,128)(2,1)}, bf16[384,1152]{1,0:T(8,128)(2,1)}, u32[]{:S(2)}, u32[]{:S(2)}) collective-permute-start(bf16[384,1152]{1,0:T(8,128)(2,1)} %get-tuple-element.32), channel_id=1, source_target_pairs={{128,0},{385,1},{130,2},{387,3},{132,4},{389,5},{134,6},{391,7},{1... | collective-permute-start | bytes 2654216 | tf_op jit(solution)/shard_map/ppermute | solution.py:295
  65.0 37.2 %all-to-all-start = ((bf16[64,2,2880]{2,1,0:T(2,128)(2,1)}), bf16[64,2,2880]{2,1,0:T(2,128)(2,1)S(1)}, u32[]{:S(2)}, u32[]{:S(2)}) async-start(bf16[64,2,2880]{2,1,0:T(2,128)(2,1)} %pad_maximum_fusion), calls=%async_computation | async-start | bytes 1507328 | tf_op jit(solution)/shard_map/all_to_all | solution.py:277
  74.5 27.7 %collective-permute-start.7 = (bf16[384,1152]{1,0:T(8,128)(2,1)S(1)}, bf16[384,1152]{1,0:T(8,128)(2,1)}, u32[]{:S(2)}, u32[]{:S(2)}) collective-permute-start(bf16[384,1152]{1,0:T(8,128)(2,1)S(1)} %collective-permute-done.4.d), channel_id=1, source_target_pairs={{0,1},{1,0},{2,3},{3,2},{4,5},{5,4},{6,7},{7,6},{8,9},{9,8},{10,11... | collective-permute-start | bytes 2654216 | tf_op jit(solution)/shard_map/ppermute | solution.py:299
  89.0 13.3 %collective-permute-start.6 = (bf16[384,1152]{1,0:T(8,128)(2,1)S(1)}, bf16[384,1152]{1,0:T(8,128)(2,1)}, u32[]{:S(2)}, u32[]{:S(2)}) collective-permute-start(bf16[384,1152]{1,0:T(8,128)(2,1)S(1)} %collective-permute-done.3.c), channel_id=1, source_target_pairs={{0,1},{1,0},{2,3},{3,2},{4,5},{5,4},{6,7},{7,6},{8,9},{9,8},{10,11... | collective-permute-start | bytes 2654216 | tf_op jit(solution)/shard_map/ppermute | solution.py:299
  92.1 10.2 %collective-permute-start.5 = (bf16[384,1152]{1,0:T(8,128)(2,1)}, bf16[384,1152]{1,0:T(8,128)(2,1)}, u32[]{:S(2)}, u32[]{:S(2)}) collective-permute-start(bf16[384,1152]{1,0:T(8,128)(2,1)} %collective-permute-done.2.b), channel_id=1, source_target_pairs={{0,1},{1,0},{2,3},{3,2},{4,5},{5,4},{6,7},{7,6},{8,9},{9,8},{10,11... | collective-permute-start | bytes 2654216 | tf_op jit(solution)/shard_map/ppermute | solution.py:299
  102.2 1.4 copy-start.5
  110.7 6.1 %copy-start.2 = (bf16[576,1152]{1,0:T(8,128)(2,1)}, bf16[576,1152]{1,0:T(8,128)(2,1)S(1)}, u32[]{:S(2)}) copy-start(bf16[576,1152]{1,0:T(8,128)(2,1)S(1)} %get-tuple-element.33.w_so) | copy-start | bytes 3981316
  110.7 6.1 %collective-permute-start.8 = (bf16[64,5184]{1,0:T(8,128)(2,1)S(1)}, bf16[64,5184]{1,0:T(8,128)(2,1)S(1)}, u32[]{:S(2)}, u32[]{:S(2)}) collective-permute-start(bf16[64,5184]{1,0:T(8,128)(2,1)S(1)} %get-tuple-element.46), channel_id=1, source_target_pairs={{0,1},{1,0},{2,3},{3,2},{4,5},{5,4},{6,7},{7,6},{8,9},{9,8},{10,11... | collective-permute-start | bytes 1990664 | tf_op jit(solution)/shard_map/ppermute | solution.py:299
  161.0 16.7 %copy-start.3 = (bf16[576,1152]{1,0:T(8,128)(2,1)S(1)}, bf16[576,1152]{1,0:T(8,128)(2,1)}, u32[]{:S(2)}) copy-start(bf16[576,1152]{1,0:T(8,128)(2,1)} %copy-done.2) | copy-start | bytes 3981316
  163.1 19.5 %all-to-all-start.2 = ((f32[8,2,5184]{2,1,0:T(2,128)}), f32[8,2,5184]{2,1,0:T(2,128)S(1)}, u32[]{:S(2)}, u32[]{:S(2)}) async-start(f32[8,2,5184]{2,1,0:T(2,128)} %get-tuple-element.49), calls=%async_computation.2 | async-start | bytes 671744 | tf_op jit(solution)/shard_map/all_to_all | solution.py:378
  175.8 6.2 %collective-permute-start.9 = (f32[2,1152]{1,0:T(2,128)S(1)}, f32[2,1152]{1,0:T(2,128)S(1)}, u32[]{:S(2)}, u32[]{:S(2)}) collective-permute-start(f32[2,1152]{1,0:T(2,128)S(1)} %get-tuple-element.48), channel_id=1, source_target_pairs={{0,1},{1,0},{2,3},{3,2},{4,5},{5,4},{6,7},{7,6},{8,9},{9,8},{10,11... | collective-permute-start | bytes 27656 | tf_op jit(solution)/shard_map/ppermute | solution.py:299
  177.7 1.0 copy-start

commit v19 on v12

--- a/solution.py
+++ b/solution.py
@@ -254,7 +254,7 @@
         for core in range(2):
             total = jnp.sum(jnp.where(first == (core == 0), rows, 0.0), 0, keepdims=True)
             for copy in range(8):
-                out_part[copy, core : core + 1, HALF * r : HALF * r + HALF] = total
+                out_part[copy, core : core + 1, HALF * r : HALF * r + HALF] = total.astype(BF)
 
 
 def call(kernel, outs, *args, scalars=0, hbm=0, scratch=(), flops=10**9):
@@ -365,10 +365,10 @@
     )
     token_grad, out_part, mine = call(
         unpack_kernel,
-        [rows(D), ((8, 2, 2 * HALF), F32), ((2, D), F32)],
+        [rows(D), ((8, 2, 2 * HALF), BF), ((2, D), F32)],
         exchange(packed), flops=10**8,
     )
-    out_part = jnp.sum(lax.all_to_all(out_part, DP, 0, 0, tiled=True), 0)
+    out_part = jnp.sum(lax.all_to_all(out_part, DP, 0, 0, tiled=True).astype(F32), 0)
     out_grad = out_part.reshape(2, 9, ATT).transpose(1, 0, 2).reshape(9, D)
 
     (qkv_grad,) = call(

time: 185 us -> 186 us (level)
  the two profiles are of different devices: /device:TPU:169 before, /device:TPU:105 now
where the time goes in v19:
time: 186 us
  starting transfers between devices  74.4 us (40%)
  waiting for transfers between devices  50.9 us (27%)
  blocking collectives  26.9 us (14%)
  Pallas kernels  20 us (11%)
  local copies, waits for them, and re-layouts  9.17 us (5%)
  other arithmetic  3.44 us (2%)
    all_to_all x2, waiting for transfers between devices, exchange(): return lax.all_to_all(a, SEQ, 0, 0, tiled=True)  47 us
    ppermute x6, starting transfers between devices, swap_cores(): return lax.ppermute(a, 'core', [(0, 1), (1, 0)])  28.5 us
    all_gather x1, blocking collectives, gather_weights(): mine = lax.all_gather(shard, 'z', axis=0, tiled=True)  26.9 us
    all_to_all x2, starting transfers between devices, exchange(): return lax.all_to_all(a, SEQ, 0, 0, tiled=True)  22.6 us
    pallas_call x7, Pallas kernels, call(): pl.pallas_call(kernel, out_shape=[jax.ShapeDtypeStruct(s, d) for s, d in...  20 us
    all_to_all x1, starting transfers between devices, body(): lax.all_to_all(out_part, DP, 0, 0, tiled=True).astype(F32)  11.7 us
    ppermute x4, starting transfers between devices, receive(): return lax.ppermute(a, AXES, pairs)  11.6 us
    unnamed x20, local copies, waits for them, and re-layouts  6.02 us
  transfers between devices with their start and end apart: 13, of which 5 were waited for; matrix products, arithmetic and copies ran while one was open for 3% of the time, Pallas kernels for 4%

profile of v19, /device:TPU:105, one launch (start us, length us, event | category | flops | bytes accessed | tf_op | source)
XLA Modules:
  0.0 185.6 jit_solution(17814430208707101793)
XLA Ops:
  0.7 1.0 maximum_maximum_fusion
  1.7 3.7 %collective-permute-start = (bf16[48,1152]{1,0:T(8,128)(2,1)S(1)}, bf16[48,1152]{1,0:T(8,128)(2,1)S(1)}, u32[]{:S(2)}, u32[]{:S(2)}) collective-permute-start(bf16[48,1152]{1,0:T(8,128)(2,1)S(1)} %maximum_maximum_fusion), channel_id=1, source_target_pairs={{0,0},{1,1},{2,2},{3,3},{4,4},{5,5},{6,6},{7,7},{8,8},{9,9},{10,10... | collective-permute-start | bytes 331784 | tf_op jit(solution)/shard_map/ppermute | solution.py:294
  5.4 1.1 concatenate.38
  6.5 1.1 concatenate.39
  7.8 1.5 shard_map.102
  9.4 1.6 pad_maximum_fusion
  11.5 26.9 %all_gather.3.mine = bf16[384,1152]{1,0:T(8,128)(2,1)S(1)} all-gather(bf16[48,1152]{1,0:T(8,128)(2,1)S(1)} %collective-permute-done), channel_id=1, replica_groups=mesh['x'=4,'ylo'=2,'yhi'=4,'z'=8,'core'=2] {'z'}, dimensions={0}, use_global_device_ids=true | all-gather | bytes 995328 | tf_op jit(solution)/shard_map/all_gather | solution.py:318
  38.3 11.0 %collective-permute-start.1 = (bf16[384,1152]{1,0:T(8,128)(2,1)S(1)}, bf16[384,1152]{1,0:T(8,128)(2,1)S(1)}, u32[]{:S(2)}, u32[]{:S(2)}) collective-permute-start(bf16[384,1152]{1,0:T(8,128)(2,1)S(1)} %all_gather.3.mine), channel_id=1, source_target_pairs={{0,1},{1,0},{2,3},{3,2},{4,5},{5,4},{6,7},{7,6},{8,9},{9,8},{10,11... | collective-permute-start | bytes 2654216 | tf_op jit(solution)/shard_map/ppermute | solution.py:298
  49.4 1.9 %collective-permute-done.1.other = bf16[384,1152]{1,0:T(8,128)(2,1)S(1)} collective-permute-done((bf16[384,1152]{1,0:T(8,128)(2,1)S(1)}, bf16[384,1152]{1,0:T(8,128)(2,1)S(1)}, u32[]{:S(2)}, u32[]{:S(2)}) %collective-permute-start.1) | collective-permute-done | bytes 884768 | tf_op jit(solution)/shard_map/ppermute | solution.py:298
  51.4 2.2 %shard_map.103 = (bf16[144,1152]{1,0:T(8,128)(2,1)S(1)}, bf16[144,1152]{1,0:T(8,128)(2,1)S(1)}, bf16[432,1152]{1,0:T(8,128)(2,1)S(1)}, bf16[384,1152]{1,0:T(8,128)(2,1)}) custom-call(s32[2]{0:T(128)S(1)} %pad_add_fusion.place, bf16[384,1152]{1,0:T(8,128)(2,1)S(1)} %all_gather.3.mine, bf16[384,1152]{1,0:T(8,128)(2,1)S(1)} %collective-permute-done.1.other), custom_call_target="tpu_custom_call" | custom-call | flops 1000000000 | bytes 10000000 | tf_op jit(solution)/shard_map/pallas_call | solution.py:264
  55.2 2.0 %collective-permute-start.4 = (bf16[384,1152]{1,0:T(8,128)(2,1)}, bf16[384,1152]{1,0:T(8,128)(2,1)S(1)}, u32[]{:S(2)}, u32[]{:S(2)}) collective-permute-start(bf16[384,1152]{1,0:T(8,128)(2,1)} %get-tuple-element.36), channel_id=1, source_target_pairs={{192,0},{497,1},{194,2},{499,3},{196,4},{501,5},{198,6},{503,7},{2... | collective-permute-start | bytes 2654216 | tf_op jit(solution)/shard_map/ppermute | solution.py:294
  57.3 1.9 %collective-permute-start.3 = (bf16[384,1152]{1,0:T(8,128)(2,1)}, bf16[384,1152]{1,0:T(8,128)(2,1)S(1)}, u32[]{:S(2)}, u32[]{:S(2)}) collective-permute-start(bf16[384,1152]{1,0:T(8,128)(2,1)} %get-tuple-element.36), channel_id=1, source_target_pairs={{64,0},{113,1},{66,2},{115,3},{68,4},{117,5},{70,6},{119,7},{72,8}... | collective-permute-start | bytes 2654216 | tf_op jit(solution)/shard_map/ppermute | solution.py:294
  59.2 4.0 %collective-permute-start.2 = (bf16[384,1152]{1,0:T(8,128)(2,1)}, bf16[384,1152]{1,0:T(8,128)(2,1)}, u32[]{:S(2)}, u32[]{:S(2)}) collective-permute-start(bf16[384,1152]{1,0:T(8,128)(2,1)} %get-tuple-element.36), channel_id=1, source_target_pairs={{128,0},{385,1},{130,2},{387,3},{132,4},{389,5},{134,6},{391,7},{1... | collective-permute-start | bytes 2654216 | tf_op jit(solution)/shard_map/ppermute | solution.py:294
  63.2 12.1 %all-to-all-start = ((bf16[64,2,2880]{2,1,0:T(2,128)(2,1)}), bf16[64,2,2880]{2,1,0:T(2,128)(2,1)S(1)}, u32[]{:S(2)}, u32[]{:S(2)}) async-start(bf16[64,2,2880]{2,1,0:T(2,128)(2,1)} %pad_maximum_fusion), calls=%async_computation | async-start | bytes 1507328 | tf_op jit(solution)/shard_map/all_to_all | solution.py:276
  75.3 2.3 %collective-permute-start.7 = (bf16[384,1152]{1,0:T(8,128)(2,1)S(1)}, bf16[384,1152]{1,0:T(8,128)(2,1)}, u32[]{:S(2)}, u32[]{:S(2)}) collective-permute-start(bf16[384,1152]{1,0:T(8,128)(2,1)S(1)} %collective-permute-done.4.d), channel_id=1, source_target_pairs={{0,1},{1,0},{2,3},{3,2},{4,5},{5,4},{6,7},{7,6},{8,9},{9,8},{10,11... | collective-permute-start | bytes 2654216 | tf_op jit(solution)/shard_map/ppermute | solution.py:298
  77.6 1.5 collective-permute-done.3.c
  79.0 7.8 %collective-permute-start.6 = (bf16[384,1152]{1,0:T(8,128)(2,1)S(1)}, bf16[384,1152]{1,0:T(8,128)(2,1)}, u32[]{:S(2)}, u32[]{:S(2)}) collective-permute-start(bf16[384,1152]{1,0:T(8,128)(2,1)S(1)} %collective-permute-done.3.c), channel_id=1, source_target_pairs={{0,1},{1,0},{2,3},{3,2},{4,5},{5,4},{6,7},{7,6},{8,9},{9,8},{10,11... | collective-permute-start | bytes 2654216 | tf_op jit(solution)/shard_map/ppermute | solution.py:298
  86.9 1.9 %collective-permute-start.5 = (bf16[384,1152]{1,0:T(8,128)(2,1)}, bf16[384,1152]{1,0:T(8,128)(2,1)}, u32[]{:S(2)}, u32[]{:S(2)}) collective-permute-start(bf16[384,1152]{1,0:T(8,128)(2,1)} %collective-permute-done.2.b), channel_id=1, source_target_pairs={{0,1},{1,0},{2,3},{3,2},{4,5},{5,4},{6,7},{7,6},{8,9},{9,8},{10,11... | collective-permute-start | bytes 2654216 | tf_op jit(solution)/shard_map/ppermute | solution.py:298
  88.8 8.8 %all-to-all-done.sent = bf16[64,2,2880]{2,1,0:T(2,128)(2,1)S(1)} async-done(((bf16[64,2,2880]{2,1,0:T(2,128)(2,1)}), bf16[64,2,2880]{2,1,0:T(2,128)(2,1)S(1)}, u32[]{:S(2)}, u32[]{:S(2)}) %all-to-all-start) | async-done | bytes 737312 | tf_op jit(solution)/shard_map/all_to_all | solution.py:276
  97.6 1.2 copy-done.5
  98.8 1.0 copy-done.7
  99.8 7.0 %shard_map.104 = (f32[64,5184]{1,0:T(8,128)S(1)}, bf16[64,5184]{1,0:T(8,128)(2,1)S(1)}, bf16[576,1152]{1,0:T(8,128)(2,1)S(1)}, bf16[576,1152]{1,0:T(8,128)(2,1)S...) custom-call(s32[2]{0:T(128)S(1)} %pad_add_fusion.place, ...), custom_call_target="tpu_custom_call" | custom-call | flops 4000000000 | bytes 10000000 | tf_op jit(solution)/shard_map/pallas_call | solution.py:264
  106.8 3.6 %collective-permute-start.8 = (bf16[64,5184]{1,0:T(8,128)(2,1)S(1)}, bf16[64,5184]{1,0:T(8,128)(2,1)S(1)}, u32[]{:S(2)}, u32[]{:S(2)}) collective-permute-start(bf16[64,5184]{1,0:T(8,128)(2,1)S(1)} %get-tuple-element.50), channel_id=1, source_target_pairs={{0,1},{1,0},{2,3},{3,2},{4,5},{5,4},{6,7},{7,6},{8,9},{9,8},{10,11... | collective-permute-start | bytes 1990664 | tf_op jit(solution)/shard_map/ppermute | solution.py:298
  110.4 3.2 %shard_map.105.packed = bf16[128,2304]{1,0:T(8,128)(2,1)S(1)} custom-call(f32[4,1152]{1,0:T(4,128)S(1)} %bitcast.20, bf16[576,1152]{1,0:T(8,128)(2,1)S(1)} %get-tuple-element.37.w_so, bf16[576,1152]{1,0:T(8,128)(2,1)S(1)} %get-tuple-element.38.w_out, bf16[1728,1152]{1,0:T(8,128)(2,1)S(1)} %get-tuple-element.39.w_qkv, ...), custom_call_target="tpu_custom_call" | custom-call | flops 4000000000 | bytes 10000000 | tf_op jit(solution)/shard_map/pallas_call | solution.py:264
  113.7 1.6 shard_map.106
  115.3 10.5 %all-to-all-start.1 = ((bf16[64,2,4896]{2,1,0:T(2,128)(2,1)}), bf16[64,2,4896]{2,1,0:T(2,128)(2,1)S(1)}, u32[]{:S(2)}, u32[]{:S(2)}) async-start(bf16[64,2,4896]{2,1,0:T(2,128)(2,1)} %shard_map.106), calls=%async_computation.1 | async-start | bytes 2555904 | tf_op jit(solution)/shard_map/all_to_all | solution.py:276
  125.9 38.2 %all-to-all-done.1.back = bf16[64,2,4896]{2,1,0:T(2,128)(2,1)S(1)} async-done(((bf16[64,2,4896]{2,1,0:T(2,128)(2,1)}), bf16[64,2,4896]{2,1,0:T(2,128)(2,1)S(1)}, u32[]{:S(2)}, u32[]{:S(2)}) %all-to-all-start.1) | async-done | bytes 1253408 | tf_op jit(solution)/shard_map/all_to_all | solution.py:276
  164.1 2.0 %shard_map.107 = (bf16[128,1152]{1,0:T(8,128)(2,1)}, bf16[8,2,5184]{2,1,0:T(2,128)(2,1)}, f32[2,1152]{1,0:T(2,128)S(1)}) custom-call(bf16[64,2,4896]{2,1,0:T(2,128)(2,1)S(1)} %all-to-all-done.1.back), custom_call_target="tpu_custom_call" | custom-call | flops 100000000 | bytes 10000000 | tf_op jit(solution)/shard_map/pallas_call | solution.py:264
  166.1 11.7 %all-to-all-start.2 = ((bf16[8,2,5184]{2,1,0:T(2,128)(2,1)}), bf16[8,2,5184]{2,1,0:T(2,128)(2,1)S(1)}, u32[]{:S(2)}, u32[]{:S(2)}) async-start(bf16[8,2,5184]{2,1,0:T(2,128)(2,1)} %get-tuple-element.53), calls=%async_computation.2 | async-start | bytes 335872 | tf_op jit(solution)/shard_map/all_to_all | solution.py:371
  177.8 1.9 %collective-permute-start.9 = (f32[2,1152]{1,0:T(2,128)S(1)}, f32[2,1152]{1,0:T(2,128)S(1)}, u32[]{:S(2)}, u32[]{:S(2)}) collective-permute-start(f32[2,1152]{1,0:T(2,128)S(1)} %get-tuple-element.52), channel_id=1, source_target_pairs={{0,1},{1,0},{2,3},{3,2},{4,5},{5,4},{6,7},{7,6},{8,9},{9,8},{10,11... | collective-permute-start | bytes 27656 | tf_op jit(solution)/shard_map/ppermute | solution.py:298
  180.6 2.3 %shard_map.108 = bf16[128,1728]{1,0:T(8,128)(2,1)S(1)} custom-call(bf16[128,1728]{1,0:T(8,128)(2,1)S(1)} %bitcast.15, bf16[128,1152]{1,0:T(8,128)(2,1)S(1)} %copy-done, f32[4,1152]{1,0:T(4,128)S(1)} %bitcast.21, bf16[576,1152]{1,0:T(8,128)(2,1)S(1)} %copy-done.3), custom_call_target="tpu_custom_call" | custom-call | flops 1000000000 | bytes 10000000 | tf_op jit(solution)/shard_map/pallas_call | solution.py:264
  183.0 1.0 copy.17
  (35 shorter events, 5.2 us)
Async XLA Ops:
  0.6 7.0 %copy-start.8 = (bf16[1,1,128,1728]{2,3,1,0:T(8,128)(2,1)S(1)}, bf16[1,1,128,1728]{2,3,1,0:T(8,128)(2,1)}, u32[]{:S(2)}) copy-start(bf16[1,1,128,1728]{2,3,1,0:T(8,128)(2,1)} %param.8) | copy-start | bytes 1327108
  1.7 9.7 %collective-permute-start = (bf16[48,1152]{1,0:T(8,128)(2,1)S(1)}, bf16[48,1152]{1,0:T(8,128)(2,1)S(1)}, u32[]{:S(2)}, u32[]{:S(2)}) collective-permute-start(bf16[48,1152]{1,0:T(8,128)(2,1)S(1)} %maximum_maximum_fusion), channel_id=1, source_target_pairs={{0,0},{1,1},{2,2},{3,3},{4,4},{5,5},{6,6},{7,7},{8,8},{9,9},{10,10... | collective-permute-start | bytes 331784 | tf_op jit(solution)/shard_map/ppermute | solution.py:294
  38.3 13.0 %collective-permute-start.1 = (bf16[384,1152]{1,0:T(8,128)(2,1)S(1)}, bf16[384,1152]{1,0:T(8,128)(2,1)S(1)}, u32[]{:S(2)}, u32[]{:S(2)}) collective-permute-start(bf16[384,1152]{1,0:T(8,128)(2,1)S(1)} %all_gather.3.mine), channel_id=1, source_target_pairs={{0,1},{1,0},{2,3},{3,2},{4,5},{5,4},{6,7},{7,6},{8,9},{9,8},{10,11... | collective-permute-start | bytes 2654216 | tf_op jit(solution)/shard_map/ppermute | solution.py:298
  53.5 1.0 copy-start.4
  54.5 0.7 copy-start.6
  55.2 42.4 %copy-start.1 = (f32[1,4,1152]{2,1,0:T(4,128)S(1)}, f32[1,4,1152]{2,1,0:T(4,128)}, u32[]{:S(2)}) copy-start(f32[1,4,1152]{2,1,0:T(4,128)} %param.12) | copy-start | bytes 55300
  55.2 20.0 %collective-permute-start.4 = (bf16[384,1152]{1,0:T(8,128)(2,1)}, bf16[384,1152]{1,0:T(8,128)(2,1)S(1)}, u32[]{:S(2)}, u32[]{:S(2)}) collective-permute-start(bf16[384,1152]{1,0:T(8,128)(2,1)} %get-tuple-element.36), channel_id=1, source_target_pairs={{192,0},{497,1},{194,2},{499,3},{196,4},{501,5},{198,6},{503,7},{2... | collective-permute-start | bytes 2654216 | tf_op jit(solution)/shard_map/ppermute | solution.py:294
  57.3 21.7 %collective-permute-start.3 = (bf16[384,1152]{1,0:T(8,128)(2,1)}, bf16[384,1152]{1,0:T(8,128)(2,1)S(1)}, u32[]{:S(2)}, u32[]{:S(2)}) collective-permute-start(bf16[384,1152]{1,0:T(8,128)(2,1)} %get-tuple-element.36), channel_id=1, source_target_pairs={{64,0},{113,1},{66,2},{115,3},{68,4},{117,5},{70,6},{119,7},{72,8}... | collective-permute-start | bytes 2654216 | tf_op jit(solution)/shard_map/ppermute | solution.py:294
  59.2 27.6 %collective-permute-start.2 = (bf16[384,1152]{1,0:T(8,128)(2,1)}, bf16[384,1152]{1,0:T(8,128)(2,1)}, u32[]{:S(2)}, u32[]{:S(2)}) collective-permute-start(bf16[384,1152]{1,0:T(8,128)(2,1)} %get-tuple-element.36), channel_id=1, source_target_pairs={{128,0},{385,1},{130,2},{387,3},{132,4},{389,5},{134,6},{391,7},{1... | collective-permute-start | bytes 2654216 | tf_op jit(solution)/shard_map/ppermute | solution.py:294
  63.2 34.4 %all-to-all-start = ((bf16[64,2,2880]{2,1,0:T(2,128)(2,1)}), bf16[64,2,2880]{2,1,0:T(2,128)(2,1)S(1)}, u32[]{:S(2)}, u32[]{:S(2)}) async-start(bf16[64,2,2880]{2,1,0:T(2,128)(2,1)} %pad_maximum_fusion), calls=%async_computation | async-start | bytes 1507328 | tf_op jit(solution)/shard_map/all_to_all | solution.py:276
  75.3 22.3 %collective-permute-start.7 = (bf16[384,1152]{1,0:T(8,128)(2,1)S(1)}, bf16[384,1152]{1,0:T(8,128)(2,1)}, u32[]{:S(2)}, u32[]{:S(2)}) collective-permute-start(bf16[384,1152]{1,0:T(8,128)(2,1)S(1)} %collective-permute-done.4.d), channel_id=1, source_target_pairs={{0,1},{1,0},{2,3},{3,2},{4,5},{5,4},{6,7},{7,6},{8,9},{9,8},{10,11... | collective-permute-start | bytes 2654216 | tf_op jit(solution)/shard_map/ppermute | solution.py:298
  79.0 18.6 %collective-permute-start.6 = (bf16[384,1152]{1,0:T(8,128)(2,1)S(1)}, bf16[384,1152]{1,0:T(8,128)(2,1)}, u32[]{:S(2)}, u32[]{:S(2)}) collective-permute-start(bf16[384,1152]{1,0:T(8,128)(2,1)S(1)} %collective-permute-done.3.c), channel_id=1, source_target_pairs={{0,1},{1,0},{2,3},{3,2},{4,5},{5,4},{6,7},{7,6},{8,9},{9,8},{10,11... | collective-permute-start | bytes 2654216 | tf_op jit(solution)/shard_map/ppermute | solution.py:298
  86.9 10.8 %collective-permute-start.5 = (bf16[384,1152]{1,0:T(8,128)(2,1)}, bf16[384,1152]{1,0:T(8,128)(2,1)}, u32[]{:S(2)}, u32[]{:S(2)}) collective-permute-start(bf16[384,1152]{1,0:T(8,128)(2,1)} %collective-permute-done.2.b), channel_id=1, source_target_pairs={{0,1},{1,0},{2,3},{3,2},{4,5},{5,4},{6,7},{7,6},{8,9},{9,8},{10,11... | collective-permute-start | bytes 2654216 | tf_op jit(solution)/shard_map/ppermute | solution.py:298
  97.6 1.2 copy-start.5
  98.8 1.0 copy-start.7
  106.8 6.8 %copy-start.2 = (bf16[576,1152]{1,0:T(8,128)(2,1)}, bf16[576,1152]{1,0:T(8,128)(2,1)S(1)}, u32[]{:S(2)}) copy-start(bf16[576,1152]{1,0:T(8,128)(2,1)S(1)} %get-tuple-element.37.w_so) | copy-start | bytes 3981316
  106.8 6.8 %collective-permute-start.8 = (bf16[64,5184]{1,0:T(8,128)(2,1)S(1)}, bf16[64,5184]{1,0:T(8,128)(2,1)S(1)}, u32[]{:S(2)}, u32[]{:S(2)}) collective-permute-start(bf16[64,5184]{1,0:T(8,128)(2,1)S(1)} %get-tuple-element.50), channel_id=1, source_target_pairs={{0,1},{1,0},{2,3},{3,2},{4,5},{5,4},{6,7},{7,6},{8,9},{9,8},{10,11... | collective-permute-start | bytes 1990664 | tf_op jit(solution)/shard_map/ppermute | solution.py:298
  115.3 64.4 %copy-start.3 = (bf16[576,1152]{1,0:T(8,128)(2,1)S(1)}, bf16[576,1152]{1,0:T(8,128)(2,1)}, u32[]{:S(2)}) copy-start(bf16[576,1152]{1,0:T(8,128)(2,1)} %copy-done.2) | copy-start | bytes 3981316
  115.3 48.8 %all-to-all-start.1 = ((bf16[64,2,4896]{2,1,0:T(2,128)(2,1)}), bf16[64,2,4896]{2,1,0:T(2,128)(2,1)S(1)}, u32[]{:S(2)}, u32[]{:S(2)}) async-start(bf16[64,2,4896]{2,1,0:T(2,128)(2,1)} %shard_map.106), calls=%async_computation.1 | async-start | bytes 2555904 | tf_op jit(solution)/shard_map/all_to_all | solution.py:276
  166.1 18.5 %all-to-all-start.2 = ((bf16[8,2,5184]{2,1,0:T(2,128)(2,1)}), bf16[8,2,5184]{2,1,0:T(2,128)(2,1)S(1)}, u32[]{:S(2)}, u32[]{:S(2)}) async-start(bf16[8,2,5184]{2,1,0:T(2,128)(2,1)} %get-tuple-element.53), calls=%async_computation.2 | async-start | bytes 335872 | tf_op jit(solution)/shard_map/all_to_all | solution.py:371
  177.8 6.2 %collective-permute-start.9 = (f32[2,1152]{1,0:T(2,128)S(1)}, f32[2,1152]{1,0:T(2,128)S(1)}, u32[]{:S(2)}, u32[]{:S(2)}) collective-permute-start(f32[2,1152]{1,0:T(2,128)S(1)} %get-tuple-element.52), channel_id=1, source_target_pairs={{0,1},{1,0},{2,3},{3,2},{4,5},{5,4},{6,7},{7,6},{8,9},{9,8},{10,11... | collective-permute-start | bytes 27656 | tf_op jit(solution)/shard_map/ppermute | solution.py:298
  179.7 1.0 copy-start
